TPU v7x, 32 devices: a whole 2x2x4 slice. The times are simulated.
32 devices in a mesh: group: 2 (over y), seq: 4 (over z), exp: 2 (over x), tp: 2 (over core).
Axes of the slice: x: 2, y: 2, z: 4, core: 2. Of those that a mesh axis runs over, the one named last changes fastest.
Arguments:
- queries: bfloat16 [4, 512, 4096], P(('group', 'exp'), ('seq', 'tp')), parts along dimension 0, may hold values from -18 to 18
- keys_values: bfloat16 [4, 768, 2, 1024], P(('group', 'exp'), ('seq', 'tp')), parts along dimension 0, may hold values from -18 to 18
- prompt_lengths: int32 [4], P(('group', 'exp')), parts along dimension 0, may hold values from 1 to 256, 384 in all
- routes: int32 [4, 512, 8], P(('group', 'exp'), ('seq', 'tp')), parts along dimension 0, may hold values from 0 to 63, all different within a row; in each aligned block of 64 rows (0 to 63, 64 to 127, ..., all dimensions but the last counted through in order) at most 16 rows name the same one
- gate_weights: float32 [4, 512, 8], P(('group', 'exp'), ('seq', 'tp')), parts along dimension 0, may hold values from 0.05 to 0.5
- norm_gain: float32 [4096], replicated, may hold values from 0.5 to 1.5
- w_gate: bfloat16 [2, 4096, 2048], P('tp', None, 'seq'), may hold values from -0.09375 to 0.09375
- w_up: bfloat16 [2, 4096, 2048], P('tp', None, 'seq'), may hold values from -0.09375 to 0.09375
- w_down: bfloat16 [2, 2048, 4096], P('tp', 'seq'), may hold values from -0.125 to 0.125
Outputs:
- mixed: bfloat16 [4, 512, 4096], P(('group', 'exp'), ('seq', 'tp')), parts along dimension 0
There are 2 independent parts, one for each index of `group`. A program takes and returns all parts, laid end to end along the dimension named above; an argument that names none is the same for every part. Nothing has to cross between parts.
Inputs may be any that keep to these rules, and one draw needn't show every extreme that they name: Each token's 8 routes name different experts. Among the 64 consecutive tokens of one device no expert is named by more than 16 tokens, a bound that some block reaches.
All inputs are finite; a program needn't handle non-finite values. No bound on the sum of `prompt_lengths` on one device may be relied on, other than what follows from the above.
Results may differ from a plain program's by a relative error of at most 0.02.
Values may be sent and summed in bfloat16 or wider, within the bound.
No kernel may reach another device: no remote copies, remote signals or barrier semaphores. Data moves between devices by JAX's collectives and lax.ppermute only.
A program may use at most 128 MiB of HBM per device.

v0:
```python
import math

import jax
import jax.numpy as jnp
from jax import lax
from jax.sharding import PartitionSpec as P

HEADS = 32
KV_HEADS = 8
HEAD_DIM = 128
TOP = 8
PROMPT = 256
CAP = 16


epsilon = 1e-06
masked_score = -1e30


def body(
    queries, keys_values, prompt_lengths, routes, gate_weights, norm_gain, w_gate, w_up, w_down
):
    tokens_here = queries.shape[1]
    width = queries.shape[2]
    group_size = HEADS // KV_HEADS
    scale_factor = 1.0 / math.sqrt(HEAD_DIM)
    prompt_length = prompt_lengths[0]
    query_count = group_size * tokens_here
    query_heads = jnp.transpose(
        queries[0].reshape(tokens_here, KV_HEADS, group_size, HEAD_DIM), (1, 2, 0, 3)
    ).reshape(KV_HEADS, query_count, HEAD_DIM)
    head_shape = (KV_HEADS, query_count)
    piece = lax.all_gather(keys_values, ("seq", "tp"), axis=1, tiled=True)
    running_max = jnp.full(head_shape, masked_score, jnp.float32)
    key_count = piece.shape[1]
    key_rows = piece[0, :, 0].reshape(key_count, KV_HEADS, HEAD_DIM)
    value_rows = piece[0, :, 1].reshape(key_count, KV_HEADS, HEAD_DIM)
    scores = (
        jnp.einsum("kqd,nkd->knq", query_heads, key_rows, preferred_element_type=jnp.float32)
        * scale_factor
    )
    position = jnp.arange(key_count, dtype=jnp.int32)
    allowed = (position >= PROMPT) | (position < prompt_length)
    scores = jnp.where(allowed[None, :, None], scores, masked_score)
    new_max = jnp.maximum(running_max, jnp.max(scores, axis=1))
    weights = jnp.exp(scores - new_max[:, None, :])
    running_total = jnp.sum(weights, axis=1)
    running_sum = jnp.einsum(
        "knq,nkd->kqd", weights.astype(jnp.bfloat16), value_rows, preferred_element_type=jnp.float32
    )
    heads_out = (
        (running_sum / running_total[..., None])
        .astype(jnp.bfloat16)
        .reshape(KV_HEADS, group_size, tokens_here, HEAD_DIM)
    )
    attended = jnp.transpose(heads_out, (2, 0, 1, 3)).reshape(tokens_here, width)
    attended_f = attended.astype(jnp.float32)
    mean_square = jnp.mean(attended_f * attended_f, axis=-1, keepdims=True)
    normed = (attended_f * lax.rsqrt(mean_square + epsilon) * norm_gain).astype(jnp.bfloat16)
    window = lax.axis_size("tp")
    route_count = tokens_here * TOP
    route_ids = routes[0].reshape(route_count)
    route_gates = gate_weights[0].reshape(route_count)
    one_hot = (route_ids[:, None] == jnp.arange(window, dtype=jnp.int32)[None, :]).astype(jnp.int32)
    earlier = jnp.cumsum(one_hot, axis=0) - one_hot
    slot_index = jnp.sum(earlier * one_hot, axis=1)
    target = jnp.where(route_ids < window, route_ids * CAP + slot_index, -1)
    route_select = (target[None, :] == jnp.arange(window * CAP, dtype=jnp.int32)[:, None]).astype(
        jnp.float32
    )
    token_of = (
        jnp.arange(route_count, dtype=jnp.int32)[:, None] // TOP
        == jnp.arange(tokens_here, dtype=jnp.int32)[None, :]
    ).astype(jnp.float32)
    selector = jnp.dot(route_select, token_of, precision=lax.Precision.HIGHEST).astype(jnp.bfloat16)
    outgoing = (
        jnp.dot(selector, normed, preferred_element_type=jnp.float32)
        .astype(jnp.bfloat16)
        .reshape(window, CAP, width)
    )
    combine_weights = jnp.dot(
        jnp.transpose(token_of),
        jnp.transpose(route_select) * route_gates[:, None],
        precision=lax.Precision.HIGHEST,
    )
    incoming = lax.all_to_all(outgoing, "tp", split_axis=0, concat_axis=0, tiled=True)
    local_gate = w_gate[0]
    local_up = w_up[0]
    local_down = w_down[0]
    piece = lax.all_gather(incoming.reshape(window * CAP, width), "seq", axis=0, tiled=True)
    gate_part = jnp.dot(piece, local_gate, preferred_element_type=jnp.float32)
    up_part = jnp.dot(piece, local_up, preferred_element_type=jnp.float32)
    hidden_units = (jax.nn.silu(gate_part) * up_part).astype(jnp.bfloat16)
    summed_rows = lax.psum_scatter(
        jnp.dot(hidden_units, local_down, preferred_element_type=jnp.float32).astype(jnp.bfloat16),
        "seq",
        scatter_dimension=0,
        tiled=True,
    )
    expert_out = summed_rows.reshape(window, CAP, width)
    returned = lax.all_to_all(expert_out, "tp", split_axis=0, concat_axis=0, tiled=True)
    returned_rows = returned.reshape(window * CAP, width).astype(jnp.float32)
    expert_total = jnp.dot(combine_weights, returned_rows, precision=lax.Precision.HIGHEST)
    mixed = (attended_f + expert_total).astype(jnp.bfloat16)
    return mixed[None]


def solution(mesh):
    return jax.shard_map(
        body,
        mesh=mesh,
        in_specs=(
            P(("group", "exp"), ("seq", "tp"), None),
            P(("group", "exp"), ("seq", "tp"), None, None),
            P(("group", "exp")),
            P(("group", "exp"), ("seq", "tp"), None),
            P(("group", "exp"), ("seq", "tp"), None),
            P(),
            P("tp", None, "seq"),
            P("tp", None, "seq"),
            P("tp", "seq", None),
        ),
        out_specs=P(("group", "exp"), ("seq", "tp"), None),
        check_vma=False,
    )
```

profile of v0, /device:TPU:0, one launch (start us, length us, event | category | flops | bytes accessed | tf_op | source)
XLA Modules:
  0.0 161.7 jit_solution(1678539097799881003)
XLA Ops:
  6.5 0.7 all-gather.3.cloned.1.call-update
  7.3 0.8 copy.41
  8.9 0.6 reduce-window.6
  9.9 1.4 reshape_squeeze.13
  11.4 1.0 copy.35
  12.5 0.3 convolution_convert_fusion.2
  12.7 37.3 %all-gather.3.cloned.1.call-done = bf16[1,768,2,1024]{3,2,0,1:T(2,128)(2,1)} async-done(((bf16[1,96,2,1024]{3,2,0,1:T(2,128)(2,1)}), bf16[1,768,2,1024]{3,2,0,1:T(2,128)(2,1)}) %all-gather.3.cloned.1.call-update) | async-done | bytes 3145744 | tf_op jit(solution)/shard_map/all_gather | solution.py:33
  50.0 8.8 %fusion.57 = (bf16[1,768,1,1024]{3,2,0,1:T(2,128)(2,1)}, bf16[1,768,1,1024]{3,2,0,1:T(2,128)(2,1)S(1)}) fusion(bf16[1,768,2,1024]{3,2,0,1:T(2,128)(2,1)} %all-gather.3.cloned.1.call-done), kind=kLoop, calls=%fused_computation.71 | loop fusion | bytes 6291456 | tf_op jit(solution)/shard_map/slice | solution.py:36
  58.8 8.2 %copy.47 = bf16[1,768,1,1024]{1,3,2,0:T(8,128)(2,1)} copy(bf16[1,768,1,1024]{3,2,0,1:T(2,128)(2,1)} %get-tuple-element.5) | data formatting | bytes 3145728
  67.0 5.6 %copy.48 = bf16[1,768,1,1024]{1,3,2,0:T(8,128)(2,1)} copy(bf16[1,768,1,1024]{3,2,0,1:T(2,128)(2,1)S(1)} %get-tuple-element.6) | data formatting | bytes 3145728
  72.6 3.1 %fusion = (f32[8,256]{1,0:T(8,128)S(1)}, f32[8,768,256]{2,1,0:T(8,128)S(1)}) fusion(pred[768]{0:T(1024)(128)(4,1)S(1)} %fusion.48, bf16[768,8,128]{0,2,1:T(8,128)(2,1)} %bitcast.58, bf16[8,256,128]{2,1,0:T(8,128)(2,1)} %bitcast.59), kind=kOutput, calls=%fused_computation.2 | convolution fusion | flops 407369728 | bytes 8397568 | tf_op jit(solution)/shard_map/kqd,nkd->knq/dot_general | solution.py:39
  75.7 1.7 %fusion.1 = f32[8,256]{1,0:T(8,128)S(1)} fusion(f32[8,768,256]{2,1,0:T(8,128)S(1)} %get-tuple-element.8, f32[8,256]{1,0:T(8,128)S(1)} %broadcast_maximum_fusion, pred[768]{0:T(1024)(128)(4,1)S(1)} %fusion.48), kind=kLoop, calls=%fused_computation.4 | loop fusion | flops 6289408 | bytes 6308608 | tf_op jit(solution)/shard_map/reduce_sum | solution.py:47
  77.4 2.1 %multiply_reduce_fusion = (f32[256]{0:T(256)S(1)}, f32[8,256,128]{2,1,0:T(8,128)S(1)}) fusion(f32[8,256]{1,0:T(8,128)S(1)} %fusion.1, bf16[768,8,128]{0,2,1:T(8,128)(2,1)S(1)} %bitcast.61, f32[8,768,256]{2,1,0:T(8,128)S(1)} %get-tuple-element.8, f32[8,256]{1,0:T(8,128)S(1)} %broadcast_maximum_fusion, pred[768]{0:T(1024)(128)(4,1)S(1)} %fusion.48), kind=kOutput, calls=%fused_computation.24 | convolution fusion | flops 410255104 | bytes 8931072 | tf_op jit(solution)/shard_map/knq,nkd->kqd/dot_general | solution.py:48
  79.5 0.7 copy.40
  80.2 0.4 reshape.118
  80.8 0.3 convolution_convert_fusion.1
  81.1 4.7 %all_to_all.10 = bf16[2,16,4096]{2,1,0:T(8,128)(2,1)} all-to-all(bf16[2,16,4096]{2,1,0:T(8,128)(2,1)S(1)} %bitcast.63), channel_id=1, replica_groups=mesh['group'=2,'seq'=4,'exp'=2,'tp'=2] {'tp'}, dimensions={0} | all-to-all | bytes 524288 | tf_op jit(solution)/shard_map/all_to_all | solution.py:86
  85.8 26.9 %all-gather.5.cloned.1.call-done = bf16[128,4096]{1,0:T(8,128)(2,1)} async-done(((bf16[32,4096]{1,0:T(8,128)(2,1)}), bf16[128,4096]{1,0:T(8,128)(2,1)}) %all-gather.5.cloned.1.call-update) | async-done | bytes 1048592 | tf_op jit(solution)/shard_map/all_gather | solution.py:90
  112.7 3.3 %fusion.8 = f32[128,512]{1,0:T(8,128)S(1)} fusion(bf16[128,4096]{1,0:T(8,128)(2,1)} %all-gather.5.cloned.1.call-done, bf16[1,4096,512]{2,1,0:T(8,128)(2,1)} %param.15), kind=kOutput, calls=%fused_computation.13 | convolution fusion | flops 536870912 | bytes 5505024 | tf_op jit(solution)/shard_map/dot_general | solution.py:91
  116.1 5.8 %convolution_convert_fusion = bf16[128,4096]{1,0:T(8,128)(2,1)} fusion(bf16[1,512,4096]{2,1,0:T(8,128)(2,1)} %param.17, bf16[128,4096]{1,0:T(8,128)(2,1)S(1)} %copy-done, bf16[1,4096,512]{2,1,0:T(8,128)(2,1)} %param.16, f32[128,512]{1,0:T(8,128)S(1)} %fusion.8), kind=kOutput, calls=%fused_computation.3 | convolution fusion | flops 1074659328 | bytes 10747904 | tf_op jit(solution)/shard_map/dot_general | solution.py:95
  122.1 0.6 fusion.36
  122.7 26.0 %reduce-scatter.2.cloned.1.call-done = bf16[32,4096]{1,0:T(8,128)(2,1)} async-done(((bf16[128,4096]{1,0:T(8,128)(2,1)}), bf16[32,4096]{1,0:T(8,128)(2,1)}) %reduce-scatter.2.cloned.1.call-update) | async-done | bytes 262160 | tf_op jit(solution)/shard_map/reduce_scatter | solution.py:94
  148.7 5.0 %all_to_all.11 = bf16[2,16,4096]{2,1,0:T(8,128)(2,1)S(1)} all-to-all(bf16[2,16,4096]{2,1,0:T(8,128)(2,1)} %bitcast.67), channel_id=1, replica_groups=mesh['group'=2,'seq'=4,'exp'=2,'tp'=2] {'tp'}, dimensions={0} | all-to-all | bytes 524288 | tf_op jit(solution)/shard_map/all_to_all | solution.py:101
  153.7 1.4 fusion.4
  (28 shorter events, 1.1 us)
Async XLA Ops:
  6.5 43.5 %all-gather.3.cloned.1.call-start = ((), (), s32[]{:S(2)}) async-start(), calls=%async_computation.3 | async-start | bytes 3538944 | tf_op jit(solution)/shard_map/all_gather | solution.py:33
  7.3 105.5 %all-gather.5.cloned.1.call-start = ((), (), s32[]{:S(2)}) async-start(), calls=%async_computation.4 | async-start | bytes 1310720 | tf_op jit(solution)/shard_map/all_gather | solution.py:90
  75.7 1.7 %copy-start.1 = (bf16[1,768,1,1024]{1,3,2,0:T(8,128)(2,1)S(1)}, bf16[1,768,1,1024]{1,3,2,0:T(8,128)(2,1)}, u32[]{:S(2)}) copy-start(bf16[1,768,1,1024]{1,3,2,0:T(8,128)(2,1)} %copy.48) | copy-start | bytes 4718596
  79.5 1.2 copy-start.2
  85.8 63.0 %reduce-scatter.2.cloned.1.call-start = ((), (), s32[]{:S(2)}) async-start(), calls=%async_computation.5 | async-start | bytes 1310720 | tf_op jit(solution)/shard_map/reduce_scatter | solution.py:94
  112.7 3.3 %copy-start = (bf16[128,4096]{1,0:T(8,128)(2,1)S(1)}, bf16[128,4096]{1,0:T(8,128)(2,1)}, u32[]{:S(2)}) copy-start(bf16[128,4096]{1,0:T(8,128)(2,1)} %all-gather.5.cloned.1.call-done) | copy-start | bytes 3145732
  116.0 5.9 %copy-start.3 = (f32[1,64,8]{1,2,0:T(8,128)S(1)}, f32[1,64,8]{1,2,0:T(8,128)}, u32[]{:S(2)}) copy-start(f32[1,64,8]{1,2,0:T(8,128)} %param.13) | copy-start | bytes 6148
Sparse Core Ops, SparseCore 0:
  9.0 40.9 all-gather.2
  85.9 26.7 all-gather.4
  122.0 26.6 reduce-scatter.1
where the time goes:
time: 162 us
  waiting for transfers between devices  90.9 us (56%)
  local copies, waits for them, and re-layouts  27.5 us (17%)
  matrix products  16.9 us (10%)
  between operations  13.9 us (9%)
  blocking collectives  9.64 us (6%)
  other arithmetic  2.66 us (2%)
    all_gather x1, waiting for transfers between devices, body(): piece = lax.all_gather(keys_values, ('seq', 'tp'), axis=1, tiled=True)  37.3 us
    all_gather x1, waiting for transfers between devices, body(): lax.all_gather(incoming.reshape(window * CAP, width), 'seq', axis=0, tile...  26.9 us
    reduce_scatter x1, waiting for transfers between devices, body(): lax.psum_scatter(jnp.dot(hidden_units, local_down, preferred_element_type...  26 us
    unnamed x12, local copies, waits for them, and re-layouts  14.6 us
    slice x1, local copies, waits for them, and re-layouts, body(): key_rows = piece[0, :, 0].reshape(key_count, KV_HEADS, HEAD_DIM)  8.83 us
    dot_general x1, matrix products, body(): jnp.dot(hidden_units, local_down, preferred_element_type=jnp.float32)  5.85 us
    all_to_all x1, blocking collectives, body(): lax.all_to_all(expert_out, 'tp', split_axis=0, concat_axis=0, tiled=True)  4.98 us
    all_to_all x1, blocking collectives, body(): lax.all_to_all(outgoing, 'tp', split_axis=0, concat_axis=0, tiled=True)  4.66 us
  transfers between devices with their start and end apart: 3, of which 3 were waited for; matrix products, arithmetic and copies ran while one was open for 3% of the time, Pallas kernels for 0%

commit v1 on v0

v1 whole, which is shorter than its diff:
```python
import functools
import math

import jax
import jax.numpy as jnp
from jax import lax
from jax.experimental import pallas as pl
from jax.experimental.pallas import tpu as pltpu
from jax.sharding import PartitionSpec as P

HEAD_DIM = 128
PROMPT = 256
CAP = 16
TILE = 16

epsilon = 1e-06
masked_score = -1e30
MIB = 1024 * 1024

VMEM = pl.BlockSpec(memory_space=pltpu.VMEM)
SMEM = pl.BlockSpec(memory_space=pltpu.SMEM)
ANY = pl.BlockSpec(memory_space=pl.ANY)


def params(mib):
    return pltpu.CompilerParams(vmem_limit_bytes=mib * MIB)


def cost(flops, moved, transcendentals=0):
    return pl.CostEstimate(
        flops=int(flops), bytes_accessed=int(moved), transcendentals=int(transcendentals)
    )


def pick_kernel(me_ref, routes_ref, gates_ref, q_ref, keep_ref, send_ref, comb_ref):
    tokens = routes_ref.shape[0]
    me = me_ref[0]
    routes = routes_ref[...]
    gates = gates_ref[...]
    column = lax.broadcasted_iota(jnp.int32, (tokens, 2 * CAP), 1)
    mine = column < CAP

    def of_expert(expert):
        hit = routes == expert
        member = jnp.sum(hit.astype(jnp.float32), axis=1, keepdims=True)
        weight = jnp.sum(jnp.where(hit, gates, 0.0), axis=1, keepdims=True)
        return member, weight

    member_a, weight_a = of_expert(me)
    member_b, weight_b = of_expert(1 - me)
    member = jnp.where(mine, member_a, member_b)
    weight = jnp.where(mine, weight_a, weight_b)
    row = lax.broadcasted_iota(jnp.int32, (tokens, tokens), 0)
    col = lax.broadcasted_iota(jnp.int32, (tokens, tokens), 1)
    before = (col < row).astype(jnp.float32).astype(jnp.bfloat16)
    slot = jnp.dot(before, member.astype(jnp.bfloat16), preferred_element_type=jnp.float32)
    wanted = jnp.where(mine, column, column - CAP).astype(jnp.float32)
    taken = jnp.where((member > 0.0) & (slot == wanted), 1.0, 0.0)
    comb_ref[...] = taken * weight
    rows = lax.dot_general(
        taken.astype(jnp.bfloat16),
        q_ref[...],
        (((0,), (0,)), ((), ())),
        preferred_element_type=jnp.float32,
    ).astype(jnp.bfloat16)
    keep_ref[...] = rows[:CAP]
    send_ref[...] = rows[CAP:]


def key_bias(place_ref, pieces, rows_each, rows_true):
    length = place_ref[pieces]
    parts = []
    lane = lax.broadcasted_iota(jnp.int32, (8, rows_each), 1)
    for i in range(pieces):
        position = lane + place_ref[i]
        allowed = (position >= PROMPT) | (position < length)
        allowed = allowed & (lane < rows_true)
        parts.append(jnp.where(allowed, 0.0, masked_score))
    return jnp.concatenate(parts, axis=1)[:1]


def attend(queries, kv_refs, bias, store, per_key):
    width = kv_refs[0].shape[1] // 2
    heads = width // HEAD_DIM
    factor = math.log2(math.e) / math.sqrt(HEAD_DIM)
    for head in range(heads):
        at = head * HEAD_DIM
        keys = jnp.concatenate([r[:, at : at + HEAD_DIM] for r in kv_refs], axis=0)
        values = jnp.concatenate(
            [r[:, width + at : width + at + HEAD_DIM] for r in kv_refs], axis=0
        )
        values = jnp.concatenate([values, jnp.ones_like(values)], axis=1)
        block = queries(head * per_key * HEAD_DIM, per_key * HEAD_DIM)
        rows = block.shape[0]
        stacked = jnp.concatenate(
            [block[:, j * HEAD_DIM : (j + 1) * HEAD_DIM] for j in range(per_key)], axis=0
        )
        scores = (
            lax.dot_general(
                stacked, keys, (((1,), (1,)), ((), ())), preferred_element_type=jnp.float32
            )
            * factor
            + bias
        )
        weights = jnp.exp2(scores - jnp.max(scores, axis=1, keepdims=True))
        summed = jnp.dot(
            weights.astype(jnp.bfloat16), values, preferred_element_type=jnp.float32
        )
        result = (summed[:, :HEAD_DIM] / summed[:, HEAD_DIM:]).astype(jnp.bfloat16)
        for j in range(per_key):
            store(
                (head * per_key + j) * HEAD_DIM, result[j * rows : (j + 1) * rows]
            )


def attend_kernel(pieces, blocks, per_key, rows_true, place_ref, *refs):
    q_refs = refs[:blocks]
    kv_refs = refs[blocks : blocks + pieces]
    out_refs = refs[blocks + pieces :]
    bias = key_bias(place_ref, pieces, kv_refs[0].shape[0], rows_true)

    def queries(at, size):
        return jnp.concatenate([r[:, at : at + size] for r in q_refs], axis=0)

    def store(at, result):
        begin = 0
        for r in out_refs:
            r[:, at : at + HEAD_DIM] = result[begin : begin + r.shape[0]]
            begin += r.shape[0]

    attend(queries, kv_refs, bias, store, per_key)


def attend_call(place, q_blocks, kv_pieces, out_rows, rows_true):
    width = q_blocks[0].shape[1]
    per_key = width // (kv_pieces[0].shape[1] // 2)
    rows = sum(q.shape[0] for q in q_blocks)
    keys = sum(p.shape[0] for p in kv_pieces)
    return pl.pallas_call(
        functools.partial(
            attend_kernel, len(kv_pieces), len(q_blocks), per_key, rows_true
        ),
        out_shape=[jax.ShapeDtypeStruct((r, width), jnp.bfloat16) for r in out_rows],
        in_specs=[SMEM] + [VMEM] * (len(q_blocks) + len(kv_pieces)),
        out_specs=[VMEM] * len(out_rows),
        compiler_params=params(40),
        cost_estimate=cost(
            4 * rows * width * keys,
            4 * rows * width + 2 * keys * kv_pieces[0].shape[1],
            rows * keys * width // HEAD_DIM,
        ),
        name="attend",
    )(place, *q_blocks, *kv_pieces)


def expert_kernel(
    pieces, homes, per_key, rows_true, place_ref, done_ref, last_ref, *refs
):
    kv_refs = refs[:pieces]
    gain_ref, gate_hbm, up_hbm, down_hbm = refs[pieces : pieces + 4]
    out_refs = refs[pieces + 4 : pieces + 4 + homes]
    x_ref, gate_ref, up_ref, down_ref, sems = refs[pieces + 4 + homes :]
    copies = [
        pltpu.make_async_copy(src, dst, sems.at[i])
        for i, (src, dst) in enumerate(
            ((gate_hbm, gate_ref), (up_hbm, up_ref), (down_hbm, down_ref))
        )
    ]
    for c in copies:
        c.start()
    bias = key_bias(place_ref, pieces, kv_refs[0].shape[0], rows_true)
    ahead = done_ref.shape[0]
    rows = x_ref.shape[0]

    def queries(at, size):
        return last_ref[:, at : at + size]

    def store(at, result):
        x_ref[ahead:rows, at : at + HEAD_DIM] = result

    attend(queries, kv_refs, bias, store, per_key)
    x_ref[:ahead, :] = done_ref[...]
    x = x_ref[...].astype(jnp.float32)
    square = jnp.mean(x * x, axis=1, keepdims=True)
    normed = (x * lax.rsqrt(square + epsilon) * gain_ref[...]).astype(jnp.bfloat16)
    copies[0].wait()
    gate = jnp.dot(normed, gate_ref[...], preferred_element_type=jnp.float32)
    copies[1].wait()
    up = jnp.dot(normed, up_ref[...], preferred_element_type=jnp.float32)
    hidden = (gate / (1.0 + jnp.exp(-gate)) * up).astype(jnp.bfloat16)
    copies[2].wait()
    part = jnp.dot(hidden, down_ref[...], preferred_element_type=jnp.float32).astype(
        jnp.bfloat16
    )
    each = rows // homes
    for i, r in enumerate(out_refs):
        r[...] = part[i * each : (i + 1) * each]


def expert_call(place, done, last, kv_pieces, gain, w_gate, w_up, w_down, rows_true):
    each, width = last.shape
    homes = done.shape[0] // each + 1
    rows = homes * each
    hidden = w_gate.shape[1]
    per_key = width // (kv_pieces[0].shape[1] // 2)
    return pl.pallas_call(
        functools.partial(expert_kernel, len(kv_pieces), homes, per_key, rows_true),
        out_shape=[jax.ShapeDtypeStruct((each, width), jnp.bfloat16)] * homes,
        in_specs=[SMEM] + [VMEM] * (3 + len(kv_pieces)) + [ANY] * 3,
        out_specs=[VMEM] * homes,
        scratch_shapes=[
            pltpu.VMEM((rows, width), jnp.bfloat16),
            pltpu.VMEM(w_gate.shape, jnp.bfloat16),
            pltpu.VMEM(w_up.shape, jnp.bfloat16),
            pltpu.VMEM(w_down.shape, jnp.bfloat16),
            pltpu.SemaphoreType.DMA((3,)),
        ],
        compiler_params=params(48),
        cost_estimate=cost(6 * rows * width * hidden, 6 * width * hidden),
        name="experts",
    )(place, done, last, *kv_pieces, gain, w_gate, w_up, w_down)


def combine_kernel(count, comb_ref, attended_ref, *refs):
    out_ref = refs[-1]

    def total(terms):
        first = terms[0][...].astype(jnp.float32)
        for t in terms[1:]:
            first = first + t[...].astype(jnp.float32)
        return first.astype(jnp.bfloat16)

    rows = jnp.concatenate([total(refs[:count]), total(refs[count:-1])], axis=0)
    comb = comb_ref[...]
    high = comb.astype(jnp.bfloat16)
    low = (comb - high.astype(jnp.float32)).astype(jnp.bfloat16)
    added = jnp.dot(high, rows, preferred_element_type=jnp.float32) + jnp.dot(
        low, rows, preferred_element_type=jnp.float32
    )
    out_ref[...] = (attended_ref[...].astype(jnp.float32) + added).astype(jnp.bfloat16)


def across(x, stride):
    n = lax.axis_size("seq")
    return lax.ppermute(x, "seq", [(i, i ^ stride) for i in range(n)])


def swap(x):
    return lax.ppermute(x, "tp", [(0, 1), (1, 0)])


def across_and_swap(x, stride):
    n = lax.axis_size("seq")
    pairs = [
        (2 * i + c, 2 * (i ^ stride) + 1 - c) for i in range(n) for c in range(2)
    ]
    return lax.ppermute(x, ("seq", "tp"), pairs)


def strides_of(n):
    return [1 << b for b in reversed(range(n.bit_length() - 1))]


def gather(own):
    blocks, order = [own], [0]
    for stride in strides_of(lax.axis_size("seq")):
        blocks = blocks + [across(b, stride) for b in blocks]
        order = order + [k ^ stride for k in order]
    return blocks, order


def body(
    queries, keys_values, prompt_lengths, routes, gate_weights, norm_gain, w_gate, w_up, w_down
):
    tokens, width = queries.shape[1:]
    rows_true = keys_values.shape[1]
    pad = -rows_true % TILE
    seq, core = lax.axis_index("seq"), lax.axis_index("tp")
    own_queries = queries[0]

    kv = keys_values[0].reshape(rows_true, -1)
    if pad:
        kv = jnp.pad(kv, ((0, pad), (0, 0)))
    kv_blocks, order = gather(kv)

    keep, send, comb = pl.pallas_call(
        pick_kernel,
        out_shape=[
            jax.ShapeDtypeStruct((CAP, width), jnp.bfloat16),
            jax.ShapeDtypeStruct((CAP, width), jnp.bfloat16),
            jax.ShapeDtypeStruct((tokens, 2 * CAP), jnp.float32),
        ],
        in_specs=[SMEM] + [VMEM] * 3,
        out_specs=[VMEM] * 3,
        compiler_params=params(16),
        cost_estimate=cost(4 * CAP * tokens * width, 4 * tokens * width),
        name="pick",
    )(core.reshape(1), routes[0], gate_weights[0], own_queries)
    routed = jnp.concatenate([keep, swap(send)], axis=0)
    routed_blocks, _ = gather(routed)

    pieces, places = [], []
    for block, k in zip(kv_blocks, order):
        pieces += [block, swap(block)]
        places += [2 * (seq ^ k) + core, 2 * (seq ^ k) + 1 - core]
    place = jnp.stack([p * rows_true for p in places] + [prompt_lengths[0]]).astype(jnp.int32)

    each = 2 * CAP
    done, attended = attend_call(
        place,
        routed_blocks[:-1] + [own_queries],
        pieces,
        [each * (len(order) - 1), tokens],
        rows_true,
    )
    parts = expert_call(
        place,
        done,
        routed_blocks[-1],
        pieces,
        norm_gain.reshape(1, width),
        w_gate[0],
        w_up[0],
        w_down[0],
        rows_true,
    )

    held = dict(zip(order, parts))
    strides = strides_of(len(order))[::-1]
    for stride in strides[:-1]:
        sent = {k: across(v, stride) for k, v in held.items() if k & stride}
        held = {
            k: (v.astype(jnp.float32) + sent[k ^ stride].astype(jnp.float32)).astype(jnp.bfloat16)
            for k, v in held.items()
            if not k & stride
        }
    mine, theirs = held[0], held[strides[-1]]
    terms = [
        mine[:CAP],
        across(theirs[:CAP], strides[-1]),
        swap(mine[CAP:]),
        across_and_swap(theirs[CAP:], strides[-1]),
    ]
    mixed = pl.pallas_call(
        functools.partial(combine_kernel, 2),
        out_shape=jax.ShapeDtypeStruct((tokens, width), jnp.bfloat16),
        in_specs=[VMEM] * 6,
        out_specs=VMEM,
        compiler_params=params(16),
        cost_estimate=cost(8 * CAP * tokens * width, 4 * tokens * width),
        name="combine",
    )(comb, attended, *terms)
    return mixed[None]


def solution(mesh):
    return jax.shard_map(
        body,
        mesh=mesh,
        in_specs=(
            P(("group", "exp"), ("seq", "tp"), None),
            P(("group", "exp"), ("seq", "tp"), None, None),
            P(("group", "exp")),
            P(("group", "exp"), ("seq", "tp"), None),
            P(("group", "exp"), ("seq", "tp"), None),
            P(),
            P("tp", None, "seq"),
            P("tp", None, "seq"),
            P("tp", "seq", None),
        ),
        out_specs=P(("group", "exp"), ("seq", "tp"), None),
        check_vma=False,
    )
```

time: 162 us -> 95.5 us (0.59)
  waiting for transfers between devices: 90.9 us -> 49.1 us
  starting transfers between devices: 0.08 us -> 21.4 us
  local copies, waits for them, and re-layouts: 27.5 us -> 8.14 us
  matrix products: 16.9 us -> 0 us
  Pallas kernels: 0 us -> 15.4 us
  between operations: 13.9 us -> 0.79 us
  blocking collectives: 9.64 us -> 0 us
  other arithmetic: 2.66 us -> 0.13 us
    all_gather x2 -> x0, waiting for transfers between devices: 64.2 us -> none  [the longest x1 37.3 us: body(): piece = lax.all_gather(keys_values, ('seq', 'tp'), axis=1, tiled=True)]
    ppermute x0 -> x16, waiting for transfers between devices: none -> 49.1 us  [the longest x9 47.8 us: across(): return lax.ppermute(x, 'seq', [(i, i ^ stride) for i in range(n)])]
    reduce_scatter x1 -> x0, waiting for transfers between devices: 26 us -> none  [body(): lax.psum_scatter(jnp.dot(hidden_units, local_down, preferred_element_type...]
    ppermute x0 -> x16, starting transfers between devices: none -> 21.4 us  [the longest x9 20.6 us: across(): return lax.ppermute(x, 'seq', [(i, i ^ stride) for i in range(n)])]
    dot_general x8 -> x0, matrix products: 16.9 us -> none  [the longest x1 5.85 us: body(): jnp.dot(hidden_units, local_down, preferred_element_type=jnp.float32)]
    pallas_call x0 -> x4, Pallas kernels: none -> 15.4 us  [the longest x1 7.26 us: expert_call(): pl.pallas_call(functools.partial(expert_kernel, len(kv_pieces), homes, pe...]
    all_to_all x2 -> x0, blocking collectives: 9.64 us -> none  [the longest x1 4.98 us: body(): lax.all_to_all(expert_out, 'tp', split_axis=0, concat_axis=0, tiled=True)]
    slice x2, local copies, waits for them, and re-layouts: 9.04 us -> 0.04 us  [the longest x1 0.02 us: body(): mine[CAP:]]
  transfers between devices with their start and end apart: 3 -> 16, of which waited for: 3 -> 7; matrix products, arithmetic and copies ran while one was open for 3% -> 2% of each run, Pallas kernels for 0% -> 7%
where the time goes in v1:
time: 95.5 us; the launch traced here: 94.9 us
  waiting for transfers between devices  49.1 us (51%)
  starting transfers between devices  21.4 us (22%)
  Pallas kernels  15.4 us (16%)
  local copies, waits for them, and re-layouts  8.14 us (9%)
    ppermute x9, waiting for transfers between devices, across(): return lax.ppermute(x, 'seq', [(i, i ^ stride) for i in range(n)])  47.8 us
    ppermute x9, starting transfers between devices, across(): return lax.ppermute(x, 'seq', [(i, i ^ stride) for i in range(n)])  20.6 us
    unnamed x18, local copies, waits for them, and re-layouts  8 us
    pallas_call x1, Pallas kernels, expert_call(): pl.pallas_call(functools.partial(expert_kernel, len(kv_pieces), homes, pe...  7.26 us
    pallas_call x1, Pallas kernels, attend_call(): pl.pallas_call(functools.partial(attend_kernel, len(kv_pieces), len(q_blo...  6.43 us
  transfers between devices with their start and end apart: 16, of which 7 were waited for; matrix products, arithmetic and copies ran while one was open for 2% of the time, Pallas kernels for 7%

profile of v1, /device:TPU:0, one launch (start us, length us, event | category | flops | bytes accessed | tf_op | source)
XLA Modules:
  0.0 94.9 jit_solution(13680454468637042335)
XLA Ops:
  0.0 1.1 %copy.12 = bf16[12,8,2,1024]{3,1,2,0:T(8,128)(2,1)S(1)} copy(bf16[12,8,2,1024]{3,2,1,0:T(2,128)(2,1)} %bitcast.33) | data formatting | bytes 786432
  1.1 4.1 %collective-permute-start.4 = (bf16[96,2048]{1,0:T(8,128)(2,1)S(1)}, bf16[96,2048]{1,0:T(8,128)(2,1)S(1)}, u32[]{:S(2)}, u32[]{:S(2)}) collective-permute-start(bf16[96,2048]{1,0:T(8,128)(2,1)S(1)} %bitcast.20), channel_id=1, source_target_pairs={{0,8},{4,12},{8,0},{12,4},{1,9},{5,13},{9,1},{13,5},{2,10},{6,14},... | collective-permute-start | bytes 1179656 | tf_op jit(solution)/shard_map/ppermute | solution.py:245
  5.2 1.6 %collective-permute-start.6 = (bf16[96,2048]{1,0:T(8,128)(2,1)S(1)}, bf16[96,2048]{1,0:T(8,128)(2,1)S(1)}, u32[]{:S(2)}, u32[]{:S(2)}) collective-permute-start(bf16[96,2048]{1,0:T(8,128)(2,1)S(1)} %bitcast.21), channel_id=1, source_target_pairs={{0,4},{4,0},{8,12},{12,8},{1,5},{5,1},{9,13},{13,9},{2,6},{6,2},{1... | collective-permute-start | bytes 1179656 | tf_op jit(solution)/shard_map/ppermute | solution.py:245
  6.8 0.8 copy.10
  7.5 0.8 copy.11
  8.3 1.0 %copy-done = bf16[1,64,4096]{2,1,0:T(8,128)(2,1)S(1)} copy-done((bf16[1,64,4096]{2,1,0:T(8,128)(2,1)S(1)}, bf16[1,64,4096]{2,1,0:T(8,128)(2,1)}, u32[]{:S(2)}) %copy-start) | copy-done | bytes 524312
  9.9 12.9 %collective-permute-done.4.refs_6_.refs_2_ = bf16[96,2048]{1,0:T(8,128)(2,1)S(1)} collective-permute-done((bf16[96,2048]{1,0:T(8,128)(2,1)S(1)}, bf16[96,2048]{1,0:T(8,128)(2,1)S(1)}, u32[]{:S(2)}, u32[]{:S(2)}) %collective-permute-start.4) | collective-permute-done | bytes 393248 | tf_op jit(solution)/shard_map/ppermute | solution.py:245
  23.5 3.4 %collective-permute-start.1 = (bf16[32,4096]{1,0:T(8,128)(2,1)S(1)}, bf16[32,4096]{1,0:T(8,128)(2,1)}, u32[]{:S(2)}, u32[]{:S(2)}) collective-permute-start(bf16[32,4096]{1,0:T(8,128)(2,1)S(1)} %constant_dynamic-update-slice_fusion.refs_0_), channel_id=1, source_target_pairs={{0,8},{4,12},{8,0},{12,4},{1,9},{5,13},{9,1},{13,5},{2,10},{6,14},... | collective-permute-start | bytes 786440 | tf_op jit(solution)/shard_map/ppermute | solution.py:245
  27.4 11.3 %collective-permute-done.8.refs_10_.refs_6_ = bf16[96,2048]{1,0:T(8,128)(2,1)S(1)} collective-permute-done((bf16[96,2048]{1,0:T(8,128)(2,1)S(1)}, bf16[96,2048]{1,0:T(8,128)(2,1)S(1)}, u32[]{:S(2)}, u32[]{:S(2)}) %collective-permute-start.8) | collective-permute-done | bytes 393248 | tf_op jit(solution)/shard_map/ppermute | solution.py:245
  38.7 3.1 %collective-permute-start.2 = (bf16[32,4096]{1,0:T(8,128)(2,1)S(1)}, bf16[32,4096]{1,0:T(8,128)(2,1)S(1)}, u32[]{:S(2)}, u32[]{:S(2)}) collective-permute-start(bf16[32,4096]{1,0:T(8,128)(2,1)S(1)} %constant_dynamic-update-slice_fusion.refs_0_), channel_id=1, source_target_pairs={{0,4},{4,0},{8,12},{12,8},{1,5},{5,1},{9,13},{13,9},{2,6},{6,2},{1... | collective-permute-start | bytes 786440 | tf_op jit(solution)/shard_map/ppermute | solution.py:245
  42.5 5.3 %collective-permute-done.2.refs_2_ = bf16[32,4096]{1,0:T(8,128)(2,1)S(1)} collective-permute-done((bf16[32,4096]{1,0:T(8,128)(2,1)S(1)}, bf16[32,4096]{1,0:T(8,128)(2,1)S(1)}, u32[]{:S(2)}, u32[]{:S(2)}) %collective-permute-start.2) | collective-permute-done | bytes 262176 | tf_op jit(solution)/shard_map/ppermute | solution.py:245
  48.5 1.7 %collective-permute-start.10 = (bf16[32,4096]{1,0:T(8,128)(2,1)}, bf16[32,4096]{1,0:T(8,128)(2,1)S(1)}, u32[]{:S(2)}, u32[]{:S(2)}) collective-permute-start(bf16[32,4096]{1,0:T(8,128)(2,1)} %collective-permute-done.1.refs_1_), channel_id=1, source_target_pairs={{0,4},{4,0},{8,12},{12,8},{1,5},{5,1},{9,13},{13,9},{2,6},{6,2},{1... | collective-permute-start | bytes 786440 | tf_op jit(solution)/shard_map/ppermute | solution.py:245
  51.0 1.0 %copy-done.1 = bf16[1,64,4096]{2,1,0:T(8,128)(2,1)S(1)} copy-done((bf16[1,64,4096]{2,1,0:T(8,128)(2,1)S(1)}, bf16[1,64,4096]{2,1,0:T(8,128)(2,1)}, u32[]{:S(2)}) %copy-start.1) | copy-done | bytes 524312
  52.1 0.9 copy-done.3
  53.0 0.9 copy-done.6
  54.0 6.4 %attend.1 = (bf16[96,4096]{1,0:T(8,128)(2,1)S(1)}, bf16[64,4096]{1,0:T(8,128)(2,1)S(1)}) custom-call(s32[9]{0:T(128)S(1)} %stack.35.place_ref, bf16[32,4096]{1,0:T(8,128)(2,1)S(1)} %copy-done.3, bf16[32,4096]{1,0:T(8,128)(2,1)} %collective-permute-done.1.refs_1_, bf16[32,4096]{1,0:T(8,128)(2,1)S(1)} %copy-done.6, bf16[64,4096]{1,0:T(8,128)(2,1)S(1)} %bitcast.26, ...), custom_call_target="tpu_custom_call" | custom-call | flops 2013265920 | bytes 5767168 | tf_op jit(solution)/shard_map/attend/pallas_call | solution.py:139
  60.4 7.3 %experts.1 = (bf16[32,4096]{1,0:T(8,128)(2,1)S(1)}, bf16[32,4096]{1,0:T(8,128)(2,1)S(1)}, bf16[32,4096]{1,0:T(8,128)(2,1)S(1)}, bf16[32,4096]{1,0:T(8,128)(2,1)S(1)}) custom-call(s32[9]{0:T(128)S(1)} %stack.35.place_ref, bf16[96,4096]{1,0:T(8,128)(2,1)S(1)} %get-tuple-element.18.done_ref, bf16[32,4096]{1,0:T(8,128)(2,1)S(1)} %collective-permute-done.10.last_ref, ...), custom_call_target="tpu_custom_call" | custom-call | flops 1610612736 | bytes 12582912 | tf_op jit(solution)/shard_map/experts/pallas_call | solution.py:206
  68.0 1.7 %collective-permute-start.12 = (bf16[32,4096]{1,0:T(8,128)(2,1)S(1)}, bf16[32,4096]{1,0:T(8,128)(2,1)S(1)}, u32[]{:S(2)}, u32[]{:S(2)}) collective-permute-start(bf16[32,4096]{1,0:T(8,128)(2,1)S(1)} %get-tuple-element.22), channel_id=1, source_target_pairs={{0,4},{4,0},{8,12},{12,8},{1,5},{5,1},{9,13},{13,9},{2,6},{6,2},{1... | collective-permute-start | bytes 786440 | tf_op jit(solution)/shard_map/ppermute | solution.py:245
  69.8 7.2 %collective-permute-done.11 = bf16[32,4096]{1,0:T(8,128)(2,1)S(1)} collective-permute-done((bf16[32,4096]{1,0:T(8,128)(2,1)S(1)}, bf16[32,4096]{1,0:T(8,128)(2,1)S(1)}, u32[]{:S(2)}, u32[]{:S(2)}) %collective-permute-start.11) | collective-permute-done | bytes 262176 | tf_op jit(solution)/shard_map/ppermute | solution.py:245
  77.1 2.8 %collective-permute-done.12 = bf16[32,4096]{1,0:T(8,128)(2,1)S(1)} collective-permute-done((bf16[32,4096]{1,0:T(8,128)(2,1)S(1)}, bf16[32,4096]{1,0:T(8,128)(2,1)S(1)}, u32[]{:S(2)}, u32[]{:S(2)}) %collective-permute-start.12) | collective-permute-done | bytes 262176 | tf_op jit(solution)/shard_map/ppermute | solution.py:245
  80.0 3.9 %collective-permute-start.13 = (bf16[16,4096]{1,0:T(8,128)(2,1)S(1)}, bf16[16,4096]{1,0:T(8,128)(2,1)S(1)}, u32[]{:S(2)}, u32[]{:S(2)}) collective-permute-start(bf16[16,4096]{1,0:T(8,128)(2,1)S(1)} %get-tuple-element.24), channel_id=1, source_target_pairs={{0,8},{4,12},{8,0},{12,4},{1,9},{5,13},{9,1},{13,5},{2,10},{6,14},... | collective-permute-start | bytes 393224 | tf_op jit(solution)/shard_map/ppermute | solution.py:245
  84.1 8.3 %collective-permute-done.13.refs_1_ = bf16[16,4096]{1,0:T(8,128)(2,1)S(1)} collective-permute-done((bf16[16,4096]{1,0:T(8,128)(2,1)S(1)}, bf16[16,4096]{1,0:T(8,128)(2,1)S(1)}, u32[]{:S(2)}, u32[]{:S(2)}) %collective-permute-start.13) | collective-permute-done | bytes 131104 | tf_op jit(solution)/shard_map/ppermute | solution.py:245
  92.4 1.3 %collective-permute-done.15.refs_3_ = bf16[16,4096]{1,0:T(8,128)(2,1)S(1)} collective-permute-done((bf16[16,4096]{1,0:T(8,128)(2,1)S(1)}, bf16[16,4096]{1,0:T(8,128)(2,1)S(1)}, u32[]{:S(2)}, u32[]{:S(2)}) %collective-permute-start.15) | collective-permute-done | bytes 131104 | tf_op jit(solution)/shard_map/ppermute | solution.py:257
  93.7 1.2 %combine.1 = bf16[64,4096]{1,0:T(8,128)(2,1)} custom-call(f32[64,32]{1,0:T(8,128)S(1)} %get-tuple-element.14.comb_ref, bf16[64,4096]{1,0:T(8,128)(2,1)S(1)} %get-tuple-element.17.attended_ref, bf16[16,4096]{1,0:T(8,128)(2,1)S(1)} %get-tuple-element.26.refs_0_, bf16[16,4096]{1,0:T(8,128)(2,1)S(1)} %collective-permute-done.13.refs_1_, ...), custom_call_target="tpu_custom_call" | custom-call | flops 33554432 | bytes 1048576 | tf_op jit(solution)/shard_map/combine/pallas_call | solution.py:344
  (36 shorter events, 3.9 us)
Async XLA Ops:
  1.1 21.7 %collective-permute-start.4 = (bf16[96,2048]{1,0:T(8,128)(2,1)S(1)}, bf16[96,2048]{1,0:T(8,128)(2,1)S(1)}, u32[]{:S(2)}, u32[]{:S(2)}) collective-permute-start(bf16[96,2048]{1,0:T(8,128)(2,1)S(1)} %bitcast.20), channel_id=1, source_target_pairs={{0,8},{4,12},{8,0},{12,4},{1,9},{5,13},{9,1},{13,5},{2,10},{6,14},... | collective-permute-start | bytes 1179656 | tf_op jit(solution)/shard_map/ppermute | solution.py:245
  5.2 22.2 %collective-permute-start.6 = (bf16[96,2048]{1,0:T(8,128)(2,1)S(1)}, bf16[96,2048]{1,0:T(8,128)(2,1)S(1)}, u32[]{:S(2)}, u32[]{:S(2)}) collective-permute-start(bf16[96,2048]{1,0:T(8,128)(2,1)S(1)} %bitcast.21), channel_id=1, source_target_pairs={{0,4},{4,0},{8,12},{12,8},{1,5},{5,1},{9,13},{13,9},{2,6},{6,2},{1... | collective-permute-start | bytes 1179656 | tf_op jit(solution)/shard_map/ppermute | solution.py:245
  8.3 1.0 %copy-start = (bf16[1,64,4096]{2,1,0:T(8,128)(2,1)S(1)}, bf16[1,64,4096]{2,1,0:T(8,128)(2,1)}, u32[]{:S(2)}) copy-start(bf16[1,64,4096]{2,1,0:T(8,128)(2,1)} %param.9) | copy-start | bytes 1572868
  9.3 51.1 %copy-start.4 = (f32[4096]{0:T(1024)S(1)}, f32[4096]{0:T(1024)}, u32[]{:S(2)}) copy-start(f32[4096]{0:T(1024)} %param.14) | copy-start | bytes 49156
  9.8 13.6 %collective-permute-start = (bf16[16,4096]{1,0:T(8,128)(2,1)S(1)}, bf16[16,4096]{1,0:T(8,128)(2,1)S(1)}, u32[]{:S(2)}, u32[]{:S(2)}) collective-permute-start(bf16[16,4096]{1,0:T(8,128)(2,1)S(1)} %get-tuple-element.16), channel_id=1, source_target_pairs={{0,1},{1,0},{2,3},{3,2},{4,5},{5,4},{6,7},{7,6},{8,9},{9,8},{10,11... | collective-permute-start | bytes 393224 | tf_op jit(solution)/shard_map/ppermute | solution.py:249
  22.8 15.9 %collective-permute-start.8 = (bf16[96,2048]{1,0:T(8,128)(2,1)S(1)}, bf16[96,2048]{1,0:T(8,128)(2,1)S(1)}, u32[]{:S(2)}, u32[]{:S(2)}) collective-permute-start(bf16[96,2048]{1,0:T(8,128)(2,1)S(1)} %collective-permute-done.4.refs_6_.refs_2_), channel_id=1, source_target_pairs={{0,4},{4,0},{8,12},{12,8},{1,5},{5,1},{9,13},{13,9},{2,6},{6,2},{1... | collective-permute-start | bytes 1179656 | tf_op jit(solution)/shard_map/ppermute | solution.py:245
  23.5 15.2 %collective-permute-start.1 = (bf16[32,4096]{1,0:T(8,128)(2,1)S(1)}, bf16[32,4096]{1,0:T(8,128)(2,1)}, u32[]{:S(2)}, u32[]{:S(2)}) collective-permute-start(bf16[32,4096]{1,0:T(8,128)(2,1)S(1)} %constant_dynamic-update-slice_fusion.refs_0_), channel_id=1, source_target_pairs={{0,8},{4,12},{8,0},{12,4},{1,9},{5,13},{9,1},{13,5},{2,10},{6,14},... | collective-permute-start | bytes 786440 | tf_op jit(solution)/shard_map/ppermute | solution.py:245
  26.9 24.1 %collective-permute-start.3 = (bf16[96,2048]{1,0:T(8,128)(2,1)S(1)}, bf16[96,2048]{1,0:T(8,128)(2,1)S(1)}, u32[]{:S(2)}, u32[]{:S(2)}) collective-permute-start(bf16[96,2048]{1,0:T(8,128)(2,1)S(1)} %bitcast.22), channel_id=1, source_target_pairs={{0,1},{1,0},{2,3},{3,2},{4,5},{5,4},{6,7},{7,6},{8,9},{9,8},{10,11... | collective-permute-start | bytes 1179656 | tf_op jit(solution)/shard_map/ppermute | solution.py:249
  26.9 24.1 %collective-permute-start.5 = (bf16[96,2048]{1,0:T(8,128)(2,1)S(1)}, bf16[96,2048]{1,0:T(8,128)(2,1)S(1)}, u32[]{:S(2)}, u32[]{:S(2)}) collective-permute-start(bf16[96,2048]{1,0:T(8,128)(2,1)S(1)} %collective-permute-done.4.refs_6_.refs_2_), channel_id=1, source_target_pairs={{0,1},{1,0},{2,3},{3,2},{4,5},{5,4},{6,7},{7,6},{8,9},{9,8},{10,11... | collective-permute-start | bytes 1179656 | tf_op jit(solution)/shard_map/ppermute | solution.py:249
  27.4 23.6 %collective-permute-start.7 = (bf16[96,2048]{1,0:T(8,128)(2,1)S(1)}, bf16[96,2048]{1,0:T(8,128)(2,1)S(1)}, u32[]{:S(2)}, u32[]{:S(2)}) collective-permute-start(bf16[96,2048]{1,0:T(8,128)(2,1)S(1)} %collective-permute-done.6.refs_8_.refs_4_), channel_id=1, source_target_pairs={{0,1},{1,0},{2,3},{3,2},{4,5},{5,4},{6,7},{7,6},{8,9},{9,8},{10,11... | collective-permute-start | bytes 1179656 | tf_op jit(solution)/shard_map/ppermute | solution.py:249
  38.7 12.3 %collective-permute-start.9 = (bf16[96,2048]{1,0:T(8,128)(2,1)S(1)}, bf16[96,2048]{1,0:T(8,128)(2,1)S(1)}, u32[]{:S(2)}, u32[]{:S(2)}) collective-permute-start(bf16[96,2048]{1,0:T(8,128)(2,1)S(1)} %collective-permute-done.8.refs_10_.refs_6_), channel_id=1, source_target_pairs={{0,1},{1,0},{2,3},{3,2},{4,5},{5,4},{6,7},{7,6},{8,9},{9,8},{10,11... | collective-permute-start | bytes 1179656 | tf_op jit(solution)/shard_map/ppermute | solution.py:249
  38.7 9.1 %collective-permute-start.2 = (bf16[32,4096]{1,0:T(8,128)(2,1)S(1)}, bf16[32,4096]{1,0:T(8,128)(2,1)S(1)}, u32[]{:S(2)}, u32[]{:S(2)}) collective-permute-start(bf16[32,4096]{1,0:T(8,128)(2,1)S(1)} %constant_dynamic-update-slice_fusion.refs_0_), channel_id=1, source_target_pairs={{0,4},{4,0},{8,12},{12,8},{1,5},{5,1},{9,13},{13,9},{2,6},{6,2},{1... | collective-permute-start | bytes 786440 | tf_op jit(solution)/shard_map/ppermute | solution.py:245
  41.8 0.7 copy-start.2
  47.8 0.7 copy-start.5
  48.5 11.9 %collective-permute-start.10 = (bf16[32,4096]{1,0:T(8,128)(2,1)}, bf16[32,4096]{1,0:T(8,128)(2,1)S(1)}, u32[]{:S(2)}, u32[]{:S(2)}) collective-permute-start(bf16[32,4096]{1,0:T(8,128)(2,1)} %collective-permute-done.1.refs_1_), channel_id=1, source_target_pairs={{0,4},{4,0},{8,12},{12,8},{1,5},{5,1},{9,13},{13,9},{2,6},{6,2},{1... | collective-permute-start | bytes 786440 | tf_op jit(solution)/shard_map/ppermute | solution.py:245
  51.0 1.0 %copy-start.1 = (bf16[1,64,4096]{2,1,0:T(8,128)(2,1)S(1)}, bf16[1,64,4096]{2,1,0:T(8,128)(2,1)}, u32[]{:S(2)}) copy-start(bf16[1,64,4096]{2,1,0:T(8,128)(2,1)} %param.9) | copy-start | bytes 1572868
  52.1 0.9 %copy-start.3 = (bf16[32,4096]{1,0:T(8,128)(2,1)S(1)}, bf16[32,4096]{1,0:T(8,128)(2,1)}, u32[]{:S(2)}) copy-start(bf16[32,4096]{1,0:T(8,128)(2,1)} %copy-done.2) | copy-start | bytes 786436
  53.0 0.9 %copy-start.6 = (bf16[32,4096]{1,0:T(8,128)(2,1)S(1)}, bf16[32,4096]{1,0:T(8,128)(2,1)}, u32[]{:S(2)}) copy-start(bf16[32,4096]{1,0:T(8,128)(2,1)} %copy-done.5) | copy-start | bytes 786436
  67.7 9.3 %collective-permute-start.11 = (bf16[32,4096]{1,0:T(8,128)(2,1)S(1)}, bf16[32,4096]{1,0:T(8,128)(2,1)S(1)}, u32[]{:S(2)}, u32[]{:S(2)}) collective-permute-start(bf16[32,4096]{1,0:T(8,128)(2,1)S(1)} %get-tuple-element.20), channel_id=1, source_target_pairs={{0,4},{4,0},{8,12},{12,8},{1,5},{5,1},{9,13},{13,9},{2,6},{6,2},{1... | collective-permute-start | bytes 786440 | tf_op jit(solution)/shard_map/ppermute | solution.py:245
  68.0 11.8 %collective-permute-start.12 = (bf16[32,4096]{1,0:T(8,128)(2,1)S(1)}, bf16[32,4096]{1,0:T(8,128)(2,1)S(1)}, u32[]{:S(2)}, u32[]{:S(2)}) collective-permute-start(bf16[32,4096]{1,0:T(8,128)(2,1)S(1)} %get-tuple-element.22), channel_id=1, source_target_pairs={{0,4},{4,0},{8,12},{12,8},{1,5},{5,1},{9,13},{13,9},{2,6},{6,2},{1... | collective-permute-start | bytes 786440 | tf_op jit(solution)/shard_map/ppermute | solution.py:245
  80.0 12.4 %collective-permute-start.13 = (bf16[16,4096]{1,0:T(8,128)(2,1)S(1)}, bf16[16,4096]{1,0:T(8,128)(2,1)S(1)}, u32[]{:S(2)}, u32[]{:S(2)}) collective-permute-start(bf16[16,4096]{1,0:T(8,128)(2,1)S(1)} %get-tuple-element.24), channel_id=1, source_target_pairs={{0,8},{4,12},{8,0},{12,4},{1,9},{5,13},{9,1},{13,5},{2,10},{6,14},... | collective-permute-start | bytes 393224 | tf_op jit(solution)/shard_map/ppermute | solution.py:245
  83.8 8.6 %collective-permute-start.14 = (bf16[16,4096]{1,0:T(8,128)(2,1)S(1)}, bf16[16,4096]{1,0:T(8,128)(2,1)S(1)}, u32[]{:S(2)}, u32[]{:S(2)}) collective-permute-start(bf16[16,4096]{1,0:T(8,128)(2,1)S(1)} %get-tuple-element.25), channel_id=1, source_target_pairs={{0,1},{1,0},{2,3},{3,2},{4,5},{5,4},{6,7},{7,6},{8,9},{9,8},{10,11... | collective-permute-start | bytes 393224 | tf_op jit(solution)/shard_map/ppermute | solution.py:249
  83.9 9.9 %collective-permute-start.15 = (bf16[16,4096]{1,0:T(8,128)(2,1)S(1)}, bf16[16,4096]{1,0:T(8,128)(2,1)S(1)}, u32[]{:S(2)}, u32[]{:S(2)}) collective-permute-start(bf16[16,4096]{1,0:T(8,128)(2,1)S(1)} %get-tuple-element.23), channel_id=1, source_target_pairs={{0,9},{1,8},{4,13},{5,12},{8,1},{9,0},{12,5},{13,4},{2,11},{3,10},... | collective-permute-start | bytes 393224 | tf_op jit(solution)/shard_map/ppermute | solution.py:257

commit v2 on v1

v2 whole, which is shorter than its diff:
```python
import functools
import math

import jax
import jax.numpy as jnp
from jax import lax
from jax.experimental import pallas as pl
from jax.experimental.pallas import tpu as pltpu
from jax.sharding import PartitionSpec as P

HEAD_DIM = 128
PROMPT = 256
CAP = 16
TILE = 16

epsilon = 1e-06
masked_score = -1e30
MIB = 1024 * 1024

VMEM = pl.BlockSpec(memory_space=pltpu.VMEM)
SMEM = pl.BlockSpec(memory_space=pltpu.SMEM)
ANY = pl.BlockSpec(memory_space=pl.ANY)


def params(mib):
    return pltpu.CompilerParams(vmem_limit_bytes=mib * MIB)


def cost(flops, moved, transcendentals=0):
    return pl.CostEstimate(
        flops=int(flops), bytes_accessed=int(moved), transcendentals=int(transcendentals)
    )


def pick_kernel(me_ref, routes_ref, gates_ref, q_ref, keep_ref, send_ref, comb_ref):
    top, tokens = routes_ref.shape
    me = me_ref[0]
    routes = routes_ref[...]
    gates = gates_ref[...]

    def of_expert(expert):
        hit = routes == expert
        member = jnp.sum(hit.astype(jnp.float32), axis=0, keepdims=True)
        weight = jnp.sum(jnp.where(hit, gates, 0.0), axis=0, keepdims=True)
        return member, weight

    member_a, weight_a = of_expert(me)
    member_b, weight_b = of_expert(1 - me)
    slot_of = lax.broadcasted_iota(jnp.int32, (2 * CAP, tokens), 0)
    mine = slot_of < CAP
    member = jnp.where(mine, member_a, member_b)
    weight = jnp.where(mine, weight_a, weight_b)
    row = lax.broadcasted_iota(jnp.int32, (tokens, tokens), 0)
    col = lax.broadcasted_iota(jnp.int32, (tokens, tokens), 1)
    before = jnp.where(row < col, 1.0, 0.0).astype(jnp.bfloat16)
    slot = jnp.dot(member.astype(jnp.bfloat16), before, preferred_element_type=jnp.float32)
    wanted = jnp.where(mine, slot_of, slot_of - CAP).astype(jnp.float32)
    taken = jnp.where((member > 0.0) & (slot == wanted), 1.0, 0.0)
    comb_ref[...] = taken * weight
    rows = jnp.dot(
        taken.astype(jnp.bfloat16), q_ref[...], preferred_element_type=jnp.float32
    ).astype(jnp.bfloat16)
    keep_ref[...] = rows[:CAP]
    send_ref[...] = rows[CAP:]


def key_bias(place_ref, pieces, rows_each, rows_true):
    length = place_ref[pieces]
    parts = []
    lane = lax.broadcasted_iota(jnp.int32, (8, rows_each), 1)
    for i in range(pieces):
        position = lane + place_ref[i]
        allowed = (position >= PROMPT) | (position < length)
        allowed = allowed & (lane < rows_true)
        parts.append(jnp.where(allowed, 0.0, masked_score))
    return jnp.concatenate(parts, axis=1)[:1]


def attend(queries, kv_refs, bias, store, per_key):
    width = kv_refs[0].shape[1] // 2
    heads = width // HEAD_DIM
    factor = math.log2(math.e) / math.sqrt(HEAD_DIM)

    def one(head, _):
        at = head * HEAD_DIM
        if not isinstance(head, int):
            at = pl.multiple_of(at, HEAD_DIM)
        keys = jnp.concatenate([r[:, pl.ds(at, HEAD_DIM)] for r in kv_refs], axis=0)
        values = jnp.concatenate(
            [r[:, pl.ds(width + at, HEAD_DIM)] for r in kv_refs], axis=0
        )
        values = jnp.concatenate([values, jnp.ones_like(values)], axis=1)
        block = queries(at * per_key, per_key * HEAD_DIM)
        rows = block.shape[0]
        stacked = jnp.concatenate(
            [block[:, j * HEAD_DIM : (j + 1) * HEAD_DIM] for j in range(per_key)], axis=0
        )
        scores = (
            lax.dot_general(
                stacked, keys, (((1,), (1,)), ((), ())), preferred_element_type=jnp.float32
            )
            * factor
            + bias
        )
        weights = jnp.exp2(scores - jnp.max(scores, axis=1, keepdims=True))
        summed = jnp.dot(
            weights.astype(jnp.bfloat16), values, preferred_element_type=jnp.float32
        )
        result = (summed[:, :HEAD_DIM] / summed[:, HEAD_DIM:]).astype(jnp.bfloat16)
        for j in range(per_key):
            store(at * per_key + j * HEAD_DIM, result[j * rows : (j + 1) * rows])

    if bias.shape[1] > 1024:
        lax.fori_loop(0, heads, one, None)
    else:
        for head in range(heads):
            one(head, None)


def norm(rows, gain):
    x = rows.astype(jnp.float32)
    square = jnp.mean(x * x, axis=1, keepdims=True)
    return (x * lax.rsqrt(square + epsilon) * gain).astype(jnp.bfloat16)


def attend_kernel(pieces, blocks, per_key, rows_true, place_ref, *refs):
    q_refs = refs[:blocks]
    kv_refs = refs[blocks : blocks + pieces]
    out_ref = refs[-1]
    bias = key_bias(place_ref, pieces, kv_refs[0].shape[0], rows_true)

    def queries(at, size):
        return jnp.concatenate([r[:, pl.ds(at, size)] for r in q_refs], axis=0)

    def store(at, result):
        out_ref[:, pl.ds(at, HEAD_DIM)] = result

    attend(queries, kv_refs, bias, store, per_key)
    if len(refs) > blocks + pieces + 1:
        out_ref[...] = norm(out_ref[...], refs[blocks + pieces][...])


def attend_call(place, q_blocks, kv_pieces, rows_true, *gain):
    width = q_blocks[0].shape[1]
    per_key = width // (kv_pieces[0].shape[1] // 2)
    rows = sum(q.shape[0] for q in q_blocks)
    keys = sum(p.shape[0] for p in kv_pieces)
    return pl.pallas_call(
        functools.partial(
            attend_kernel, len(kv_pieces), len(q_blocks), per_key, rows_true
        ),
        out_shape=jax.ShapeDtypeStruct((rows, width), jnp.bfloat16),
        in_specs=[SMEM] + [VMEM] * (len(q_blocks) + len(kv_pieces) + len(gain)),
        out_specs=VMEM,
        compiler_params=params(20 if rows * keys < 1 << 18 else 56),
        cost_estimate=cost(
            4 * rows * width * keys,
            4 * rows * width + 2 * keys * kv_pieces[0].shape[1],
            rows * keys * width // HEAD_DIM,
        ),
        name="attend",
    )(place, *q_blocks, *kv_pieces, *gain)


def split_of(k, width):
    half = width // 2
    return [(0, width)] if k < 2 else [(0, half), (half, width)]


def expert_kernel(
    pieces, order, per_key, rows_true, last_ref, place_ref, done_ref, *refs
):
    kv_refs = refs[:pieces]
    gain_ref, gate_hbm, up_hbm, down_hbm = refs[pieces : pieces + 4]
    out_refs = refs[pieces + 4 : -5]
    x_ref, gate_ref, up_ref, down_ref, sems = refs[-5:]
    copies = [
        pltpu.make_async_copy(src, dst, sems.at[i])
        for i, (src, dst) in enumerate(
            ((gate_hbm, gate_ref), (up_hbm, up_ref), (down_hbm, down_ref))
        )
    ]
    for c in copies:
        c.start()
    bias = key_bias(place_ref, pieces, kv_refs[0].shape[0], rows_true)

    def queries(at, size):
        return last_ref[:, pl.ds(at, size)]

    def store(at, result):
        x_ref[:, pl.ds(at, HEAD_DIM)] = result

    attend(queries, kv_refs, bias, store, per_key)
    normed = jnp.concatenate([done_ref[...], norm(x_ref[...], gain_ref[...])], axis=0)
    copies[0].wait()
    gate = jnp.dot(normed, gate_ref[...], preferred_element_type=jnp.float32)
    copies[1].wait()
    up = jnp.dot(normed, up_ref[...], preferred_element_type=jnp.float32)
    hidden = (gate / (1.0 + jnp.exp(-gate)) * up).astype(jnp.bfloat16)
    copies[2].wait()
    part = jnp.dot(hidden, down_ref[...], preferred_element_type=jnp.float32).astype(
        jnp.bfloat16
    )
    each, width = last_ref.shape
    out = iter(out_refs)
    for i, k in enumerate(order):
        for begin, end in split_of(k, width):
            next(out)[...] = part[i * each : (i + 1) * each, begin:end]


def expert_call(place, done, last, kv_pieces, gain, w_gate, w_up, w_down, order, rows_true):
    each, width = last.shape
    rows = len(order) * each
    hidden = w_gate.shape[1]
    per_key = width // (kv_pieces[0].shape[1] // 2)
    splits = [split_of(k, width) for k in order]
    shapes = [
        jax.ShapeDtypeStruct((each, end - begin), jnp.bfloat16)
        for split in splits
        for begin, end in split
    ]
    outs = iter(
        pl.pallas_call(
            functools.partial(expert_kernel, len(kv_pieces), tuple(order), per_key, rows_true),
            out_shape=shapes,
            in_specs=[VMEM, SMEM] + [VMEM] * (2 + len(kv_pieces)) + [ANY] * 3,
            out_specs=[VMEM] * len(shapes),
            scratch_shapes=[
                pltpu.VMEM((each, width), jnp.bfloat16),
                pltpu.VMEM(w_gate.shape, jnp.bfloat16),
                pltpu.VMEM(w_up.shape, jnp.bfloat16),
                pltpu.VMEM(w_down.shape, jnp.bfloat16),
                pltpu.SemaphoreType.DMA((3,)),
            ],
            compiler_params=params(48),
            cost_estimate=cost(6 * rows * width * hidden, 6 * width * hidden),
            name="experts",
        )(last, place, done, *kv_pieces, gain, w_gate, w_up, w_down)
    )
    return [[next(outs) for _ in split] for split in splits]


def add(*terms):
    total = terms[0].astype(jnp.float32)
    for t in terms[1:]:
        total = total + t.astype(jnp.float32)
    return total.astype(jnp.bfloat16)


def combine_kernel(
    late_ref, late_theirs_ref, comb_ref, attended_ref, mine_ref, theirs_ref, out_ref
):
    width = out_ref.shape[1]
    half = width - late_ref.shape[1]
    comb = comb_ref[...]
    high = comb.astype(jnp.bfloat16)
    low = (comb - high.astype(jnp.float32)).astype(jnp.bfloat16)
    both = (((0,), (0,)), ((), ()))

    def finish(rows, begin, end):
        rows = jnp.concatenate(rows, axis=0)
        added = lax.dot_general(
            high, rows, both, preferred_element_type=jnp.float32
        ) + lax.dot_general(low, rows, both, preferred_element_type=jnp.float32)
        out_ref[:, begin:end] = (
            attended_ref[:, begin:end].astype(jnp.float32) + added
        ).astype(jnp.bfloat16)

    finish([mine_ref[:, :half], theirs_ref[:, :half]], 0, half)
    finish(
        [
            add(mine_ref[:, half:], late_ref[...]),
            add(theirs_ref[:, half:], late_theirs_ref[...]),
        ],
        half,
        width,
    )


def across(x, stride):
    n = lax.axis_size("seq")
    return lax.ppermute(x, "seq", [(i, i ^ stride) for i in range(n)])


def swap(x):
    return lax.ppermute(x, "tp", [(0, 1), (1, 0)])


def across_and_swap(x, stride):
    n = lax.axis_size("seq")
    pairs = [
        (2 * i + c, 2 * (i ^ stride) + 1 - c) for i in range(n) for c in range(2)
    ]
    return lax.ppermute(x, ("seq", "tp"), pairs)


def tied(*values):
    return lax.optimization_barrier(values)


def body(
    queries, keys_values, prompt_lengths, routes, gate_weights, norm_gain, w_gate, w_up, w_down
):
    tokens, width = queries.shape[1:]
    rows_true = keys_values.shape[1]
    pad = -rows_true % TILE
    seq, core = lax.axis_index("seq"), lax.axis_index("tp")
    own_queries = queries[0]
    strides = [1 << b for b in reversed(range(lax.axis_size("seq").bit_length() - 1))]

    kv = keys_values[0].reshape(rows_true, -1)
    if pad:
        kv = jnp.pad(kv, ((0, pad), (0, 0)))
    keep, send, comb = pl.pallas_call(
        pick_kernel,
        out_shape=[
            jax.ShapeDtypeStruct((CAP, width), jnp.bfloat16),
            jax.ShapeDtypeStruct((CAP, width), jnp.bfloat16),
            jax.ShapeDtypeStruct((2 * CAP, tokens), jnp.float32),
        ],
        in_specs=[SMEM] + [VMEM] * 3,
        out_specs=[VMEM] * 3,
        compiler_params=params(16),
        cost_estimate=cost(4 * CAP * tokens * width, 4 * tokens * width),
        name="pick",
    )(core.reshape(1), routes[0].T, gate_weights[0].T, own_queries)
    routed = jnp.concatenate([keep, swap(send)], axis=0)

    kv_blocks, routed_blocks, order = [kv], [routed], [0]
    for stride in strides[:-1]:
        kv_blocks = kv_blocks + [across(b, stride) for b in kv_blocks]
        routed_blocks = routed_blocks + [across(b, stride) for b in routed_blocks]
        order = order + [k ^ stride for k in order]
    first_kv, first_routed = across(kv, strides[-1]), across(routed, strides[-1])
    kv_blocks, routed_blocks, first_kv, first_routed = tied(
        kv_blocks, routed_blocks, first_kv, first_routed
    )
    kv_blocks = kv_blocks + [first_kv] + [across(b, strides[-1]) for b in kv_blocks[1:]]
    routed_blocks = (
        routed_blocks + [first_routed] + [across(b, strides[-1]) for b in routed_blocks[1:]]
    )
    order = order + [k ^ strides[-1] for k in order]

    pieces, places = [], []
    for block, k in zip([kv] + kv_blocks[1:], order):
        pieces += [block, swap(block)]
        places += [2 * (seq ^ k) + core, 2 * (seq ^ k) + 1 - core]
    place = jnp.stack([p * rows_true for p in places] + [prompt_lengths[0]]).astype(jnp.int32)

    gain = norm_gain.reshape(1, width)
    done = attend_call(place, routed_blocks[:-1], pieces, rows_true, gain)
    parts = expert_call(
        place, done, routed_blocks[-1], pieces, gain, w_gate[0], w_up[0], w_down[0], order, rows_true
    )

    own_queries, parts = tied(own_queries, parts)
    attended = attend_call(place, [own_queries], pieces, rows_true)
    parts = dict(zip(order, parts))
    straight = {k: v[0] for k, v in parts.items()}
    half = width // 2
    held = {k: v[-1][:, -half:] for k, v in parts.items()}
    for stride in strides[::-1][:-1]:
        sent = {k: across(v, stride) for k, v in held.items() if k & stride and k != 1}
        held = {
            k: add(v, sent[k ^ stride]) if k ^ stride in sent else v
            for k, v in held.items()
            if not k & stride
        }
    late, attended = tied(held[strides[0]], attended)
    late_mine = across(late[:CAP], strides[0])
    late_theirs = across_and_swap(late[CAP:], strides[0])
    arrived = [across(v, k) for k, v in straight.items() if k]
    arrived, late = tied(arrived, late)
    so_far = [
        jnp.concatenate(
            [
                add(straight[0][rows, :half], *[a[rows, :half] for a in arrived]),
                add(
                    held[0][rows],
                    *[a[rows, half:] for a in arrived if a.shape[1] == width],
                ),
            ],
            axis=1,
        )
        for rows in (slice(None, CAP), slice(CAP, None))
    ]
    theirs = swap(so_far[1])
    mixed = pl.pallas_call(
        combine_kernel,
        out_shape=jax.ShapeDtypeStruct((tokens, width), jnp.bfloat16),
        in_specs=[VMEM] * 6,
        out_specs=VMEM,
        compiler_params=params(16),
        cost_estimate=cost(8 * CAP * tokens * width, 4 * tokens * width),
        name="combine",
    )(late_mine, late_theirs, comb, attended, so_far[0], theirs)
    return mixed[None]


def solution(mesh):
    return jax.shard_map(
        body,
        mesh=mesh,
        in_specs=(
            P(("group", "exp"), ("seq", "tp"), None),
            P(("group", "exp"), ("seq", "tp"), None, None),
            P(("group", "exp")),
            P(("group", "exp"), ("seq", "tp"), None),
            P(("group", "exp"), ("seq", "tp"), None),
            P(),
            P("tp", None, "seq"),
            P("tp", None, "seq"),
            P("tp", "seq", None),
        ),
        out_specs=P(("group", "exp"), ("seq", "tp"), None),
        check_vma=False,
    )
```

time: 95.5 us -> 84.2 us (0.88)
  waiting for transfers between devices: 49.1 us -> 43.8 us
  starting transfers between devices: 21.4 us -> 16.4 us
  local copies, waits for them, and re-layouts: 8.14 us -> 5.99 us
  Pallas kernels: 15.4 us -> 16.7 us
    ppermute x9 -> x11, waiting for transfers between devices: 47.8 us -> 42.3 us  [across(): return lax.ppermute(x, 'seq', [(i, i ^ stride) for i in range(n)])]
    ppermute x9 -> x11, starting transfers between devices: 20.6 us -> 15.6 us  [across(): return lax.ppermute(x, 'seq', [(i, i ^ stride) for i in range(n)])]
    unnamed x18, local copies, waits for them, and re-layouts: 8 us -> 5.88 us
    ppermute x6, waiting for transfers between devices: 0.02 us -> 1.33 us  [swap(): return lax.ppermute(x, 'tp', [(0, 1), (1, 0)])]
    ppermute x1, waiting for transfers between devices: 1.31 us -> 0.13 us  [across_and_swap(): return lax.ppermute(x, ('seq', 'tp'), pairs)]
    pallas_call x1 -> x2, Pallas kernels: 6.43 us -> 7.33 us  [attend_call(): pl.pallas_call(functools.partial(attend_kernel, len(kv_pieces), len(q_blo...]
  transfers between devices with their start and end apart: 16 -> 18, of which waited for: 7 -> 9; matrix products, arithmetic and copies ran while one was open for 2% -> 0% of each run, Pallas kernels for 7% -> 9%
where the time goes in v2:
time: 84.2 us; the launch traced here: 83.8 us
  waiting for transfers between devices  43.8 us (52%)
  Pallas kernels  16.7 us (20%)
  starting transfers between devices  16.4 us (19%)
  local copies, waits for them, and re-layouts  5.99 us (7%)
    ppermute x11, waiting for transfers between devices, across(): return lax.ppermute(x, 'seq', [(i, i ^ stride) for i in range(n)])  42.3 us
    ppermute x11, starting transfers between devices, across(): return lax.ppermute(x, 'seq', [(i, i ^ stride) for i in range(n)])  15.6 us
    pallas_call x1, Pallas kernels, expert_call(): pl.pallas_call(functools.partial(expert_kernel, len(kv_pieces), tuple(ord...  7.73 us
    pallas_call x2, Pallas kernels, attend_call(): pl.pallas_call(functools.partial(attend_kernel, len(kv_pieces), len(q_blo...  7.33 us
    unnamed x18, local copies, waits for them, and re-layouts  5.88 us
  transfers between devices with their start and end apart: 18, of which 9 were waited for; matrix products, arithmetic and copies ran while one was open for 0% of the time, Pallas kernels for 9%

profile of v2, /device:TPU:0, one launch (start us, length us, event | category | flops | bytes accessed | tf_op | source)
XLA Modules:
  0.0 83.8 jit_solution(16861840490350327001)
XLA Ops:
  0.0 1.1 %copy.10 = bf16[12,8,2,1024]{3,1,2,0:T(8,128)(2,1)S(1)} copy(bf16[12,8,2,1024]{3,2,1,0:T(2,128)(2,1)} %bitcast.39) | data formatting | bytes 786432
  1.1 3.1 %collective-permute-start.3 = (bf16[96,2048]{1,0:T(8,128)(2,1)S(1)}, bf16[96,2048]{1,0:T(8,128)(2,1)S(1)}, u32[]{:S(2)}, u32[]{:S(2)}) collective-permute-start(bf16[96,2048]{1,0:T(8,128)(2,1)S(1)} %bitcast.24), channel_id=1, source_target_pairs={{0,4},{4,0},{8,12},{12,8},{1,5},{5,1},{9,13},{13,9},{2,6},{6,2},{1... | collective-permute-start | bytes 1179656 | tf_op jit(solution)/shard_map/ppermute | solution.py:282
  4.2 2.6 %collective-permute-start = (bf16[96,2048]{1,0:T(8,128)(2,1)S(1)}, bf16[96,2048]{1,0:T(8,128)(2,1)S(1)}, u32[]{:S(2)}, u32[]{:S(2)}) collective-permute-start(bf16[96,2048]{1,0:T(8,128)(2,1)S(1)} %bitcast.25), channel_id=1, source_target_pairs={{0,8},{4,12},{8,0},{12,4},{1,9},{5,13},{9,1},{13,5},{2,10},{6,14},... | collective-permute-start | bytes 1179656 | tf_op jit(solution)/shard_map/ppermute | solution.py:282
  6.8 1.0 %copy-done = bf16[1,64,4096]{2,1,0:T(8,128)(2,1)S(1)} copy-done((bf16[1,64,4096]{2,1,0:T(8,128)(2,1)S(1)}, bf16[1,64,4096]{2,1,0:T(8,128)(2,1)}, u32[]{:S(2)}) %copy-start) | copy-done | bytes 524312
  9.6 1.3 %collective-permute-done.1 = bf16[16,4096]{1,0:T(8,128)(2,1)S(1)} collective-permute-done((bf16[16,4096]{1,0:T(8,128)(2,1)S(1)}, bf16[16,4096]{1,0:T(8,128)(2,1)S(1)}, u32[]{:S(2)}, u32[]{:S(2)}) %collective-permute-start.1) | collective-permute-done | bytes 131104 | tf_op jit(solution)/shard_map/ppermute | solution.py:286
  11.5 21.4 %collective-permute-done.4.refs_2_ = bf16[32,4096]{1,0:T(8,128)(2,1)S(1)} collective-permute-done((bf16[32,4096]{1,0:T(8,128)(2,1)S(1)}, bf16[32,4096]{1,0:T(8,128)(2,1)S(1)}, u32[]{:S(2)}, u32[]{:S(2)}) %collective-permute-start.4) | collective-permute-done | bytes 262176 | tf_op jit(solution)/shard_map/ppermute | solution.py:282
  32.8 0.7 copy-done.2
  33.5 2.0 %collective-permute-done.2.refs_1_ = bf16[32,4096]{1,0:T(8,128)(2,1)} collective-permute-done((bf16[32,4096]{1,0:T(8,128)(2,1)S(1)}, bf16[32,4096]{1,0:T(8,128)(2,1)}, u32[]{:S(2)}, u32[]{:S(2)}) %collective-permute-start.2) | collective-permute-done | bytes 262176 | tf_op jit(solution)/shard_map/ppermute | solution.py:282
  36.5 7.7 %collective-permute-done.9.refs_9_.refs_6_.refs_7_ = bf16[96,2048]{1,0:T(8,128)(2,1)S(1)} collective-permute-done((bf16[96,2048]{1,0:T(8,128)(2,1)S(1)}, bf16[96,2048]{1,0:T(8,128)(2,1)S(1)}, u32[]{:S(2)}, u32[]{:S(2)}) %collective-permute-start.9) | collective-permute-done | bytes 393248 | tf_op jit(solution)/shard_map/ppermute | solution.py:282
  44.2 1.7 %collective-permute-start.5 = (bf16[32,4096]{1,0:T(8,128)(2,1)}, bf16[32,4096]{1,0:T(8,128)(2,1)}, u32[]{:S(2)}, u32[]{:S(2)}) collective-permute-start(bf16[32,4096]{1,0:T(8,128)(2,1)} %collective-permute-done.2.refs_1_), channel_id=1, source_target_pairs={{0,4},{4,0},{8,12},{12,8},{1,5},{5,1},{9,13},{13,9},{2,6},{6,2},{1... | collective-permute-start | bytes 786440 | tf_op jit(solution)/shard_map/ppermute | solution.py:282
  46.7 0.9 %copy-done.3 = bf16[32,4096]{1,0:T(8,128)(2,1)S(1)} copy-done((bf16[32,4096]{1,0:T(8,128)(2,1)S(1)}, bf16[32,4096]{1,0:T(8,128)(2,1)}, u32[]{:S(2)}) %copy-start.3) | copy-done | bytes 262168
  47.6 0.7 copy-done.4
  48.4 4.5 %attend.2.done_ref = bf16[96,4096]{1,0:T(8,128)(2,1)S(1)} custom-call(s32[9]{0:T(128)S(1)} %stack.35.place_ref, bf16[32,4096]{1,0:T(8,128)(2,1)S(1)} %constant_dynamic-update-slice_fusion.refs_0_, bf16[32,4096]{1,0:T(8,128)(2,1)} %collective-permute-done.2.refs_1_, bf16[32,4096]{1,0:T(8,128)(2,1)S(1)} %copy-done.3, bf16[96,2048]{1,0:T(8,128)(2,1)S(1)} %bitcast.27, ...), custom_call_target="tpu_custom_call" | custom-call | flops 1207959552 | bytes 4718592 | tf_op jit(solution)/shard_map/attend/pallas_call | solution.py:148
  53.2 7.7 %experts.1 = (bf16[32,4096]{1,0:T(8,128)(2,1)S(1)}, bf16[32,2048]{1,0:T(8,128)(2,1)S(1)}, bf16[32,2048]{1,0:T(8,128)(2,1)S(1)}, bf16[32,4096]{1,0:T(8,128)(2,1)S...) custom-call(bf16[32,4096]{1,0:T(8,128)(2,1)} %collective-permute-done.5.last_ref, s32[9]{0:T(128)S(1)} %stack.35.place_ref, ...), custom_call_target="tpu_custom_call" | custom-call | flops 1610612736 | bytes 12582912 | tf_op jit(solution)/shard_map/experts/pallas_call | solution.py:223
  60.9 1.8 %collective-permute-start.11 = (bf16[32,2048]{1,0:T(8,128)(2,1)S(1)}, bf16[32,2048]{1,0:T(8,128)(2,1)S(1)}, u32[]{:S(2)}, u32[]{:S(2)}) collective-permute-start(bf16[32,2048]{1,0:T(8,128)(2,1)S(1)} %get-tuple-element.45), channel_id=1, source_target_pairs={{0,4},{4,0},{8,12},{12,8},{1,5},{5,1},{9,13},{13,9},{2,6},{6,2},{1... | collective-permute-start | bytes 393224 | tf_op jit(solution)/shard_map/ppermute | solution.py:282
  62.8 1.0 %collective-permute-start.14 = (bf16[32,2048]{1,0:T(8,128)(2,1)S(1)}, bf16[32,2048]{1,0:T(8,128)(2,1)S(1)}, u32[]{:S(2)}, u32[]{:S(2)}) collective-permute-start(bf16[32,2048]{1,0:T(8,128)(2,1)S(1)} %get-tuple-element.51), channel_id=1, source_target_pairs={{0,8},{4,12},{8,0},{12,4},{1,9},{5,13},{9,1},{13,5},{2,10},{6,14},... | collective-permute-start | bytes 393224 | tf_op jit(solution)/shard_map/ppermute | solution.py:282
  63.8 1.6 %collective-permute-start.16 = (bf16[32,2048]{1,0:T(8,128)(2,1)S(1)}, bf16[32,2048]{1,0:T(8,128)(2,1)S(1)}, u32[]{:S(2)}, u32[]{:S(2)}) collective-permute-start(bf16[32,2048]{1,0:T(8,128)(2,1)S(1)} %get-tuple-element.53), channel_id=1, source_target_pairs={{0,12},{4,8},{8,4},{12,0},{1,13},{5,9},{9,5},{13,1},{2,14},{6,10},... | collective-permute-start | bytes 393224 | tf_op jit(solution)/shard_map/ppermute | solution.py:282
  65.4 0.8 %collective-permute-start.15 = (bf16[32,4096]{1,0:T(8,128)(2,1)S(1)}, bf16[32,4096]{1,0:T(8,128)(2,1)S(1)}, u32[]{:S(2)}, u32[]{:S(2)}) collective-permute-start(bf16[32,4096]{1,0:T(8,128)(2,1)S(1)} %get-tuple-element.52), channel_id=1, source_target_pairs={{0,4},{4,0},{8,12},{12,8},{1,5},{5,1},{9,13},{13,9},{2,6},{6,2},{1... | collective-permute-start | bytes 786440 | tf_op jit(solution)/shard_map/ppermute | solution.py:282
  66.2 2.9 %attend.3.attended_ref = bf16[64,4096]{1,0:T(8,128)(2,1)S(1)} custom-call(s32[9]{0:T(128)S(1)} %stack.35.place_ref, bf16[64,4096]{1,0:T(8,128)(2,1)S(1)} %bitcast.31, bf16[96,2048]{1,0:T(8,128)(2,1)S(1)} %bitcast.29, bf16[96,2048]{1,0:T(8,128)(2,1)S(1)} %collective-permute-done.6.refs_4_.refs_1_.refs_2_, ...), custom_call_target="tpu_custom_call" | custom-call | flops 805306368 | bytes 4194304 | tf_op jit(solution)/shard_map/attend/pallas_call | solution.py:148
  69.4 1.9 %collective-permute-start.12 = (bf16[16,2048]{1,0:T(8,128)(2,1)S(1)}, bf16[16,2048]{1,0:T(8,128)(2,1)S(1)}, u32[]{:S(2)}, u32[]{:S(2)}) collective-permute-start(bf16[16,2048]{1,0:T(8,128)(2,1)S(1)} %get-tuple-element.62), channel_id=1, source_target_pairs={{0,8},{4,12},{8,0},{12,4},{1,9},{5,13},{9,1},{13,5},{2,10},{6,14},... | collective-permute-start | bytes 196616 | tf_op jit(solution)/shard_map/ppermute | solution.py:282
  71.3 3.8 %collective-permute-done.14 = bf16[32,2048]{1,0:T(8,128)(2,1)S(1)} collective-permute-done((bf16[32,2048]{1,0:T(8,128)(2,1)S(1)}, bf16[32,2048]{1,0:T(8,128)(2,1)S(1)}, u32[]{:S(2)}, u32[]{:S(2)}) %collective-permute-start.14) | collective-permute-done | bytes 131104 | tf_op jit(solution)/shard_map/ppermute | solution.py:282
  75.1 3.4 %collective-permute-done.15 = bf16[32,4096]{1,0:T(8,128)(2,1)S(1)} collective-permute-done((bf16[32,4096]{1,0:T(8,128)(2,1)S(1)}, bf16[32,4096]{1,0:T(8,128)(2,1)S(1)}, u32[]{:S(2)}, u32[]{:S(2)}) %collective-permute-start.15) | collective-permute-done | bytes 262176 | tf_op jit(solution)/shard_map/ppermute | solution.py:282
  78.8 3.8 %collective-permute-done.12.late_ref = bf16[16,2048]{1,0:T(8,128)(2,1)S(1)} collective-permute-done((bf16[16,2048]{1,0:T(8,128)(2,1)S(1)}, bf16[16,2048]{1,0:T(8,128)(2,1)S(1)}, u32[]{:S(2)}, u32[]{:S(2)}) %collective-permute-start.12) | collective-permute-done | bytes 65568 | tf_op jit(solution)/shard_map/ppermute | solution.py:282
  82.6 1.3 %combine.1 = bf16[64,4096]{1,0:T(8,128)(2,1)} custom-call(bf16[16,2048]{1,0:T(8,128)(2,1)S(1)} %collective-permute-done.12.late_ref, bf16[16,2048]{1,0:T(8,128)(2,1)S(1)} %collective-permute-done.13.late_theirs_ref, f32[32,64]{1,0:T(8,128)S(1)} %get-tuple-element.48.comb_ref, bf16[64,4096]{1,0:T(8,128)(2,1)S(1)} %attend.3.attended_ref, ...), custom_call_target="tpu_custom_call" | custom-call | flops 33554432 | bytes 1048576 | tf_op jit(solution)/shard_map/combine/pallas_call | solution.py:388
  (42 shorter events, 4.4 us)
Async XLA Ops:
  0.0 53.2 %copy-start.5 = (f32[4096]{0:T(1024)S(1)}, f32[4096]{0:T(1024)}, u32[]{:S(2)}) copy-start(f32[4096]{0:T(1024)} %param.14) | copy-start | bytes 49156
  1.1 34.4 %collective-permute-start.3 = (bf16[96,2048]{1,0:T(8,128)(2,1)S(1)}, bf16[96,2048]{1,0:T(8,128)(2,1)S(1)}, u32[]{:S(2)}, u32[]{:S(2)}) collective-permute-start(bf16[96,2048]{1,0:T(8,128)(2,1)S(1)} %bitcast.24), channel_id=1, source_target_pairs={{0,4},{4,0},{8,12},{12,8},{1,5},{5,1},{9,13},{13,9},{2,6},{6,2},{1... | collective-permute-start | bytes 1179656 | tf_op jit(solution)/shard_map/ppermute | solution.py:282
  4.2 31.3 %collective-permute-start = (bf16[96,2048]{1,0:T(8,128)(2,1)S(1)}, bf16[96,2048]{1,0:T(8,128)(2,1)S(1)}, u32[]{:S(2)}, u32[]{:S(2)}) collective-permute-start(bf16[96,2048]{1,0:T(8,128)(2,1)S(1)} %bitcast.25), channel_id=1, source_target_pairs={{0,8},{4,12},{8,0},{12,4},{1,9},{5,13},{9,1},{13,5},{2,10},{6,14},... | collective-permute-start | bytes 1179656 | tf_op jit(solution)/shard_map/ppermute | solution.py:282
  6.8 1.0 %copy-start = (bf16[1,64,4096]{2,1,0:T(8,128)(2,1)S(1)}, bf16[1,64,4096]{2,1,0:T(8,128)(2,1)}, u32[]{:S(2)}) copy-start(bf16[1,64,4096]{2,1,0:T(8,128)(2,1)} %param.9) | copy-start | bytes 1572868
  9.5 1.4 %collective-permute-start.1 = (bf16[16,4096]{1,0:T(8,128)(2,1)S(1)}, bf16[16,4096]{1,0:T(8,128)(2,1)S(1)}, u32[]{:S(2)}, u32[]{:S(2)}) collective-permute-start(bf16[16,4096]{1,0:T(8,128)(2,1)S(1)} %get-tuple-element.32), channel_id=1, source_target_pairs={{0,1},{1,0},{2,3},{3,2},{4,5},{5,4},{6,7},{7,6},{8,9},{9,8},{10,11... | collective-permute-start | bytes 393224 | tf_op jit(solution)/shard_map/ppermute | solution.py:286
  11.0 21.9 %collective-permute-start.4 = (bf16[32,4096]{1,0:T(8,128)(2,1)S(1)}, bf16[32,4096]{1,0:T(8,128)(2,1)S(1)}, u32[]{:S(2)}, u32[]{:S(2)}) collective-permute-start(bf16[32,4096]{1,0:T(8,128)(2,1)S(1)} %constant_dynamic-update-slice_fusion.refs_0_), channel_id=1, source_target_pairs={{0,4},{4,0},{8,12},{12,8},{1,5},{5,1},{9,13},{13,9},{2,6},{6,2},{1... | collective-permute-start | bytes 786440 | tf_op jit(solution)/shard_map/ppermute | solution.py:282
  11.5 24.0 %collective-permute-start.2 = (bf16[32,4096]{1,0:T(8,128)(2,1)S(1)}, bf16[32,4096]{1,0:T(8,128)(2,1)}, u32[]{:S(2)}, u32[]{:S(2)}) collective-permute-start(bf16[32,4096]{1,0:T(8,128)(2,1)S(1)} %constant_dynamic-update-slice_fusion.refs_0_), channel_id=1, source_target_pairs={{0,8},{4,12},{8,0},{12,4},{1,9},{5,13},{9,1},{13,5},{2,10},{6,14},... | collective-permute-start | bytes 786440 | tf_op jit(solution)/shard_map/ppermute | solution.py:282
  32.8 0.7 copy-start.2
  35.5 8.6 %collective-permute-start.9 = (bf16[96,2048]{1,0:T(8,128)(2,1)S(1)}, bf16[96,2048]{1,0:T(8,128)(2,1)S(1)}, u32[]{:S(2)}, u32[]{:S(2)}) collective-permute-start(bf16[96,2048]{1,0:T(8,128)(2,1)S(1)} %collective-permute-done.refs_5_.refs_2_.refs_3_), channel_id=1, source_target_pairs={{0,4},{4,0},{8,12},{12,8},{1,5},{5,1},{9,13},{13,9},{2,6},{6,2},{1... | collective-permute-start | bytes 1179656 | tf_op jit(solution)/shard_map/ppermute | solution.py:282
  36.0 10.7 %collective-permute-start.6 = (bf16[96,2048]{1,0:T(8,128)(2,1)S(1)}, bf16[96,2048]{1,0:T(8,128)(2,1)S(1)}, u32[]{:S(2)}, u32[]{:S(2)}) collective-permute-start(bf16[96,2048]{1,0:T(8,128)(2,1)S(1)} %bitcast.26), channel_id=1, source_target_pairs={{0,1},{1,0},{2,3},{3,2},{4,5},{5,4},{6,7},{7,6},{8,9},{9,8},{10,11... | collective-permute-start | bytes 1179656 | tf_op jit(solution)/shard_map/ppermute | solution.py:286
  36.0 10.7 %collective-permute-start.7 = (bf16[96,2048]{1,0:T(8,128)(2,1)S(1)}, bf16[96,2048]{1,0:T(8,128)(2,1)S(1)}, u32[]{:S(2)}, u32[]{:S(2)}) collective-permute-start(bf16[96,2048]{1,0:T(8,128)(2,1)S(1)} %collective-permute-done.refs_5_.refs_2_.refs_3_), channel_id=1, source_target_pairs={{0,1},{1,0},{2,3},{3,2},{4,5},{5,4},{6,7},{7,6},{8,9},{9,8},{10,11... | collective-permute-start | bytes 1179656 | tf_op jit(solution)/shard_map/ppermute | solution.py:286
  36.5 10.2 %collective-permute-start.8 = (bf16[96,2048]{1,0:T(8,128)(2,1)S(1)}, bf16[96,2048]{1,0:T(8,128)(2,1)S(1)}, u32[]{:S(2)}, u32[]{:S(2)}) collective-permute-start(bf16[96,2048]{1,0:T(8,128)(2,1)S(1)} %collective-permute-done.3.refs_7_.refs_4_.refs_5_), channel_id=1, source_target_pairs={{0,1},{1,0},{2,3},{3,2},{4,5},{5,4},{6,7},{7,6},{8,9},{9,8},{10,11... | collective-permute-start | bytes 1179656 | tf_op jit(solution)/shard_map/ppermute | solution.py:286
  44.2 2.5 %collective-permute-start.10 = (bf16[96,2048]{1,0:T(8,128)(2,1)S(1)}, bf16[96,2048]{1,0:T(8,128)(2,1)S(1)}, u32[]{:S(2)}, u32[]{:S(2)}) collective-permute-start(bf16[96,2048]{1,0:T(8,128)(2,1)S(1)} %collective-permute-done.9.refs_9_.refs_6_.refs_7_), channel_id=1, source_target_pairs={{0,1},{1,0},{2,3},{3,2},{4,5},{5,4},{6,7},{7,6},{8,9},{9,8},{10,11... | collective-permute-start | bytes 1179656 | tf_op jit(solution)/shard_map/ppermute | solution.py:286
  44.2 9.0 %collective-permute-start.5 = (bf16[32,4096]{1,0:T(8,128)(2,1)}, bf16[32,4096]{1,0:T(8,128)(2,1)}, u32[]{:S(2)}, u32[]{:S(2)}) collective-permute-start(bf16[32,4096]{1,0:T(8,128)(2,1)} %collective-permute-done.2.refs_1_), channel_id=1, source_target_pairs={{0,4},{4,0},{8,12},{12,8},{1,5},{5,1},{9,13},{13,9},{2,6},{6,2},{1... | collective-permute-start | bytes 786440 | tf_op jit(solution)/shard_map/ppermute | solution.py:282
  46.7 1.0 %copy-start.3 = (bf16[32,4096]{1,0:T(8,128)(2,1)S(1)}, bf16[32,4096]{1,0:T(8,128)(2,1)}, u32[]{:S(2)}) copy-start(bf16[32,4096]{1,0:T(8,128)(2,1)} %copy-done.2) | copy-start | bytes 786436
  47.6 0.7 copy-start.4
  53.2 13.0 %copy-start.1 = (bf16[1,64,4096]{2,1,0:T(8,128)(2,1)S(1)}, bf16[1,64,4096]{2,1,0:T(8,128)(2,1)}, u32[]{:S(2)}) copy-start(bf16[1,64,4096]{2,1,0:T(8,128)(2,1)} %param.9) | copy-start | bytes 1572868
  60.9 8.2 %collective-permute-start.11 = (bf16[32,2048]{1,0:T(8,128)(2,1)S(1)}, bf16[32,2048]{1,0:T(8,128)(2,1)S(1)}, u32[]{:S(2)}, u32[]{:S(2)}) collective-permute-start(bf16[32,2048]{1,0:T(8,128)(2,1)S(1)} %get-tuple-element.45), channel_id=1, source_target_pairs={{0,4},{4,0},{8,12},{12,8},{1,5},{5,1},{9,13},{13,9},{2,6},{6,2},{1... | collective-permute-start | bytes 393224 | tf_op jit(solution)/shard_map/ppermute | solution.py:282
  62.8 12.3 %collective-permute-start.14 = (bf16[32,2048]{1,0:T(8,128)(2,1)S(1)}, bf16[32,2048]{1,0:T(8,128)(2,1)S(1)}, u32[]{:S(2)}, u32[]{:S(2)}) collective-permute-start(bf16[32,2048]{1,0:T(8,128)(2,1)S(1)} %get-tuple-element.51), channel_id=1, source_target_pairs={{0,8},{4,12},{8,0},{12,4},{1,9},{5,13},{9,1},{13,5},{2,10},{6,14},... | collective-permute-start | bytes 393224 | tf_op jit(solution)/shard_map/ppermute | solution.py:282
  63.8 11.3 %collective-permute-start.16 = (bf16[32,2048]{1,0:T(8,128)(2,1)S(1)}, bf16[32,2048]{1,0:T(8,128)(2,1)S(1)}, u32[]{:S(2)}, u32[]{:S(2)}) collective-permute-start(bf16[32,2048]{1,0:T(8,128)(2,1)S(1)} %get-tuple-element.53), channel_id=1, source_target_pairs={{0,12},{4,8},{8,4},{12,0},{1,13},{5,9},{9,5},{13,1},{2,14},{6,10},... | collective-permute-start | bytes 393224 | tf_op jit(solution)/shard_map/ppermute | solution.py:282
  65.4 13.0 %collective-permute-start.15 = (bf16[32,4096]{1,0:T(8,128)(2,1)S(1)}, bf16[32,4096]{1,0:T(8,128)(2,1)S(1)}, u32[]{:S(2)}, u32[]{:S(2)}) collective-permute-start(bf16[32,4096]{1,0:T(8,128)(2,1)S(1)} %get-tuple-element.52), channel_id=1, source_target_pairs={{0,4},{4,0},{8,12},{12,8},{1,5},{5,1},{9,13},{13,9},{2,6},{6,2},{1... | collective-permute-start | bytes 786440 | tf_op jit(solution)/shard_map/ppermute | solution.py:282
  69.2 9.6 %collective-permute-start.13 = (bf16[16,2048]{1,0:T(8,128)(2,1)S(1)}, bf16[16,2048]{1,0:T(8,128)(2,1)S(1)}, u32[]{:S(2)}, u32[]{:S(2)}) collective-permute-start(bf16[16,2048]{1,0:T(8,128)(2,1)S(1)} %get-tuple-element.61), channel_id=1, source_target_pairs={{0,9},{1,8},{4,13},{5,12},{8,1},{9,0},{12,5},{13,4},{2,11},{3,10},... | collective-permute-start | bytes 196616 | tf_op jit(solution)/shard_map/ppermute | solution.py:294
  69.4 13.2 %collective-permute-start.12 = (bf16[16,2048]{1,0:T(8,128)(2,1)S(1)}, bf16[16,2048]{1,0:T(8,128)(2,1)S(1)}, u32[]{:S(2)}, u32[]{:S(2)}) collective-permute-start(bf16[16,2048]{1,0:T(8,128)(2,1)S(1)} %get-tuple-element.62), channel_id=1, source_target_pairs={{0,8},{4,12},{8,0},{12,4},{1,9},{5,13},{9,1},{13,5},{2,10},{6,14},... | collective-permute-start | bytes 196616 | tf_op jit(solution)/shard_map/ppermute | solution.py:282
  78.6 4.0 %collective-permute-start.17 = (bf16[16,4096]{1,0:T(8,128)(2,1)S(1)}, bf16[16,4096]{1,0:T(8,128)(2,1)S(1)}, u32[]{:S(2)}, u32[]{:S(2)}) collective-permute-start(bf16[16,4096]{1,0:T(8,128)(2,1)S(1)} %pad_maximum_fusion.1), channel_id=1, source_target_pairs={{0,1},{1,0},{2,3},{3,2},{4,5},{5,4},{6,7},{7,6},{8,9},{9,8},{10,11... | collective-permute-start | bytes 393224 | tf_op jit(solution)/shard_map/ppermute | solution.py:286
  (2 other events, 1.4 us)

commit v3 on v2

--- a/solution.py
+++ b/solution.py
@@ -153,63 +153,102 @@
         in_specs=[SMEM] + [VMEM] * (len(q_blocks) + len(kv_pieces) + len(gain)),
         out_specs=VMEM,
         compiler_params=params(20 if rows * keys < 1 << 18 else 56),
-        cost_estimate=cost(
-            4 * rows * width * keys,
-            4 * rows * width + 2 * keys * kv_pieces[0].shape[1],
-            rows * keys * width // HEAD_DIM,
-        ),
+        cost_estimate=cost(1, 1),
         name="attend",
     )(place, *q_blocks, *kv_pieces, *gain)
 
 
+def cut_of(width):
+    return width * 3 // 8 // HEAD_DIM * HEAD_DIM
+
+
 def split_of(k, width):
-    half = width // 2
-    return [(0, width)] if k < 2 else [(0, half), (half, width)]
-
-
-def expert_kernel(
-    pieces, order, per_key, rows_true, last_ref, place_ref, done_ref, *refs
-):
+    return [(0, width)] if k < 2 else [(0, cut_of(width)), (cut_of(width), width)]
+
+
+def start_copies(pairs, sems):
+    copies = [pltpu.make_async_copy(s, d, sems.at[i]) for i, (s, d) in enumerate(pairs)]
+    for c in copies:
+        c.start()
+    return copies
+
+
+def gated(normed, gate_copy, gate_ref, up_copy, up_ref):
+    gate_copy.wait()
+    gate = jnp.dot(normed, gate_ref[...], preferred_element_type=jnp.float32)
+    up_copy.wait()
+    up = jnp.dot(normed, up_ref[...], preferred_element_type=jnp.float32)
+    return (gate / (1.0 + jnp.exp(-gate)) * up).astype(jnp.bfloat16)
+
+
+def attend_block(place_ref, block_ref, kv_refs, gain_ref, x_ref, per_key, rows_true):
+    bias = key_bias(place_ref, len(kv_refs), kv_refs[0].shape[0], rows_true)
+
+    def queries(at, size):
+        return block_ref[:, pl.ds(at, size)]
+
+    def store(at, result):
+        x_ref[:, pl.ds(at, HEAD_DIM)] = result
+
+    attend(queries, kv_refs, bias, store, per_key)
+    return norm(x_ref[...], gain_ref[...])
+
+
+def hidden_kernel(pieces, per_key, rows_true, block_ref, place_ref, done_ref, *refs):
+    kv_refs = refs[:pieces]
+    gain_ref, gate_hbm, up_hbm, out_ref, x_ref, gate_ref, up_ref, sems = refs[pieces:]
+    copies = start_copies(((gate_hbm, gate_ref), (up_hbm, up_ref)), sems)
+    last = attend_block(place_ref, block_ref, kv_refs, gain_ref, x_ref, per_key, rows_true)
+    normed = jnp.concatenate([done_ref[...], last], axis=0)
+    out_ref[...] = gated(normed, copies[0], gate_ref, copies[1], up_ref)
+
+
+def expert_kernel(pieces, order, per_key, rows_true, block_ref, place_ref, done_ref, *refs):
     kv_refs = refs[:pieces]
     gain_ref, gate_hbm, up_hbm, down_hbm = refs[pieces : pieces + 4]
     out_refs = refs[pieces + 4 : -5]
     x_ref, gate_ref, up_ref, down_ref, sems = refs[-5:]
-    copies = [
-        pltpu.make_async_copy(src, dst, sems.at[i])
-        for i, (src, dst) in enumerate(
-            ((gate_hbm, gate_ref), (up_hbm, up_ref), (down_hbm, down_ref))
-        )
-    ]
-    for c in copies:
-        c.start()
-    bias = key_bias(place_ref, pieces, kv_refs[0].shape[0], rows_true)
-
-    def queries(at, size):
-        return last_ref[:, pl.ds(at, size)]
-
-    def store(at, result):
-        x_ref[:, pl.ds(at, HEAD_DIM)] = result
-
-    attend(queries, kv_refs, bias, store, per_key)
-    normed = jnp.concatenate([done_ref[...], norm(x_ref[...], gain_ref[...])], axis=0)
-    copies[0].wait()
-    gate = jnp.dot(normed, gate_ref[...], preferred_element_type=jnp.float32)
-    copies[1].wait()
-    up = jnp.dot(normed, up_ref[...], preferred_element_type=jnp.float32)
-    hidden = (gate / (1.0 + jnp.exp(-gate)) * up).astype(jnp.bfloat16)
+    copies = start_copies(
+        ((gate_hbm, gate_ref), (up_hbm, up_ref), (down_hbm, down_ref)), sems
+    )
+    last = attend_block(place_ref, block_ref, kv_refs, gain_ref, x_ref, per_key, rows_true)
+    hidden = jnp.concatenate(
+        [done_ref[...], gated(last, copies[0], gate_ref, copies[1], up_ref)], axis=0
+    )
     copies[2].wait()
     part = jnp.dot(hidden, down_ref[...], preferred_element_type=jnp.float32).astype(
         jnp.bfloat16
     )
-    each, width = last_ref.shape
+    each, width = block_ref.shape
     out = iter(out_refs)
     for i, k in enumerate(order):
         for begin, end in split_of(k, width):
             next(out)[...] = part[i * each : (i + 1) * each, begin:end]
 
 
-def expert_call(place, done, last, kv_pieces, gain, w_gate, w_up, w_down, order, rows_true):
-    each, width = last.shape
+def hidden_call(place, done, block, kv_pieces, gain, w_gate, w_up, rows_true):
+    each, width = block.shape
+    rows, hidden = done.shape[0] + each, w_gate.shape[1]
+    per_key = width // (kv_pieces[0].shape[1] // 2)
+    return pl.pallas_call(
+        functools.partial(hidden_kernel, len(kv_pieces), per_key, rows_true),
+        out_shape=jax.ShapeDtypeStruct((rows, hidden), jnp.bfloat16),
+        in_specs=[VMEM, SMEM] + [VMEM] * (2 + len(kv_pieces)) + [ANY] * 2,
+        out_specs=VMEM,
+        scratch_shapes=[
+            pltpu.VMEM((each, width), jnp.bfloat16),
+            pltpu.VMEM(w_gate.shape, jnp.bfloat16),
+            pltpu.VMEM(w_up.shape, jnp.bfloat16),
+            pltpu.SemaphoreType.DMA((2,)),
+        ],
+        compiler_params=params(44),
+        cost_estimate=cost(1, 1),
+        name="hidden",
+    )(block, place, done, *kv_pieces, gain, w_gate, w_up)
+
+
+def expert_call(place, done, block, kv_pieces, gain, w_gate, w_up, w_down, order, rows_true):
+    each, width = block.shape
     rows = len(order) * each
     hidden = w_gate.shape[1]
     per_key = width // (kv_pieces[0].shape[1] // 2)
@@ -235,7 +274,7 @@
             compiler_params=params(48),
             cost_estimate=cost(6 * rows * width * hidden, 6 * width * hidden),
             name="experts",
-        )(last, place, done, *kv_pieces, gain, w_gate, w_up, w_down)
+        )(block, place, done, *kv_pieces, gain, w_gate, w_up, w_down)
     )
     return [[next(outs) for _ in split] for split in splits]
 
@@ -324,41 +363,38 @@
         cost_estimate=cost(4 * CAP * tokens * width, 4 * tokens * width),
         name="pick",
     )(core.reshape(1), routes[0].T, gate_weights[0].T, own_queries)
-    routed = jnp.concatenate([keep, swap(send)], axis=0)
-
-    kv_blocks, routed_blocks, order = [kv], [routed], [0]
+    came = swap(send)
+
+    kv_blocks, order = [kv], [0]
     for stride in strides[:-1]:
         kv_blocks = kv_blocks + [across(b, stride) for b in kv_blocks]
+        order = order + [k ^ stride for k in order]
+    first_kv, own_swapped = across(kv, strides[-1]), swap(kv)
+    kv_blocks, first_kv, own_swapped, came = tied(kv_blocks, first_kv, own_swapped, came)
+    kv_blocks = kv_blocks + [first_kv] + [across(b, strides[-1]) for b in kv_blocks[1:]]
+    order = order + [k ^ strides[-1] for k in order]
+    routed_blocks = [jnp.concatenate([keep, came], axis=0)]
+    for stride in strides:
         routed_blocks = routed_blocks + [across(b, stride) for b in routed_blocks]
-        order = order + [k ^ stride for k in order]
-    first_kv, first_routed = across(kv, strides[-1]), across(routed, strides[-1])
-    kv_blocks, routed_blocks, first_kv, first_routed = tied(
-        kv_blocks, routed_blocks, first_kv, first_routed
-    )
-    kv_blocks = kv_blocks + [first_kv] + [across(b, strides[-1]) for b in kv_blocks[1:]]
-    routed_blocks = (
-        routed_blocks + [first_routed] + [across(b, strides[-1]) for b in routed_blocks[1:]]
-    )
-    order = order + [k ^ strides[-1] for k in order]
 
     pieces, places = [], []
-    for block, k in zip([kv] + kv_blocks[1:], order):
-        pieces += [block, swap(block)]
+    for block, k in zip(kv_blocks, order):
+        pieces += [block, swap(block) if k else own_swapped]
         places += [2 * (seq ^ k) + core, 2 * (seq ^ k) + 1 - core]
     place = jnp.stack([p * rows_true for p in places] + [prompt_lengths[0]]).astype(jnp.int32)
 
     gain = norm_gain.reshape(1, width)
-    done = attend_call(place, routed_blocks[:-1], pieces, rows_true, gain)
+    weights = w_gate[0], w_up[0]
+    done = attend_call(place, routed_blocks[:-2], pieces, rows_true, gain)
+    done = hidden_call(place, done, routed_blocks[-2], pieces, gain, *weights, rows_true)
     parts = expert_call(
-        place, done, routed_blocks[-1], pieces, gain, w_gate[0], w_up[0], w_down[0], order, rows_true
-    )
-
-    own_queries, parts = tied(own_queries, parts)
-    attended = attend_call(place, [own_queries], pieces, rows_true)
+        place, done, routed_blocks[-1], pieces, gain, *weights, w_down[0], order, rows_true
+    )
+
     parts = dict(zip(order, parts))
     straight = {k: v[0] for k, v in parts.items()}
-    half = width // 2
-    held = {k: v[-1][:, -half:] for k, v in parts.items()}
+    cut = cut_of(width)
+    held = {k: v[-1][:, cut - width :] for k, v in parts.items()}
     for stride in strides[::-1][:-1]:
         sent = {k: across(v, stride) for k, v in held.items() if k & stride and k != 1}
         held = {
@@ -366,7 +402,8 @@
             for k, v in held.items()
             if not k & stride
         }
-    late, attended = tied(held[strides[0]], attended)
+    late, own_queries = tied(held[strides[0]], own_queries)
+    attended = attend_call(place, [own_queries], pieces, rows_true)
     late_mine = across(late[:CAP], strides[0])
     late_theirs = across_and_swap(late[CAP:], strides[0])
     arrived = [across(v, k) for k, v in straight.items() if k]
@@ -374,10 +411,10 @@
     so_far = [
         jnp.concatenate(
             [
-                add(straight[0][rows, :half], *[a[rows, :half] for a in arrived]),
+                add(straight[0][rows, :cut], *[a[rows, :cut] for a in arrived]),
                 add(
                     held[0][rows],
-                    *[a[rows, half:] for a in arrived if a.shape[1] == width],
+                    *[a[rows, cut:] for a in arrived if a.shape[1] == width],
                 ),
             ],
             axis=1,

time: 84.2 us -> 86.5 us (1.027)
  waiting for transfers between devices: 43.8 us -> 36.9 us
  starting transfers between devices: 16.4 us -> 22.1 us
  Pallas kernels: 16.7 us -> 21.6 us
  local copies, waits for them, and re-layouts: 5.99 us -> 4.49 us
    ppermute x11, waiting for transfers between devices: 42.3 us -> 35.5 us  [across(): return lax.ppermute(x, 'seq', [(i, i ^ stride) for i in range(n)])]
    pallas_call x0 -> x1, Pallas kernels: none -> 5.79 us  [hidden_call(): pl.pallas_call(functools.partial(hidden_kernel, len(kv_pieces), per_key,...]
    ppermute x11, starting transfers between devices: 15.6 us -> 20.9 us  [across(): return lax.ppermute(x, 'seq', [(i, i ^ stride) for i in range(n)])]
    unnamed x18 -> x16, local copies, waits for them, and re-layouts: 5.88 us -> 4.38 us
  transfers between devices with their start and end apart: 18 -> 18, of which waited for: 9 -> 9; matrix products, arithmetic and copies ran while one was open for 0% -> 0% of each run, Pallas kernels for 9% -> 15%
where the time goes in v3:
time: 86.5 us; the launch traced here: 86.1 us
  waiting for transfers between devices  36.9 us (43%)
  starting transfers between devices  22.1 us (26%)
  Pallas kernels  21.6 us (25%)
  local copies, waits for them, and re-layouts  4.49 us (5%)
    ppermute x11, waiting for transfers between devices, across(): return lax.ppermute(x, 'seq', [(i, i ^ stride) for i in range(n)])  35.5 us
    ppermute x11, starting transfers between devices, across(): return lax.ppermute(x, 'seq', [(i, i ^ stride) for i in range(n)])  20.9 us
    pallas_call x1, Pallas kernels, expert_call(): pl.pallas_call(functools.partial(expert_kernel, len(kv_pieces), tuple(ord...  7.71 us
    pallas_call x2, Pallas kernels, attend_call(): pl.pallas_call(functools.partial(attend_kernel, len(kv_pieces), len(q_blo...  6.52 us
    pallas_call x1, Pallas kernels, hidden_call(): pl.pallas_call(functools.partial(hidden_kernel, len(kv_pieces), per_key,...  5.79 us
    unnamed x16, local copies, waits for them, and re-layouts  4.38 us
  transfers between devices with their start and end apart: 18, of which 9 were waited for; matrix products, arithmetic and copies ran while one was open for 0% of the time, Pallas kernels for 15%

profile of v3, /device:TPU:0, one launch (start us, length us, event | category | flops | bytes accessed | tf_op | source)
XLA Modules:
  0.0 86.1 jit_solution(6605794260336783034)
XLA Ops:
  0.0 1.1 %copy.10 = bf16[12,8,2,1024]{3,1,2,0:T(8,128)(2,1)S(1)} copy(bf16[12,8,2,1024]{3,2,1,0:T(2,128)(2,1)} %bitcast.43) | data formatting | bytes 786432
  1.1 4.1 %collective-permute-start = (bf16[96,2048]{1,0:T(8,128)(2,1)S(1)}, bf16[96,2048]{1,0:T(8,128)(2,1)S(1)}, u32[]{:S(2)}, u32[]{:S(2)}) collective-permute-start(bf16[96,2048]{1,0:T(8,128)(2,1)S(1)} %bitcast.26), channel_id=1, source_target_pairs={{0,8},{4,12},{8,0},{12,4},{1,9},{5,13},{9,1},{13,5},{2,10},{6,14},... | collective-permute-start | bytes 1179656 | tf_op jit(solution)/shard_map/ppermute | solution.py:321
  5.2 1.6 %collective-permute-start.1 = (bf16[96,2048]{1,0:T(8,128)(2,1)S(1)}, bf16[96,2048]{1,0:T(8,128)(2,1)S(1)}, u32[]{:S(2)}, u32[]{:S(2)}) collective-permute-start(bf16[96,2048]{1,0:T(8,128)(2,1)S(1)} %bitcast.27), channel_id=1, source_target_pairs={{0,4},{4,0},{8,12},{12,8},{1,5},{5,1},{9,13},{13,9},{2,6},{6,2},{1... | collective-permute-start | bytes 1179656 | tf_op jit(solution)/shard_map/ppermute | solution.py:321
  6.8 1.0 %copy-done.1 = bf16[1,64,4096]{2,1,0:T(8,128)(2,1)S(1)} copy-done((bf16[1,64,4096]{2,1,0:T(8,128)(2,1)S(1)}, bf16[1,64,4096]{2,1,0:T(8,128)(2,1)}, u32[]{:S(2)}) %copy-start.1) | copy-done | bytes 524312
  10.1 1.0 %collective-permute-done.3 = bf16[16,4096]{1,0:T(8,128)(2,1)S(1)} collective-permute-done((bf16[16,4096]{1,0:T(8,128)(2,1)S(1)}, bf16[16,4096]{1,0:T(8,128)(2,1)S(1)}, u32[]{:S(2)}, u32[]{:S(2)}) %collective-permute-start.3) | collective-permute-done | bytes 131104 | tf_op jit(solution)/shard_map/ppermute | solution.py:325
  11.1 11.8 %collective-permute-done.refs_4_.refs_2_.refs_3_ = bf16[96,2048]{1,0:T(8,128)(2,1)S(1)} collective-permute-done((bf16[96,2048]{1,0:T(8,128)(2,1)S(1)}, bf16[96,2048]{1,0:T(8,128)(2,1)S(1)}, u32[]{:S(2)}, u32[]{:S(2)}) %collective-permute-start) | collective-permute-done | bytes 393248 | tf_op jit(solution)/shard_map/ppermute | solution.py:321
  23.0 1.5 %collective-permute-start.9 = (bf16[96,2048]{1,0:T(8,128)(2,1)S(1)}, bf16[96,2048]{1,0:T(8,128)(2,1)S(1)}, u32[]{:S(2)}, u32[]{:S(2)}) collective-permute-start(bf16[96,2048]{1,0:T(8,128)(2,1)S(1)} %collective-permute-done.refs_4_.refs_2_.refs_3_), channel_id=1, source_target_pairs={{0,4},{4,0},{8,12},{12,8},{1,5},{5,1},{9,13},{13,9},{2,6},{6,2},{1... | collective-permute-start | bytes 1179656 | tf_op jit(solution)/shard_map/ppermute | solution.py:321
  24.5 2.4 %collective-permute-start.4 = (bf16[32,4096]{1,0:T(8,128)(2,1)S(1)}, bf16[32,4096]{1,0:T(8,128)(2,1)}, u32[]{:S(2)}, u32[]{:S(2)}) collective-permute-start(bf16[32,4096]{1,0:T(8,128)(2,1)S(1)} %constant_dynamic-update-slice_fusion.refs_0_), channel_id=1, source_target_pairs={{0,8},{4,12},{8,0},{12,4},{1,9},{5,13},{9,1},{13,5},{2,10},{6,14},... | collective-permute-start | bytes 786440 | tf_op jit(solution)/shard_map/ppermute | solution.py:321
  27.4 11.3 %collective-permute-done.9.refs_8_.refs_6_.refs_7_ = bf16[96,2048]{1,0:T(8,128)(2,1)S(1)} collective-permute-done((bf16[96,2048]{1,0:T(8,128)(2,1)S(1)}, bf16[96,2048]{1,0:T(8,128)(2,1)S(1)}, u32[]{:S(2)}, u32[]{:S(2)}) %collective-permute-start.9) | collective-permute-done | bytes 393248 | tf_op jit(solution)/shard_map/ppermute | solution.py:321
  38.7 3.1 %collective-permute-start.5 = (bf16[32,4096]{1,0:T(8,128)(2,1)}, bf16[32,4096]{1,0:T(8,128)(2,1)}, u32[]{:S(2)}, u32[]{:S(2)}) collective-permute-start(bf16[32,4096]{1,0:T(8,128)(2,1)} %collective-permute-done.4.refs_1_), channel_id=1, source_target_pairs={{0,4},{4,0},{8,12},{12,8},{1,5},{5,1},{9,13},{13,9},{2,6},{6,2},{1... | collective-permute-start | bytes 786440 | tf_op jit(solution)/shard_map/ppermute | solution.py:321
  42.6 0.9 copy-done.3
  43.5 3.7 %attend.2.done_ref = bf16[64,4096]{1,0:T(8,128)(2,1)S(1)} custom-call(s32[9]{0:T(128)S(1)} %stack.35.place_ref, bf16[32,4096]{1,0:T(8,128)(2,1)S(1)} %constant_dynamic-update-slice_fusion.refs_0_, bf16[32,4096]{1,0:T(8,128)(2,1)} %collective-permute-done.4.refs_1_, bf16[96,2048]{1,0:T(8,128)(2,1)S(1)} %bitcast.29, ...), custom_call_target="tpu_custom_call" | custom-call | flops 1 | bytes 1 | tf_op jit(solution)/shard_map/attend/pallas_call | solution.py:148
  47.2 0.7 collective-permute-done.6.block_ref
  47.9 5.8 %hidden.1.done_ref = bf16[96,512]{1,0:T(8,128)(2,1)S(1)} custom-call(bf16[32,4096]{1,0:T(8,128)(2,1)} %collective-permute-done.6.block_ref, s32[9]{0:T(128)S(1)} %stack.35.place_ref, bf16[64,4096]{1,0:T(8,128)(2,1)S(1)} %attend.2.done_ref, bf16[96,2048]{1,0:T(8,128)(2,1)S(1)} %bitcast.30, ...), custom_call_target="tpu_custom_call" | custom-call | flops 1 | bytes 1 | tf_op jit(solution)/shard_map/hidden/pallas_call | solution.py:233
  53.7 7.7 %experts.1 = (bf16[32,4096]{1,0:T(8,128)(2,1)S(1)}, bf16[32,1536]{1,0:T(8,128)(2,1)S(1)}, bf16[32,2560]{1,0:T(8,128)(2,1)S(1)}, bf16[32,4096]{1,0:T(8,128)(2,1)S...) custom-call(bf16[32,4096]{1,0:T(8,128)(2,1)} %collective-permute-done.5.block_ref, ...), custom_call_target="tpu_custom_call" | custom-call | flops 1610612736 | bytes 12582912 | tf_op jit(solution)/shard_map/experts/pallas_call | solution.py:262
  61.6 1.9 %collective-permute-start.15 = (bf16[32,4096]{1,0:T(8,128)(2,1)S(1)}, bf16[32,4096]{1,0:T(8,128)(2,1)S(1)}, u32[]{:S(2)}, u32[]{:S(2)}) collective-permute-start(bf16[32,4096]{1,0:T(8,128)(2,1)S(1)} %get-tuple-element.38), channel_id=1, source_target_pairs={{0,4},{4,0},{8,12},{12,8},{1,5},{5,1},{9,13},{13,9},{2,6},{6,2},{1... | collective-permute-start | bytes 786440 | tf_op jit(solution)/shard_map/ppermute | solution.py:321
  63.6 2.9 %collective-permute-start.14 = (bf16[32,1536]{1,0:T(8,128)(2,1)S(1)}, bf16[32,1536]{1,0:T(8,128)(2,1)S(1)}, u32[]{:S(2)}, u32[]{:S(2)}) collective-permute-start(bf16[32,1536]{1,0:T(8,128)(2,1)S(1)} %get-tuple-element.37), channel_id=1, source_target_pairs={{0,8},{4,12},{8,0},{12,4},{1,9},{5,13},{9,1},{13,5},{2,10},{6,14},... | collective-permute-start | bytes 294920 | tf_op jit(solution)/shard_map/ppermute | solution.py:321
  66.4 1.4 %collective-permute-start.16 = (bf16[32,1536]{1,0:T(8,128)(2,1)S(1)}, bf16[32,1536]{1,0:T(8,128)(2,1)S(1)}, u32[]{:S(2)}, u32[]{:S(2)}) collective-permute-start(bf16[32,1536]{1,0:T(8,128)(2,1)S(1)} %get-tuple-element.39), channel_id=1, source_target_pairs={{0,12},{4,8},{8,4},{12,0},{1,13},{5,9},{9,5},{13,1},{2,14},{6,10},... | collective-permute-start | bytes 294920 | tf_op jit(solution)/shard_map/ppermute | solution.py:321
  67.8 3.9 %collective-permute-done.11 = bf16[32,2560]{1,0:T(8,128)(2,1)S(1)} collective-permute-done((bf16[32,2560]{1,0:T(8,128)(2,1)S(1)}, bf16[32,2560]{1,0:T(8,128)(2,1)S(1)}, u32[]{:S(2)}, u32[]{:S(2)}) %collective-permute-start.11) | collective-permute-done | bytes 163872 | tf_op jit(solution)/shard_map/ppermute | solution.py:321
  71.7 1.9 %collective-permute-start.12 = (bf16[16,2560]{1,0:T(8,128)(2,1)S(1)}, bf16[16,2560]{1,0:T(8,128)(2,1)S(1)}, u32[]{:S(2)}, u32[]{:S(2)}) collective-permute-start(bf16[16,2560]{1,0:T(8,128)(2,1)S(1)} %get-tuple-element.48), channel_id=1, source_target_pairs={{0,8},{4,12},{8,0},{12,4},{1,9},{5,13},{9,1},{13,5},{2,10},{6,14},... | collective-permute-start | bytes 245768 | tf_op jit(solution)/shard_map/ppermute | solution.py:321
  73.6 2.9 %attend.3.attended_ref = bf16[64,4096]{1,0:T(8,128)(2,1)S(1)} custom-call(s32[9]{0:T(128)S(1)} %stack.35.place_ref, bf16[64,4096]{1,0:T(8,128)(2,1)S(1)} %bitcast.34, bf16[96,2048]{1,0:T(8,128)(2,1)S(1)} %bitcast.32, bf16[96,2048]{1,0:T(8,128)(2,1)S(1)} %collective-permute-done.2.refs_3_.refs_1_.refs_2_, ...), custom_call_target="tpu_custom_call" | custom-call | flops 1 | bytes 1 | tf_op jit(solution)/shard_map/attend/pallas_call | solution.py:148
  76.5 4.4 %collective-permute-done.16 = bf16[32,1536]{1,0:T(8,128)(2,1)S(1)} collective-permute-done((bf16[32,1536]{1,0:T(8,128)(2,1)S(1)}, bf16[32,1536]{1,0:T(8,128)(2,1)S(1)}, u32[]{:S(2)}, u32[]{:S(2)}) %collective-permute-start.16) | collective-permute-done | bytes 98336 | tf_op jit(solution)/shard_map/ppermute | solution.py:321
  81.1 3.3 %collective-permute-done.12.late_ref = bf16[16,2560]{1,0:T(8,128)(2,1)S(1)} collective-permute-done((bf16[16,2560]{1,0:T(8,128)(2,1)S(1)}, bf16[16,2560]{1,0:T(8,128)(2,1)S(1)}, u32[]{:S(2)}, u32[]{:S(2)}) %collective-permute-start.12) | collective-permute-done | bytes 81952 | tf_op jit(solution)/shard_map/ppermute | solution.py:321
  84.9 1.3 %combine.1 = bf16[64,4096]{1,0:T(8,128)(2,1)} custom-call(bf16[16,2560]{1,0:T(8,128)(2,1)S(1)} %collective-permute-done.12.late_ref, bf16[16,2560]{1,0:T(8,128)(2,1)S(1)} %collective-permute-done.13.late_theirs_ref, f32[32,64]{1,0:T(8,128)S(1)} %get-tuple-element.34.comb_ref, bf16[64,4096]{1,0:T(8,128)(2,1)S(1)} %attend.3.attended_ref, ...), custom_call_target="tpu_custom_call" | custom-call | flops 33554432 | bytes 1048576 | tf_op jit(solution)/shard_map/combine/pallas_call | solution.py:425
  (42 shorter events, 4.0 us)
Async XLA Ops:
  0.0 47.9 %copy-start.4 = (f32[4096]{0:T(1024)S(1)}, f32[4096]{0:T(1024)}, u32[]{:S(2)}) copy-start(f32[4096]{0:T(1024)} %param.14) | copy-start | bytes 49156
  1.1 21.7 %collective-permute-start = (bf16[96,2048]{1,0:T(8,128)(2,1)S(1)}, bf16[96,2048]{1,0:T(8,128)(2,1)S(1)}, u32[]{:S(2)}, u32[]{:S(2)}) collective-permute-start(bf16[96,2048]{1,0:T(8,128)(2,1)S(1)} %bitcast.26), channel_id=1, source_target_pairs={{0,8},{4,12},{8,0},{12,4},{1,9},{5,13},{9,1},{13,5},{2,10},{6,14},... | collective-permute-start | bytes 1179656 | tf_op jit(solution)/shard_map/ppermute | solution.py:321
  5.2 17.8 %collective-permute-start.1 = (bf16[96,2048]{1,0:T(8,128)(2,1)S(1)}, bf16[96,2048]{1,0:T(8,128)(2,1)S(1)}, u32[]{:S(2)}, u32[]{:S(2)}) collective-permute-start(bf16[96,2048]{1,0:T(8,128)(2,1)S(1)} %bitcast.27), channel_id=1, source_target_pairs={{0,4},{4,0},{8,12},{12,8},{1,5},{5,1},{9,13},{13,9},{2,6},{6,2},{1... | collective-permute-start | bytes 1179656 | tf_op jit(solution)/shard_map/ppermute | solution.py:321
  6.8 16.3 %collective-permute-start.2 = (bf16[96,2048]{1,0:T(8,128)(2,1)S(1)}, bf16[96,2048]{1,0:T(8,128)(2,1)S(1)}, u32[]{:S(2)}, u32[]{:S(2)}) collective-permute-start(bf16[96,2048]{1,0:T(8,128)(2,1)S(1)} %bitcast.28), channel_id=1, source_target_pairs={{0,1},{1,0},{2,3},{3,2},{4,5},{5,4},{6,7},{7,6},{8,9},{9,8},{10,11... | collective-permute-start | bytes 1179656 | tf_op jit(solution)/shard_map/ppermute | solution.py:325
  6.8 1.0 %copy-start.1 = (bf16[1,64,4096]{2,1,0:T(8,128)(2,1)S(1)}, bf16[1,64,4096]{2,1,0:T(8,128)(2,1)}, u32[]{:S(2)}) copy-start(bf16[1,64,4096]{2,1,0:T(8,128)(2,1)} %param.9) | copy-start | bytes 1572868
  7.8 0.7 copy-start.5
  9.5 1.6 %collective-permute-start.3 = (bf16[16,4096]{1,0:T(8,128)(2,1)S(1)}, bf16[16,4096]{1,0:T(8,128)(2,1)S(1)}, u32[]{:S(2)}, u32[]{:S(2)}) collective-permute-start(bf16[16,4096]{1,0:T(8,128)(2,1)S(1)} %get-tuple-element.25), channel_id=1, source_target_pairs={{0,1},{1,0},{2,3},{3,2},{4,5},{5,4},{6,7},{7,6},{8,9},{9,8},{10,11... | collective-permute-start | bytes 393224 | tf_op jit(solution)/shard_map/ppermute | solution.py:325
  23.0 15.7 %collective-permute-start.9 = (bf16[96,2048]{1,0:T(8,128)(2,1)S(1)}, bf16[96,2048]{1,0:T(8,128)(2,1)S(1)}, u32[]{:S(2)}, u32[]{:S(2)}) collective-permute-start(bf16[96,2048]{1,0:T(8,128)(2,1)S(1)} %collective-permute-done.refs_4_.refs_2_.refs_3_), channel_id=1, source_target_pairs={{0,4},{4,0},{8,12},{12,8},{1,5},{5,1},{9,13},{13,9},{2,6},{6,2},{1... | collective-permute-start | bytes 1179656 | tf_op jit(solution)/shard_map/ppermute | solution.py:321
  24.5 14.2 %collective-permute-start.4 = (bf16[32,4096]{1,0:T(8,128)(2,1)S(1)}, bf16[32,4096]{1,0:T(8,128)(2,1)}, u32[]{:S(2)}, u32[]{:S(2)}) collective-permute-start(bf16[32,4096]{1,0:T(8,128)(2,1)S(1)} %constant_dynamic-update-slice_fusion.refs_0_), channel_id=1, source_target_pairs={{0,8},{4,12},{8,0},{12,4},{1,9},{5,13},{9,1},{13,5},{2,10},{6,14},... | collective-permute-start | bytes 786440 | tf_op jit(solution)/shard_map/ppermute | solution.py:321
  26.9 15.7 %collective-permute-start.7 = (bf16[96,2048]{1,0:T(8,128)(2,1)S(1)}, bf16[96,2048]{1,0:T(8,128)(2,1)S(1)}, u32[]{:S(2)}, u32[]{:S(2)}) collective-permute-start(bf16[96,2048]{1,0:T(8,128)(2,1)S(1)} %collective-permute-done.refs_4_.refs_2_.refs_3_), channel_id=1, source_target_pairs={{0,1},{1,0},{2,3},{3,2},{4,5},{5,4},{6,7},{7,6},{8,9},{9,8},{10,11... | collective-permute-start | bytes 1179656 | tf_op jit(solution)/shard_map/ppermute | solution.py:325
  26.9 15.7 %collective-permute-start.8 = (bf16[96,2048]{1,0:T(8,128)(2,1)S(1)}, bf16[96,2048]{1,0:T(8,128)(2,1)S(1)}, u32[]{:S(2)}, u32[]{:S(2)}) collective-permute-start(bf16[96,2048]{1,0:T(8,128)(2,1)S(1)} %collective-permute-done.1.refs_6_.refs_4_.refs_5_), channel_id=1, source_target_pairs={{0,1},{1,0},{2,3},{3,2},{4,5},{5,4},{6,7},{7,6},{8,9},{9,8},{10,11... | collective-permute-start | bytes 1179656 | tf_op jit(solution)/shard_map/ppermute | solution.py:325
  38.7 3.9 %collective-permute-start.10 = (bf16[96,2048]{1,0:T(8,128)(2,1)S(1)}, bf16[96,2048]{1,0:T(8,128)(2,1)S(1)}, u32[]{:S(2)}, u32[]{:S(2)}) collective-permute-start(bf16[96,2048]{1,0:T(8,128)(2,1)S(1)} %collective-permute-done.9.refs_8_.refs_6_.refs_7_), channel_id=1, source_target_pairs={{0,1},{1,0},{2,3},{3,2},{4,5},{5,4},{6,7},{7,6},{8,9},{9,8},{10,11... | collective-permute-start | bytes 1179656 | tf_op jit(solution)/shard_map/ppermute | solution.py:325
  38.7 9.2 %collective-permute-start.6 = (bf16[32,4096]{1,0:T(8,128)(2,1)S(1)}, bf16[32,4096]{1,0:T(8,128)(2,1)}, u32[]{:S(2)}, u32[]{:S(2)}) collective-permute-start(bf16[32,4096]{1,0:T(8,128)(2,1)S(1)} %constant_dynamic-update-slice_fusion.refs_0_), channel_id=1, source_target_pairs={{0,4},{4,0},{8,12},{12,8},{1,5},{5,1},{9,13},{13,9},{2,6},{6,2},{1... | collective-permute-start | bytes 786440 | tf_op jit(solution)/shard_map/ppermute | solution.py:321
  38.7 15.0 %collective-permute-start.5 = (bf16[32,4096]{1,0:T(8,128)(2,1)}, bf16[32,4096]{1,0:T(8,128)(2,1)}, u32[]{:S(2)}, u32[]{:S(2)}) collective-permute-start(bf16[32,4096]{1,0:T(8,128)(2,1)} %collective-permute-done.4.refs_1_), channel_id=1, source_target_pairs={{0,4},{4,0},{8,12},{12,8},{1,5},{5,1},{9,13},{13,9},{2,6},{6,2},{1... | collective-permute-start | bytes 786440 | tf_op jit(solution)/shard_map/ppermute | solution.py:321
  42.6 5.3 %copy-start = (bf16[1,4096,512]{2,1,0:T(8,128)(2,1)S(1)}, bf16[1,4096,512]{2,1,0:T(8,128)(2,1)}, u32[]{:S(2)}) copy-start(bf16[1,4096,512]{2,1,0:T(8,128)(2,1)} %param.15) | copy-start | bytes 12582916
  42.6 0.9 %copy-start.3 = (f32[4096]{0:T(1024)S(1)}, f32[4096]{0:T(1024)}, u32[]{:S(2)}) copy-start(f32[4096]{0:T(1024)} %param.14) | copy-start | bytes 49156
  53.7 19.9 %copy-start.2 = (bf16[1,64,4096]{2,1,0:T(8,128)(2,1)S(1)}, bf16[1,64,4096]{2,1,0:T(8,128)(2,1)}, u32[]{:S(2)}) copy-start(bf16[1,64,4096]{2,1,0:T(8,128)(2,1)} %param.9) | copy-start | bytes 1572868
  61.5 10.2 %collective-permute-start.11 = (bf16[32,2560]{1,0:T(8,128)(2,1)S(1)}, bf16[32,2560]{1,0:T(8,128)(2,1)S(1)}, u32[]{:S(2)}, u32[]{:S(2)}) collective-permute-start(bf16[32,2560]{1,0:T(8,128)(2,1)S(1)} %get-tuple-element.32), channel_id=1, source_target_pairs={{0,4},{4,0},{8,12},{12,8},{1,5},{5,1},{9,13},{13,9},{2,6},{6,2},{1... | collective-permute-start | bytes 491528 | tf_op jit(solution)/shard_map/ppermute | solution.py:321
  61.6 19.3 %collective-permute-start.15 = (bf16[32,4096]{1,0:T(8,128)(2,1)S(1)}, bf16[32,4096]{1,0:T(8,128)(2,1)S(1)}, u32[]{:S(2)}, u32[]{:S(2)}) collective-permute-start(bf16[32,4096]{1,0:T(8,128)(2,1)S(1)} %get-tuple-element.38), channel_id=1, source_target_pairs={{0,4},{4,0},{8,12},{12,8},{1,5},{5,1},{9,13},{13,9},{2,6},{6,2},{1... | collective-permute-start | bytes 786440 | tf_op jit(solution)/shard_map/ppermute | solution.py:321
  63.6 12.9 %collective-permute-start.14 = (bf16[32,1536]{1,0:T(8,128)(2,1)S(1)}, bf16[32,1536]{1,0:T(8,128)(2,1)S(1)}, u32[]{:S(2)}, u32[]{:S(2)}) collective-permute-start(bf16[32,1536]{1,0:T(8,128)(2,1)S(1)} %get-tuple-element.37), channel_id=1, source_target_pairs={{0,8},{4,12},{8,0},{12,4},{1,9},{5,13},{9,1},{13,5},{2,10},{6,14},... | collective-permute-start | bytes 294920 | tf_op jit(solution)/shard_map/ppermute | solution.py:321
  66.4 14.4 %collective-permute-start.16 = (bf16[32,1536]{1,0:T(8,128)(2,1)S(1)}, bf16[32,1536]{1,0:T(8,128)(2,1)S(1)}, u32[]{:S(2)}, u32[]{:S(2)}) collective-permute-start(bf16[32,1536]{1,0:T(8,128)(2,1)S(1)} %get-tuple-element.39), channel_id=1, source_target_pairs={{0,12},{4,8},{8,4},{12,0},{1,13},{5,9},{9,5},{13,1},{2,14},{6,10},... | collective-permute-start | bytes 294920 | tf_op jit(solution)/shard_map/ppermute | solution.py:321
  71.7 12.6 %collective-permute-start.12 = (bf16[16,2560]{1,0:T(8,128)(2,1)S(1)}, bf16[16,2560]{1,0:T(8,128)(2,1)S(1)}, u32[]{:S(2)}, u32[]{:S(2)}) collective-permute-start(bf16[16,2560]{1,0:T(8,128)(2,1)S(1)} %get-tuple-element.48), channel_id=1, source_target_pairs={{0,8},{4,12},{8,0},{12,4},{1,9},{5,13},{9,1},{13,5},{2,10},{6,14},... | collective-permute-start | bytes 245768 | tf_op jit(solution)/shard_map/ppermute | solution.py:321
  73.6 11.2 %collective-permute-start.13 = (bf16[16,2560]{1,0:T(8,128)(2,1)S(1)}, bf16[16,2560]{1,0:T(8,128)(2,1)S(1)}, u32[]{:S(2)}, u32[]{:S(2)}) collective-permute-start(bf16[16,2560]{1,0:T(8,128)(2,1)S(1)} %get-tuple-element.47), channel_id=1, source_target_pairs={{0,9},{1,8},{4,13},{5,12},{8,1},{9,0},{12,5},{13,4},{2,11},{3,10},... | collective-permute-start | bytes 245768 | tf_op jit(solution)/shard_map/ppermute | solution.py:333
  81.0 3.9 %collective-permute-start.17 = (bf16[16,4096]{1,0:T(8,128)(2,1)S(1)}, bf16[16,4096]{1,0:T(8,128)(2,1)S(1)}, u32[]{:S(2)}, u32[]{:S(2)}) collective-permute-start(bf16[16,4096]{1,0:T(8,128)(2,1)S(1)} %pad_maximum_fusion.1), channel_id=1, source_target_pairs={{0,1},{1,0},{2,3},{3,2},{4,5},{5,4},{6,7},{7,6},{8,9},{9,8},{10,11... | collective-permute-start | bytes 393224 | tf_op jit(solution)/shard_map/ppermute | solution.py:325
  (1 other events, 0.7 us)

commit v4 on v2

--- a/solution.py
+++ b/solution.py
@@ -19,7 +19,7 @@
 
 VMEM = pl.BlockSpec(memory_space=pltpu.VMEM)
 SMEM = pl.BlockSpec(memory_space=pltpu.SMEM)
-ANY = pl.BlockSpec(memory_space=pl.ANY)
+HBM = pl.BlockSpec(memory_space=pltpu.HBM)
 
 
 def params(mib):
@@ -162,22 +162,25 @@
     )(place, *q_blocks, *kv_pieces, *gain)
 
 
+def cut_of(width):
+    return width * 3 // 8 // HEAD_DIM * HEAD_DIM
+
+
 def split_of(k, width):
-    half = width // 2
-    return [(0, width)] if k < 2 else [(0, half), (half, width)]
+    return [(0, width)] if k < 2 else [(0, cut_of(width)), (cut_of(width), width)]
 
 
 def expert_kernel(
     pieces, order, per_key, rows_true, last_ref, place_ref, done_ref, *refs
 ):
     kv_refs = refs[:pieces]
-    gain_ref, gate_hbm, up_hbm, down_hbm = refs[pieces : pieces + 4]
-    out_refs = refs[pieces + 4 : -5]
-    x_ref, gate_ref, up_ref, down_ref, sems = refs[-5:]
+    gain_ref, gate_ref, up_hbm, down_hbm = refs[pieces : pieces + 4]
+    out_refs = refs[pieces + 4 : -4]
+    x_ref, up_ref, down_ref, sems = refs[-4:]
     copies = [
         pltpu.make_async_copy(src, dst, sems.at[i])
         for i, (src, dst) in enumerate(
-            ((gate_hbm, gate_ref), (up_hbm, up_ref), (down_hbm, down_ref))
+            ((up_hbm, up_ref), (down_hbm, down_ref))
         )
     ]
     for c in copies:
@@ -192,12 +195,11 @@
 
     attend(queries, kv_refs, bias, store, per_key)
     normed = jnp.concatenate([done_ref[...], norm(x_ref[...], gain_ref[...])], axis=0)
+    gate = jnp.dot(normed, gate_ref[...], preferred_element_type=jnp.float32)
     copies[0].wait()
-    gate = jnp.dot(normed, gate_ref[...], preferred_element_type=jnp.float32)
-    copies[1].wait()
     up = jnp.dot(normed, up_ref[...], preferred_element_type=jnp.float32)
     hidden = (gate / (1.0 + jnp.exp(-gate)) * up).astype(jnp.bfloat16)
-    copies[2].wait()
+    copies[1].wait()
     part = jnp.dot(hidden, down_ref[...], preferred_element_type=jnp.float32).astype(
         jnp.bfloat16
     )
@@ -223,16 +225,15 @@
         pl.pallas_call(
             functools.partial(expert_kernel, len(kv_pieces), tuple(order), per_key, rows_true),
             out_shape=shapes,
-            in_specs=[VMEM, SMEM] + [VMEM] * (2 + len(kv_pieces)) + [ANY] * 3,
+            in_specs=[VMEM, SMEM] + [VMEM] * (3 + len(kv_pieces)) + [HBM] * 2,
             out_specs=[VMEM] * len(shapes),
             scratch_shapes=[
                 pltpu.VMEM((each, width), jnp.bfloat16),
-                pltpu.VMEM(w_gate.shape, jnp.bfloat16),
                 pltpu.VMEM(w_up.shape, jnp.bfloat16),
                 pltpu.VMEM(w_down.shape, jnp.bfloat16),
-                pltpu.SemaphoreType.DMA((3,)),
+                pltpu.SemaphoreType.DMA((2,)),
             ],
-            compiler_params=params(48),
+            compiler_params=params(26 if rows * hidden < 1 << 17 else 44),
             cost_estimate=cost(6 * rows * width * hidden, 6 * width * hidden),
             name="experts",
         )(last, place, done, *kv_pieces, gain, w_gate, w_up, w_down)
@@ -292,6 +293,10 @@
         (2 * i + c, 2 * (i ^ stride) + 1 - c) for i in range(n) for c in range(2)
     ]
     return lax.ppermute(x, ("seq", "tp"), pairs)
+
+
+def in_hbm(x):
+    return pltpu.with_memory_space_constraint(x, pltpu.HBM)
 
 
 def tied(*values):
@@ -350,15 +355,15 @@
     gain = norm_gain.reshape(1, width)
     done = attend_call(place, routed_blocks[:-1], pieces, rows_true, gain)
     parts = expert_call(
-        place, done, routed_blocks[-1], pieces, gain, w_gate[0], w_up[0], w_down[0], order, rows_true
+        place, done, routed_blocks[-1], pieces, gain, w_gate[0], in_hbm(w_up[0]), in_hbm(w_down[0]), order, rows_true
     )
 
     own_queries, parts = tied(own_queries, parts)
     attended = attend_call(place, [own_queries], pieces, rows_true)
     parts = dict(zip(order, parts))
     straight = {k: v[0] for k, v in parts.items()}
-    half = width // 2
-    held = {k: v[-1][:, -half:] for k, v in parts.items()}
+    cut = cut_of(width)
+    held = {k: v[-1][:, cut - width :] for k, v in parts.items()}
     for stride in strides[::-1][:-1]:
         sent = {k: across(v, stride) for k, v in held.items() if k & stride and k != 1}
         held = {
@@ -374,10 +379,10 @@
     so_far = [
         jnp.concatenate(
             [
-                add(straight[0][rows, :half], *[a[rows, :half] for a in arrived]),
+                add(straight[0][rows, :cut], *[a[rows, :cut] for a in arrived]),
                 add(
                     held[0][rows],
-                    *[a[rows, half:] for a in arrived if a.shape[1] == width],
+                    *[a[rows, cut:] for a in arrived if a.shape[1] == width],
                 ),
             ],
             axis=1,

time: 84.2 us -> 83.5 us (level)
  starting transfers between devices: 16.4 us -> 15.1 us
    ppermute x6, waiting for transfers between devices: 1.33 us -> 2.62 us  [swap(): return lax.ppermute(x, 'tp', [(0, 1), (1, 0)])]
    ppermute x11, starting transfers between devices: 15.6 us -> 14.4 us  [across(): return lax.ppermute(x, 'seq', [(i, i ^ stride) for i in range(n)])]
    unnamed x18 -> x20, local copies, waits for them, and re-layouts: 5.88 us -> 6.24 us
where the time goes in v4:
time: 83.5 us; the launch traced here: 83.2 us
  waiting for transfers between devices  44.4 us (53%)
  Pallas kernels  16.3 us (20%)
  starting transfers between devices  15.1 us (18%)
  local copies, waits for them, and re-layouts  6.35 us (8%)
  between operations  0.84 us (1%)
    ppermute x11, waiting for transfers between devices, across(): return lax.ppermute(x, 'seq', [(i, i ^ stride) for i in range(n)])  41.7 us
    ppermute x11, starting transfers between devices, across(): return lax.ppermute(x, 'seq', [(i, i ^ stride) for i in range(n)])  14.4 us
    pallas_call x1, Pallas kernels, expert_call(): pl.pallas_call(functools.partial(expert_kernel, len(kv_pieces), tuple(ord...  7.39 us
    pallas_call x2, Pallas kernels, attend_call(): pl.pallas_call(functools.partial(attend_kernel, len(kv_pieces), len(q_blo...  7.33 us
    unnamed x20, local copies, waits for them, and re-layouts  6.24 us
    ppermute x6, waiting for transfers between devices, swap(): return lax.ppermute(x, 'tp', [(0, 1), (1, 0)])  2.62 us
  transfers between devices with their start and end apart: 18, of which 9 were waited for; matrix products, arithmetic and copies ran while one was open for 0% of the time, Pallas kernels for 9%

profile of v4, /device:TPU:0, one launch (start us, length us, event | category | flops | bytes accessed | tf_op | source)
XLA Modules:
  0.0 83.2 jit_solution(17375589279645379155)
XLA Ops:
  0.0 1.1 %copy.10 = bf16[12,8,2,1024]{3,1,2,0:T(8,128)(2,1)S(1)} copy(bf16[12,8,2,1024]{3,2,1,0:T(2,128)(2,1)} %bitcast.39) | data formatting | bytes 786432
  1.1 3.1 %collective-permute-start.3 = (bf16[96,2048]{1,0:T(8,128)(2,1)S(1)}, bf16[96,2048]{1,0:T(8,128)(2,1)S(1)}, u32[]{:S(2)}, u32[]{:S(2)}) collective-permute-start(bf16[96,2048]{1,0:T(8,128)(2,1)S(1)} %bitcast.24), channel_id=1, source_target_pairs={{0,4},{4,0},{8,12},{12,8},{1,5},{5,1},{9,13},{13,9},{2,6},{6,2},{1... | collective-permute-start | bytes 1179656 | tf_op jit(solution)/shard_map/ppermute | solution.py:283
  4.2 2.6 %collective-permute-start = (bf16[96,2048]{1,0:T(8,128)(2,1)S(1)}, bf16[96,2048]{1,0:T(8,128)(2,1)S(1)}, u32[]{:S(2)}, u32[]{:S(2)}) collective-permute-start(bf16[96,2048]{1,0:T(8,128)(2,1)S(1)} %bitcast.25), channel_id=1, source_target_pairs={{0,8},{4,12},{8,0},{12,4},{1,9},{5,13},{9,1},{13,5},{2,10},{6,14},... | collective-permute-start | bytes 1179656 | tf_op jit(solution)/shard_map/ppermute | solution.py:283
  6.8 1.0 %copy-done.1 = bf16[1,64,4096]{2,1,0:T(8,128)(2,1)S(1)} copy-done((bf16[1,64,4096]{2,1,0:T(8,128)(2,1)S(1)}, bf16[1,64,4096]{2,1,0:T(8,128)(2,1)}, u32[]{:S(2)}) %copy-start.1) | copy-done | bytes 524312
  9.6 1.3 %collective-permute-done.1 = bf16[16,4096]{1,0:T(8,128)(2,1)S(1)} collective-permute-done((bf16[16,4096]{1,0:T(8,128)(2,1)S(1)}, bf16[16,4096]{1,0:T(8,128)(2,1)S(1)}, u32[]{:S(2)}, u32[]{:S(2)}) %collective-permute-start.1) | collective-permute-done | bytes 131104 | tf_op jit(solution)/shard_map/ppermute | solution.py:287
  11.5 21.4 %collective-permute-done.4.refs_2_ = bf16[32,4096]{1,0:T(8,128)(2,1)S(1)} collective-permute-done((bf16[32,4096]{1,0:T(8,128)(2,1)S(1)}, bf16[32,4096]{1,0:T(8,128)(2,1)S(1)}, u32[]{:S(2)}, u32[]{:S(2)}) %collective-permute-start.4) | collective-permute-done | bytes 262176 | tf_op jit(solution)/shard_map/ppermute | solution.py:283
  33.5 2.0 %collective-permute-done.2.refs_1_ = bf16[32,4096]{1,0:T(8,128)(2,1)} collective-permute-done((bf16[32,4096]{1,0:T(8,128)(2,1)S(1)}, bf16[32,4096]{1,0:T(8,128)(2,1)}, u32[]{:S(2)}, u32[]{:S(2)}) %collective-permute-start.2) | collective-permute-done | bytes 262176 | tf_op jit(solution)/shard_map/ppermute | solution.py:283
  36.5 7.7 %collective-permute-done.9.refs_9_.refs_6_.refs_7_ = bf16[96,2048]{1,0:T(8,128)(2,1)S(1)} collective-permute-done((bf16[96,2048]{1,0:T(8,128)(2,1)S(1)}, bf16[96,2048]{1,0:T(8,128)(2,1)S(1)}, u32[]{:S(2)}, u32[]{:S(2)}) %collective-permute-start.9) | collective-permute-done | bytes 393248 | tf_op jit(solution)/shard_map/ppermute | solution.py:283
  44.2 1.7 %collective-permute-start.5 = (bf16[32,4096]{1,0:T(8,128)(2,1)}, bf16[32,4096]{1,0:T(8,128)(2,1)}, u32[]{:S(2)}, u32[]{:S(2)}) collective-permute-start(bf16[32,4096]{1,0:T(8,128)(2,1)} %collective-permute-done.2.refs_1_), channel_id=1, source_target_pairs={{0,4},{4,0},{8,12},{12,8},{1,5},{5,1},{9,13},{13,9},{2,6},{6,2},{1... | collective-permute-start | bytes 786440 | tf_op jit(solution)/shard_map/ppermute | solution.py:283
  46.7 1.1 %copy-done.4 = bf16[32,4096]{1,0:T(8,128)(2,1)S(1)} copy-done((bf16[32,4096]{1,0:T(8,128)(2,1)S(1)}, bf16[32,4096]{1,0:T(8,128)(2,1)}, u32[]{:S(2)}) %copy-start.4) | copy-done | bytes 262168
  47.8 0.9 %copy-done.5 = f32[4096]{0:T(1024)S(1)} copy-done((f32[4096]{0:T(1024)S(1)}, f32[4096]{0:T(1024)}, u32[]{:S(2)}) %copy-start.5) | copy-done | bytes 16408
  48.7 4.5 %attend.2.done_ref = bf16[96,4096]{1,0:T(8,128)(2,1)S(1)} custom-call(s32[9]{0:T(128)S(1)} %stack.35.place_ref, bf16[32,4096]{1,0:T(8,128)(2,1)S(1)} %constant_dynamic-update-slice_fusion.refs_0_, bf16[32,4096]{1,0:T(8,128)(2,1)} %collective-permute-done.2.refs_1_, bf16[32,4096]{1,0:T(8,128)(2,1)S(1)} %copy-done.4, bf16[96,2048]{1,0:T(8,128)(2,1)S(1)} %bitcast.27, ...), custom_call_target="tpu_custom_call" | custom-call | flops 1207959552 | bytes 4718592 | tf_op jit(solution)/shard_map/attend/pallas_call | solution.py:148
  53.2 7.4 %experts.1 = (bf16[32,4096]{1,0:T(8,128)(2,1)S(1)}, bf16[32,1536]{1,0:T(8,128)(2,1)S(1)}, bf16[32,2560]{1,0:T(8,128)(2,1)S(1)}, bf16[32,4096]{1,0:T(8,128)(2,1)S...) custom-call(bf16[32,4096]{1,0:T(8,128)(2,1)} %collective-permute-done.5.last_ref, s32[9]{0:T(128)S(1)} %stack.35.place_ref, ...), custom_call_target="tpu_custom_call" | custom-call | flops 1610612736 | bytes 12582912 | tf_op jit(solution)/shard_map/experts/pallas_call | solution.py:225
  60.6 1.8 %collective-permute-start.11 = (bf16[32,2560]{1,0:T(8,128)(2,1)S(1)}, bf16[32,2560]{1,0:T(8,128)(2,1)S(1)}, u32[]{:S(2)}, u32[]{:S(2)}) collective-permute-start(bf16[32,2560]{1,0:T(8,128)(2,1)S(1)} %get-tuple-element.45), channel_id=1, source_target_pairs={{0,4},{4,0},{8,12},{12,8},{1,5},{5,1},{9,13},{13,9},{2,6},{6,2},{1... | collective-permute-start | bytes 491528 | tf_op jit(solution)/shard_map/ppermute | solution.py:283
  62.4 1.0 %collective-permute-start.14 = (bf16[32,1536]{1,0:T(8,128)(2,1)S(1)}, bf16[32,1536]{1,0:T(8,128)(2,1)S(1)}, u32[]{:S(2)}, u32[]{:S(2)}) collective-permute-start(bf16[32,1536]{1,0:T(8,128)(2,1)S(1)} %get-tuple-element.51), channel_id=1, source_target_pairs={{0,8},{4,12},{8,0},{12,4},{1,9},{5,13},{9,1},{13,5},{2,10},{6,14},... | collective-permute-start | bytes 294920 | tf_op jit(solution)/shard_map/ppermute | solution.py:283
  63.4 1.6 %collective-permute-start.16 = (bf16[32,1536]{1,0:T(8,128)(2,1)S(1)}, bf16[32,1536]{1,0:T(8,128)(2,1)S(1)}, u32[]{:S(2)}, u32[]{:S(2)}) collective-permute-start(bf16[32,1536]{1,0:T(8,128)(2,1)S(1)} %get-tuple-element.53), channel_id=1, source_target_pairs={{0,12},{4,8},{8,4},{12,0},{1,13},{5,9},{9,5},{13,1},{2,14},{6,10},... | collective-permute-start | bytes 294920 | tf_op jit(solution)/shard_map/ppermute | solution.py:283
  65.1 0.8 %collective-permute-start.15 = (bf16[32,4096]{1,0:T(8,128)(2,1)S(1)}, bf16[32,4096]{1,0:T(8,128)(2,1)S(1)}, u32[]{:S(2)}, u32[]{:S(2)}) collective-permute-start(bf16[32,4096]{1,0:T(8,128)(2,1)S(1)} %get-tuple-element.52), channel_id=1, source_target_pairs={{0,4},{4,0},{8,12},{12,8},{1,5},{5,1},{9,13},{13,9},{2,6},{6,2},{1... | collective-permute-start | bytes 786440 | tf_op jit(solution)/shard_map/ppermute | solution.py:283
  65.9 2.9 %attend.3.attended_ref = bf16[64,4096]{1,0:T(8,128)(2,1)S(1)} custom-call(s32[9]{0:T(128)S(1)} %stack.35.place_ref, bf16[64,4096]{1,0:T(8,128)(2,1)S(1)} %bitcast.32, bf16[96,2048]{1,0:T(8,128)(2,1)S(1)} %bitcast.29, bf16[96,2048]{1,0:T(8,128)(2,1)S(1)} %collective-permute-done.6.refs_4_.refs_1_.refs_2_, ...), custom_call_target="tpu_custom_call" | custom-call | flops 805306368 | bytes 4194304 | tf_op jit(solution)/shard_map/attend/pallas_call | solution.py:148
  68.8 1.3 %collective-permute-done.11 = bf16[32,2560]{1,0:T(8,128)(2,1)S(1)} collective-permute-done((bf16[32,2560]{1,0:T(8,128)(2,1)S(1)}, bf16[32,2560]{1,0:T(8,128)(2,1)S(1)}, u32[]{:S(2)}, u32[]{:S(2)}) %collective-permute-start.11) | collective-permute-done | bytes 163872 | tf_op jit(solution)/shard_map/ppermute | solution.py:283
  70.2 0.7 collective-permute-start.12
  70.9 1.5 %collective-permute-done.14 = bf16[32,1536]{1,0:T(8,128)(2,1)S(1)} collective-permute-done((bf16[32,1536]{1,0:T(8,128)(2,1)S(1)}, bf16[32,1536]{1,0:T(8,128)(2,1)S(1)}, u32[]{:S(2)}, u32[]{:S(2)}) %collective-permute-start.14) | collective-permute-done | bytes 98336 | tf_op jit(solution)/shard_map/ppermute | solution.py:283
  73.1 7.3 %collective-permute-done.15 = bf16[32,4096]{1,0:T(8,128)(2,1)S(1)} collective-permute-done((bf16[32,4096]{1,0:T(8,128)(2,1)S(1)}, bf16[32,4096]{1,0:T(8,128)(2,1)S(1)}, u32[]{:S(2)}, u32[]{:S(2)}) %collective-permute-start.15) | collective-permute-done | bytes 262176 | tf_op jit(solution)/shard_map/ppermute | solution.py:283
  80.6 1.3 %collective-permute-done.17.theirs_ref = bf16[16,4096]{1,0:T(8,128)(2,1)S(1)} collective-permute-done((bf16[16,4096]{1,0:T(8,128)(2,1)S(1)}, bf16[16,4096]{1,0:T(8,128)(2,1)S(1)}, u32[]{:S(2)}, u32[]{:S(2)}) %collective-permute-start.17) | collective-permute-done | bytes 131104 | tf_op jit(solution)/shard_map/ppermute | solution.py:287
  81.9 1.3 %combine.1 = bf16[64,4096]{1,0:T(8,128)(2,1)} custom-call(bf16[16,2560]{1,0:T(8,128)(2,1)S(1)} %collective-permute-done.12.late_ref, bf16[16,2560]{1,0:T(8,128)(2,1)S(1)} %collective-permute-done.13.late_theirs_ref, f32[32,64]{1,0:T(8,128)S(1)} %get-tuple-element.48.comb_ref, bf16[64,4096]{1,0:T(8,128)(2,1)S(1)} %attend.3.attended_ref, ...), custom_call_target="tpu_custom_call" | custom-call | flops 33554432 | bytes 1048576 | tf_op jit(solution)/shard_map/combine/pallas_call | solution.py:393
  (45 shorter events, 5.0 us)
Async XLA Ops:
  0.0 53.2 %copy-start.6 = (f32[4096]{0:T(1024)S(1)}, f32[4096]{0:T(1024)}, u32[]{:S(2)}) copy-start(f32[4096]{0:T(1024)} %param.14) | copy-start | bytes 49156
  1.1 34.4 %collective-permute-start.3 = (bf16[96,2048]{1,0:T(8,128)(2,1)S(1)}, bf16[96,2048]{1,0:T(8,128)(2,1)S(1)}, u32[]{:S(2)}, u32[]{:S(2)}) collective-permute-start(bf16[96,2048]{1,0:T(8,128)(2,1)S(1)} %bitcast.24), channel_id=1, source_target_pairs={{0,4},{4,0},{8,12},{12,8},{1,5},{5,1},{9,13},{13,9},{2,6},{6,2},{1... | collective-permute-start | bytes 1179656 | tf_op jit(solution)/shard_map/ppermute | solution.py:283
  4.2 31.3 %collective-permute-start = (bf16[96,2048]{1,0:T(8,128)(2,1)S(1)}, bf16[96,2048]{1,0:T(8,128)(2,1)S(1)}, u32[]{:S(2)}, u32[]{:S(2)}) collective-permute-start(bf16[96,2048]{1,0:T(8,128)(2,1)S(1)} %bitcast.25), channel_id=1, source_target_pairs={{0,8},{4,12},{8,0},{12,4},{1,9},{5,13},{9,1},{13,5},{2,10},{6,14},... | collective-permute-start | bytes 1179656 | tf_op jit(solution)/shard_map/ppermute | solution.py:283
  6.8 1.0 %copy-start.1 = (bf16[1,64,4096]{2,1,0:T(8,128)(2,1)S(1)}, bf16[1,64,4096]{2,1,0:T(8,128)(2,1)}, u32[]{:S(2)}) copy-start(bf16[1,64,4096]{2,1,0:T(8,128)(2,1)} %param.9) | copy-start | bytes 1572868
  9.5 1.4 %collective-permute-start.1 = (bf16[16,4096]{1,0:T(8,128)(2,1)S(1)}, bf16[16,4096]{1,0:T(8,128)(2,1)S(1)}, u32[]{:S(2)}, u32[]{:S(2)}) collective-permute-start(bf16[16,4096]{1,0:T(8,128)(2,1)S(1)} %get-tuple-element.32), channel_id=1, source_target_pairs={{0,1},{1,0},{2,3},{3,2},{4,5},{5,4},{6,7},{7,6},{8,9},{9,8},{10,11... | collective-permute-start | bytes 393224 | tf_op jit(solution)/shard_map/ppermute | solution.py:287
  11.0 21.9 %collective-permute-start.4 = (bf16[32,4096]{1,0:T(8,128)(2,1)S(1)}, bf16[32,4096]{1,0:T(8,128)(2,1)S(1)}, u32[]{:S(2)}, u32[]{:S(2)}) collective-permute-start(bf16[32,4096]{1,0:T(8,128)(2,1)S(1)} %constant_dynamic-update-slice_fusion.refs_0_), channel_id=1, source_target_pairs={{0,4},{4,0},{8,12},{12,8},{1,5},{5,1},{9,13},{13,9},{2,6},{6,2},{1... | collective-permute-start | bytes 786440 | tf_op jit(solution)/shard_map/ppermute | solution.py:283
  11.5 24.0 %collective-permute-start.2 = (bf16[32,4096]{1,0:T(8,128)(2,1)S(1)}, bf16[32,4096]{1,0:T(8,128)(2,1)}, u32[]{:S(2)}, u32[]{:S(2)}) collective-permute-start(bf16[32,4096]{1,0:T(8,128)(2,1)S(1)} %constant_dynamic-update-slice_fusion.refs_0_), channel_id=1, source_target_pairs={{0,8},{4,12},{8,0},{12,4},{1,9},{5,13},{9,1},{13,5},{2,10},{6,14},... | collective-permute-start | bytes 786440 | tf_op jit(solution)/shard_map/ppermute | solution.py:283
  35.5 8.6 %collective-permute-start.9 = (bf16[96,2048]{1,0:T(8,128)(2,1)S(1)}, bf16[96,2048]{1,0:T(8,128)(2,1)S(1)}, u32[]{:S(2)}, u32[]{:S(2)}) collective-permute-start(bf16[96,2048]{1,0:T(8,128)(2,1)S(1)} %collective-permute-done.refs_5_.refs_2_.refs_3_), channel_id=1, source_target_pairs={{0,4},{4,0},{8,12},{12,8},{1,5},{5,1},{9,13},{13,9},{2,6},{6,2},{1... | collective-permute-start | bytes 1179656 | tf_op jit(solution)/shard_map/ppermute | solution.py:283
  36.0 10.7 %collective-permute-start.6 = (bf16[96,2048]{1,0:T(8,128)(2,1)S(1)}, bf16[96,2048]{1,0:T(8,128)(2,1)S(1)}, u32[]{:S(2)}, u32[]{:S(2)}) collective-permute-start(bf16[96,2048]{1,0:T(8,128)(2,1)S(1)} %bitcast.26), channel_id=1, source_target_pairs={{0,1},{1,0},{2,3},{3,2},{4,5},{5,4},{6,7},{7,6},{8,9},{9,8},{10,11... | collective-permute-start | bytes 1179656 | tf_op jit(solution)/shard_map/ppermute | solution.py:287
  36.0 10.7 %collective-permute-start.7 = (bf16[96,2048]{1,0:T(8,128)(2,1)S(1)}, bf16[96,2048]{1,0:T(8,128)(2,1)S(1)}, u32[]{:S(2)}, u32[]{:S(2)}) collective-permute-start(bf16[96,2048]{1,0:T(8,128)(2,1)S(1)} %collective-permute-done.refs_5_.refs_2_.refs_3_), channel_id=1, source_target_pairs={{0,1},{1,0},{2,3},{3,2},{4,5},{5,4},{6,7},{7,6},{8,9},{9,8},{10,11... | collective-permute-start | bytes 1179656 | tf_op jit(solution)/shard_map/ppermute | solution.py:287
  36.5 10.2 %collective-permute-start.8 = (bf16[96,2048]{1,0:T(8,128)(2,1)S(1)}, bf16[96,2048]{1,0:T(8,128)(2,1)S(1)}, u32[]{:S(2)}, u32[]{:S(2)}) collective-permute-start(bf16[96,2048]{1,0:T(8,128)(2,1)S(1)} %collective-permute-done.3.refs_7_.refs_4_.refs_5_), channel_id=1, source_target_pairs={{0,1},{1,0},{2,3},{3,2},{4,5},{5,4},{6,7},{7,6},{8,9},{9,8},{10,11... | collective-permute-start | bytes 1179656 | tf_op jit(solution)/shard_map/ppermute | solution.py:287
  44.2 2.5 %collective-permute-start.10 = (bf16[96,2048]{1,0:T(8,128)(2,1)S(1)}, bf16[96,2048]{1,0:T(8,128)(2,1)S(1)}, u32[]{:S(2)}, u32[]{:S(2)}) collective-permute-start(bf16[96,2048]{1,0:T(8,128)(2,1)S(1)} %collective-permute-done.9.refs_9_.refs_6_.refs_7_), channel_id=1, source_target_pairs={{0,1},{1,0},{2,3},{3,2},{4,5},{5,4},{6,7},{7,6},{8,9},{9,8},{10,11... | collective-permute-start | bytes 1179656 | tf_op jit(solution)/shard_map/ppermute | solution.py:287
  44.2 9.0 %collective-permute-start.5 = (bf16[32,4096]{1,0:T(8,128)(2,1)}, bf16[32,4096]{1,0:T(8,128)(2,1)}, u32[]{:S(2)}, u32[]{:S(2)}) collective-permute-start(bf16[32,4096]{1,0:T(8,128)(2,1)} %collective-permute-done.2.refs_1_), channel_id=1, source_target_pairs={{0,4},{4,0},{8,12},{12,8},{1,5},{5,1},{9,13},{13,9},{2,6},{6,2},{1... | collective-permute-start | bytes 786440 | tf_op jit(solution)/shard_map/ppermute | solution.py:283
  46.6 6.6 %copy-start = (bf16[1,4096,512]{2,1,0:T(8,128)(2,1)S(1)}, bf16[1,4096,512]{2,1,0:T(8,128)(2,1)}, u32[]{:S(2)}) copy-start(bf16[1,4096,512]{2,1,0:T(8,128)(2,1)} %param.15) | copy-start | bytes 12582916
  46.7 1.1 %copy-start.4 = (bf16[32,4096]{1,0:T(8,128)(2,1)S(1)}, bf16[32,4096]{1,0:T(8,128)(2,1)}, u32[]{:S(2)}) copy-start(bf16[32,4096]{1,0:T(8,128)(2,1)} %copy-done.3) | copy-start | bytes 786436
  47.8 0.9 %copy-start.5 = (f32[4096]{0:T(1024)S(1)}, f32[4096]{0:T(1024)}, u32[]{:S(2)}) copy-start(f32[4096]{0:T(1024)} %param.14) | copy-start | bytes 49156
  53.2 12.7 %copy-start.2 = (bf16[1,64,4096]{2,1,0:T(8,128)(2,1)S(1)}, bf16[1,64,4096]{2,1,0:T(8,128)(2,1)}, u32[]{:S(2)}) copy-start(bf16[1,64,4096]{2,1,0:T(8,128)(2,1)} %param.9) | copy-start | bytes 1572868
  60.6 9.4 %collective-permute-start.11 = (bf16[32,2560]{1,0:T(8,128)(2,1)S(1)}, bf16[32,2560]{1,0:T(8,128)(2,1)S(1)}, u32[]{:S(2)}, u32[]{:S(2)}) collective-permute-start(bf16[32,2560]{1,0:T(8,128)(2,1)S(1)} %get-tuple-element.45), channel_id=1, source_target_pairs={{0,4},{4,0},{8,12},{12,8},{1,5},{5,1},{9,13},{13,9},{2,6},{6,2},{1... | collective-permute-start | bytes 491528 | tf_op jit(solution)/shard_map/ppermute | solution.py:283
  62.4 10.1 %collective-permute-start.14 = (bf16[32,1536]{1,0:T(8,128)(2,1)S(1)}, bf16[32,1536]{1,0:T(8,128)(2,1)S(1)}, u32[]{:S(2)}, u32[]{:S(2)}) collective-permute-start(bf16[32,1536]{1,0:T(8,128)(2,1)S(1)} %get-tuple-element.51), channel_id=1, source_target_pairs={{0,8},{4,12},{8,0},{12,4},{1,9},{5,13},{9,1},{13,5},{2,10},{6,14},... | collective-permute-start | bytes 294920 | tf_op jit(solution)/shard_map/ppermute | solution.py:283
  63.4 9.6 %collective-permute-start.16 = (bf16[32,1536]{1,0:T(8,128)(2,1)S(1)}, bf16[32,1536]{1,0:T(8,128)(2,1)S(1)}, u32[]{:S(2)}, u32[]{:S(2)}) collective-permute-start(bf16[32,1536]{1,0:T(8,128)(2,1)S(1)} %get-tuple-element.53), channel_id=1, source_target_pairs={{0,12},{4,8},{8,4},{12,0},{1,13},{5,9},{9,5},{13,1},{2,14},{6,10},... | collective-permute-start | bytes 294920 | tf_op jit(solution)/shard_map/ppermute | solution.py:283
  65.1 15.3 %collective-permute-start.15 = (bf16[32,4096]{1,0:T(8,128)(2,1)S(1)}, bf16[32,4096]{1,0:T(8,128)(2,1)S(1)}, u32[]{:S(2)}, u32[]{:S(2)}) collective-permute-start(bf16[32,4096]{1,0:T(8,128)(2,1)S(1)} %get-tuple-element.52), channel_id=1, source_target_pairs={{0,4},{4,0},{8,12},{12,8},{1,5},{5,1},{9,13},{13,9},{2,6},{6,2},{1... | collective-permute-start | bytes 786440 | tf_op jit(solution)/shard_map/ppermute | solution.py:283
  70.1 10.5 %collective-permute-start.13 = (bf16[16,2560]{1,0:T(8,128)(2,1)S(1)}, bf16[16,2560]{1,0:T(8,128)(2,1)S(1)}, u32[]{:S(2)}, u32[]{:S(2)}) collective-permute-start(bf16[16,2560]{1,0:T(8,128)(2,1)S(1)} %get-tuple-element.61), channel_id=1, source_target_pairs={{0,9},{1,8},{4,13},{5,12},{8,1},{9,0},{12,5},{13,4},{2,11},{3,10},... | collective-permute-start | bytes 245768 | tf_op jit(solution)/shard_map/ppermute | solution.py:295
  70.2 10.4 %collective-permute-start.12 = (bf16[16,2560]{1,0:T(8,128)(2,1)S(1)}, bf16[16,2560]{1,0:T(8,128)(2,1)S(1)}, u32[]{:S(2)}, u32[]{:S(2)}) collective-permute-start(bf16[16,2560]{1,0:T(8,128)(2,1)S(1)} %get-tuple-element.62), channel_id=1, source_target_pairs={{0,8},{4,12},{8,0},{12,4},{1,9},{5,13},{9,1},{13,5},{2,10},{6,14},... | collective-permute-start | bytes 245768 | tf_op jit(solution)/shard_map/ppermute | solution.py:283
  80.5 1.4 %collective-permute-start.17 = (bf16[16,4096]{1,0:T(8,128)(2,1)S(1)}, bf16[16,4096]{1,0:T(8,128)(2,1)S(1)}, u32[]{:S(2)}, u32[]{:S(2)}) collective-permute-start(bf16[16,4096]{1,0:T(8,128)(2,1)S(1)} %pad_maximum_fusion.1), channel_id=1, source_target_pairs={{0,1},{1,0},{2,3},{3,2},{4,5},{5,4},{6,7},{7,6},{8,9},{9,8},{10,11... | collective-permute-start | bytes 393224 | tf_op jit(solution)/shard_map/ppermute | solution.py:287
  (3 other events, 2.1 us)

commit v5 on v4

--- a/solution.py
+++ b/solution.py
@@ -20,6 +20,7 @@
 VMEM = pl.BlockSpec(memory_space=pltpu.VMEM)
 SMEM = pl.BlockSpec(memory_space=pltpu.SMEM)
 HBM = pl.BlockSpec(memory_space=pltpu.HBM)
+ANY = pl.BlockSpec(memory_space=pl.ANY)
 
 
 def params(mib):
@@ -64,11 +65,12 @@
     send_ref[...] = rows[CAP:]
 
 
-def key_bias(place_ref, pieces, rows_each, rows_true):
+def key_bias(place_ref, kv_refs, rows_true):
+    pieces = len(kv_refs)
     length = place_ref[pieces]
     parts = []
-    lane = lax.broadcasted_iota(jnp.int32, (8, rows_each), 1)
-    for i in range(pieces):
+    for i, r in enumerate(kv_refs):
+        lane = lax.broadcasted_iota(jnp.int32, (8, r.shape[0]), 1)
         position = lane + place_ref[i]
         allowed = (position >= PROMPT) | (position < length)
         allowed = allowed & (lane < rows_true)
@@ -124,20 +126,31 @@
 
 
 def attend_kernel(pieces, blocks, per_key, rows_true, place_ref, *refs):
-    q_refs = refs[:blocks]
+    q_blocks = refs[:blocks]
     kv_refs = refs[blocks : blocks + pieces]
-    out_ref = refs[-1]
-    bias = key_bias(place_ref, pieces, kv_refs[0].shape[0], rows_true)
+    *gain, out_ref, q_ref, gain_ref, sems = refs[blocks + pieces :]
+    copies = []
+    for i, r in enumerate(q_blocks):
+        rows = pl.ds(i * r.shape[0], r.shape[0])
+        copies.append(pltpu.make_async_copy(r, q_ref.at[rows], sems.at[i]))
+    for g in gain:
+        copies.append(pltpu.make_async_copy(g, gain_ref, sems.at[blocks]))
+    for c in copies:
+        c.start()
+    bias = key_bias(place_ref, kv_refs, rows_true)
+    for c in copies[:blocks]:
+        c.wait()
 
     def queries(at, size):
-        return jnp.concatenate([r[:, pl.ds(at, size)] for r in q_refs], axis=0)
+        return q_ref[:, pl.ds(at, size)]
 
     def store(at, result):
         out_ref[:, pl.ds(at, HEAD_DIM)] = result
 
     attend(queries, kv_refs, bias, store, per_key)
-    if len(refs) > blocks + pieces + 1:
-        out_ref[...] = norm(out_ref[...], refs[blocks + pieces][...])
+    for c in copies[blocks:]:
+        c.wait()
+        out_ref[...] = norm(out_ref[...], gain_ref[...])
 
 
 def attend_call(place, q_blocks, kv_pieces, rows_true, *gain):
@@ -150,10 +163,18 @@
             attend_kernel, len(kv_pieces), len(q_blocks), per_key, rows_true
         ),
         out_shape=jax.ShapeDtypeStruct((rows, width), jnp.bfloat16),
-        in_specs=[SMEM] + [VMEM] * (len(q_blocks) + len(kv_pieces) + len(gain)),
+        in_specs=[SMEM]
+        + [ANY] * len(q_blocks)
+        + [VMEM] * len(kv_pieces)
+        + [HBM] * len(gain),
         out_specs=VMEM,
+        scratch_shapes=[
+            pltpu.VMEM((rows, width), jnp.bfloat16),
+            pltpu.VMEM((1, width), jnp.float32),
+            pltpu.SemaphoreType.DMA((len(q_blocks) + 1,)),
+        ],
         compiler_params=params(20 if rows * keys < 1 << 18 else 56),
-        cost_estimate=cost(
+        cost_estimate=cost(1, 1) if gain else cost(
             4 * rows * width * keys,
             4 * rows * width + 2 * keys * kv_pieces[0].shape[1],
             rows * keys * width // HEAD_DIM,
@@ -185,7 +206,7 @@
     ]
     for c in copies:
         c.start()
-    bias = key_bias(place_ref, pieces, kv_refs[0].shape[0], rows_true)
+    bias = key_bias(place_ref, kv_refs, rows_true)
 
     def queries(at, size):
         return last_ref[:, pl.ds(at, size)]
@@ -346,14 +367,22 @@
     )
     order = order + [k ^ strides[-1] for k in order]
 
-    pieces, places = [], []
-    for block, k in zip([kv] + kv_blocks[1:], order):
-        pieces += [block, swap(block)]
-        places += [2 * (seq ^ k) + core, 2 * (seq ^ k) + 1 - core]
-    place = jnp.stack([p * rows_true for p in places] + [prompt_lengths[0]]).astype(jnp.int32)
+    swapped = [swap(b) for b in kv_blocks[:-1]]
+    last, swapped = tied(kv_blocks[-1], swapped)
+    rows = kv.shape[0]
+    parts = 2 if rows % (2 * TILE) == 0 and not pad else 1
+    cuts = range(0, rows, rows // parts)
+    pieces = kv_blocks[:-1] + swapped + [last]
+    pieces += [swap(last[c : c + rows // parts]) for c in cuts]
+    places = [(2 * (seq ^ k) + core) * rows_true for k in order[:-1]]
+    places += [(2 * (seq ^ k) + 1 - core) * rows_true for k in order[:-1]]
+    places += [(2 * (seq ^ order[-1]) + core) * rows_true]
+    places += [(2 * (seq ^ order[-1]) + 1 - core) * rows_true + c for c in cuts]
+    place = jnp.stack(places + [prompt_lengths[0]]).astype(jnp.int32)
 
     gain = norm_gain.reshape(1, width)
-    done = attend_call(place, routed_blocks[:-1], pieces, rows_true, gain)
+    early = [in_hbm(b) for b in routed_blocks[:-1]]
+    done = attend_call(place, early, pieces, rows_true, in_hbm(gain))
     parts = expert_call(
         place, done, routed_blocks[-1], pieces, gain, w_gate[0], in_hbm(w_up[0]), in_hbm(w_down[0]), order, rows_true
     )

time: 83.5 us -> 86 us (1.030)
  waiting for transfers between devices: 44.4 us -> 47.3 us
  local copies, waits for them, and re-layouts: 6.35 us -> 4.43 us
  starting transfers between devices: 15.1 us -> 16 us
    unnamed x20 -> x18, local copies, waits for them, and re-layouts: 6.24 us -> 3.53 us
    ppermute x11, waiting for transfers between devices: 41.7 us -> 43.8 us  [across(): return lax.ppermute(x, 'seq', [(i, i ^ stride) for i in range(n)])]
    pallas_call x2, Pallas kernels: 7.33 us -> 8.45 us  [attend_call(): pl.pallas_call(functools.partial(attend_kernel, len(kv_pieces), len(q_blo...]
    ppermute x6 -> x7, waiting for transfers between devices: 2.62 us -> 3.52 us  [swap(): return lax.ppermute(x, 'tp', [(0, 1), (1, 0)])]
  transfers between devices with their start and end apart: 18 -> 19, of which waited for: 9 -> 11; matrix products, arithmetic and copies ran while one was open for 0% -> 1% of each run, Pallas kernels for 9% -> 10%
where the time goes in v5:
time: 86 us; the launch traced here: 85.8 us
  waiting for transfers between devices  47.3 us (55%)
  Pallas kernels  17 us (20%)
  starting transfers between devices  16 us (19%)
  local copies, waits for them, and re-layouts  4.43 us (5%)
  between operations  0.86 us (1%)
    ppermute x11, waiting for transfers between devices, across(): return lax.ppermute(x, 'seq', [(i, i ^ stride) for i in range(n)])  43.8 us
    ppermute x11, starting transfers between devices, across(): return lax.ppermute(x, 'seq', [(i, i ^ stride) for i in range(n)])  14.7 us
    pallas_call x2, Pallas kernels, attend_call(): pl.pallas_call(functools.partial(attend_kernel, len(kv_pieces), len(q_blo...  8.45 us
    pallas_call x1, Pallas kernels, expert_call(): pl.pallas_call(functools.partial(expert_kernel, len(kv_pieces), tuple(ord...  6.92 us
    unnamed x18, local copies, waits for them, and re-layouts  3.53 us
    ppermute x7, waiting for transfers between devices, swap(): return lax.ppermute(x, 'tp', [(0, 1), (1, 0)])  3.52 us
  transfers between devices with their start and end apart: 19, of which 11 were waited for; matrix products, arithmetic and copies ran while one was open for 1% of the time, Pallas kernels for 10%

profile of v5, /device:TPU:0, one launch (start us, length us, event | category | flops | bytes accessed | tf_op | source)
XLA Modules:
  0.0 85.8 jit_solution(15632566846651302642)
XLA Ops:
  0.0 1.1 %copy.10 = bf16[12,8,2,1024]{3,1,2,0:T(8,128)(2,1)S(1)} copy(bf16[12,8,2,1024]{3,2,1,0:T(2,128)(2,1)} %bitcast.40) | data formatting | bytes 786432
  1.1 3.1 %collective-permute-start.3 = (bf16[96,2048]{1,0:T(8,128)(2,1)S(1)}, bf16[96,2048]{1,0:T(8,128)(2,1)S(1)}, u32[]{:S(2)}, u32[]{:S(2)}) collective-permute-start(bf16[96,2048]{1,0:T(8,128)(2,1)S(1)} %bitcast.25), channel_id=1, source_target_pairs={{0,4},{4,0},{8,12},{12,8},{1,5},{5,1},{9,13},{13,9},{2,6},{6,2},{1... | collective-permute-start | bytes 1179656 | tf_op jit(solution)/shard_map/ppermute | solution.py:304
  4.2 2.6 %collective-permute-start = (bf16[96,2048]{1,0:T(8,128)(2,1)S(1)}, bf16[96,2048]{1,0:T(8,128)(2,1)S(1)}, u32[]{:S(2)}, u32[]{:S(2)}) collective-permute-start(bf16[96,2048]{1,0:T(8,128)(2,1)S(1)} %bitcast.26), channel_id=1, source_target_pairs={{0,8},{4,12},{8,0},{12,4},{1,9},{5,13},{9,1},{13,5},{2,10},{6,14},... | collective-permute-start | bytes 1179656 | tf_op jit(solution)/shard_map/ppermute | solution.py:304
  6.8 1.0 %copy-done.1 = bf16[1,64,4096]{2,1,0:T(8,128)(2,1)S(1)} copy-done((bf16[1,64,4096]{2,1,0:T(8,128)(2,1)S(1)}, bf16[1,64,4096]{2,1,0:T(8,128)(2,1)}, u32[]{:S(2)}) %copy-start.1) | copy-done | bytes 524312
  7.8 0.7 copy-done.4
  8.5 0.7 copy-done.5
  9.6 1.3 %collective-permute-done.1 = bf16[16,4096]{1,0:T(8,128)(2,1)S(1)} collective-permute-done((bf16[16,4096]{1,0:T(8,128)(2,1)S(1)}, bf16[16,4096]{1,0:T(8,128)(2,1)S(1)}, u32[]{:S(2)}, u32[]{:S(2)}) %collective-permute-start.1) | collective-permute-done | bytes 131104 | tf_op jit(solution)/shard_map/ppermute | solution.py:308
  11.0 0.5 collective-permute-start.4
  11.5 21.4 %collective-permute-done.4.refs_2_ = bf16[32,4096]{1,0:T(8,128)(2,1)S(1)} collective-permute-done((bf16[32,4096]{1,0:T(8,128)(2,1)S(1)}, bf16[32,4096]{1,0:T(8,128)(2,1)S(1)}, u32[]{:S(2)}, u32[]{:S(2)}) %collective-permute-start.4) | collective-permute-done | bytes 262176 | tf_op jit(solution)/shard_map/ppermute | solution.py:304
  32.8 2.7 %collective-permute-done.2.refs_1_ = bf16[32,4096]{1,0:T(8,128)(2,1)} collective-permute-done((bf16[32,4096]{1,0:T(8,128)(2,1)S(1)}, bf16[32,4096]{1,0:T(8,128)(2,1)}, u32[]{:S(2)}, u32[]{:S(2)}) %collective-permute-start.2) | collective-permute-done | bytes 262176 | tf_op jit(solution)/shard_map/ppermute | solution.py:304
  36.6 1.6 %collective-permute-start.5 = (bf16[32,4096]{1,0:T(8,128)(2,1)}, bf16[32,4096]{1,0:T(8,128)(2,1)S(1)}, u32[]{:S(2)}, u32[]{:S(2)}) collective-permute-start(bf16[32,4096]{1,0:T(8,128)(2,1)} %collective-permute-done.2.refs_1_), channel_id=1, source_target_pairs={{0,4},{4,0},{8,12},{12,8},{1,5},{5,1},{9,13},{13,9},{2,6},{6,2},{1... | collective-permute-start | bytes 786440 | tf_op jit(solution)/shard_map/ppermute | solution.py:304
  38.4 9.7 %collective-permute-done.6.refs_9_.refs_6_.refs_7_ = bf16[96,2048]{1,0:T(8,128)(2,1)S(1)} collective-permute-done((bf16[96,2048]{1,0:T(8,128)(2,1)S(1)}, bf16[96,2048]{1,0:T(8,128)(2,1)S(1)}, u32[]{:S(2)}, u32[]{:S(2)}) %collective-permute-start.6) | collective-permute-done | bytes 393248 | tf_op jit(solution)/shard_map/ppermute | solution.py:304
  48.1 0.8 fusion
  50.8 5.5 %attend.2.done_ref = bf16[96,4096]{1,0:T(8,128)(2,1)S(1)} custom-call(s32[10]{0:T(128)S(1)} %stack.39.place_ref, bf16[32,4096]{1,0:T(8,128)(2,1)} %copy-done.6, bf16[32,4096]{1,0:T(8,128)(2,1)} %collective-permute-done.2.refs_1_, bf16[32,4096]{1,0:T(8,128)(2,1)} %copy-done.7, bf16[96,2048]{1,0:T(8,128)(2,1)S(1)} %bitcast.28, ...), custom_call_target="tpu_custom_call" | custom-call | flops 1 | bytes 1 | tf_op jit(solution)/shard_map/attend/pallas_call | solution.py:161
  56.3 6.9 %experts.1 = (bf16[32,4096]{1,0:T(8,128)(2,1)S(1)}, bf16[32,1536]{1,0:T(8,128)(2,1)S(1)}, bf16[32,2560]{1,0:T(8,128)(2,1)S(1)}, bf16[32,4096]{1,0:T(8,128)(2,1)S...) custom-call(bf16[32,4096]{1,0:T(8,128)(2,1)S(1)} %collective-permute-done.5.last_ref, ...), custom_call_target="tpu_custom_call" | custom-call | flops 1610612736 | bytes 12582912 | tf_op jit(solution)/shard_map/experts/pallas_call | solution.py:246
  63.3 0.5 collective-permute-start.12
  63.8 2.6 %collective-permute-start.15 = (bf16[32,1536]{1,0:T(8,128)(2,1)S(1)}, bf16[32,1536]{1,0:T(8,128)(2,1)S(1)}, u32[]{:S(2)}, u32[]{:S(2)}) collective-permute-start(bf16[32,1536]{1,0:T(8,128)(2,1)S(1)} %get-tuple-element.61), channel_id=1, source_target_pairs={{0,8},{4,12},{8,0},{12,4},{1,9},{5,13},{9,1},{13,5},{2,10},{6,14},... | collective-permute-start | bytes 294920 | tf_op jit(solution)/shard_map/ppermute | solution.py:304
  66.4 1.3 %collective-permute-start.17 = (bf16[32,1536]{1,0:T(8,128)(2,1)S(1)}, bf16[32,1536]{1,0:T(8,128)(2,1)S(1)}, u32[]{:S(2)}, u32[]{:S(2)}) collective-permute-start(bf16[32,1536]{1,0:T(8,128)(2,1)S(1)} %get-tuple-element.63), channel_id=1, source_target_pairs={{0,12},{4,8},{8,4},{12,0},{1,13},{5,9},{9,5},{13,1},{2,14},{6,10},... | collective-permute-start | bytes 294920 | tf_op jit(solution)/shard_map/ppermute | solution.py:304
  67.7 3.0 %attend.3.attended_ref = bf16[64,4096]{1,0:T(8,128)(2,1)S(1)} custom-call(s32[10]{0:T(128)S(1)} %stack.39.place_ref, bf16[64,4096]{1,0:T(8,128)(2,1)S(1)} %bitcast.33, bf16[96,2048]{1,0:T(8,128)(2,1)S(1)} %bitcast.30, bf16[96,2048]{1,0:T(8,128)(2,1)S(1)} %collective-permute-done.refs_4_.refs_1_.refs_2_, ...), custom_call_target="tpu_custom_call" | custom-call | flops 805306368 | bytes 4194304 | tf_op jit(solution)/shard_map/attend/pallas_call | solution.py:161
  70.7 2.2 %collective-permute-done.12 = bf16[32,2560]{1,0:T(8,128)(2,1)S(1)} collective-permute-done((bf16[32,2560]{1,0:T(8,128)(2,1)S(1)}, bf16[32,2560]{1,0:T(8,128)(2,1)S(1)}, u32[]{:S(2)}, u32[]{:S(2)}) %collective-permute-start.12) | collective-permute-done | bytes 163872 | tf_op jit(solution)/shard_map/ppermute | solution.py:304
  73.1 2.0 %collective-permute-start.13 = (bf16[16,2560]{1,0:T(8,128)(2,1)S(1)}, bf16[16,2560]{1,0:T(8,128)(2,1)S(1)}, u32[]{:S(2)}, u32[]{:S(2)}) collective-permute-start(bf16[16,2560]{1,0:T(8,128)(2,1)S(1)} %get-tuple-element.74), channel_id=1, source_target_pairs={{0,8},{4,12},{8,0},{12,4},{1,9},{5,13},{9,1},{13,5},{2,10},{6,14},... | collective-permute-start | bytes 245768 | tf_op jit(solution)/shard_map/ppermute | solution.py:304
  75.1 7.8 %collective-permute-done.16 = bf16[32,4096]{1,0:T(8,128)(2,1)S(1)} collective-permute-done((bf16[32,4096]{1,0:T(8,128)(2,1)S(1)}, bf16[32,4096]{1,0:T(8,128)(2,1)S(1)}, u32[]{:S(2)}, u32[]{:S(2)}) %collective-permute-start.16) | collective-permute-done | bytes 262176 | tf_op jit(solution)/shard_map/ppermute | solution.py:304
  83.2 1.3 %collective-permute-done.18.theirs_ref = bf16[16,4096]{1,0:T(8,128)(2,1)S(1)} collective-permute-done((bf16[16,4096]{1,0:T(8,128)(2,1)S(1)}, bf16[16,4096]{1,0:T(8,128)(2,1)S(1)}, u32[]{:S(2)}, u32[]{:S(2)}) %collective-permute-start.18) | collective-permute-done | bytes 131104 | tf_op jit(solution)/shard_map/ppermute | solution.py:308
  84.5 1.3 %combine.1 = bf16[64,4096]{1,0:T(8,128)(2,1)} custom-call(bf16[16,2560]{1,0:T(8,128)(2,1)S(1)} %collective-permute-done.13.late_ref, bf16[16,2560]{1,0:T(8,128)(2,1)S(1)} %collective-permute-done.14.late_theirs_ref, f32[32,64]{1,0:T(8,128)S(1)} %get-tuple-element.58.comb_ref, bf16[64,4096]{1,0:T(8,128)(2,1)S(1)} %attend.3.attended_ref, ...), custom_call_target="tpu_custom_call" | custom-call | flops 33554432 | bytes 1048576 | tf_op jit(solution)/shard_map/combine/pallas_call | solution.py:422
  (46 shorter events, 3.5 us)
Async XLA Ops:
  0.0 56.3 %copy-start.3 = (f32[4096]{0:T(1024)S(1)}, f32[4096]{0:T(1024)}, u32[]{:S(2)}) copy-start(f32[4096]{0:T(1024)} %param.14) | copy-start | bytes 49156
  1.1 34.4 %collective-permute-start.3 = (bf16[96,2048]{1,0:T(8,128)(2,1)S(1)}, bf16[96,2048]{1,0:T(8,128)(2,1)S(1)}, u32[]{:S(2)}, u32[]{:S(2)}) collective-permute-start(bf16[96,2048]{1,0:T(8,128)(2,1)S(1)} %bitcast.25), channel_id=1, source_target_pairs={{0,4},{4,0},{8,12},{12,8},{1,5},{5,1},{9,13},{13,9},{2,6},{6,2},{1... | collective-permute-start | bytes 1179656 | tf_op jit(solution)/shard_map/ppermute | solution.py:304
  4.2 31.3 %collective-permute-start = (bf16[96,2048]{1,0:T(8,128)(2,1)S(1)}, bf16[96,2048]{1,0:T(8,128)(2,1)S(1)}, u32[]{:S(2)}, u32[]{:S(2)}) collective-permute-start(bf16[96,2048]{1,0:T(8,128)(2,1)S(1)} %bitcast.26), channel_id=1, source_target_pairs={{0,8},{4,12},{8,0},{12,4},{1,9},{5,13},{9,1},{13,5},{2,10},{6,14},... | collective-permute-start | bytes 1179656 | tf_op jit(solution)/shard_map/ppermute | solution.py:304
  9.5 1.4 %collective-permute-start.1 = (bf16[16,4096]{1,0:T(8,128)(2,1)S(1)}, bf16[16,4096]{1,0:T(8,128)(2,1)S(1)}, u32[]{:S(2)}, u32[]{:S(2)}) collective-permute-start(bf16[16,4096]{1,0:T(8,128)(2,1)S(1)} %get-tuple-element.37), channel_id=1, source_target_pairs={{0,1},{1,0},{2,3},{3,2},{4,5},{5,4},{6,7},{7,6},{8,9},{9,8},{10,11... | collective-permute-start | bytes 393224 | tf_op jit(solution)/shard_map/ppermute | solution.py:308
  11.0 25.2 %copy-start.6 = (bf16[32,4096]{1,0:T(8,128)(2,1)}, bf16[32,4096]{1,0:T(8,128)(2,1)S(1)}, u32[]{:S(2)}) copy-start(bf16[32,4096]{1,0:T(8,128)(2,1)S(1)} %constant_dynamic-update-slice_fusion.refs_0_) | copy-start | bytes 786436
  11.0 21.9 %collective-permute-start.4 = (bf16[32,4096]{1,0:T(8,128)(2,1)S(1)}, bf16[32,4096]{1,0:T(8,128)(2,1)S(1)}, u32[]{:S(2)}, u32[]{:S(2)}) collective-permute-start(bf16[32,4096]{1,0:T(8,128)(2,1)S(1)} %constant_dynamic-update-slice_fusion.refs_0_), channel_id=1, source_target_pairs={{0,4},{4,0},{8,12},{12,8},{1,5},{5,1},{9,13},{13,9},{2,6},{6,2},{1... | collective-permute-start | bytes 786440 | tf_op jit(solution)/shard_map/ppermute | solution.py:304
  11.5 24.0 %collective-permute-start.2 = (bf16[32,4096]{1,0:T(8,128)(2,1)S(1)}, bf16[32,4096]{1,0:T(8,128)(2,1)}, u32[]{:S(2)}, u32[]{:S(2)}) collective-permute-start(bf16[32,4096]{1,0:T(8,128)(2,1)S(1)} %constant_dynamic-update-slice_fusion.refs_0_), channel_id=1, source_target_pairs={{0,8},{4,12},{8,0},{12,4},{1,9},{5,13},{9,1},{13,5},{2,10},{6,14},... | collective-permute-start | bytes 786440 | tf_op jit(solution)/shard_map/ppermute | solution.py:304
  32.8 2.7 %copy-start.7 = (bf16[32,4096]{1,0:T(8,128)(2,1)}, bf16[32,4096]{1,0:T(8,128)(2,1)S(1)}, u32[]{:S(2)}) copy-start(bf16[32,4096]{1,0:T(8,128)(2,1)S(1)} %collective-permute-done.4.refs_2_) | copy-start | bytes 786436
  35.5 2.7 %collective-permute-start.7 = (bf16[96,2048]{1,0:T(8,128)(2,1)S(1)}, bf16[96,2048]{1,0:T(8,128)(2,1)S(1)}, u32[]{:S(2)}, u32[]{:S(2)}) collective-permute-start(bf16[96,2048]{1,0:T(8,128)(2,1)S(1)} %bitcast.27), channel_id=1, source_target_pairs={{0,1},{1,0},{2,3},{3,2},{4,5},{5,4},{6,7},{7,6},{8,9},{9,8},{10,11... | collective-permute-start | bytes 1179656 | tf_op jit(solution)/shard_map/ppermute | solution.py:308
  35.6 2.6 %collective-permute-start.9 = (bf16[96,2048]{1,0:T(8,128)(2,1)S(1)}, bf16[96,2048]{1,0:T(8,128)(2,1)S(1)}, u32[]{:S(2)}, u32[]{:S(2)}) collective-permute-start(bf16[96,2048]{1,0:T(8,128)(2,1)S(1)} %collective-permute-done.3.refs_5_.refs_2_.refs_3_), channel_id=1, source_target_pairs={{0,1},{1,0},{2,3},{3,2},{4,5},{5,4},{6,7},{7,6},{8,9},{9,8},{10,11... | collective-permute-start | bytes 1179656 | tf_op jit(solution)/shard_map/ppermute | solution.py:308
  36.1 2.3 %collective-permute-start.8 = (bf16[96,2048]{1,0:T(8,128)(2,1)S(1)}, bf16[96,2048]{1,0:T(8,128)(2,1)S(1)}, u32[]{:S(2)}, u32[]{:S(2)}) collective-permute-start(bf16[96,2048]{1,0:T(8,128)(2,1)S(1)} %collective-permute-done.refs_4_.refs_1_.refs_2_), channel_id=1, source_target_pairs={{0,1},{1,0},{2,3},{3,2},{4,5},{5,4},{6,7},{7,6},{8,9},{9,8},{10,11... | collective-permute-start | bytes 1179656 | tf_op jit(solution)/shard_map/ppermute | solution.py:308
  36.2 11.9 %collective-permute-start.6 = (bf16[96,2048]{1,0:T(8,128)(2,1)S(1)}, bf16[96,2048]{1,0:T(8,128)(2,1)S(1)}, u32[]{:S(2)}, u32[]{:S(2)}) collective-permute-start(bf16[96,2048]{1,0:T(8,128)(2,1)S(1)} %collective-permute-done.refs_4_.refs_1_.refs_2_), channel_id=1, source_target_pairs={{0,4},{4,0},{8,12},{12,8},{1,5},{5,1},{9,13},{13,9},{2,6},{6,2},{1... | collective-permute-start | bytes 1179656 | tf_op jit(solution)/shard_map/ppermute | solution.py:304
  36.6 19.7 %collective-permute-start.5 = (bf16[32,4096]{1,0:T(8,128)(2,1)}, bf16[32,4096]{1,0:T(8,128)(2,1)S(1)}, u32[]{:S(2)}, u32[]{:S(2)}) collective-permute-start(bf16[32,4096]{1,0:T(8,128)(2,1)} %collective-permute-done.2.refs_1_), channel_id=1, source_target_pairs={{0,4},{4,0},{8,12},{12,8},{1,5},{5,1},{9,13},{13,9},{2,6},{6,2},{1... | collective-permute-start | bytes 786440 | tf_op jit(solution)/shard_map/ppermute | solution.py:304
  48.9 1.7 %collective-permute-start.11 = (bf16[48,2048]{1,0:T(8,128)(2,1)}, bf16[48,2048]{1,0:T(8,128)(2,1)S(1)}, u32[]{:S(2)}, u32[]{:S(2)}) collective-permute-start(bf16[48,2048]{1,0:T(8,128)(2,1)} %get-tuple-element.71), channel_id=1, source_target_pairs={{0,1},{1,0},{2,3},{3,2},{4,5},{5,4},{6,7},{7,6},{8,9},{9,8},{10,11... | collective-permute-start | bytes 589832 | tf_op jit(solution)/shard_map/ppermute | solution.py:308
  48.9 1.9 %collective-permute-start.10 = (bf16[48,2048]{1,0:T(8,128)(2,1)}, bf16[48,2048]{1,0:T(8,128)(2,1)S(1)}, u32[]{:S(2)}, u32[]{:S(2)}) collective-permute-start(bf16[48,2048]{1,0:T(8,128)(2,1)} %get-tuple-element.72), channel_id=1, source_target_pairs={{0,1},{1,0},{2,3},{3,2},{4,5},{5,4},{6,7},{7,6},{8,9},{9,8},{10,11... | collective-permute-start | bytes 589832 | tf_op jit(solution)/shard_map/ppermute | solution.py:308
  50.1 6.2 %copy-start = (bf16[1,4096,512]{2,1,0:T(8,128)(2,1)S(1)}, bf16[1,4096,512]{2,1,0:T(8,128)(2,1)}, u32[]{:S(2)}) copy-start(bf16[1,4096,512]{2,1,0:T(8,128)(2,1)} %param.15) | copy-start | bytes 12582916
  56.3 11.4 %copy-start.2 = (bf16[1,64,4096]{2,1,0:T(8,128)(2,1)S(1)}, bf16[1,64,4096]{2,1,0:T(8,128)(2,1)}, u32[]{:S(2)}) copy-start(bf16[1,64,4096]{2,1,0:T(8,128)(2,1)} %param.9) | copy-start | bytes 1572868
  63.3 9.6 %collective-permute-start.12 = (bf16[32,2560]{1,0:T(8,128)(2,1)S(1)}, bf16[32,2560]{1,0:T(8,128)(2,1)S(1)}, u32[]{:S(2)}, u32[]{:S(2)}) collective-permute-start(bf16[32,2560]{1,0:T(8,128)(2,1)S(1)} %get-tuple-element.55), channel_id=1, source_target_pairs={{0,4},{4,0},{8,12},{12,8},{1,5},{5,1},{9,13},{13,9},{2,6},{6,2},{1... | collective-permute-start | bytes 491528 | tf_op jit(solution)/shard_map/ppermute | solution.py:304
  63.8 11.3 %collective-permute-start.15 = (bf16[32,1536]{1,0:T(8,128)(2,1)S(1)}, bf16[32,1536]{1,0:T(8,128)(2,1)S(1)}, u32[]{:S(2)}, u32[]{:S(2)}) collective-permute-start(bf16[32,1536]{1,0:T(8,128)(2,1)S(1)} %get-tuple-element.61), channel_id=1, source_target_pairs={{0,8},{4,12},{8,0},{12,4},{1,9},{5,13},{9,1},{13,5},{2,10},{6,14},... | collective-permute-start | bytes 294920 | tf_op jit(solution)/shard_map/ppermute | solution.py:304
  66.4 8.8 %collective-permute-start.17 = (bf16[32,1536]{1,0:T(8,128)(2,1)S(1)}, bf16[32,1536]{1,0:T(8,128)(2,1)S(1)}, u32[]{:S(2)}, u32[]{:S(2)}) collective-permute-start(bf16[32,1536]{1,0:T(8,128)(2,1)S(1)} %get-tuple-element.63), channel_id=1, source_target_pairs={{0,12},{4,8},{8,4},{12,0},{1,13},{5,9},{9,5},{13,1},{2,14},{6,10},... | collective-permute-start | bytes 294920 | tf_op jit(solution)/shard_map/ppermute | solution.py:304
  67.7 15.2 %collective-permute-start.16 = (bf16[32,4096]{1,0:T(8,128)(2,1)S(1)}, bf16[32,4096]{1,0:T(8,128)(2,1)S(1)}, u32[]{:S(2)}, u32[]{:S(2)}) collective-permute-start(bf16[32,4096]{1,0:T(8,128)(2,1)S(1)} %get-tuple-element.62), channel_id=1, source_target_pairs={{0,4},{4,0},{8,12},{12,8},{1,5},{5,1},{9,13},{13,9},{2,6},{6,2},{1... | collective-permute-start | bytes 786440 | tf_op jit(solution)/shard_map/ppermute | solution.py:304
  73.0 10.2 %collective-permute-start.14 = (bf16[16,2560]{1,0:T(8,128)(2,1)S(1)}, bf16[16,2560]{1,0:T(8,128)(2,1)S(1)}, u32[]{:S(2)}, u32[]{:S(2)}) collective-permute-start(bf16[16,2560]{1,0:T(8,128)(2,1)S(1)} %get-tuple-element.73), channel_id=1, source_target_pairs={{0,9},{1,8},{4,13},{5,12},{8,1},{9,0},{12,5},{13,4},{2,11},{3,10},... | collective-permute-start | bytes 245768 | tf_op jit(solution)/shard_map/ppermute | solution.py:316
  73.1 10.2 %collective-permute-start.13 = (bf16[16,2560]{1,0:T(8,128)(2,1)S(1)}, bf16[16,2560]{1,0:T(8,128)(2,1)S(1)}, u32[]{:S(2)}, u32[]{:S(2)}) collective-permute-start(bf16[16,2560]{1,0:T(8,128)(2,1)S(1)} %get-tuple-element.74), channel_id=1, source_target_pairs={{0,8},{4,12},{8,0},{12,4},{1,9},{5,13},{9,1},{13,5},{2,10},{6,14},... | collective-permute-start | bytes 245768 | tf_op jit(solution)/shard_map/ppermute | solution.py:304
  83.1 1.4 %collective-permute-start.18 = (bf16[16,4096]{1,0:T(8,128)(2,1)S(1)}, bf16[16,4096]{1,0:T(8,128)(2,1)S(1)}, u32[]{:S(2)}, u32[]{:S(2)}) collective-permute-start(bf16[16,4096]{1,0:T(8,128)(2,1)S(1)} %pad_maximum_fusion.1), channel_id=1, source_target_pairs={{0,1},{1,0},{2,3},{3,2},{4,5},{5,4},{6,7},{7,6},{8,9},{9,8},{10,11... | collective-permute-start | bytes 393224 | tf_op jit(solution)/shard_map/ppermute | solution.py:308
  (3 other events, 2.4 us)

commit v6 on v4

--- a/solution.py
+++ b/solution.py
@@ -64,19 +64,20 @@
     send_ref[...] = rows[CAP:]
 
 
-def key_bias(place_ref, pieces, rows_each, rows_true):
-    length = place_ref[pieces]
+def key_bias(length_ref, kv_refs, origins, rows_true):
+    seq, core = lax.axis_index("seq"), lax.axis_index("tp")
+    length = length_ref[0]
     parts = []
-    lane = lax.broadcasted_iota(jnp.int32, (8, rows_each), 1)
-    for i in range(pieces):
-        position = lane + place_ref[i]
+    for r, (k, side, first) in zip(kv_refs, origins):
+        row = lax.broadcasted_iota(jnp.int32, (8, r.shape[0]), 1) + first
+        position = row + (2 * (seq ^ k) + (core ^ side)) * rows_true
         allowed = (position >= PROMPT) | (position < length)
-        allowed = allowed & (lane < rows_true)
+        allowed = allowed & (row < rows_true)
         parts.append(jnp.where(allowed, 0.0, masked_score))
     return jnp.concatenate(parts, axis=1)[:1]
 
 
-def attend(queries, kv_refs, bias, store, per_key):
+def attend(queries, kv_refs, bias, store, per_key, before=None, after=None):
     width = kv_refs[0].shape[1] // 2
     heads = width // HEAD_DIM
     factor = math.log2(math.e) / math.sqrt(HEAD_DIM)
@@ -102,15 +103,26 @@
             * factor
             + bias
         )
-        weights = jnp.exp2(scores - jnp.max(scores, axis=1, keepdims=True))
+        largest = jnp.max(scores, axis=1, keepdims=True)
+        mine = pl.ds(head * per_key * rows, per_key * rows)
+        if before is not None:
+            earlier = before[1][mine, :][:, :1]
+            largest = jnp.maximum(largest, earlier)
+        weights = jnp.exp2(scores - largest)
         summed = jnp.dot(
             weights.astype(jnp.bfloat16), values, preferred_element_type=jnp.float32
         )
+        if before is not None:
+            summed = summed + before[0][mine, :] * jnp.exp2(earlier - largest)
+        if after is not None:
+            after[0][mine, :] = summed
+            after[1][mine, :] = jnp.broadcast_to(largest, (per_key * rows, HEAD_DIM))
+            return
         result = (summed[:, :HEAD_DIM] / summed[:, HEAD_DIM:]).astype(jnp.bfloat16)
         for j in range(per_key):
             store(at * per_key + j * HEAD_DIM, result[j * rows : (j + 1) * rows])
 
-    if bias.shape[1] > 1024:
+    if bias.shape[1] > 1024 or per_key * HEAD_DIM * heads > 1 << 13:
         lax.fori_loop(0, heads, one, None)
     else:
         for head in range(heads):
@@ -123,43 +135,118 @@
     return (x * lax.rsqrt(square + epsilon) * gain).astype(jnp.bfloat16)
 
 
-def attend_kernel(pieces, blocks, per_key, rows_true, place_ref, *refs):
-    q_refs = refs[:blocks]
-    kv_refs = refs[blocks : blocks + pieces]
-    out_ref = refs[-1]
-    bias = key_bias(place_ref, pieces, kv_refs[0].shape[0], rows_true)
-
+def columns_of(q_refs):
     def queries(at, size):
         return jnp.concatenate([r[:, pl.ds(at, size)] for r in q_refs], axis=0)
 
+    return queries
+
+
+def into(ref):
     def store(at, result):
-        out_ref[:, pl.ds(at, HEAD_DIM)] = result
-
-    attend(queries, kv_refs, bias, store, per_key)
-    if len(refs) > blocks + pieces + 1:
-        out_ref[...] = norm(out_ref[...], refs[blocks + pieces][...])
-
-
-def attend_call(place, q_blocks, kv_pieces, rows_true, *gain):
-    width = q_blocks[0].shape[1]
-    per_key = width // (kv_pieces[0].shape[1] // 2)
+        ref[:, pl.ds(at, HEAD_DIM)] = result
+
+    return store
+
+
+def attend_kernel(origins, per_key, rows_true, length_ref, q_ref, *refs):
+    kv_refs = refs[: len(origins)]
+    bias = key_bias(length_ref, kv_refs, origins, rows_true)
+    attend(columns_of([q_ref]), kv_refs, bias, into(refs[-1]), per_key)
+
+
+def begin_kernel(origins, per_key, rows_true, length_ref, *refs):
+    pieces = len(origins)
+    kv_refs, after, mark_ref = refs[-pieces - 3 : -3], refs[-3:-1], refs[-1]
+    bias = key_bias(length_ref, kv_refs, origins, rows_true)
+    attend(columns_of(refs[: -pieces - 3]), kv_refs, bias, None, per_key, after=after)
+    mark_ref[...] = jnp.zeros_like(mark_ref)
+
+
+def finish_kernel(origins, per_key, rows_true, length_ref, *refs):
+    pieces = len(origins)
+    gain_ref, sums_ref, largest_ref, _, out_ref = refs[-5:]
+    kv_refs = refs[-pieces - 5 : -5]
+    bias = key_bias(length_ref, kv_refs, origins, rows_true)
+    attend(
+        columns_of(refs[: -pieces - 5]),
+        kv_refs,
+        bias,
+        into(out_ref),
+        per_key,
+        before=(sums_ref, largest_ref),
+    )
+    out_ref[...] = norm(out_ref[...], gain_ref[...])
+
+
+def attention(kernel, name, length, q_blocks, pieces, rows_true, more, out_shape, price):
+    kv_pieces, origins = pieces
+    per_key = q_blocks[0].shape[1] // (kv_pieces[0].shape[1] // 2)
+    large = sum(q.shape[0] for q in q_blocks) * sum(p.shape[0] for p in kv_pieces)
+    count = len(q_blocks) + len(kv_pieces) + len(more)
+    return pl.pallas_call(
+        functools.partial(kernel, tuple(origins), per_key, rows_true),
+        out_shape=out_shape,
+        in_specs=[SMEM] + [VMEM] * count,
+        out_specs=jax.tree.map(lambda _: VMEM, out_shape),
+        compiler_params=params(20 if large < 1 << 17 else 58),
+        cost_estimate=price,
+        name=name,
+    )(length, *q_blocks, *kv_pieces, *more)
+
+
+def attend_call(length, queries, pieces, rows_true):
+    rows, width = queries.shape
+    keys = sum(p.shape[0] for p in pieces[0])
+    shape = jax.ShapeDtypeStruct((rows, width), jnp.bfloat16)
+    price = cost(
+        4 * rows * width * keys,
+        4 * rows * width + 2 * keys * pieces[0][0].shape[1],
+        rows * keys * width // HEAD_DIM,
+    )
+    return attention(
+        attend_kernel, "attend", length, [queries], pieces, rows_true, [], shape, price
+    )
+
+
+def begin_call(length, q_blocks, pieces, rows_true):
+    rows = sum(q.shape[0] for q in q_blocks) * q_blocks[0].shape[1] // HEAD_DIM
+    shapes = [
+        jax.ShapeDtypeStruct((rows, 2 * HEAD_DIM), jnp.float32),
+        jax.ShapeDtypeStruct((rows, HEAD_DIM), jnp.float32),
+        jax.ShapeDtypeStruct((8, HEAD_DIM), jnp.float32),
+    ]
+    return attention(
+        begin_kernel, "begin", length, q_blocks, pieces, rows_true, [], shapes, cost(1, 1)
+    )
+
+
+def finish_call(length, q_blocks, pieces, rows_true, gain, begun):
     rows = sum(q.shape[0] for q in q_blocks)
-    keys = sum(p.shape[0] for p in kv_pieces)
+    shape = jax.ShapeDtypeStruct((rows, q_blocks[0].shape[1]), jnp.bfloat16)
+    more = [gain, *begun]
+    return attention(
+        finish_kernel, "finish", length, q_blocks, pieces, rows_true, more, shape, cost(1, 1)
+    )
+
+
+def halve_kernel(whole_ref, top_ref, bottom_ref):
+    rows = top_ref.shape[0]
+    top_ref[...] = whole_ref[:rows]
+    bottom_ref[...] = whole_ref[rows:]
+
+
+def halve_call(whole):
+    rows, width = whole.shape
     return pl.pallas_call(
-        functools.partial(
-            attend_kernel, len(kv_pieces), len(q_blocks), per_key, rows_true
-        ),
-        out_shape=jax.ShapeDtypeStruct((rows, width), jnp.bfloat16),
-        in_specs=[SMEM] + [VMEM] * (len(q_blocks) + len(kv_pieces) + len(gain)),
-        out_specs=VMEM,
-        compiler_params=params(20 if rows * keys < 1 << 18 else 56),
-        cost_estimate=cost(
-            4 * rows * width * keys,
-            4 * rows * width + 2 * keys * kv_pieces[0].shape[1],
-            rows * keys * width // HEAD_DIM,
-        ),
-        name="attend",
-    )(place, *q_blocks, *kv_pieces, *gain)
+        halve_kernel,
+        out_shape=[jax.ShapeDtypeStruct((rows // 2, width), whole.dtype)] * 2,
+        in_specs=[VMEM],
+        out_specs=[VMEM] * 2,
+        compiler_params=params(4),
+        cost_estimate=cost(1, 1),
+        name="halve",
+    )(whole)
 
 
 def cut_of(width):
@@ -171,8 +258,9 @@
 
 
 def expert_kernel(
-    pieces, order, per_key, rows_true, last_ref, place_ref, done_ref, *refs
+    origins, order, per_key, rows_true, last_ref, length_ref, done_ref, *refs
 ):
+    pieces = len(origins)
     kv_refs = refs[:pieces]
     gain_ref, gate_ref, up_hbm, down_hbm = refs[pieces : pieces + 4]
     out_refs = refs[pieces + 4 : -4]
@@ -185,7 +273,7 @@
     ]
     for c in copies:
         c.start()
-    bias = key_bias(place_ref, pieces, kv_refs[0].shape[0], rows_true)
+    bias = key_bias(length_ref, kv_refs, origins, rows_true)
 
     def queries(at, size):
         return last_ref[:, pl.ds(at, size)]
@@ -210,7 +298,8 @@
             next(out)[...] = part[i * each : (i + 1) * each, begin:end]
 
 
-def expert_call(place, done, last, kv_pieces, gain, w_gate, w_up, w_down, order, rows_true):
+def expert_call(length, done, last, pieces, gain, w_gate, w_up, w_down, order, rows_true):
+    kv_pieces, origins = pieces
     each, width = last.shape
     rows = len(order) * each
     hidden = w_gate.shape[1]
@@ -223,7 +312,7 @@
     ]
     outs = iter(
         pl.pallas_call(
-            functools.partial(expert_kernel, len(kv_pieces), tuple(order), per_key, rows_true),
+            functools.partial(expert_kernel, tuple(origins), tuple(order), per_key, rows_true),
             out_shape=shapes,
             in_specs=[VMEM, SMEM] + [VMEM] * (3 + len(kv_pieces)) + [HBM] * 2,
             out_specs=[VMEM] * len(shapes),
@@ -236,7 +325,7 @@
             compiler_params=params(26 if rows * hidden < 1 << 17 else 44),
             cost_estimate=cost(6 * rows * width * hidden, 6 * width * hidden),
             name="experts",
-        )(last, place, done, *kv_pieces, gain, w_gate, w_up, w_down)
+        )(last, length, done, *kv_pieces, gain, w_gate, w_up, w_down)
     )
     return [[next(outs) for _ in split] for split in splits]
 
@@ -309,7 +398,7 @@
     tokens, width = queries.shape[1:]
     rows_true = keys_values.shape[1]
     pad = -rows_true % TILE
-    seq, core = lax.axis_index("seq"), lax.axis_index("tp")
+    core = lax.axis_index("tp")
     own_queries = queries[0]
     strides = [1 << b for b in reversed(range(lax.axis_size("seq").bit_length() - 1))]
 
@@ -340,26 +429,41 @@
     kv_blocks, routed_blocks, first_kv, first_routed = tied(
         kv_blocks, routed_blocks, first_kv, first_routed
     )
-    kv_blocks = kv_blocks + [first_kv] + [across(b, strides[-1]) for b in kv_blocks[1:]]
-    routed_blocks = (
-        routed_blocks + [first_routed] + [across(b, strides[-1]) for b in routed_blocks[1:]]
-    )
+    last_kv = [across(b, strides[-1]) for b in kv_blocks[1:]]
+    kv_blocks = kv_blocks + [first_kv] + last_kv
     order = order + [k ^ strides[-1] for k in order]
-
-    pieces, places = [], []
-    for block, k in zip([kv] + kv_blocks[1:], order):
-        pieces += [block, swap(block)]
-        places += [2 * (seq ^ k) + core, 2 * (seq ^ k) + 1 - core]
-    place = jnp.stack([p * rows_true for p in places] + [prompt_lengths[0]]).astype(jnp.int32)
+    rows = kv.shape[0]
+    shares = 2 if rows % (2 * TILE) == 0 and not pad else 1
+    cuts = range(0, rows, rows // shares)
+    swapped = [swap(b) for b in kv_blocks[:-1]]
+
+    origins = [(k, side, 0) for side in (0, 1) for k in order[:-1]]
+    first_pieces = kv_blocks[:-1] + swapped, origins
+    length = prompt_lengths
+
+    early = routed_blocks + [first_routed]
+    late_blocks = [across(b, strides[-1]) for b in routed_blocks[1:-1]]
+    early += late_blocks
+    *begun, mark = begin_call(length, early, first_pieces, rows_true)
+    held_back, mark = tied(routed_blocks[-1], mark)
+    last_routed = across(held_back, strides[-1])
+    last, mark = tied(kv_blocks[-1], mark)
+    halves = halve_call(last) if shares == 2 else [last]
+    last_pieces = (
+        [last] + [swap(h) for h in halves],
+        [(order[-1], 0, 0)] + [(order[-1], 1, c) for c in cuts],
+    )
+    pieces = tuple(a + b for a, b in zip(first_pieces, last_pieces))
 
     gain = norm_gain.reshape(1, width)
-    done = attend_call(place, routed_blocks[:-1], pieces, rows_true, gain)
+    done = finish_call(length, early, last_pieces, rows_true, gain, [*begun, mark])
     parts = expert_call(
-        place, done, routed_blocks[-1], pieces, gain, w_gate[0], in_hbm(w_up[0]), in_hbm(w_down[0]), order, rows_true
+        length, done, last_routed, pieces, gain, w_gate[0], in_hbm(w_up[0]), in_hbm(w_down[0]),
+        order, rows_true,
     )
 
     own_queries, parts = tied(own_queries, parts)
-    attended = attend_call(place, [own_queries], pieces, rows_true)
+    attended = attend_call(length, own_queries, pieces, rows_true)
     parts = dict(zip(order, parts))
     straight = {k: v[0] for k, v in parts.items()}
     cut = cut_of(width)

time: 83.5 us -> 85.2 us (1.020)
  starting transfers between devices: 15.1 us -> 18.2 us
  Pallas kernels: 16.3 us -> 19.4 us
  local copies, waits for them, and re-layouts: 6.35 us -> 3.55 us
  waiting for transfers between devices: 44.4 us -> 42.7 us
    pallas_call x3 -> x5, Pallas kernels: 14.7 us -> 17.8 us  [the longest x3 11.5 us: attention(): pl.pallas_call(functools.partial(kernel, tuple(origins), per_key, rows_tr...]
    unnamed x20 -> x14, local copies, waits for them, and re-layouts: 6.24 us -> 3.52 us
    ppermute x11, starting transfers between devices: 14.4 us -> 16.9 us  [across(): return lax.ppermute(x, 'seq', [(i, i ^ stride) for i in range(n)])]
    ppermute x11, waiting for transfers between devices: 41.7 us -> 39.6 us  [across(): return lax.ppermute(x, 'seq', [(i, i ^ stride) for i in range(n)])]
    ppermute x6 -> x7, waiting for transfers between devices: 2.62 us -> 2.6 us  [swap(): return lax.ppermute(x, 'tp', [(0, 1), (1, 0)])]
  transfers between devices with their start and end apart: 18 -> 19, of which waited for: 9 -> 12; matrix products, arithmetic and copies ran while one was open for 0% -> 0% of each run, Pallas kernels for 9% -> 14%
where the time goes in v6:
time: 85.2 us; the launch traced here: 84.9 us
  waiting for transfers between devices  42.7 us (50%)
  Pallas kernels  19.4 us (23%)
  starting transfers between devices  18.2 us (21%)
  local copies, waits for them, and re-layouts  3.55 us (4%)
    ppermute x11, waiting for transfers between devices, across(): return lax.ppermute(x, 'seq', [(i, i ^ stride) for i in range(n)])  39.6 us
    ppermute x11, starting transfers between devices, across(): return lax.ppermute(x, 'seq', [(i, i ^ stride) for i in range(n)])  16.9 us
    pallas_call x3, Pallas kernels, attention(): pl.pallas_call(functools.partial(kernel, tuple(origins), per_key, rows_tr...  11.5 us
    pallas_call x1, Pallas kernels, expert_call(): pl.pallas_call(functools.partial(expert_kernel, tuple(origins), tuple(ord...  6.35 us
    unnamed x14, local copies, waits for them, and re-layouts  3.52 us
    ppermute x7, waiting for transfers between devices, swap(): return lax.ppermute(x, 'tp', [(0, 1), (1, 0)])  2.6 us
  transfers between devices with their start and end apart: 19, of which 12 were waited for; matrix products, arithmetic and copies ran while one was open for 0% of the time, Pallas kernels for 14%

profile of v6, /device:TPU:0, one launch (start us, length us, event | category | flops | bytes accessed | tf_op | source)
XLA Modules:
  0.0 84.9 jit_solution(16786671770106148619)
XLA Ops:
  0.0 1.1 %copy.10 = bf16[12,8,2,1024]{3,1,2,0:T(8,128)(2,1)S(1)} copy(bf16[12,8,2,1024]{3,2,1,0:T(2,128)(2,1)} %bitcast.31) | data formatting | bytes 786432
  1.1 4.1 %collective-permute-start = (bf16[96,2048]{1,0:T(8,128)(2,1)S(1)}, bf16[96,2048]{1,0:T(8,128)(2,1)S(1)}, u32[]{:S(2)}, u32[]{:S(2)}) collective-permute-start(bf16[96,2048]{1,0:T(8,128)(2,1)S(1)} %bitcast.16), channel_id=1, source_target_pairs={{0,8},{4,12},{8,0},{12,4},{1,9},{5,13},{9,1},{13,5},{2,10},{6,14},... | collective-permute-start | bytes 1179656 | tf_op jit(solution)/shard_map/ppermute | solution.py:372
  5.2 1.6 %collective-permute-start.3 = (bf16[96,2048]{1,0:T(8,128)(2,1)S(1)}, bf16[96,2048]{1,0:T(8,128)(2,1)S(1)}, u32[]{:S(2)}, u32[]{:S(2)}) collective-permute-start(bf16[96,2048]{1,0:T(8,128)(2,1)S(1)} %bitcast.17), channel_id=1, source_target_pairs={{0,4},{4,0},{8,12},{12,8},{1,5},{5,1},{9,13},{13,9},{2,6},{6,2},{1... | collective-permute-start | bytes 1179656 | tf_op jit(solution)/shard_map/ppermute | solution.py:372
  6.8 1.0 %copy-done.1 = bf16[1,64,4096]{2,1,0:T(8,128)(2,1)S(1)} copy-done((bf16[1,64,4096]{2,1,0:T(8,128)(2,1)S(1)}, bf16[1,64,4096]{2,1,0:T(8,128)(2,1)}, u32[]{:S(2)}) %copy-start.1) | copy-done | bytes 524312
  7.8 0.7 copy-done.4
  9.6 1.3 %collective-permute-done.1 = bf16[16,4096]{1,0:T(8,128)(2,1)S(1)} collective-permute-done((bf16[16,4096]{1,0:T(8,128)(2,1)S(1)}, bf16[16,4096]{1,0:T(8,128)(2,1)S(1)}, u32[]{:S(2)}, u32[]{:S(2)}) %collective-permute-start.1) | collective-permute-done | bytes 131104 | tf_op jit(solution)/shard_map/ppermute | solution.py:376
  11.6 22.6 %collective-permute-done.2.refs_1_ = bf16[32,4096]{1,0:T(8,128)(2,1)S(1)} collective-permute-done((bf16[32,4096]{1,0:T(8,128)(2,1)S(1)}, bf16[32,4096]{1,0:T(8,128)(2,1)S(1)}, u32[]{:S(2)}, u32[]{:S(2)}) %collective-permute-start.2) | collective-permute-done | bytes 262176 | tf_op jit(solution)/shard_map/ppermute | solution.py:372
  34.9 1.5 %collective-permute-start.9 = (bf16[96,2048]{1,0:T(8,128)(2,1)S(1)}, bf16[96,2048]{1,0:T(8,128)(2,1)S(1)}, u32[]{:S(2)}, u32[]{:S(2)}) collective-permute-start(bf16[96,2048]{1,0:T(8,128)(2,1)S(1)} %collective-permute-done.refs_4_.refs_1_), channel_id=1, source_target_pairs={{0,4},{4,0},{8,12},{12,8},{1,5},{5,1},{9,13},{13,9},{2,6},{6,2},{1... | collective-permute-start | bytes 1179656 | tf_op jit(solution)/shard_map/ppermute | solution.py:372
  37.1 3.9 %begin.1 = (f32[3072,256]{1,0:T(8,128)S(1)}, f32[3072,128]{1,0:T(8,128)S(1)}, f32[8,128]{1,0:T(8,128)S(1)}) custom-call(s32[1]{0:T(128)S(6)} %copy.12.length_ref, bf16[32,4096]{1,0:T(8,128)(2,1)S(1)} %constant_dynamic-update-slice_fusion.refs_0_, bf16[32,4096]{1,0:T(8,128)(2,1)S(1)} %collective-permute-done.2.refs_1_, ...), custom_call_target="tpu_custom_call" | custom-call | flops 1 | bytes 1 | tf_op jit(solution)/shard_map/begin/pallas_call | solution.py:187
  41.0 1.6 %collective-permute-start.8 = (bf16[32,4096]{1,0:T(8,128)(2,1)S(1)}, bf16[32,4096]{1,0:T(8,128)(2,1)S(1)}, u32[]{:S(2)}, u32[]{:S(2)}) collective-permute-start(bf16[32,4096]{1,0:T(8,128)(2,1)S(1)} %collective-permute-done.2.refs_1_), channel_id=1, source_target_pairs={{0,4},{4,0},{8,12},{12,8},{1,5},{5,1},{9,13},{13,9},{2,6},{6,2},{1... | collective-permute-start | bytes 786440 | tf_op jit(solution)/shard_map/ppermute | solution.py:372
  42.6 4.2 %collective-permute-done.9.whole_ref.refs_3_.refs_6_ = bf16[96,2048]{1,0:T(8,128)(2,1)S(1)} collective-permute-done((bf16[96,2048]{1,0:T(8,128)(2,1)S(1)}, bf16[96,2048]{1,0:T(8,128)(2,1)S(1)}, u32[]{:S(2)}, u32[]{:S(2)}) %collective-permute-start.9) | collective-permute-done | bytes 393248 | tf_op jit(solution)/shard_map/ppermute | solution.py:372
  47.4 0.9 %collective-permute-done.10.refs_4_.refs_7_ = bf16[48,2048]{1,0:T(8,128)(2,1)S(1)} collective-permute-done((bf16[48,2048]{1,0:T(8,128)(2,1)S(1)}, bf16[48,2048]{1,0:T(8,128)(2,1)S(1)}, u32[]{:S(2)}, u32[]{:S(2)}) %collective-permute-start.10) | collective-permute-done | bytes 196640 | tf_op jit(solution)/shard_map/ppermute | solution.py:376
  48.6 5.3 %finish.1.done_ref = bf16[96,4096]{1,0:T(8,128)(2,1)S(1)} custom-call(s32[1]{0:T(128)S(6)} %copy.12.length_ref, bf16[32,4096]{1,0:T(8,128)(2,1)S(1)} %constant_dynamic-update-slice_fusion.refs_0_, bf16[32,4096]{1,0:T(8,128)(2,1)S(1)} %collective-permute-done.2.refs_1_, bf16[32,4096]{1,0:T(8,128)(2,1)S(1)} %collective-permute-done.4.refs_2_, ...), custom_call_target="tpu_custom_call" | custom-call | flops 1 | bytes 1 | tf_op jit(solution)/shard_map/finish/pallas_call | solution.py:187
  53.9 6.4 %experts.1 = (bf16[32,4096]{1,0:T(8,128)(2,1)S(1)}, bf16[32,1536]{1,0:T(8,128)(2,1)S(1)}, bf16[32,2560]{1,0:T(8,128)(2,1)S(1)}, bf16[32,4096]{1,0:T(8,128)(2,1)S...) custom-call(bf16[32,4096]{1,0:T(8,128)(2,1)S(1)} %collective-permute-done.8.last_ref, ...), custom_call_target="tpu_custom_call" | custom-call | flops 1610612736 | bytes 12582912 | tf_op jit(solution)/shard_map/experts/pallas_call | solution.py:314
  60.3 1.8 %collective-permute-start.12 = (bf16[32,2560]{1,0:T(8,128)(2,1)S(1)}, bf16[32,2560]{1,0:T(8,128)(2,1)S(1)}, u32[]{:S(2)}, u32[]{:S(2)}) collective-permute-start(bf16[32,2560]{1,0:T(8,128)(2,1)S(1)} %get-tuple-element.65), channel_id=1, source_target_pairs={{0,4},{4,0},{8,12},{12,8},{1,5},{5,1},{9,13},{13,9},{2,6},{6,2},{1... | collective-permute-start | bytes 491528 | tf_op jit(solution)/shard_map/ppermute | solution.py:372
  62.5 2.0 %collective-permute-start.15 = (bf16[32,1536]{1,0:T(8,128)(2,1)S(1)}, bf16[32,1536]{1,0:T(8,128)(2,1)S(1)}, u32[]{:S(2)}, u32[]{:S(2)}) collective-permute-start(bf16[32,1536]{1,0:T(8,128)(2,1)S(1)} %get-tuple-element.71), channel_id=1, source_target_pairs={{0,8},{4,12},{8,0},{12,4},{1,9},{5,13},{9,1},{13,5},{2,10},{6,14},... | collective-permute-start | bytes 294920 | tf_op jit(solution)/shard_map/ppermute | solution.py:372
  64.5 1.9 %collective-permute-start.17 = (bf16[32,1536]{1,0:T(8,128)(2,1)S(1)}, bf16[32,1536]{1,0:T(8,128)(2,1)S(1)}, u32[]{:S(2)}, u32[]{:S(2)}) collective-permute-start(bf16[32,1536]{1,0:T(8,128)(2,1)S(1)} %get-tuple-element.73), channel_id=1, source_target_pairs={{0,12},{4,8},{8,4},{12,0},{1,13},{5,9},{9,5},{13,1},{2,14},{6,10},... | collective-permute-start | bytes 294920 | tf_op jit(solution)/shard_map/ppermute | solution.py:372
  66.4 2.3 %attend.1.attended_ref = bf16[64,4096]{1,0:T(8,128)(2,1)S(1)} custom-call(s32[1]{0:T(128)S(6)} %copy.12.length_ref, bf16[64,4096]{1,0:T(8,128)(2,1)S(1)} %bitcast.24, bf16[96,2048]{1,0:T(8,128)(2,1)S(1)} %bitcast.21, bf16[96,2048]{1,0:T(8,128)(2,1)S(1)} %collective-permute-done.refs_4_.refs_1_, bf16[96,2048]{1,0:T(8,128)(2,1)S(1)} %collective-permute-done.3.refs_5_.refs_2_, ...), custom_call_target="tpu_custom_call" | custom-call | flops 805306368 | bytes 4194304 | tf_op jit(solution)/shard_map/attend/pallas_call | solution.py:187
  68.7 0.9 %collective-permute-done.12 = bf16[32,2560]{1,0:T(8,128)(2,1)S(1)} collective-permute-done((bf16[32,2560]{1,0:T(8,128)(2,1)S(1)}, bf16[32,2560]{1,0:T(8,128)(2,1)S(1)}, u32[]{:S(2)}, u32[]{:S(2)}) %collective-permute-start.12) | collective-permute-done | bytes 163872 | tf_op jit(solution)/shard_map/ppermute | solution.py:372
  69.7 1.4 %collective-permute-start.13 = (bf16[16,2560]{1,0:T(8,128)(2,1)S(1)}, bf16[16,2560]{1,0:T(8,128)(2,1)S(1)}, u32[]{:S(2)}, u32[]{:S(2)}) collective-permute-start(bf16[16,2560]{1,0:T(8,128)(2,1)S(1)} %get-tuple-element.82), channel_id=1, source_target_pairs={{0,8},{4,12},{8,0},{12,4},{1,9},{5,13},{9,1},{13,5},{2,10},{6,14},... | collective-permute-start | bytes 245768 | tf_op jit(solution)/shard_map/ppermute | solution.py:372
  71.1 3.2 %collective-permute-done.15 = bf16[32,1536]{1,0:T(8,128)(2,1)S(1)} collective-permute-done((bf16[32,1536]{1,0:T(8,128)(2,1)S(1)}, bf16[32,1536]{1,0:T(8,128)(2,1)S(1)}, u32[]{:S(2)}, u32[]{:S(2)}) %collective-permute-start.15) | collective-permute-done | bytes 98336 | tf_op jit(solution)/shard_map/ppermute | solution.py:372
  74.3 4.5 %collective-permute-done.17 = bf16[32,1536]{1,0:T(8,128)(2,1)S(1)} collective-permute-done((bf16[32,1536]{1,0:T(8,128)(2,1)S(1)}, bf16[32,1536]{1,0:T(8,128)(2,1)S(1)}, u32[]{:S(2)}, u32[]{:S(2)}) %collective-permute-start.17) | collective-permute-done | bytes 98336 | tf_op jit(solution)/shard_map/ppermute | solution.py:372
  79.1 4.1 %collective-permute-done.13.late_ref = bf16[16,2560]{1,0:T(8,128)(2,1)S(1)} collective-permute-done((bf16[16,2560]{1,0:T(8,128)(2,1)S(1)}, bf16[16,2560]{1,0:T(8,128)(2,1)S(1)}, u32[]{:S(2)}, u32[]{:S(2)}) %collective-permute-start.13) | collective-permute-done | bytes 81952 | tf_op jit(solution)/shard_map/ppermute | solution.py:372
  83.7 1.2 %combine.1 = bf16[64,4096]{1,0:T(8,128)(2,1)} custom-call(bf16[16,2560]{1,0:T(8,128)(2,1)S(1)} %collective-permute-done.13.late_ref, bf16[16,2560]{1,0:T(8,128)(2,1)S(1)} %collective-permute-done.14.late_theirs_ref, f32[32,64]{1,0:T(8,128)S(1)} %get-tuple-element.68.comb_ref, bf16[64,4096]{1,0:T(8,128)(2,1)S(1)} %attend.1.attended_ref, ...), custom_call_target="tpu_custom_call" | custom-call | flops 33554432 | bytes 1048576 | tf_op jit(solution)/shard_map/combine/pallas_call | solution.py:497
  (42 shorter events, 4.6 us)
Async XLA Ops:
  0.0 48.6 %copy-start.3 = (f32[4096]{0:T(1024)S(1)}, f32[4096]{0:T(1024)}, u32[]{:S(2)}) copy-start(f32[4096]{0:T(1024)} %param.14) | copy-start | bytes 49156
  1.1 33.2 %collective-permute-start = (bf16[96,2048]{1,0:T(8,128)(2,1)S(1)}, bf16[96,2048]{1,0:T(8,128)(2,1)S(1)}, u32[]{:S(2)}, u32[]{:S(2)}) collective-permute-start(bf16[96,2048]{1,0:T(8,128)(2,1)S(1)} %bitcast.16), channel_id=1, source_target_pairs={{0,8},{4,12},{8,0},{12,4},{1,9},{5,13},{9,1},{13,5},{2,10},{6,14},... | collective-permute-start | bytes 1179656 | tf_op jit(solution)/shard_map/ppermute | solution.py:372
  5.2 29.1 %collective-permute-start.3 = (bf16[96,2048]{1,0:T(8,128)(2,1)S(1)}, bf16[96,2048]{1,0:T(8,128)(2,1)S(1)}, u32[]{:S(2)}, u32[]{:S(2)}) collective-permute-start(bf16[96,2048]{1,0:T(8,128)(2,1)S(1)} %bitcast.17), channel_id=1, source_target_pairs={{0,4},{4,0},{8,12},{12,8},{1,5},{5,1},{9,13},{13,9},{2,6},{6,2},{1... | collective-permute-start | bytes 1179656 | tf_op jit(solution)/shard_map/ppermute | solution.py:372
  6.8 1.0 %copy-start.1 = (bf16[1,64,4096]{2,1,0:T(8,128)(2,1)S(1)}, bf16[1,64,4096]{2,1,0:T(8,128)(2,1)}, u32[]{:S(2)}) copy-start(bf16[1,64,4096]{2,1,0:T(8,128)(2,1)} %param.9) | copy-start | bytes 1572868
  7.8 0.7 copy-start.4
  9.5 1.4 %collective-permute-start.1 = (bf16[16,4096]{1,0:T(8,128)(2,1)S(1)}, bf16[16,4096]{1,0:T(8,128)(2,1)S(1)}, u32[]{:S(2)}, u32[]{:S(2)}) collective-permute-start(bf16[16,4096]{1,0:T(8,128)(2,1)S(1)} %get-tuple-element.42), channel_id=1, source_target_pairs={{0,1},{1,0},{2,3},{3,2},{4,5},{5,4},{6,7},{7,6},{8,9},{9,8},{10,11... | collective-permute-start | bytes 393224 | tf_op jit(solution)/shard_map/ppermute | solution.py:376
  11.0 23.2 %collective-permute-start.2 = (bf16[32,4096]{1,0:T(8,128)(2,1)S(1)}, bf16[32,4096]{1,0:T(8,128)(2,1)S(1)}, u32[]{:S(2)}, u32[]{:S(2)}) collective-permute-start(bf16[32,4096]{1,0:T(8,128)(2,1)S(1)} %constant_dynamic-update-slice_fusion.refs_0_), channel_id=1, source_target_pairs={{0,8},{4,12},{8,0},{12,4},{1,9},{5,13},{9,1},{13,5},{2,10},{6,14},... | collective-permute-start | bytes 786440 | tf_op jit(solution)/shard_map/ppermute | solution.py:372
  11.4 22.9 %collective-permute-start.4 = (bf16[32,4096]{1,0:T(8,128)(2,1)S(1)}, bf16[32,4096]{1,0:T(8,128)(2,1)S(1)}, u32[]{:S(2)}, u32[]{:S(2)}) collective-permute-start(bf16[32,4096]{1,0:T(8,128)(2,1)S(1)} %constant_dynamic-update-slice_fusion.refs_0_), channel_id=1, source_target_pairs={{0,4},{4,0},{8,12},{12,8},{1,5},{5,1},{9,13},{13,9},{2,6},{6,2},{1... | collective-permute-start | bytes 786440 | tf_op jit(solution)/shard_map/ppermute | solution.py:372
  34.3 2.8 %collective-permute-start.6 = (bf16[96,2048]{1,0:T(8,128)(2,1)S(1)}, bf16[96,2048]{1,0:T(8,128)(2,1)S(1)}, u32[]{:S(2)}, u32[]{:S(2)}) collective-permute-start(bf16[96,2048]{1,0:T(8,128)(2,1)S(1)} %collective-permute-done.refs_4_.refs_1_), channel_id=1, source_target_pairs={{0,1},{1,0},{2,3},{3,2},{4,5},{5,4},{6,7},{7,6},{8,9},{9,8},{10,11... | collective-permute-start | bytes 1179656 | tf_op jit(solution)/shard_map/ppermute | solution.py:376
  34.3 2.8 %collective-permute-start.5 = (bf16[96,2048]{1,0:T(8,128)(2,1)S(1)}, bf16[96,2048]{1,0:T(8,128)(2,1)S(1)}, u32[]{:S(2)}, u32[]{:S(2)}) collective-permute-start(bf16[96,2048]{1,0:T(8,128)(2,1)S(1)} %bitcast.18), channel_id=1, source_target_pairs={{0,1},{1,0},{2,3},{3,2},{4,5},{5,4},{6,7},{7,6},{8,9},{9,8},{10,11... | collective-permute-start | bytes 1179656 | tf_op jit(solution)/shard_map/ppermute | solution.py:376
  34.8 2.3 %collective-permute-start.7 = (bf16[96,2048]{1,0:T(8,128)(2,1)S(1)}, bf16[96,2048]{1,0:T(8,128)(2,1)S(1)}, u32[]{:S(2)}, u32[]{:S(2)}) collective-permute-start(bf16[96,2048]{1,0:T(8,128)(2,1)S(1)} %collective-permute-done.3.refs_5_.refs_2_), channel_id=1, source_target_pairs={{0,1},{1,0},{2,3},{3,2},{4,5},{5,4},{6,7},{7,6},{8,9},{9,8},{10,11... | collective-permute-start | bytes 1179656 | tf_op jit(solution)/shard_map/ppermute | solution.py:376
  34.9 11.9 %collective-permute-start.9 = (bf16[96,2048]{1,0:T(8,128)(2,1)S(1)}, bf16[96,2048]{1,0:T(8,128)(2,1)S(1)}, u32[]{:S(2)}, u32[]{:S(2)}) collective-permute-start(bf16[96,2048]{1,0:T(8,128)(2,1)S(1)} %collective-permute-done.refs_4_.refs_1_), channel_id=1, source_target_pairs={{0,4},{4,0},{8,12},{12,8},{1,5},{5,1},{9,13},{13,9},{2,6},{6,2},{1... | collective-permute-start | bytes 1179656 | tf_op jit(solution)/shard_map/ppermute | solution.py:372
  41.0 12.9 %copy-start = (bf16[1,4096,512]{2,1,0:T(8,128)(2,1)S(1)}, bf16[1,4096,512]{2,1,0:T(8,128)(2,1)}, u32[]{:S(2)}) copy-start(bf16[1,4096,512]{2,1,0:T(8,128)(2,1)} %param.15) | copy-start | bytes 12582916
  41.0 12.8 %collective-permute-start.8 = (bf16[32,4096]{1,0:T(8,128)(2,1)S(1)}, bf16[32,4096]{1,0:T(8,128)(2,1)S(1)}, u32[]{:S(2)}, u32[]{:S(2)}) collective-permute-start(bf16[32,4096]{1,0:T(8,128)(2,1)S(1)} %collective-permute-done.2.refs_1_), channel_id=1, source_target_pairs={{0,4},{4,0},{8,12},{12,8},{1,5},{5,1},{9,13},{13,9},{2,6},{6,2},{1... | collective-permute-start | bytes 786440 | tf_op jit(solution)/shard_map/ppermute | solution.py:372
  46.8 1.5 %collective-permute-start.10 = (bf16[48,2048]{1,0:T(8,128)(2,1)S(1)}, bf16[48,2048]{1,0:T(8,128)(2,1)S(1)}, u32[]{:S(2)}, u32[]{:S(2)}) collective-permute-start(bf16[48,2048]{1,0:T(8,128)(2,1)S(1)} %get-tuple-element.53), channel_id=1, source_target_pairs={{0,1},{1,0},{2,3},{3,2},{4,5},{5,4},{6,7},{7,6},{8,9},{9,8},{10,11... | collective-permute-start | bytes 589832 | tf_op jit(solution)/shard_map/ppermute | solution.py:376
  46.9 1.7 %collective-permute-start.11 = (bf16[48,2048]{1,0:T(8,128)(2,1)S(1)}, bf16[48,2048]{1,0:T(8,128)(2,1)S(1)}, u32[]{:S(2)}, u32[]{:S(2)}) collective-permute-start(bf16[48,2048]{1,0:T(8,128)(2,1)S(1)} %get-tuple-element.54), channel_id=1, source_target_pairs={{0,1},{1,0},{2,3},{3,2},{4,5},{5,4},{6,7},{7,6},{8,9},{9,8},{10,11... | collective-permute-start | bytes 589832 | tf_op jit(solution)/shard_map/ppermute | solution.py:376
  53.9 12.5 %copy-start.2 = (bf16[1,64,4096]{2,1,0:T(8,128)(2,1)S(1)}, bf16[1,64,4096]{2,1,0:T(8,128)(2,1)}, u32[]{:S(2)}) copy-start(bf16[1,64,4096]{2,1,0:T(8,128)(2,1)} %param.9) | copy-start | bytes 1572868
  60.3 9.4 %collective-permute-start.12 = (bf16[32,2560]{1,0:T(8,128)(2,1)S(1)}, bf16[32,2560]{1,0:T(8,128)(2,1)S(1)}, u32[]{:S(2)}, u32[]{:S(2)}) collective-permute-start(bf16[32,2560]{1,0:T(8,128)(2,1)S(1)} %get-tuple-element.65), channel_id=1, source_target_pairs={{0,4},{4,0},{8,12},{12,8},{1,5},{5,1},{9,13},{13,9},{2,6},{6,2},{1... | collective-permute-start | bytes 491528 | tf_op jit(solution)/shard_map/ppermute | solution.py:372
  62.0 16.8 %collective-permute-start.16 = (bf16[32,4096]{1,0:T(8,128)(2,1)S(1)}, bf16[32,4096]{1,0:T(8,128)(2,1)S(1)}, u32[]{:S(2)}, u32[]{:S(2)}) collective-permute-start(bf16[32,4096]{1,0:T(8,128)(2,1)S(1)} %get-tuple-element.72), channel_id=1, source_target_pairs={{0,4},{4,0},{8,12},{12,8},{1,5},{5,1},{9,13},{13,9},{2,6},{6,2},{1... | collective-permute-start | bytes 786440 | tf_op jit(solution)/shard_map/ppermute | solution.py:372
  62.5 11.8 %collective-permute-start.15 = (bf16[32,1536]{1,0:T(8,128)(2,1)S(1)}, bf16[32,1536]{1,0:T(8,128)(2,1)S(1)}, u32[]{:S(2)}, u32[]{:S(2)}) collective-permute-start(bf16[32,1536]{1,0:T(8,128)(2,1)S(1)} %get-tuple-element.71), channel_id=1, source_target_pairs={{0,8},{4,12},{8,0},{12,4},{1,9},{5,13},{9,1},{13,5},{2,10},{6,14},... | collective-permute-start | bytes 294920 | tf_op jit(solution)/shard_map/ppermute | solution.py:372
  64.5 14.3 %collective-permute-start.17 = (bf16[32,1536]{1,0:T(8,128)(2,1)S(1)}, bf16[32,1536]{1,0:T(8,128)(2,1)S(1)}, u32[]{:S(2)}, u32[]{:S(2)}) collective-permute-start(bf16[32,1536]{1,0:T(8,128)(2,1)S(1)} %get-tuple-element.73), channel_id=1, source_target_pairs={{0,12},{4,8},{8,4},{12,0},{1,13},{5,9},{9,5},{13,1},{2,14},{6,10},... | collective-permute-start | bytes 294920 | tf_op jit(solution)/shard_map/ppermute | solution.py:372
  69.7 13.4 %collective-permute-start.13 = (bf16[16,2560]{1,0:T(8,128)(2,1)S(1)}, bf16[16,2560]{1,0:T(8,128)(2,1)S(1)}, u32[]{:S(2)}, u32[]{:S(2)}) collective-permute-start(bf16[16,2560]{1,0:T(8,128)(2,1)S(1)} %get-tuple-element.82), channel_id=1, source_target_pairs={{0,8},{4,12},{8,0},{12,4},{1,9},{5,13},{9,1},{13,5},{2,10},{6,14},... | collective-permute-start | bytes 245768 | tf_op jit(solution)/shard_map/ppermute | solution.py:372
  71.1 12.6 %collective-permute-start.14 = (bf16[16,2560]{1,0:T(8,128)(2,1)S(1)}, bf16[16,2560]{1,0:T(8,128)(2,1)S(1)}, u32[]{:S(2)}, u32[]{:S(2)}) collective-permute-start(bf16[16,2560]{1,0:T(8,128)(2,1)S(1)} %get-tuple-element.81), channel_id=1, source_target_pairs={{0,9},{1,8},{4,13},{5,12},{8,1},{9,0},{12,5},{13,4},{2,11},{3,10},... | collective-permute-start | bytes 245768 | tf_op jit(solution)/shard_map/ppermute | solution.py:384
  79.0 4.7 %collective-permute-start.18 = (bf16[16,4096]{1,0:T(8,128)(2,1)S(1)}, bf16[16,4096]{1,0:T(8,128)(2,1)S(1)}, u32[]{:S(2)}, u32[]{:S(2)}) collective-permute-start(bf16[16,4096]{1,0:T(8,128)(2,1)S(1)} %pad_maximum_fusion.1), channel_id=1, source_target_pairs={{0,1},{1,0},{2,3},{3,2},{4,5},{5,4},{6,7},{7,6},{8,9},{9,8},{10,11... | collective-permute-start | bytes 393224 | tf_op jit(solution)/shard_map/ppermute | solution.py:376
  (1 other events, 0.7 us)

commit v7 on v6

--- a/solution.py
+++ b/solution.py
@@ -106,14 +106,17 @@
         largest = jnp.max(scores, axis=1, keepdims=True)
         mine = pl.ds(head * per_key * rows, per_key * rows)
         if before is not None:
-            earlier = before[1][mine, :][:, :1]
-            largest = jnp.maximum(largest, earlier)
+            earlier = before[1][mine, :]
+            largest = jnp.maximum(earlier, largest)
+            scale = jnp.exp2(earlier - largest)
+            count = -(-scores.shape[1] // HEAD_DIM)
+            largest = jnp.concatenate([largest] * count, axis=1)[:, : scores.shape[1]]
         weights = jnp.exp2(scores - largest)
         summed = jnp.dot(
             weights.astype(jnp.bfloat16), values, preferred_element_type=jnp.float32
         )
         if before is not None:
-            summed = summed + before[0][mine, :] * jnp.exp2(earlier - largest)
+            summed = summed + before[0][mine, :] * jnp.concatenate([scale, scale], axis=1)
         if after is not None:
             after[0][mine, :] = summed
             after[1][mine, :] = jnp.broadcast_to(largest, (per_key * rows, HEAD_DIM))
@@ -478,6 +481,7 @@
     late, attended = tied(held[strides[0]], attended)
     late_mine = across(late[:CAP], strides[0])
     late_theirs = across_and_swap(late[CAP:], strides[0])
+    straight[1], attended = tied(straight[1], attended)
     arrived = [across(v, k) for k, v in straight.items() if k]
     arrived, late = tied(arrived, late)
     so_far = [

time: 85.2 us -> 81.2 us (0.953)
  Pallas kernels: 19.4 us -> 16 us
  waiting for transfers between devices: 42.7 us -> 40.1 us
  starting transfers between devices: 18.2 us -> 20.2 us
    ppermute x11, waiting for transfers between devices: 39.6 us -> 36.2 us  [across(): return lax.ppermute(x, 'seq', [(i, i ^ stride) for i in range(n)])]
    pallas_call x3, Pallas kernels: 11.5 us -> 8.07 us  [attention(): pl.pallas_call(functools.partial(kernel, tuple(origins), per_key, rows_tr...]
    ppermute x11, starting transfers between devices: 16.9 us -> 18.9 us  [across(): return lax.ppermute(x, 'seq', [(i, i ^ stride) for i in range(n)])]
    ppermute x7, waiting for transfers between devices: 2.6 us -> 3.89 us  [swap(): return lax.ppermute(x, 'tp', [(0, 1), (1, 0)])]
  transfers between devices with their start and end apart: 19 -> 19, of which waited for: 12 -> 12; matrix products, arithmetic and copies ran while one was open for 0% -> 0% of each run, Pallas kernels for 14% -> 10%
where the time goes in v7:
time: 81.2 us; the launch traced here: 80.9 us
  waiting for transfers between devices  40.1 us (49%)
  starting transfers between devices  20.2 us (25%)
  Pallas kernels  16 us (20%)
  local copies, waits for them, and re-layouts  3.54 us (4%)
  between operations  0.84 us (1%)
    ppermute x11, waiting for transfers between devices, across(): return lax.ppermute(x, 'seq', [(i, i ^ stride) for i in range(n)])  36.2 us
    ppermute x11, starting transfers between devices, across(): return lax.ppermute(x, 'seq', [(i, i ^ stride) for i in range(n)])  18.9 us
    pallas_call x3, Pallas kernels, attention(): pl.pallas_call(functools.partial(kernel, tuple(origins), per_key, rows_tr...  8.07 us
    pallas_call x1, Pallas kernels, expert_call(): pl.pallas_call(functools.partial(expert_kernel, tuple(origins), tuple(ord...  6.35 us
    ppermute x7, waiting for transfers between devices, swap(): return lax.ppermute(x, 'tp', [(0, 1), (1, 0)])  3.89 us
    unnamed x14, local copies, waits for them, and re-layouts  3.52 us
  transfers between devices with their start and end apart: 19, of which 12 were waited for; matrix products, arithmetic and copies ran while one was open for 0% of the time, Pallas kernels for 10%

profile of v7, /device:TPU:0, one launch (start us, length us, event | category | flops | bytes accessed | tf_op | source)
XLA Modules:
  0.0 80.9 jit_solution(17065263814727525376)
XLA Ops:
  0.0 1.1 %copy.10 = bf16[12,8,2,1024]{3,1,2,0:T(8,128)(2,1)S(1)} copy(bf16[12,8,2,1024]{3,2,1,0:T(2,128)(2,1)} %bitcast.31) | data formatting | bytes 786432
  1.1 4.1 %collective-permute-start = (bf16[96,2048]{1,0:T(8,128)(2,1)S(1)}, bf16[96,2048]{1,0:T(8,128)(2,1)S(1)}, u32[]{:S(2)}, u32[]{:S(2)}) collective-permute-start(bf16[96,2048]{1,0:T(8,128)(2,1)S(1)} %bitcast.16), channel_id=1, source_target_pairs={{0,8},{4,12},{8,0},{12,4},{1,9},{5,13},{9,1},{13,5},{2,10},{6,14},... | collective-permute-start | bytes 1179656 | tf_op jit(solution)/shard_map/ppermute | solution.py:375
  5.2 1.6 %collective-permute-start.3 = (bf16[96,2048]{1,0:T(8,128)(2,1)S(1)}, bf16[96,2048]{1,0:T(8,128)(2,1)S(1)}, u32[]{:S(2)}, u32[]{:S(2)}) collective-permute-start(bf16[96,2048]{1,0:T(8,128)(2,1)S(1)} %bitcast.17), channel_id=1, source_target_pairs={{0,4},{4,0},{8,12},{12,8},{1,5},{5,1},{9,13},{13,9},{2,6},{6,2},{1... | collective-permute-start | bytes 1179656 | tf_op jit(solution)/shard_map/ppermute | solution.py:375
  6.8 1.0 %copy-done.1 = bf16[1,64,4096]{2,1,0:T(8,128)(2,1)S(1)} copy-done((bf16[1,64,4096]{2,1,0:T(8,128)(2,1)S(1)}, bf16[1,64,4096]{2,1,0:T(8,128)(2,1)}, u32[]{:S(2)}) %copy-start.1) | copy-done | bytes 524312
  7.8 0.7 copy-done.4
  8.5 0.7 copy-done.5
  9.6 1.3 %collective-permute-done.1 = bf16[16,4096]{1,0:T(8,128)(2,1)S(1)} collective-permute-done((bf16[16,4096]{1,0:T(8,128)(2,1)S(1)}, bf16[16,4096]{1,0:T(8,128)(2,1)S(1)}, u32[]{:S(2)}, u32[]{:S(2)}) %collective-permute-start.1) | collective-permute-done | bytes 131104 | tf_op jit(solution)/shard_map/ppermute | solution.py:379
  11.6 22.6 %collective-permute-done.2.refs_1_ = bf16[32,4096]{1,0:T(8,128)(2,1)S(1)} collective-permute-done((bf16[32,4096]{1,0:T(8,128)(2,1)S(1)}, bf16[32,4096]{1,0:T(8,128)(2,1)S(1)}, u32[]{:S(2)}, u32[]{:S(2)}) %collective-permute-start.2) | collective-permute-done | bytes 262176 | tf_op jit(solution)/shard_map/ppermute | solution.py:375
  34.9 1.5 %collective-permute-start.9 = (bf16[96,2048]{1,0:T(8,128)(2,1)S(1)}, bf16[96,2048]{1,0:T(8,128)(2,1)S(1)}, u32[]{:S(2)}, u32[]{:S(2)}) collective-permute-start(bf16[96,2048]{1,0:T(8,128)(2,1)S(1)} %collective-permute-done.refs_4_.refs_1_), channel_id=1, source_target_pairs={{0,4},{4,0},{8,12},{12,8},{1,5},{5,1},{9,13},{13,9},{2,6},{6,2},{1... | collective-permute-start | bytes 1179656 | tf_op jit(solution)/shard_map/ppermute | solution.py:375
  37.1 3.9 %begin.1 = (f32[3072,256]{1,0:T(8,128)S(1)}, f32[3072,128]{1,0:T(8,128)S(1)}, f32[8,128]{1,0:T(8,128)S(1)}) custom-call(s32[1]{0:T(128)S(6)} %copy.12.length_ref, bf16[32,4096]{1,0:T(8,128)(2,1)S(1)} %constant_dynamic-update-slice_fusion.refs_0_, bf16[32,4096]{1,0:T(8,128)(2,1)S(1)} %collective-permute-done.2.refs_1_, ...), custom_call_target="tpu_custom_call" | custom-call | flops 1 | bytes 1 | tf_op jit(solution)/shard_map/begin/pallas_call | solution.py:190
  41.0 1.6 %collective-permute-start.8 = (bf16[32,4096]{1,0:T(8,128)(2,1)S(1)}, bf16[32,4096]{1,0:T(8,128)(2,1)S(1)}, u32[]{:S(2)}, u32[]{:S(2)}) collective-permute-start(bf16[32,4096]{1,0:T(8,128)(2,1)S(1)} %collective-permute-done.2.refs_1_), channel_id=1, source_target_pairs={{0,4},{4,0},{8,12},{12,8},{1,5},{5,1},{9,13},{13,9},{2,6},{6,2},{1... | collective-permute-start | bytes 786440 | tf_op jit(solution)/shard_map/ppermute | solution.py:375
  42.6 4.1 %collective-permute-done.9.whole_ref.refs_3_.refs_6_ = bf16[96,2048]{1,0:T(8,128)(2,1)S(1)} collective-permute-done((bf16[96,2048]{1,0:T(8,128)(2,1)S(1)}, bf16[96,2048]{1,0:T(8,128)(2,1)S(1)}, u32[]{:S(2)}, u32[]{:S(2)}) %collective-permute-start.9) | collective-permute-done | bytes 393248 | tf_op jit(solution)/shard_map/ppermute | solution.py:375
  47.4 0.9 %collective-permute-done.10.refs_4_.refs_7_ = bf16[48,2048]{1,0:T(8,128)(2,1)S(1)} collective-permute-done((bf16[48,2048]{1,0:T(8,128)(2,1)S(1)}, bf16[48,2048]{1,0:T(8,128)(2,1)S(1)}, u32[]{:S(2)}, u32[]{:S(2)}) %collective-permute-start.10) | collective-permute-done | bytes 196640 | tf_op jit(solution)/shard_map/ppermute | solution.py:379
  48.6 1.9 %finish.1.done_ref = bf16[96,4096]{1,0:T(8,128)(2,1)S(1)} custom-call(s32[1]{0:T(128)S(6)} %copy.12.length_ref, bf16[32,4096]{1,0:T(8,128)(2,1)S(1)} %constant_dynamic-update-slice_fusion.refs_0_, bf16[32,4096]{1,0:T(8,128)(2,1)S(1)} %collective-permute-done.2.refs_1_, bf16[32,4096]{1,0:T(8,128)(2,1)S(1)} %collective-permute-done.4.refs_2_, ...), custom_call_target="tpu_custom_call" | custom-call | flops 1 | bytes 1 | tf_op jit(solution)/shard_map/finish/pallas_call | solution.py:190
  50.5 1.4 %collective-permute-done.8.last_ref = bf16[32,4096]{1,0:T(8,128)(2,1)S(1)} collective-permute-done((bf16[32,4096]{1,0:T(8,128)(2,1)S(1)}, bf16[32,4096]{1,0:T(8,128)(2,1)S(1)}, u32[]{:S(2)}, u32[]{:S(2)}) %collective-permute-start.8) | collective-permute-done | bytes 262176 | tf_op jit(solution)/shard_map/ppermute | solution.py:375
  51.9 6.3 %experts.1 = (bf16[32,4096]{1,0:T(8,128)(2,1)S(1)}, bf16[32,1536]{1,0:T(8,128)(2,1)S(1)}, bf16[32,2560]{1,0:T(8,128)(2,1)S(1)}, bf16[32,4096]{1,0:T(8,128)(2,1)S...) custom-call(bf16[32,4096]{1,0:T(8,128)(2,1)S(1)} %collective-permute-done.8.last_ref, ...), custom_call_target="tpu_custom_call" | custom-call | flops 1610612736 | bytes 12582912 | tf_op jit(solution)/shard_map/experts/pallas_call | solution.py:317
  58.3 1.6 %collective-permute-start.12 = (bf16[32,2560]{1,0:T(8,128)(2,1)S(1)}, bf16[32,2560]{1,0:T(8,128)(2,1)S(1)}, u32[]{:S(2)}, u32[]{:S(2)}) collective-permute-start(bf16[32,2560]{1,0:T(8,128)(2,1)S(1)} %get-tuple-element.67), channel_id=1, source_target_pairs={{0,4},{4,0},{8,12},{12,8},{1,5},{5,1},{9,13},{13,9},{2,6},{6,2},{1... | collective-permute-start | bytes 491528 | tf_op jit(solution)/shard_map/ppermute | solution.py:375
  59.9 2.4 %collective-permute-start.15 = (bf16[32,1536]{1,0:T(8,128)(2,1)S(1)}, bf16[32,1536]{1,0:T(8,128)(2,1)S(1)}, u32[]{:S(2)}, u32[]{:S(2)}) collective-permute-start(bf16[32,1536]{1,0:T(8,128)(2,1)S(1)} %get-tuple-element.75), channel_id=1, source_target_pairs={{0,8},{4,12},{8,0},{12,4},{1,9},{5,13},{9,1},{13,5},{2,10},{6,14},... | collective-permute-start | bytes 294920 | tf_op jit(solution)/shard_map/ppermute | solution.py:375
  62.8 2.3 %attend.1.attended_ref = bf16[64,4096]{1,0:T(8,128)(2,1)S(1)} custom-call(s32[1]{0:T(128)S(6)} %copy.12.length_ref, bf16[64,4096]{1,0:T(8,128)(2,1)S(1)} %bitcast.24, bf16[96,2048]{1,0:T(8,128)(2,1)S(1)} %bitcast.21, bf16[96,2048]{1,0:T(8,128)(2,1)S(1)} %collective-permute-done.refs_4_.refs_1_, bf16[96,2048]{1,0:T(8,128)(2,1)S(1)} %collective-permute-done.3.refs_5_.refs_2_, ...), custom_call_target="tpu_custom_call" | custom-call | flops 805306368 | bytes 4194304 | tf_op jit(solution)/shard_map/attend/pallas_call | solution.py:190
  65.7 1.4 %collective-permute-start.16 = (bf16[32,4096]{1,0:T(8,128)(2,1)S(1)}, bf16[32,4096]{1,0:T(8,128)(2,1)S(1)}, u32[]{:S(2)}, u32[]{:S(2)}) collective-permute-start(bf16[32,4096]{1,0:T(8,128)(2,1)S(1)} %get-tuple-element.76), channel_id=1, source_target_pairs={{0,4},{4,0},{8,12},{12,8},{1,5},{5,1},{9,13},{13,9},{2,6},{6,2},{1... | collective-permute-start | bytes 786440 | tf_op jit(solution)/shard_map/ppermute | solution.py:375
  67.1 3.6 %collective-permute-start.13 = (bf16[16,2560]{1,0:T(8,128)(2,1)S(1)}, bf16[16,2560]{1,0:T(8,128)(2,1)S(1)}, u32[]{:S(2)}, u32[]{:S(2)}) collective-permute-start(bf16[16,2560]{1,0:T(8,128)(2,1)S(1)} %get-tuple-element.86), channel_id=1, source_target_pairs={{0,8},{4,12},{8,0},{12,4},{1,9},{5,13},{9,1},{13,5},{2,10},{6,14},... | collective-permute-start | bytes 245768 | tf_op jit(solution)/shard_map/ppermute | solution.py:375
  71.3 6.8 %collective-permute-done.16 = bf16[32,4096]{1,0:T(8,128)(2,1)S(1)} collective-permute-done((bf16[32,4096]{1,0:T(8,128)(2,1)S(1)}, bf16[32,4096]{1,0:T(8,128)(2,1)S(1)}, u32[]{:S(2)}, u32[]{:S(2)}) %collective-permute-start.16) | collective-permute-done | bytes 262176 | tf_op jit(solution)/shard_map/ppermute | solution.py:375
  78.4 1.3 %collective-permute-done.18.theirs_ref = bf16[16,4096]{1,0:T(8,128)(2,1)S(1)} collective-permute-done((bf16[16,4096]{1,0:T(8,128)(2,1)S(1)}, bf16[16,4096]{1,0:T(8,128)(2,1)S(1)}, u32[]{:S(2)}, u32[]{:S(2)}) %collective-permute-start.18) | collective-permute-done | bytes 131104 | tf_op jit(solution)/shard_map/ppermute | solution.py:379
  79.7 1.3 %combine.1 = bf16[64,4096]{1,0:T(8,128)(2,1)} custom-call(bf16[16,2560]{1,0:T(8,128)(2,1)S(1)} %collective-permute-done.13.late_ref, bf16[16,2560]{1,0:T(8,128)(2,1)S(1)} %collective-permute-done.14.late_theirs_ref, f32[32,64]{1,0:T(8,128)S(1)} %get-tuple-element.70.comb_ref, bf16[64,4096]{1,0:T(8,128)(2,1)S(1)} %attend.1.attended_ref, ...), custom_call_target="tpu_custom_call" | custom-call | flops 33554432 | bytes 1048576 | tf_op jit(solution)/shard_map/combine/pallas_call | solution.py:501
  (42 shorter events, 4.5 us)
Async XLA Ops:
  0.0 48.6 %copy-start.3 = (f32[4096]{0:T(1024)S(1)}, f32[4096]{0:T(1024)}, u32[]{:S(2)}) copy-start(f32[4096]{0:T(1024)} %param.14) | copy-start | bytes 49156
  1.1 33.2 %collective-permute-start = (bf16[96,2048]{1,0:T(8,128)(2,1)S(1)}, bf16[96,2048]{1,0:T(8,128)(2,1)S(1)}, u32[]{:S(2)}, u32[]{:S(2)}) collective-permute-start(bf16[96,2048]{1,0:T(8,128)(2,1)S(1)} %bitcast.16), channel_id=1, source_target_pairs={{0,8},{4,12},{8,0},{12,4},{1,9},{5,13},{9,1},{13,5},{2,10},{6,14},... | collective-permute-start | bytes 1179656 | tf_op jit(solution)/shard_map/ppermute | solution.py:375
  5.2 29.1 %collective-permute-start.3 = (bf16[96,2048]{1,0:T(8,128)(2,1)S(1)}, bf16[96,2048]{1,0:T(8,128)(2,1)S(1)}, u32[]{:S(2)}, u32[]{:S(2)}) collective-permute-start(bf16[96,2048]{1,0:T(8,128)(2,1)S(1)} %bitcast.17), channel_id=1, source_target_pairs={{0,4},{4,0},{8,12},{12,8},{1,5},{5,1},{9,13},{13,9},{2,6},{6,2},{1... | collective-permute-start | bytes 1179656 | tf_op jit(solution)/shard_map/ppermute | solution.py:375
  6.8 1.0 %copy-start.1 = (bf16[1,64,4096]{2,1,0:T(8,128)(2,1)S(1)}, bf16[1,64,4096]{2,1,0:T(8,128)(2,1)}, u32[]{:S(2)}) copy-start(bf16[1,64,4096]{2,1,0:T(8,128)(2,1)} %param.9) | copy-start | bytes 1572868
  7.8 0.7 copy-start.4
  9.5 1.4 %collective-permute-start.1 = (bf16[16,4096]{1,0:T(8,128)(2,1)S(1)}, bf16[16,4096]{1,0:T(8,128)(2,1)S(1)}, u32[]{:S(2)}, u32[]{:S(2)}) collective-permute-start(bf16[16,4096]{1,0:T(8,128)(2,1)S(1)} %get-tuple-element.44), channel_id=1, source_target_pairs={{0,1},{1,0},{2,3},{3,2},{4,5},{5,4},{6,7},{7,6},{8,9},{9,8},{10,11... | collective-permute-start | bytes 393224 | tf_op jit(solution)/shard_map/ppermute | solution.py:379
  11.0 23.2 %collective-permute-start.2 = (bf16[32,4096]{1,0:T(8,128)(2,1)S(1)}, bf16[32,4096]{1,0:T(8,128)(2,1)S(1)}, u32[]{:S(2)}, u32[]{:S(2)}) collective-permute-start(bf16[32,4096]{1,0:T(8,128)(2,1)S(1)} %constant_dynamic-update-slice_fusion.refs_0_), channel_id=1, source_target_pairs={{0,8},{4,12},{8,0},{12,4},{1,9},{5,13},{9,1},{13,5},{2,10},{6,14},... | collective-permute-start | bytes 786440 | tf_op jit(solution)/shard_map/ppermute | solution.py:375
  11.4 22.9 %collective-permute-start.4 = (bf16[32,4096]{1,0:T(8,128)(2,1)S(1)}, bf16[32,4096]{1,0:T(8,128)(2,1)S(1)}, u32[]{:S(2)}, u32[]{:S(2)}) collective-permute-start(bf16[32,4096]{1,0:T(8,128)(2,1)S(1)} %constant_dynamic-update-slice_fusion.refs_0_), channel_id=1, source_target_pairs={{0,4},{4,0},{8,12},{12,8},{1,5},{5,1},{9,13},{13,9},{2,6},{6,2},{1... | collective-permute-start | bytes 786440 | tf_op jit(solution)/shard_map/ppermute | solution.py:375
  34.3 2.8 %collective-permute-start.6 = (bf16[96,2048]{1,0:T(8,128)(2,1)S(1)}, bf16[96,2048]{1,0:T(8,128)(2,1)S(1)}, u32[]{:S(2)}, u32[]{:S(2)}) collective-permute-start(bf16[96,2048]{1,0:T(8,128)(2,1)S(1)} %collective-permute-done.refs_4_.refs_1_), channel_id=1, source_target_pairs={{0,1},{1,0},{2,3},{3,2},{4,5},{5,4},{6,7},{7,6},{8,9},{9,8},{10,11... | collective-permute-start | bytes 1179656 | tf_op jit(solution)/shard_map/ppermute | solution.py:379
  34.3 2.8 %collective-permute-start.5 = (bf16[96,2048]{1,0:T(8,128)(2,1)S(1)}, bf16[96,2048]{1,0:T(8,128)(2,1)S(1)}, u32[]{:S(2)}, u32[]{:S(2)}) collective-permute-start(bf16[96,2048]{1,0:T(8,128)(2,1)S(1)} %bitcast.18), channel_id=1, source_target_pairs={{0,1},{1,0},{2,3},{3,2},{4,5},{5,4},{6,7},{7,6},{8,9},{9,8},{10,11... | collective-permute-start | bytes 1179656 | tf_op jit(solution)/shard_map/ppermute | solution.py:379
  34.8 2.3 %collective-permute-start.7 = (bf16[96,2048]{1,0:T(8,128)(2,1)S(1)}, bf16[96,2048]{1,0:T(8,128)(2,1)S(1)}, u32[]{:S(2)}, u32[]{:S(2)}) collective-permute-start(bf16[96,2048]{1,0:T(8,128)(2,1)S(1)} %collective-permute-done.3.refs_5_.refs_2_), channel_id=1, source_target_pairs={{0,1},{1,0},{2,3},{3,2},{4,5},{5,4},{6,7},{7,6},{8,9},{9,8},{10,11... | collective-permute-start | bytes 1179656 | tf_op jit(solution)/shard_map/ppermute | solution.py:379
  34.9 11.9 %collective-permute-start.9 = (bf16[96,2048]{1,0:T(8,128)(2,1)S(1)}, bf16[96,2048]{1,0:T(8,128)(2,1)S(1)}, u32[]{:S(2)}, u32[]{:S(2)}) collective-permute-start(bf16[96,2048]{1,0:T(8,128)(2,1)S(1)} %collective-permute-done.refs_4_.refs_1_), channel_id=1, source_target_pairs={{0,4},{4,0},{8,12},{12,8},{1,5},{5,1},{9,13},{13,9},{2,6},{6,2},{1... | collective-permute-start | bytes 1179656 | tf_op jit(solution)/shard_map/ppermute | solution.py:375
  41.0 10.9 %copy-start = (bf16[1,4096,512]{2,1,0:T(8,128)(2,1)S(1)}, bf16[1,4096,512]{2,1,0:T(8,128)(2,1)}, u32[]{:S(2)}) copy-start(bf16[1,4096,512]{2,1,0:T(8,128)(2,1)} %param.15) | copy-start | bytes 12582916
  41.0 10.9 %collective-permute-start.8 = (bf16[32,4096]{1,0:T(8,128)(2,1)S(1)}, bf16[32,4096]{1,0:T(8,128)(2,1)S(1)}, u32[]{:S(2)}, u32[]{:S(2)}) collective-permute-start(bf16[32,4096]{1,0:T(8,128)(2,1)S(1)} %collective-permute-done.2.refs_1_), channel_id=1, source_target_pairs={{0,4},{4,0},{8,12},{12,8},{1,5},{5,1},{9,13},{13,9},{2,6},{6,2},{1... | collective-permute-start | bytes 786440 | tf_op jit(solution)/shard_map/ppermute | solution.py:375
  46.8 1.5 %collective-permute-start.10 = (bf16[48,2048]{1,0:T(8,128)(2,1)S(1)}, bf16[48,2048]{1,0:T(8,128)(2,1)S(1)}, u32[]{:S(2)}, u32[]{:S(2)}) collective-permute-start(bf16[48,2048]{1,0:T(8,128)(2,1)S(1)} %get-tuple-element.55), channel_id=1, source_target_pairs={{0,1},{1,0},{2,3},{3,2},{4,5},{5,4},{6,7},{7,6},{8,9},{9,8},{10,11... | collective-permute-start | bytes 589832 | tf_op jit(solution)/shard_map/ppermute | solution.py:379
  46.9 1.7 %collective-permute-start.11 = (bf16[48,2048]{1,0:T(8,128)(2,1)S(1)}, bf16[48,2048]{1,0:T(8,128)(2,1)S(1)}, u32[]{:S(2)}, u32[]{:S(2)}) collective-permute-start(bf16[48,2048]{1,0:T(8,128)(2,1)S(1)} %get-tuple-element.56), channel_id=1, source_target_pairs={{0,1},{1,0},{2,3},{3,2},{4,5},{5,4},{6,7},{7,6},{8,9},{9,8},{10,11... | collective-permute-start | bytes 589832 | tf_op jit(solution)/shard_map/ppermute | solution.py:379
  51.9 10.8 %copy-start.2 = (bf16[1,64,4096]{2,1,0:T(8,128)(2,1)S(1)}, bf16[1,64,4096]{2,1,0:T(8,128)(2,1)}, u32[]{:S(2)}) copy-start(bf16[1,64,4096]{2,1,0:T(8,128)(2,1)} %param.9) | copy-start | bytes 1572868
  58.3 7.3 %collective-permute-start.12 = (bf16[32,2560]{1,0:T(8,128)(2,1)S(1)}, bf16[32,2560]{1,0:T(8,128)(2,1)S(1)}, u32[]{:S(2)}, u32[]{:S(2)}) collective-permute-start(bf16[32,2560]{1,0:T(8,128)(2,1)S(1)} %get-tuple-element.67), channel_id=1, source_target_pairs={{0,4},{4,0},{8,12},{12,8},{1,5},{5,1},{9,13},{13,9},{2,6},{6,2},{1... | collective-permute-start | bytes 491528 | tf_op jit(solution)/shard_map/ppermute | solution.py:375
  59.9 10.9 %collective-permute-start.15 = (bf16[32,1536]{1,0:T(8,128)(2,1)S(1)}, bf16[32,1536]{1,0:T(8,128)(2,1)S(1)}, u32[]{:S(2)}, u32[]{:S(2)}) collective-permute-start(bf16[32,1536]{1,0:T(8,128)(2,1)S(1)} %get-tuple-element.75), channel_id=1, source_target_pairs={{0,8},{4,12},{8,0},{12,4},{1,9},{5,13},{9,1},{13,5},{2,10},{6,14},... | collective-permute-start | bytes 294920 | tf_op jit(solution)/shard_map/ppermute | solution.py:375
  62.3 9.0 %collective-permute-start.17 = (bf16[32,1536]{1,0:T(8,128)(2,1)S(1)}, bf16[32,1536]{1,0:T(8,128)(2,1)S(1)}, u32[]{:S(2)}, u32[]{:S(2)}) collective-permute-start(bf16[32,1536]{1,0:T(8,128)(2,1)S(1)} %get-tuple-element.77), channel_id=1, source_target_pairs={{0,12},{4,8},{8,4},{12,0},{1,13},{5,9},{9,5},{13,1},{2,14},{6,10},... | collective-permute-start | bytes 294920 | tf_op jit(solution)/shard_map/ppermute | solution.py:375
  65.7 12.4 %collective-permute-start.16 = (bf16[32,4096]{1,0:T(8,128)(2,1)S(1)}, bf16[32,4096]{1,0:T(8,128)(2,1)S(1)}, u32[]{:S(2)}, u32[]{:S(2)}) collective-permute-start(bf16[32,4096]{1,0:T(8,128)(2,1)S(1)} %get-tuple-element.76), channel_id=1, source_target_pairs={{0,4},{4,0},{8,12},{12,8},{1,5},{5,1},{9,13},{13,9},{2,6},{6,2},{1... | collective-permute-start | bytes 786440 | tf_op jit(solution)/shard_map/ppermute | solution.py:375
  67.1 11.2 %collective-permute-start.13 = (bf16[16,2560]{1,0:T(8,128)(2,1)S(1)}, bf16[16,2560]{1,0:T(8,128)(2,1)S(1)}, u32[]{:S(2)}, u32[]{:S(2)}) collective-permute-start(bf16[16,2560]{1,0:T(8,128)(2,1)S(1)} %get-tuple-element.86), channel_id=1, source_target_pairs={{0,8},{4,12},{8,0},{12,4},{1,9},{5,13},{9,1},{13,5},{2,10},{6,14},... | collective-permute-start | bytes 245768 | tf_op jit(solution)/shard_map/ppermute | solution.py:375
  70.8 7.6 %collective-permute-start.14 = (bf16[16,2560]{1,0:T(8,128)(2,1)S(1)}, bf16[16,2560]{1,0:T(8,128)(2,1)S(1)}, u32[]{:S(2)}, u32[]{:S(2)}) collective-permute-start(bf16[16,2560]{1,0:T(8,128)(2,1)S(1)} %get-tuple-element.85), channel_id=1, source_target_pairs={{0,9},{1,8},{4,13},{5,12},{8,1},{9,0},{12,5},{13,4},{2,11},{3,10},... | collective-permute-start | bytes 245768 | tf_op jit(solution)/shard_map/ppermute | solution.py:387
  78.3 1.4 %collective-permute-start.18 = (bf16[16,4096]{1,0:T(8,128)(2,1)S(1)}, bf16[16,4096]{1,0:T(8,128)(2,1)S(1)}, u32[]{:S(2)}, u32[]{:S(2)}) collective-permute-start(bf16[16,4096]{1,0:T(8,128)(2,1)S(1)} %pad_maximum_fusion.1), channel_id=1, source_target_pairs={{0,1},{1,0},{2,3},{3,2},{4,5},{5,4},{6,7},{7,6},{8,9},{9,8},{10,11... | collective-permute-start | bytes 393224 | tf_op jit(solution)/shard_map/ppermute | solution.py:379
  (1 other events, 0.7 us)

commit v8 on v7

--- a/solution.py
+++ b/solution.py
@@ -125,7 +125,7 @@
         for j in range(per_key):
             store(at * per_key + j * HEAD_DIM, result[j * rows : (j + 1) * rows])
 
-    if bias.shape[1] > 1024 or per_key * HEAD_DIM * heads > 1 << 13:
+    if bias.shape[1] > 1024:
         lax.fori_loop(0, heads, one, None)
     else:
         for head in range(heads):
@@ -150,6 +150,15 @@
         ref[:, pl.ds(at, HEAD_DIM)] = result
 
     return store
+
+
+def attended_rows(queries, kv_refs, bias, scratch_ref, per_key, before=None):
+    parts = []
+    if bias.shape[1] > 1024:
+        attend(queries, kv_refs, bias, into(scratch_ref), per_key, before)
+        return scratch_ref[...]
+    attend(queries, kv_refs, bias, lambda at, result: parts.append(result), per_key, before)
+    return jnp.concatenate(parts, axis=1)
 
 
 def attend_kernel(origins, per_key, rows_true, length_ref, q_ref, *refs):
@@ -171,15 +180,10 @@
     gain_ref, sums_ref, largest_ref, _, out_ref = refs[-5:]
     kv_refs = refs[-pieces - 5 : -5]
     bias = key_bias(length_ref, kv_refs, origins, rows_true)
-    attend(
-        columns_of(refs[: -pieces - 5]),
-        kv_refs,
-        bias,
-        into(out_ref),
-        per_key,
-        before=(sums_ref, largest_ref),
-    )
-    out_ref[...] = norm(out_ref[...], gain_ref[...])
+    queries = columns_of(refs[: -pieces - 5])
+    state = sums_ref, largest_ref
+    rows = attended_rows(queries, kv_refs, bias, out_ref, per_key, state)
+    out_ref[...] = norm(rows, gain_ref[...])
 
 
 def attention(kernel, name, length, q_blocks, pieces, rows_true, more, out_shape, price):
@@ -278,14 +282,8 @@
         c.start()
     bias = key_bias(length_ref, kv_refs, origins, rows_true)
 
-    def queries(at, size):
-        return last_ref[:, pl.ds(at, size)]
-
-    def store(at, result):
-        x_ref[:, pl.ds(at, HEAD_DIM)] = result
-
-    attend(queries, kv_refs, bias, store, per_key)
-    normed = jnp.concatenate([done_ref[...], norm(x_ref[...], gain_ref[...])], axis=0)
+    last = attended_rows(columns_of([last_ref]), kv_refs, bias, x_ref, per_key)
+    normed = jnp.concatenate([done_ref[...], norm(last, gain_ref[...])], axis=0)
     gate = jnp.dot(normed, gate_ref[...], preferred_element_type=jnp.float32)
     copies[0].wait()
     up = jnp.dot(normed, up_ref[...], preferred_element_type=jnp.float32)
@@ -429,8 +427,9 @@
         routed_blocks = routed_blocks + [across(b, stride) for b in routed_blocks]
         order = order + [k ^ stride for k in order]
     first_kv, first_routed = across(kv, strides[-1]), across(routed, strides[-1])
-    kv_blocks, routed_blocks, first_kv, first_routed = tied(
-        kv_blocks, routed_blocks, first_kv, first_routed
+    own_swapped = swap(kv)
+    kv_blocks, routed_blocks, first_kv, own_swapped, first_routed = tied(
+        kv_blocks, routed_blocks, first_kv, own_swapped, first_routed
     )
     last_kv = [across(b, strides[-1]) for b in kv_blocks[1:]]
     kv_blocks = kv_blocks + [first_kv] + last_kv
@@ -438,7 +437,7 @@
     rows = kv.shape[0]
     shares = 2 if rows % (2 * TILE) == 0 and not pad else 1
     cuts = range(0, rows, rows // shares)
-    swapped = [swap(b) for b in kv_blocks[:-1]]
+    swapped = [own_swapped] + [swap(b) for b in kv_blocks[1:-1]]
 
     origins = [(k, side, 0) for side in (0, 1) for k in order[:-1]]
     first_pieces = kv_blocks[:-1] + swapped, origins

time: 81.2 us -> 80.6 us (level)
  transfers between devices with their start and end apart: 19 -> 19, of which waited for: 12 -> 10; matrix products, arithmetic and copies ran while one was open for 0% -> 0% of each run, Pallas kernels for 10% -> 11%
where the time goes in v8:
time: 80.6 us; the launch traced here: 80.4 us
  waiting for transfers between devices  39.4 us (49%)
  starting transfers between devices  20.2 us (25%)
  Pallas kernels  16.2 us (20%)
  local copies, waits for them, and re-layouts  3.54 us (4%)
  between operations  0.83 us (1%)
    ppermute x11, waiting for transfers between devices, across(): return lax.ppermute(x, 'seq', [(i, i ^ stride) for i in range(n)])  35.9 us
    ppermute x11, starting transfers between devices, across(): return lax.ppermute(x, 'seq', [(i, i ^ stride) for i in range(n)])  18.4 us
    pallas_call x3, Pallas kernels, attention(): pl.pallas_call(functools.partial(kernel, tuple(origins), per_key, rows_tr...  8.19 us
    pallas_call x1, Pallas kernels, expert_call(): pl.pallas_call(functools.partial(expert_kernel, tuple(origins), tuple(ord...  6.39 us
    unnamed x14, local copies, waits for them, and re-layouts  3.52 us
    ppermute x7, waiting for transfers between devices, swap(): return lax.ppermute(x, 'tp', [(0, 1), (1, 0)])  3.49 us
    ppermute x7, starting transfers between devices, swap(): return lax.ppermute(x, 'tp', [(0, 1), (1, 0)])  1.78 us
  transfers between devices with their start and end apart: 19, of which 10 were waited for; matrix products, arithmetic and copies ran while one was open for 0% of the time, Pallas kernels for 11%

profile of v8, /device:TPU:0, one launch (start us, length us, event | category | flops | bytes accessed | tf_op | source)
XLA Modules:
  0.0 80.4 jit_solution(9821204680910417483)
XLA Ops:
  0.0 1.1 %copy.10 = bf16[12,8,2,1024]{3,1,2,0:T(8,128)(2,1)S(1)} copy(bf16[12,8,2,1024]{3,2,1,0:T(2,128)(2,1)} %bitcast.31) | data formatting | bytes 786432
  1.1 4.1 %collective-permute-start = (bf16[96,2048]{1,0:T(8,128)(2,1)S(1)}, bf16[96,2048]{1,0:T(8,128)(2,1)S(1)}, u32[]{:S(2)}, u32[]{:S(2)}) collective-permute-start(bf16[96,2048]{1,0:T(8,128)(2,1)S(1)} %bitcast.16), channel_id=1, source_target_pairs={{0,8},{4,12},{8,0},{12,4},{1,9},{5,13},{9,1},{13,5},{2,10},{6,14},... | collective-permute-start | bytes 1179656 | tf_op jit(solution)/shard_map/ppermute | solution.py:373
  5.2 1.6 %collective-permute-start.3 = (bf16[96,2048]{1,0:T(8,128)(2,1)S(1)}, bf16[96,2048]{1,0:T(8,128)(2,1)S(1)}, u32[]{:S(2)}, u32[]{:S(2)}) collective-permute-start(bf16[96,2048]{1,0:T(8,128)(2,1)S(1)} %bitcast.17), channel_id=1, source_target_pairs={{0,4},{4,0},{8,12},{12,8},{1,5},{5,1},{9,13},{13,9},{2,6},{6,2},{1... | collective-permute-start | bytes 1179656 | tf_op jit(solution)/shard_map/ppermute | solution.py:373
  6.8 1.0 %copy-done.1 = bf16[1,64,4096]{2,1,0:T(8,128)(2,1)S(1)} copy-done((bf16[1,64,4096]{2,1,0:T(8,128)(2,1)S(1)}, bf16[1,64,4096]{2,1,0:T(8,128)(2,1)}, u32[]{:S(2)}) %copy-start.1) | copy-done | bytes 524312
  7.8 0.7 copy-done.4
  10.1 1.0 %collective-permute-done.1 = bf16[16,4096]{1,0:T(8,128)(2,1)S(1)} collective-permute-done((bf16[16,4096]{1,0:T(8,128)(2,1)S(1)}, bf16[16,4096]{1,0:T(8,128)(2,1)S(1)}, u32[]{:S(2)}, u32[]{:S(2)}) %collective-permute-start.1) | collective-permute-done | bytes 131104 | tf_op jit(solution)/shard_map/ppermute | solution.py:377
  11.7 22.4 %collective-permute-done.2.refs_1_ = bf16[32,4096]{1,0:T(8,128)(2,1)S(1)} collective-permute-done((bf16[32,4096]{1,0:T(8,128)(2,1)S(1)}, bf16[32,4096]{1,0:T(8,128)(2,1)S(1)}, u32[]{:S(2)}, u32[]{:S(2)}) %collective-permute-start.2) | collective-permute-done | bytes 262176 | tf_op jit(solution)/shard_map/ppermute | solution.py:373
  34.9 1.5 %collective-permute-start.9 = (bf16[96,2048]{1,0:T(8,128)(2,1)S(1)}, bf16[96,2048]{1,0:T(8,128)(2,1)S(1)}, u32[]{:S(2)}, u32[]{:S(2)}) collective-permute-start(bf16[96,2048]{1,0:T(8,128)(2,1)S(1)} %collective-permute-done.refs_4_.refs_1_), channel_id=1, source_target_pairs={{0,4},{4,0},{8,12},{12,8},{1,5},{5,1},{9,13},{13,9},{2,6},{6,2},{1... | collective-permute-start | bytes 1179656 | tf_op jit(solution)/shard_map/ppermute | solution.py:373
  37.1 3.9 %begin.1 = (f32[3072,256]{1,0:T(8,128)S(1)}, f32[3072,128]{1,0:T(8,128)S(1)}, f32[8,128]{1,0:T(8,128)S(1)}) custom-call(s32[1]{0:T(128)S(6)} %copy.12.length_ref, bf16[32,4096]{1,0:T(8,128)(2,1)S(1)} %constant_dynamic-update-slice_fusion.refs_0_, bf16[32,4096]{1,0:T(8,128)(2,1)S(1)} %collective-permute-done.2.refs_1_, ...), custom_call_target="tpu_custom_call" | custom-call | flops 1 | bytes 1 | tf_op jit(solution)/shard_map/begin/pallas_call | solution.py:194
  41.0 1.2 %collective-permute-start.8 = (bf16[32,4096]{1,0:T(8,128)(2,1)S(1)}, bf16[32,4096]{1,0:T(8,128)(2,1)S(1)}, u32[]{:S(2)}, u32[]{:S(2)}) collective-permute-start(bf16[32,4096]{1,0:T(8,128)(2,1)S(1)} %collective-permute-done.2.refs_1_), channel_id=1, source_target_pairs={{0,4},{4,0},{8,12},{12,8},{1,5},{5,1},{9,13},{13,9},{2,6},{6,2},{1... | collective-permute-start | bytes 786440 | tf_op jit(solution)/shard_map/ppermute | solution.py:373
  42.1 4.7 %collective-permute-done.9.whole_ref.refs_3_.refs_6_ = bf16[96,2048]{1,0:T(8,128)(2,1)S(1)} collective-permute-done((bf16[96,2048]{1,0:T(8,128)(2,1)S(1)}, bf16[96,2048]{1,0:T(8,128)(2,1)S(1)}, u32[]{:S(2)}, u32[]{:S(2)}) %collective-permute-start.9) | collective-permute-done | bytes 393248 | tf_op jit(solution)/shard_map/ppermute | solution.py:373
  47.4 0.9 %collective-permute-done.10.refs_4_.refs_7_ = bf16[48,2048]{1,0:T(8,128)(2,1)S(1)} collective-permute-done((bf16[48,2048]{1,0:T(8,128)(2,1)S(1)}, bf16[48,2048]{1,0:T(8,128)(2,1)S(1)}, u32[]{:S(2)}, u32[]{:S(2)}) %collective-permute-start.10) | collective-permute-done | bytes 196640 | tf_op jit(solution)/shard_map/ppermute | solution.py:377
  48.7 1.9 %finish.1.done_ref = bf16[96,4096]{1,0:T(8,128)(2,1)S(1)} custom-call(s32[1]{0:T(128)S(6)} %copy.12.length_ref, bf16[32,4096]{1,0:T(8,128)(2,1)S(1)} %constant_dynamic-update-slice_fusion.refs_0_, bf16[32,4096]{1,0:T(8,128)(2,1)S(1)} %collective-permute-done.2.refs_1_, bf16[32,4096]{1,0:T(8,128)(2,1)S(1)} %collective-permute-done.5.refs_2_, ...), custom_call_target="tpu_custom_call" | custom-call | flops 1 | bytes 1 | tf_op jit(solution)/shard_map/finish/pallas_call | solution.py:194
  50.6 1.0 %collective-permute-done.8.last_ref = bf16[32,4096]{1,0:T(8,128)(2,1)S(1)} collective-permute-done((bf16[32,4096]{1,0:T(8,128)(2,1)S(1)}, bf16[32,4096]{1,0:T(8,128)(2,1)S(1)}, u32[]{:S(2)}, u32[]{:S(2)}) %collective-permute-start.8) | collective-permute-done | bytes 262176 | tf_op jit(solution)/shard_map/ppermute | solution.py:373
  51.6 6.4 %experts.1 = (bf16[32,4096]{1,0:T(8,128)(2,1)S(1)}, bf16[32,1536]{1,0:T(8,128)(2,1)S(1)}, bf16[32,2560]{1,0:T(8,128)(2,1)S(1)}, bf16[32,4096]{1,0:T(8,128)(2,1)S...) custom-call(bf16[32,4096]{1,0:T(8,128)(2,1)S(1)} %collective-permute-done.8.last_ref, ...), custom_call_target="tpu_custom_call" | custom-call | flops 1610612736 | bytes 12582912 | tf_op jit(solution)/shard_map/experts/pallas_call | solution.py:315
  58.0 1.6 %collective-permute-start.12 = (bf16[32,2560]{1,0:T(8,128)(2,1)S(1)}, bf16[32,2560]{1,0:T(8,128)(2,1)S(1)}, u32[]{:S(2)}, u32[]{:S(2)}) collective-permute-start(bf16[32,2560]{1,0:T(8,128)(2,1)S(1)} %get-tuple-element.69), channel_id=1, source_target_pairs={{0,4},{4,0},{8,12},{12,8},{1,5},{5,1},{9,13},{13,9},{2,6},{6,2},{1... | collective-permute-start | bytes 491528 | tf_op jit(solution)/shard_map/ppermute | solution.py:373
  59.6 2.3 %collective-permute-start.15 = (bf16[32,1536]{1,0:T(8,128)(2,1)S(1)}, bf16[32,1536]{1,0:T(8,128)(2,1)S(1)}, u32[]{:S(2)}, u32[]{:S(2)}) collective-permute-start(bf16[32,1536]{1,0:T(8,128)(2,1)S(1)} %get-tuple-element.77), channel_id=1, source_target_pairs={{0,8},{4,12},{8,0},{12,4},{1,9},{5,13},{9,1},{13,5},{2,10},{6,14},... | collective-permute-start | bytes 294920 | tf_op jit(solution)/shard_map/ppermute | solution.py:373
  62.4 2.4 %attend.1.attended_ref = bf16[64,4096]{1,0:T(8,128)(2,1)S(1)} custom-call(s32[1]{0:T(128)S(6)} %copy.12.length_ref, bf16[64,4096]{1,0:T(8,128)(2,1)S(1)} %bitcast.24, bf16[96,2048]{1,0:T(8,128)(2,1)S(1)} %bitcast.21, bf16[96,2048]{1,0:T(8,128)(2,1)S(1)} %collective-permute-done.refs_4_.refs_1_, bf16[96,2048]{1,0:T(8,128)(2,1)S(1)} %collective-permute-done.3.refs_5_.refs_2_, ...), custom_call_target="tpu_custom_call" | custom-call | flops 805306368 | bytes 4194304 | tf_op jit(solution)/shard_map/attend/pallas_call | solution.py:194
  64.9 1.7 %collective-permute-start.16 = (bf16[32,4096]{1,0:T(8,128)(2,1)S(1)}, bf16[32,4096]{1,0:T(8,128)(2,1)S(1)}, u32[]{:S(2)}, u32[]{:S(2)}) collective-permute-start(bf16[32,4096]{1,0:T(8,128)(2,1)S(1)} %get-tuple-element.78), channel_id=1, source_target_pairs={{0,4},{4,0},{8,12},{12,8},{1,5},{5,1},{9,13},{13,9},{2,6},{6,2},{1... | collective-permute-start | bytes 786440 | tf_op jit(solution)/shard_map/ppermute | solution.py:373
  66.5 3.4 %collective-permute-start.13 = (bf16[16,2560]{1,0:T(8,128)(2,1)S(1)}, bf16[16,2560]{1,0:T(8,128)(2,1)S(1)}, u32[]{:S(2)}, u32[]{:S(2)}) collective-permute-start(bf16[16,2560]{1,0:T(8,128)(2,1)S(1)} %get-tuple-element.88), channel_id=1, source_target_pairs={{0,8},{4,12},{8,0},{12,4},{1,9},{5,13},{9,1},{13,5},{2,10},{6,14},... | collective-permute-start | bytes 245768 | tf_op jit(solution)/shard_map/ppermute | solution.py:373
  69.9 1.1 %collective-permute-done.17 = bf16[32,1536]{1,0:T(8,128)(2,1)S(1)} collective-permute-done((bf16[32,1536]{1,0:T(8,128)(2,1)S(1)}, bf16[32,1536]{1,0:T(8,128)(2,1)S(1)}, u32[]{:S(2)}, u32[]{:S(2)}) %collective-permute-start.17) | collective-permute-done | bytes 98336 | tf_op jit(solution)/shard_map/ppermute | solution.py:373
  71.0 6.6 %collective-permute-done.16 = bf16[32,4096]{1,0:T(8,128)(2,1)S(1)} collective-permute-done((bf16[32,4096]{1,0:T(8,128)(2,1)S(1)}, bf16[32,4096]{1,0:T(8,128)(2,1)S(1)}, u32[]{:S(2)}, u32[]{:S(2)}) %collective-permute-start.16) | collective-permute-done | bytes 262176 | tf_op jit(solution)/shard_map/ppermute | solution.py:373
  77.9 1.3 %collective-permute-done.18.theirs_ref = bf16[16,4096]{1,0:T(8,128)(2,1)S(1)} collective-permute-done((bf16[16,4096]{1,0:T(8,128)(2,1)S(1)}, bf16[16,4096]{1,0:T(8,128)(2,1)S(1)}, u32[]{:S(2)}, u32[]{:S(2)}) %collective-permute-start.18) | collective-permute-done | bytes 131104 | tf_op jit(solution)/shard_map/ppermute | solution.py:377
  79.1 1.3 %combine.1 = bf16[64,4096]{1,0:T(8,128)(2,1)} custom-call(bf16[16,2560]{1,0:T(8,128)(2,1)S(1)} %collective-permute-done.13.late_ref, bf16[16,2560]{1,0:T(8,128)(2,1)S(1)} %collective-permute-done.14.late_theirs_ref, f32[32,64]{1,0:T(8,128)S(1)} %get-tuple-element.72.comb_ref, bf16[64,4096]{1,0:T(8,128)(2,1)S(1)} %attend.1.attended_ref, ...), custom_call_target="tpu_custom_call" | custom-call | flops 33554432 | bytes 1048576 | tf_op jit(solution)/shard_map/combine/pallas_call | solution.py:500
  (42 shorter events, 4.6 us)
Async XLA Ops:
  0.0 48.7 %copy-start.3 = (f32[4096]{0:T(1024)S(1)}, f32[4096]{0:T(1024)}, u32[]{:S(2)}) copy-start(f32[4096]{0:T(1024)} %param.14) | copy-start | bytes 49156
  1.1 33.2 %collective-permute-start = (bf16[96,2048]{1,0:T(8,128)(2,1)S(1)}, bf16[96,2048]{1,0:T(8,128)(2,1)S(1)}, u32[]{:S(2)}, u32[]{:S(2)}) collective-permute-start(bf16[96,2048]{1,0:T(8,128)(2,1)S(1)} %bitcast.16), channel_id=1, source_target_pairs={{0,8},{4,12},{8,0},{12,4},{1,9},{5,13},{9,1},{13,5},{2,10},{6,14},... | collective-permute-start | bytes 1179656 | tf_op jit(solution)/shard_map/ppermute | solution.py:373
  5.2 29.1 %collective-permute-start.3 = (bf16[96,2048]{1,0:T(8,128)(2,1)S(1)}, bf16[96,2048]{1,0:T(8,128)(2,1)S(1)}, u32[]{:S(2)}, u32[]{:S(2)}) collective-permute-start(bf16[96,2048]{1,0:T(8,128)(2,1)S(1)} %bitcast.17), channel_id=1, source_target_pairs={{0,4},{4,0},{8,12},{12,8},{1,5},{5,1},{9,13},{13,9},{2,6},{6,2},{1... | collective-permute-start | bytes 1179656 | tf_op jit(solution)/shard_map/ppermute | solution.py:373
  6.8 27.5 %collective-permute-start.4 = (bf16[96,2048]{1,0:T(8,128)(2,1)S(1)}, bf16[96,2048]{1,0:T(8,128)(2,1)S(1)}, u32[]{:S(2)}, u32[]{:S(2)}) collective-permute-start(bf16[96,2048]{1,0:T(8,128)(2,1)S(1)} %bitcast.18), channel_id=1, source_target_pairs={{0,1},{1,0},{2,3},{3,2},{4,5},{5,4},{6,7},{7,6},{8,9},{9,8},{10,11... | collective-permute-start | bytes 1179656 | tf_op jit(solution)/shard_map/ppermute | solution.py:377
  6.8 1.0 %copy-start.1 = (bf16[1,64,4096]{2,1,0:T(8,128)(2,1)S(1)}, bf16[1,64,4096]{2,1,0:T(8,128)(2,1)}, u32[]{:S(2)}) copy-start(bf16[1,64,4096]{2,1,0:T(8,128)(2,1)} %param.9) | copy-start | bytes 1572868
  7.8 0.7 copy-start.4
  9.5 1.6 %collective-permute-start.1 = (bf16[16,4096]{1,0:T(8,128)(2,1)S(1)}, bf16[16,4096]{1,0:T(8,128)(2,1)S(1)}, u32[]{:S(2)}, u32[]{:S(2)}) collective-permute-start(bf16[16,4096]{1,0:T(8,128)(2,1)S(1)} %get-tuple-element.45), channel_id=1, source_target_pairs={{0,1},{1,0},{2,3},{3,2},{4,5},{5,4},{6,7},{7,6},{8,9},{9,8},{10,11... | collective-permute-start | bytes 393224 | tf_op jit(solution)/shard_map/ppermute | solution.py:377
  11.1 23.0 %collective-permute-start.2 = (bf16[32,4096]{1,0:T(8,128)(2,1)S(1)}, bf16[32,4096]{1,0:T(8,128)(2,1)S(1)}, u32[]{:S(2)}, u32[]{:S(2)}) collective-permute-start(bf16[32,4096]{1,0:T(8,128)(2,1)S(1)} %constant_dynamic-update-slice_fusion.refs_0_), channel_id=1, source_target_pairs={{0,8},{4,12},{8,0},{12,4},{1,9},{5,13},{9,1},{13,5},{2,10},{6,14},... | collective-permute-start | bytes 786440 | tf_op jit(solution)/shard_map/ppermute | solution.py:373
  11.5 22.8 %collective-permute-start.5 = (bf16[32,4096]{1,0:T(8,128)(2,1)S(1)}, bf16[32,4096]{1,0:T(8,128)(2,1)S(1)}, u32[]{:S(2)}, u32[]{:S(2)}) collective-permute-start(bf16[32,4096]{1,0:T(8,128)(2,1)S(1)} %constant_dynamic-update-slice_fusion.refs_0_), channel_id=1, source_target_pairs={{0,4},{4,0},{8,12},{12,8},{1,5},{5,1},{9,13},{13,9},{2,6},{6,2},{1... | collective-permute-start | bytes 786440 | tf_op jit(solution)/shard_map/ppermute | solution.py:373
  34.3 2.8 %collective-permute-start.6 = (bf16[96,2048]{1,0:T(8,128)(2,1)S(1)}, bf16[96,2048]{1,0:T(8,128)(2,1)S(1)}, u32[]{:S(2)}, u32[]{:S(2)}) collective-permute-start(bf16[96,2048]{1,0:T(8,128)(2,1)S(1)} %collective-permute-done.refs_4_.refs_1_), channel_id=1, source_target_pairs={{0,1},{1,0},{2,3},{3,2},{4,5},{5,4},{6,7},{7,6},{8,9},{9,8},{10,11... | collective-permute-start | bytes 1179656 | tf_op jit(solution)/shard_map/ppermute | solution.py:377
  34.4 2.7 %collective-permute-start.7 = (bf16[96,2048]{1,0:T(8,128)(2,1)S(1)}, bf16[96,2048]{1,0:T(8,128)(2,1)S(1)}, u32[]{:S(2)}, u32[]{:S(2)}) collective-permute-start(bf16[96,2048]{1,0:T(8,128)(2,1)S(1)} %collective-permute-done.3.refs_5_.refs_2_), channel_id=1, source_target_pairs={{0,1},{1,0},{2,3},{3,2},{4,5},{5,4},{6,7},{7,6},{8,9},{9,8},{10,11... | collective-permute-start | bytes 1179656 | tf_op jit(solution)/shard_map/ppermute | solution.py:377
  34.9 12.0 %collective-permute-start.9 = (bf16[96,2048]{1,0:T(8,128)(2,1)S(1)}, bf16[96,2048]{1,0:T(8,128)(2,1)S(1)}, u32[]{:S(2)}, u32[]{:S(2)}) collective-permute-start(bf16[96,2048]{1,0:T(8,128)(2,1)S(1)} %collective-permute-done.refs_4_.refs_1_), channel_id=1, source_target_pairs={{0,4},{4,0},{8,12},{12,8},{1,5},{5,1},{9,13},{13,9},{2,6},{6,2},{1... | collective-permute-start | bytes 1179656 | tf_op jit(solution)/shard_map/ppermute | solution.py:373
  41.0 10.6 %copy-start = (bf16[1,4096,512]{2,1,0:T(8,128)(2,1)S(1)}, bf16[1,4096,512]{2,1,0:T(8,128)(2,1)}, u32[]{:S(2)}) copy-start(bf16[1,4096,512]{2,1,0:T(8,128)(2,1)} %param.15) | copy-start | bytes 12582916
  41.0 10.6 %collective-permute-start.8 = (bf16[32,4096]{1,0:T(8,128)(2,1)S(1)}, bf16[32,4096]{1,0:T(8,128)(2,1)S(1)}, u32[]{:S(2)}, u32[]{:S(2)}) collective-permute-start(bf16[32,4096]{1,0:T(8,128)(2,1)S(1)} %collective-permute-done.2.refs_1_), channel_id=1, source_target_pairs={{0,4},{4,0},{8,12},{12,8},{1,5},{5,1},{9,13},{13,9},{2,6},{6,2},{1... | collective-permute-start | bytes 786440 | tf_op jit(solution)/shard_map/ppermute | solution.py:373
  46.9 1.5 %collective-permute-start.10 = (bf16[48,2048]{1,0:T(8,128)(2,1)S(1)}, bf16[48,2048]{1,0:T(8,128)(2,1)S(1)}, u32[]{:S(2)}, u32[]{:S(2)}) collective-permute-start(bf16[48,2048]{1,0:T(8,128)(2,1)S(1)} %get-tuple-element.57), channel_id=1, source_target_pairs={{0,1},{1,0},{2,3},{3,2},{4,5},{5,4},{6,7},{7,6},{8,9},{9,8},{10,11... | collective-permute-start | bytes 589832 | tf_op jit(solution)/shard_map/ppermute | solution.py:377
  46.9 1.7 %collective-permute-start.11 = (bf16[48,2048]{1,0:T(8,128)(2,1)S(1)}, bf16[48,2048]{1,0:T(8,128)(2,1)S(1)}, u32[]{:S(2)}, u32[]{:S(2)}) collective-permute-start(bf16[48,2048]{1,0:T(8,128)(2,1)S(1)} %get-tuple-element.58), channel_id=1, source_target_pairs={{0,1},{1,0},{2,3},{3,2},{4,5},{5,4},{6,7},{7,6},{8,9},{9,8},{10,11... | collective-permute-start | bytes 589832 | tf_op jit(solution)/shard_map/ppermute | solution.py:377
  51.6 10.9 %copy-start.2 = (bf16[1,64,4096]{2,1,0:T(8,128)(2,1)S(1)}, bf16[1,64,4096]{2,1,0:T(8,128)(2,1)}, u32[]{:S(2)}) copy-start(bf16[1,64,4096]{2,1,0:T(8,128)(2,1)} %param.9) | copy-start | bytes 1572868
  58.0 6.8 %collective-permute-start.12 = (bf16[32,2560]{1,0:T(8,128)(2,1)S(1)}, bf16[32,2560]{1,0:T(8,128)(2,1)S(1)}, u32[]{:S(2)}, u32[]{:S(2)}) collective-permute-start(bf16[32,2560]{1,0:T(8,128)(2,1)S(1)} %get-tuple-element.69), channel_id=1, source_target_pairs={{0,4},{4,0},{8,12},{12,8},{1,5},{5,1},{9,13},{13,9},{2,6},{6,2},{1... | collective-permute-start | bytes 491528 | tf_op jit(solution)/shard_map/ppermute | solution.py:373
  59.6 10.3 %collective-permute-start.15 = (bf16[32,1536]{1,0:T(8,128)(2,1)S(1)}, bf16[32,1536]{1,0:T(8,128)(2,1)S(1)}, u32[]{:S(2)}, u32[]{:S(2)}) collective-permute-start(bf16[32,1536]{1,0:T(8,128)(2,1)S(1)} %get-tuple-element.77), channel_id=1, source_target_pairs={{0,8},{4,12},{8,0},{12,4},{1,9},{5,13},{9,1},{13,5},{2,10},{6,14},... | collective-permute-start | bytes 294920 | tf_op jit(solution)/shard_map/ppermute | solution.py:373
  61.9 9.1 %collective-permute-start.17 = (bf16[32,1536]{1,0:T(8,128)(2,1)S(1)}, bf16[32,1536]{1,0:T(8,128)(2,1)S(1)}, u32[]{:S(2)}, u32[]{:S(2)}) collective-permute-start(bf16[32,1536]{1,0:T(8,128)(2,1)S(1)} %get-tuple-element.79), channel_id=1, source_target_pairs={{0,12},{4,8},{8,4},{12,0},{1,13},{5,9},{9,5},{13,1},{2,14},{6,10},... | collective-permute-start | bytes 294920 | tf_op jit(solution)/shard_map/ppermute | solution.py:373
  64.9 12.7 %collective-permute-start.16 = (bf16[32,4096]{1,0:T(8,128)(2,1)S(1)}, bf16[32,4096]{1,0:T(8,128)(2,1)S(1)}, u32[]{:S(2)}, u32[]{:S(2)}) collective-permute-start(bf16[32,4096]{1,0:T(8,128)(2,1)S(1)} %get-tuple-element.78), channel_id=1, source_target_pairs={{0,4},{4,0},{8,12},{12,8},{1,5},{5,1},{9,13},{13,9},{2,6},{6,2},{1... | collective-permute-start | bytes 786440 | tf_op jit(solution)/shard_map/ppermute | solution.py:373
  66.5 11.3 %collective-permute-start.13 = (bf16[16,2560]{1,0:T(8,128)(2,1)S(1)}, bf16[16,2560]{1,0:T(8,128)(2,1)S(1)}, u32[]{:S(2)}, u32[]{:S(2)}) collective-permute-start(bf16[16,2560]{1,0:T(8,128)(2,1)S(1)} %get-tuple-element.88), channel_id=1, source_target_pairs={{0,8},{4,12},{8,0},{12,4},{1,9},{5,13},{9,1},{13,5},{2,10},{6,14},... | collective-permute-start | bytes 245768 | tf_op jit(solution)/shard_map/ppermute | solution.py:373
  69.9 7.9 %collective-permute-start.14 = (bf16[16,2560]{1,0:T(8,128)(2,1)S(1)}, bf16[16,2560]{1,0:T(8,128)(2,1)S(1)}, u32[]{:S(2)}, u32[]{:S(2)}) collective-permute-start(bf16[16,2560]{1,0:T(8,128)(2,1)S(1)} %get-tuple-element.87), channel_id=1, source_target_pairs={{0,9},{1,8},{4,13},{5,12},{8,1},{9,0},{12,5},{13,4},{2,11},{3,10},... | collective-permute-start | bytes 245768 | tf_op jit(solution)/shard_map/ppermute | solution.py:385
  77.7 1.4 %collective-permute-start.18 = (bf16[16,4096]{1,0:T(8,128)(2,1)S(1)}, bf16[16,4096]{1,0:T(8,128)(2,1)S(1)}, u32[]{:S(2)}, u32[]{:S(2)}) collective-permute-start(bf16[16,4096]{1,0:T(8,128)(2,1)S(1)} %pad_maximum_fusion.1), channel_id=1, source_target_pairs={{0,1},{1,0},{2,3},{3,2},{4,5},{5,4},{6,7},{7,6},{8,9},{9,8},{10,11... | collective-permute-start | bytes 393224 | tf_op jit(solution)/shard_map/ppermute | solution.py:377
  (1 other events, 0.7 us)

commit v9 on v8

--- a/solution.py
+++ b/solution.py
@@ -338,34 +338,38 @@
     return total.astype(jnp.bfloat16)
 
 
-def combine_kernel(
-    late_ref, late_theirs_ref, comb_ref, attended_ref, mine_ref, theirs_ref, out_ref
-):
-    width = out_ref.shape[1]
-    half = width - late_ref.shape[1]
-    comb = comb_ref[...]
+def weighted(comb_ref, first, rows):
+    comb = comb_ref[first : first + CAP, :]
     high = comb.astype(jnp.bfloat16)
     low = (comb - high.astype(jnp.float32)).astype(jnp.bfloat16)
     both = (((0,), (0,)), ((), ()))
-
-    def finish(rows, begin, end):
-        rows = jnp.concatenate(rows, axis=0)
-        added = lax.dot_general(
-            high, rows, both, preferred_element_type=jnp.float32
-        ) + lax.dot_general(low, rows, both, preferred_element_type=jnp.float32)
-        out_ref[:, begin:end] = (
-            attended_ref[:, begin:end].astype(jnp.float32) + added
-        ).astype(jnp.bfloat16)
-
-    finish([mine_ref[:, :half], theirs_ref[:, :half]], 0, half)
-    finish(
-        [
-            add(mine_ref[:, half:], late_ref[...]),
-            add(theirs_ref[:, half:], late_theirs_ref[...]),
-        ],
-        half,
-        width,
-    )
+    return lax.dot_general(
+        high, rows, both, preferred_element_type=jnp.float32
+    ) + lax.dot_general(low, rows, both, preferred_element_type=jnp.float32)
+
+
+def mix_kernel(first, late_ref, comb_ref, base_ref, sums_ref, out_ref):
+    width = out_ref.shape[1]
+    half = width - late_ref.shape[1]
+    for columns, rows in (
+        (slice(0, half), sums_ref[:, :half]),
+        (slice(half, width), add(sums_ref[:, half:], late_ref[...])),
+    ):
+        out_ref[:, columns] = (
+            base_ref[:, columns].astype(jnp.float32) + weighted(comb_ref, first, rows)
+        ).astype(out_ref.dtype)
+
+
+def mix_call(first, late, comb, base, sums, dtype):
+    return pl.pallas_call(
+        functools.partial(mix_kernel, first),
+        out_shape=jax.ShapeDtypeStruct(base.shape, dtype),
+        in_specs=[VMEM] * 4,
+        out_specs=VMEM,
+        compiler_params=params(16),
+        cost_estimate=cost(1, 1),
+        name="mix",
+    )(late, comb, base, sums)
 
 
 def across(x, stride):
@@ -497,15 +501,8 @@
         for rows in (slice(None, CAP), slice(CAP, None))
     ]
     theirs = swap(so_far[1])
-    mixed = pl.pallas_call(
-        combine_kernel,
-        out_shape=jax.ShapeDtypeStruct((tokens, width), jnp.bfloat16),
-        in_specs=[VMEM] * 6,
-        out_specs=VMEM,
-        compiler_params=params(16),
-        cost_estimate=cost(8 * CAP * tokens * width, 4 * tokens * width),
-        name="combine",
-    )(late_mine, late_theirs, comb, attended, so_far[0], theirs)
+    mixed = mix_call(0, late_mine, comb, attended, so_far[0], jnp.float32)
+    mixed = mix_call(CAP, late_theirs, comb, mixed, theirs, jnp.bfloat16)
     return mixed[None]
 
 

time: 80.6 us -> 80.7 us (level)
    pallas_call x1 -> x2, Pallas kernels: 1.25 us -> 1.73 us  [mix_call(): pl.pallas_call(functools.partial(mix_kernel, first), out_shape=jax.ShapeD...]
where the time goes in v9:
time: 80.7 us; the launch traced here: 80.4 us
  waiting for transfers between devices  39 us (48%)
  starting transfers between devices  20.2 us (25%)
  Pallas kernels  16.7 us (21%)
  local copies, waits for them, and re-layouts  3.54 us (4%)
  between operations  0.85 us (1%)
    ppermute x11, waiting for transfers between devices, across(): return lax.ppermute(x, 'seq', [(i, i ^ stride) for i in range(n)])  35.9 us
    ppermute x11, starting transfers between devices, across(): return lax.ppermute(x, 'seq', [(i, i ^ stride) for i in range(n)])  18.4 us
    pallas_call x3, Pallas kernels, attention(): pl.pallas_call(functools.partial(kernel, tuple(origins), per_key, rows_tr...  8.19 us
    pallas_call x1, Pallas kernels, expert_call(): pl.pallas_call(functools.partial(expert_kernel, tuple(origins), tuple(ord...  6.39 us
    unnamed x14, local copies, waits for them, and re-layouts  3.52 us
    ppermute x7, waiting for transfers between devices, swap(): return lax.ppermute(x, 'tp', [(0, 1), (1, 0)])  3.02 us
    ppermute x7, starting transfers between devices, swap(): return lax.ppermute(x, 'tp', [(0, 1), (1, 0)])  1.78 us
    pallas_call x2, Pallas kernels, mix_call(): pl.pallas_call(functools.partial(mix_kernel, first), out_shape=jax.ShapeD...  1.73 us
  transfers between devices with their start and end apart: 19, of which 10 were waited for; matrix products, arithmetic and copies ran while one was open for 0% of the time, Pallas kernels for 11%

profile of v9, /device:TPU:0, one launch (start us, length us, event | category | flops | bytes accessed | tf_op | source)
XLA Modules:
  0.0 80.4 jit_solution(17809444250840728753)
XLA Ops:
  0.0 1.1 %copy.10 = bf16[12,8,2,1024]{3,1,2,0:T(8,128)(2,1)S(1)} copy(bf16[12,8,2,1024]{3,2,1,0:T(2,128)(2,1)} %bitcast.31) | data formatting | bytes 786432
  1.1 4.1 %collective-permute-start = (bf16[96,2048]{1,0:T(8,128)(2,1)S(1)}, bf16[96,2048]{1,0:T(8,128)(2,1)S(1)}, u32[]{:S(2)}, u32[]{:S(2)}) collective-permute-start(bf16[96,2048]{1,0:T(8,128)(2,1)S(1)} %bitcast.16), channel_id=1, source_target_pairs={{0,8},{4,12},{8,0},{12,4},{1,9},{5,13},{9,1},{13,5},{2,10},{6,14},... | collective-permute-start | bytes 1179656 | tf_op jit(solution)/shard_map/ppermute | solution.py:377
  5.2 1.6 %collective-permute-start.3 = (bf16[96,2048]{1,0:T(8,128)(2,1)S(1)}, bf16[96,2048]{1,0:T(8,128)(2,1)S(1)}, u32[]{:S(2)}, u32[]{:S(2)}) collective-permute-start(bf16[96,2048]{1,0:T(8,128)(2,1)S(1)} %bitcast.17), channel_id=1, source_target_pairs={{0,4},{4,0},{8,12},{12,8},{1,5},{5,1},{9,13},{13,9},{2,6},{6,2},{1... | collective-permute-start | bytes 1179656 | tf_op jit(solution)/shard_map/ppermute | solution.py:377
  6.8 1.0 %copy-done.1 = bf16[1,64,4096]{2,1,0:T(8,128)(2,1)S(1)} copy-done((bf16[1,64,4096]{2,1,0:T(8,128)(2,1)S(1)}, bf16[1,64,4096]{2,1,0:T(8,128)(2,1)}, u32[]{:S(2)}) %copy-start.1) | copy-done | bytes 524312
  7.8 0.7 copy-done.4
  10.1 1.0 %collective-permute-done.1 = bf16[16,4096]{1,0:T(8,128)(2,1)S(1)} collective-permute-done((bf16[16,4096]{1,0:T(8,128)(2,1)S(1)}, bf16[16,4096]{1,0:T(8,128)(2,1)S(1)}, u32[]{:S(2)}, u32[]{:S(2)}) %collective-permute-start.1) | collective-permute-done | bytes 131104 | tf_op jit(solution)/shard_map/ppermute | solution.py:381
  11.7 22.4 %collective-permute-done.2.refs_1_ = bf16[32,4096]{1,0:T(8,128)(2,1)S(1)} collective-permute-done((bf16[32,4096]{1,0:T(8,128)(2,1)S(1)}, bf16[32,4096]{1,0:T(8,128)(2,1)S(1)}, u32[]{:S(2)}, u32[]{:S(2)}) %collective-permute-start.2) | collective-permute-done | bytes 262176 | tf_op jit(solution)/shard_map/ppermute | solution.py:377
  34.9 1.5 %collective-permute-start.9 = (bf16[96,2048]{1,0:T(8,128)(2,1)S(1)}, bf16[96,2048]{1,0:T(8,128)(2,1)S(1)}, u32[]{:S(2)}, u32[]{:S(2)}) collective-permute-start(bf16[96,2048]{1,0:T(8,128)(2,1)S(1)} %collective-permute-done.refs_4_.refs_1_), channel_id=1, source_target_pairs={{0,4},{4,0},{8,12},{12,8},{1,5},{5,1},{9,13},{13,9},{2,6},{6,2},{1... | collective-permute-start | bytes 1179656 | tf_op jit(solution)/shard_map/ppermute | solution.py:377
  37.1 3.9 %begin.1 = (f32[3072,256]{1,0:T(8,128)S(1)}, f32[3072,128]{1,0:T(8,128)S(1)}, f32[8,128]{1,0:T(8,128)S(1)}) custom-call(s32[1]{0:T(128)S(6)} %copy.12.length_ref, bf16[32,4096]{1,0:T(8,128)(2,1)S(1)} %constant_dynamic-update-slice_fusion.refs_0_, bf16[32,4096]{1,0:T(8,128)(2,1)S(1)} %collective-permute-done.2.refs_1_, ...), custom_call_target="tpu_custom_call" | custom-call | flops 1 | bytes 1 | tf_op jit(solution)/shard_map/begin/pallas_call | solution.py:194
  41.0 1.2 %collective-permute-start.8 = (bf16[32,4096]{1,0:T(8,128)(2,1)S(1)}, bf16[32,4096]{1,0:T(8,128)(2,1)S(1)}, u32[]{:S(2)}, u32[]{:S(2)}) collective-permute-start(bf16[32,4096]{1,0:T(8,128)(2,1)S(1)} %collective-permute-done.2.refs_1_), channel_id=1, source_target_pairs={{0,4},{4,0},{8,12},{12,8},{1,5},{5,1},{9,13},{13,9},{2,6},{6,2},{1... | collective-permute-start | bytes 786440 | tf_op jit(solution)/shard_map/ppermute | solution.py:377
  42.1 4.7 %collective-permute-done.9.whole_ref.refs_3_.refs_6_ = bf16[96,2048]{1,0:T(8,128)(2,1)S(1)} collective-permute-done((bf16[96,2048]{1,0:T(8,128)(2,1)S(1)}, bf16[96,2048]{1,0:T(8,128)(2,1)S(1)}, u32[]{:S(2)}, u32[]{:S(2)}) %collective-permute-start.9) | collective-permute-done | bytes 393248 | tf_op jit(solution)/shard_map/ppermute | solution.py:377
  47.4 0.9 %collective-permute-done.10.refs_4_.refs_7_ = bf16[48,2048]{1,0:T(8,128)(2,1)S(1)} collective-permute-done((bf16[48,2048]{1,0:T(8,128)(2,1)S(1)}, bf16[48,2048]{1,0:T(8,128)(2,1)S(1)}, u32[]{:S(2)}, u32[]{:S(2)}) %collective-permute-start.10) | collective-permute-done | bytes 196640 | tf_op jit(solution)/shard_map/ppermute | solution.py:381
  48.7 1.9 %finish.1.done_ref = bf16[96,4096]{1,0:T(8,128)(2,1)S(1)} custom-call(s32[1]{0:T(128)S(6)} %copy.12.length_ref, bf16[32,4096]{1,0:T(8,128)(2,1)S(1)} %constant_dynamic-update-slice_fusion.refs_0_, bf16[32,4096]{1,0:T(8,128)(2,1)S(1)} %collective-permute-done.2.refs_1_, bf16[32,4096]{1,0:T(8,128)(2,1)S(1)} %collective-permute-done.5.refs_2_, ...), custom_call_target="tpu_custom_call" | custom-call | flops 1 | bytes 1 | tf_op jit(solution)/shard_map/finish/pallas_call | solution.py:194
  50.6 1.0 %collective-permute-done.8.last_ref = bf16[32,4096]{1,0:T(8,128)(2,1)S(1)} collective-permute-done((bf16[32,4096]{1,0:T(8,128)(2,1)S(1)}, bf16[32,4096]{1,0:T(8,128)(2,1)S(1)}, u32[]{:S(2)}, u32[]{:S(2)}) %collective-permute-start.8) | collective-permute-done | bytes 262176 | tf_op jit(solution)/shard_map/ppermute | solution.py:377
  51.6 6.4 %experts.1 = (bf16[32,4096]{1,0:T(8,128)(2,1)S(1)}, bf16[32,1536]{1,0:T(8,128)(2,1)S(1)}, bf16[32,2560]{1,0:T(8,128)(2,1)S(1)}, bf16[32,4096]{1,0:T(8,128)(2,1)S...) custom-call(bf16[32,4096]{1,0:T(8,128)(2,1)S(1)} %collective-permute-done.8.last_ref, ...), custom_call_target="tpu_custom_call" | custom-call | flops 1610612736 | bytes 12582912 | tf_op jit(solution)/shard_map/experts/pallas_call | solution.py:315
  58.0 1.6 %collective-permute-start.12 = (bf16[32,2560]{1,0:T(8,128)(2,1)S(1)}, bf16[32,2560]{1,0:T(8,128)(2,1)S(1)}, u32[]{:S(2)}, u32[]{:S(2)}) collective-permute-start(bf16[32,2560]{1,0:T(8,128)(2,1)S(1)} %get-tuple-element.69), channel_id=1, source_target_pairs={{0,4},{4,0},{8,12},{12,8},{1,5},{5,1},{9,13},{13,9},{2,6},{6,2},{1... | collective-permute-start | bytes 491528 | tf_op jit(solution)/shard_map/ppermute | solution.py:377
  59.6 2.3 %collective-permute-start.15 = (bf16[32,1536]{1,0:T(8,128)(2,1)S(1)}, bf16[32,1536]{1,0:T(8,128)(2,1)S(1)}, u32[]{:S(2)}, u32[]{:S(2)}) collective-permute-start(bf16[32,1536]{1,0:T(8,128)(2,1)S(1)} %get-tuple-element.77), channel_id=1, source_target_pairs={{0,8},{4,12},{8,0},{12,4},{1,9},{5,13},{9,1},{13,5},{2,10},{6,14},... | collective-permute-start | bytes 294920 | tf_op jit(solution)/shard_map/ppermute | solution.py:377
  62.4 2.4 %attend.1.base_ref = bf16[64,4096]{1,0:T(8,128)(2,1)S(1)} custom-call(s32[1]{0:T(128)S(6)} %copy.12.length_ref, bf16[64,4096]{1,0:T(8,128)(2,1)S(1)} %bitcast.24, bf16[96,2048]{1,0:T(8,128)(2,1)S(1)} %bitcast.21, bf16[96,2048]{1,0:T(8,128)(2,1)S(1)} %collective-permute-done.refs_4_.refs_1_, bf16[96,2048]{1,0:T(8,128)(2,1)S(1)} %collective-permute-done.3.refs_5_.refs_2_, ...), custom_call_target="tpu_custom_call" | custom-call | flops 805306368 | bytes 4194304 | tf_op jit(solution)/shard_map/attend/pallas_call | solution.py:194
  64.9 1.7 %collective-permute-start.16 = (bf16[32,4096]{1,0:T(8,128)(2,1)S(1)}, bf16[32,4096]{1,0:T(8,128)(2,1)S(1)}, u32[]{:S(2)}, u32[]{:S(2)}) collective-permute-start(bf16[32,4096]{1,0:T(8,128)(2,1)S(1)} %get-tuple-element.78), channel_id=1, source_target_pairs={{0,4},{4,0},{8,12},{12,8},{1,5},{5,1},{9,13},{13,9},{2,6},{6,2},{1... | collective-permute-start | bytes 786440 | tf_op jit(solution)/shard_map/ppermute | solution.py:377
  66.5 3.4 %collective-permute-start.14 = (bf16[16,2560]{1,0:T(8,128)(2,1)S(1)}, bf16[16,2560]{1,0:T(8,128)(2,1)S(1)}, u32[]{:S(2)}, u32[]{:S(2)}) collective-permute-start(bf16[16,2560]{1,0:T(8,128)(2,1)S(1)} %get-tuple-element.87), channel_id=1, source_target_pairs={{0,8},{4,12},{8,0},{12,4},{1,9},{5,13},{9,1},{13,5},{2,10},{6,14},... | collective-permute-start | bytes 245768 | tf_op jit(solution)/shard_map/ppermute | solution.py:377
  69.9 1.1 %collective-permute-done.17 = bf16[32,1536]{1,0:T(8,128)(2,1)S(1)} collective-permute-done((bf16[32,1536]{1,0:T(8,128)(2,1)S(1)}, bf16[32,1536]{1,0:T(8,128)(2,1)S(1)}, u32[]{:S(2)}, u32[]{:S(2)}) %collective-permute-start.17) | collective-permute-done | bytes 98336 | tf_op jit(solution)/shard_map/ppermute | solution.py:377
  71.0 6.6 %collective-permute-done.16 = bf16[32,4096]{1,0:T(8,128)(2,1)S(1)} collective-permute-done((bf16[32,4096]{1,0:T(8,128)(2,1)S(1)}, bf16[32,4096]{1,0:T(8,128)(2,1)S(1)}, u32[]{:S(2)}, u32[]{:S(2)}) %collective-permute-start.16) | collective-permute-done | bytes 262176 | tf_op jit(solution)/shard_map/ppermute | solution.py:377
  78.3 0.8 %collective-permute-done.18.sums_ref = bf16[16,4096]{1,0:T(8,128)(2,1)S(1)} collective-permute-done((bf16[16,4096]{1,0:T(8,128)(2,1)S(1)}, bf16[16,4096]{1,0:T(8,128)(2,1)S(1)}, u32[]{:S(2)}, u32[]{:S(2)}) %collective-permute-start.18) | collective-permute-done | bytes 131104 | tf_op jit(solution)/shard_map/ppermute | solution.py:381
  79.1 1.3 %mix.3 = bf16[64,4096]{1,0:T(8,128)(2,1)} custom-call(bf16[16,2560]{1,0:T(8,128)(2,1)S(1)} %collective-permute-done.13.late_ref, f32[32,64]{1,0:T(8,128)S(1)} %get-tuple-element.72.comb_ref, f32[64,4096]{1,0:T(8,128)S(1)} %mix.2.base_ref, bf16[16,4096]{1,0:T(8,128)(2,1)S(1)} %collective-permute-done.18.sums_ref), custom_call_target="tpu_custom_call" | custom-call | flops 1 | bytes 1 | tf_op jit(solution)/shard_map/mix/pallas_call | solution.py:364
  (43 shorter events, 5.1 us)
Async XLA Ops:
  0.0 48.7 %copy-start.3 = (f32[4096]{0:T(1024)S(1)}, f32[4096]{0:T(1024)}, u32[]{:S(2)}) copy-start(f32[4096]{0:T(1024)} %param.14) | copy-start | bytes 49156
  1.1 33.2 %collective-permute-start = (bf16[96,2048]{1,0:T(8,128)(2,1)S(1)}, bf16[96,2048]{1,0:T(8,128)(2,1)S(1)}, u32[]{:S(2)}, u32[]{:S(2)}) collective-permute-start(bf16[96,2048]{1,0:T(8,128)(2,1)S(1)} %bitcast.16), channel_id=1, source_target_pairs={{0,8},{4,12},{8,0},{12,4},{1,9},{5,13},{9,1},{13,5},{2,10},{6,14},... | collective-permute-start | bytes 1179656 | tf_op jit(solution)/shard_map/ppermute | solution.py:377
  5.2 29.1 %collective-permute-start.3 = (bf16[96,2048]{1,0:T(8,128)(2,1)S(1)}, bf16[96,2048]{1,0:T(8,128)(2,1)S(1)}, u32[]{:S(2)}, u32[]{:S(2)}) collective-permute-start(bf16[96,2048]{1,0:T(8,128)(2,1)S(1)} %bitcast.17), channel_id=1, source_target_pairs={{0,4},{4,0},{8,12},{12,8},{1,5},{5,1},{9,13},{13,9},{2,6},{6,2},{1... | collective-permute-start | bytes 1179656 | tf_op jit(solution)/shard_map/ppermute | solution.py:377
  6.8 27.5 %collective-permute-start.4 = (bf16[96,2048]{1,0:T(8,128)(2,1)S(1)}, bf16[96,2048]{1,0:T(8,128)(2,1)S(1)}, u32[]{:S(2)}, u32[]{:S(2)}) collective-permute-start(bf16[96,2048]{1,0:T(8,128)(2,1)S(1)} %bitcast.18), channel_id=1, source_target_pairs={{0,1},{1,0},{2,3},{3,2},{4,5},{5,4},{6,7},{7,6},{8,9},{9,8},{10,11... | collective-permute-start | bytes 1179656 | tf_op jit(solution)/shard_map/ppermute | solution.py:381
  6.8 1.0 %copy-start.1 = (bf16[1,64,4096]{2,1,0:T(8,128)(2,1)S(1)}, bf16[1,64,4096]{2,1,0:T(8,128)(2,1)}, u32[]{:S(2)}) copy-start(bf16[1,64,4096]{2,1,0:T(8,128)(2,1)} %param.9) | copy-start | bytes 1572868
  7.8 0.7 copy-start.4
  9.5 1.6 %collective-permute-start.1 = (bf16[16,4096]{1,0:T(8,128)(2,1)S(1)}, bf16[16,4096]{1,0:T(8,128)(2,1)S(1)}, u32[]{:S(2)}, u32[]{:S(2)}) collective-permute-start(bf16[16,4096]{1,0:T(8,128)(2,1)S(1)} %get-tuple-element.45), channel_id=1, source_target_pairs={{0,1},{1,0},{2,3},{3,2},{4,5},{5,4},{6,7},{7,6},{8,9},{9,8},{10,11... | collective-permute-start | bytes 393224 | tf_op jit(solution)/shard_map/ppermute | solution.py:381
  11.1 23.0 %collective-permute-start.2 = (bf16[32,4096]{1,0:T(8,128)(2,1)S(1)}, bf16[32,4096]{1,0:T(8,128)(2,1)S(1)}, u32[]{:S(2)}, u32[]{:S(2)}) collective-permute-start(bf16[32,4096]{1,0:T(8,128)(2,1)S(1)} %constant_dynamic-update-slice_fusion.refs_0_), channel_id=1, source_target_pairs={{0,8},{4,12},{8,0},{12,4},{1,9},{5,13},{9,1},{13,5},{2,10},{6,14},... | collective-permute-start | bytes 786440 | tf_op jit(solution)/shard_map/ppermute | solution.py:377
  11.5 22.8 %collective-permute-start.5 = (bf16[32,4096]{1,0:T(8,128)(2,1)S(1)}, bf16[32,4096]{1,0:T(8,128)(2,1)S(1)}, u32[]{:S(2)}, u32[]{:S(2)}) collective-permute-start(bf16[32,4096]{1,0:T(8,128)(2,1)S(1)} %constant_dynamic-update-slice_fusion.refs_0_), channel_id=1, source_target_pairs={{0,4},{4,0},{8,12},{12,8},{1,5},{5,1},{9,13},{13,9},{2,6},{6,2},{1... | collective-permute-start | bytes 786440 | tf_op jit(solution)/shard_map/ppermute | solution.py:377
  34.3 2.8 %collective-permute-start.6 = (bf16[96,2048]{1,0:T(8,128)(2,1)S(1)}, bf16[96,2048]{1,0:T(8,128)(2,1)S(1)}, u32[]{:S(2)}, u32[]{:S(2)}) collective-permute-start(bf16[96,2048]{1,0:T(8,128)(2,1)S(1)} %collective-permute-done.refs_4_.refs_1_), channel_id=1, source_target_pairs={{0,1},{1,0},{2,3},{3,2},{4,5},{5,4},{6,7},{7,6},{8,9},{9,8},{10,11... | collective-permute-start | bytes 1179656 | tf_op jit(solution)/shard_map/ppermute | solution.py:381
  34.4 2.7 %collective-permute-start.7 = (bf16[96,2048]{1,0:T(8,128)(2,1)S(1)}, bf16[96,2048]{1,0:T(8,128)(2,1)S(1)}, u32[]{:S(2)}, u32[]{:S(2)}) collective-permute-start(bf16[96,2048]{1,0:T(8,128)(2,1)S(1)} %collective-permute-done.3.refs_5_.refs_2_), channel_id=1, source_target_pairs={{0,1},{1,0},{2,3},{3,2},{4,5},{5,4},{6,7},{7,6},{8,9},{9,8},{10,11... | collective-permute-start | bytes 1179656 | tf_op jit(solution)/shard_map/ppermute | solution.py:381
  34.9 12.0 %collective-permute-start.9 = (bf16[96,2048]{1,0:T(8,128)(2,1)S(1)}, bf16[96,2048]{1,0:T(8,128)(2,1)S(1)}, u32[]{:S(2)}, u32[]{:S(2)}) collective-permute-start(bf16[96,2048]{1,0:T(8,128)(2,1)S(1)} %collective-permute-done.refs_4_.refs_1_), channel_id=1, source_target_pairs={{0,4},{4,0},{8,12},{12,8},{1,5},{5,1},{9,13},{13,9},{2,6},{6,2},{1... | collective-permute-start | bytes 1179656 | tf_op jit(solution)/shard_map/ppermute | solution.py:377
  41.0 10.6 %copy-start = (bf16[1,4096,512]{2,1,0:T(8,128)(2,1)S(1)}, bf16[1,4096,512]{2,1,0:T(8,128)(2,1)}, u32[]{:S(2)}) copy-start(bf16[1,4096,512]{2,1,0:T(8,128)(2,1)} %param.15) | copy-start | bytes 12582916
  41.0 10.6 %collective-permute-start.8 = (bf16[32,4096]{1,0:T(8,128)(2,1)S(1)}, bf16[32,4096]{1,0:T(8,128)(2,1)S(1)}, u32[]{:S(2)}, u32[]{:S(2)}) collective-permute-start(bf16[32,4096]{1,0:T(8,128)(2,1)S(1)} %collective-permute-done.2.refs_1_), channel_id=1, source_target_pairs={{0,4},{4,0},{8,12},{12,8},{1,5},{5,1},{9,13},{13,9},{2,6},{6,2},{1... | collective-permute-start | bytes 786440 | tf_op jit(solution)/shard_map/ppermute | solution.py:377
  46.9 1.5 %collective-permute-start.10 = (bf16[48,2048]{1,0:T(8,128)(2,1)S(1)}, bf16[48,2048]{1,0:T(8,128)(2,1)S(1)}, u32[]{:S(2)}, u32[]{:S(2)}) collective-permute-start(bf16[48,2048]{1,0:T(8,128)(2,1)S(1)} %get-tuple-element.57), channel_id=1, source_target_pairs={{0,1},{1,0},{2,3},{3,2},{4,5},{5,4},{6,7},{7,6},{8,9},{9,8},{10,11... | collective-permute-start | bytes 589832 | tf_op jit(solution)/shard_map/ppermute | solution.py:381
  46.9 1.7 %collective-permute-start.11 = (bf16[48,2048]{1,0:T(8,128)(2,1)S(1)}, bf16[48,2048]{1,0:T(8,128)(2,1)S(1)}, u32[]{:S(2)}, u32[]{:S(2)}) collective-permute-start(bf16[48,2048]{1,0:T(8,128)(2,1)S(1)} %get-tuple-element.58), channel_id=1, source_target_pairs={{0,1},{1,0},{2,3},{3,2},{4,5},{5,4},{6,7},{7,6},{8,9},{9,8},{10,11... | collective-permute-start | bytes 589832 | tf_op jit(solution)/shard_map/ppermute | solution.py:381
  51.6 10.9 %copy-start.2 = (bf16[1,64,4096]{2,1,0:T(8,128)(2,1)S(1)}, bf16[1,64,4096]{2,1,0:T(8,128)(2,1)}, u32[]{:S(2)}) copy-start(bf16[1,64,4096]{2,1,0:T(8,128)(2,1)} %param.9) | copy-start | bytes 1572868
  58.0 6.8 %collective-permute-start.12 = (bf16[32,2560]{1,0:T(8,128)(2,1)S(1)}, bf16[32,2560]{1,0:T(8,128)(2,1)S(1)}, u32[]{:S(2)}, u32[]{:S(2)}) collective-permute-start(bf16[32,2560]{1,0:T(8,128)(2,1)S(1)} %get-tuple-element.69), channel_id=1, source_target_pairs={{0,4},{4,0},{8,12},{12,8},{1,5},{5,1},{9,13},{13,9},{2,6},{6,2},{1... | collective-permute-start | bytes 491528 | tf_op jit(solution)/shard_map/ppermute | solution.py:377
  59.6 10.3 %collective-permute-start.15 = (bf16[32,1536]{1,0:T(8,128)(2,1)S(1)}, bf16[32,1536]{1,0:T(8,128)(2,1)S(1)}, u32[]{:S(2)}, u32[]{:S(2)}) collective-permute-start(bf16[32,1536]{1,0:T(8,128)(2,1)S(1)} %get-tuple-element.77), channel_id=1, source_target_pairs={{0,8},{4,12},{8,0},{12,4},{1,9},{5,13},{9,1},{13,5},{2,10},{6,14},... | collective-permute-start | bytes 294920 | tf_op jit(solution)/shard_map/ppermute | solution.py:377
  61.9 9.1 %collective-permute-start.17 = (bf16[32,1536]{1,0:T(8,128)(2,1)S(1)}, bf16[32,1536]{1,0:T(8,128)(2,1)S(1)}, u32[]{:S(2)}, u32[]{:S(2)}) collective-permute-start(bf16[32,1536]{1,0:T(8,128)(2,1)S(1)} %get-tuple-element.79), channel_id=1, source_target_pairs={{0,12},{4,8},{8,4},{12,0},{1,13},{5,9},{9,5},{13,1},{2,14},{6,10},... | collective-permute-start | bytes 294920 | tf_op jit(solution)/shard_map/ppermute | solution.py:377
  64.9 12.7 %collective-permute-start.16 = (bf16[32,4096]{1,0:T(8,128)(2,1)S(1)}, bf16[32,4096]{1,0:T(8,128)(2,1)S(1)}, u32[]{:S(2)}, u32[]{:S(2)}) collective-permute-start(bf16[32,4096]{1,0:T(8,128)(2,1)S(1)} %get-tuple-element.78), channel_id=1, source_target_pairs={{0,4},{4,0},{8,12},{12,8},{1,5},{5,1},{9,13},{13,9},{2,6},{6,2},{1... | collective-permute-start | bytes 786440 | tf_op jit(solution)/shard_map/ppermute | solution.py:377
  66.5 11.3 %collective-permute-start.14 = (bf16[16,2560]{1,0:T(8,128)(2,1)S(1)}, bf16[16,2560]{1,0:T(8,128)(2,1)S(1)}, u32[]{:S(2)}, u32[]{:S(2)}) collective-permute-start(bf16[16,2560]{1,0:T(8,128)(2,1)S(1)} %get-tuple-element.87), channel_id=1, source_target_pairs={{0,8},{4,12},{8,0},{12,4},{1,9},{5,13},{9,1},{13,5},{2,10},{6,14},... | collective-permute-start | bytes 245768 | tf_op jit(solution)/shard_map/ppermute | solution.py:377
  69.9 8.4 %collective-permute-start.13 = (bf16[16,2560]{1,0:T(8,128)(2,1)S(1)}, bf16[16,2560]{1,0:T(8,128)(2,1)S(1)}, u32[]{:S(2)}, u32[]{:S(2)}) collective-permute-start(bf16[16,2560]{1,0:T(8,128)(2,1)S(1)} %get-tuple-element.88), channel_id=1, source_target_pairs={{0,9},{1,8},{4,13},{5,12},{8,1},{9,0},{12,5},{13,4},{2,11},{3,10},... | collective-permute-start | bytes 245768 | tf_op jit(solution)/shard_map/ppermute | solution.py:389
  77.7 1.4 %collective-permute-start.18 = (bf16[16,4096]{1,0:T(8,128)(2,1)S(1)}, bf16[16,4096]{1,0:T(8,128)(2,1)S(1)}, u32[]{:S(2)}, u32[]{:S(2)}) collective-permute-start(bf16[16,4096]{1,0:T(8,128)(2,1)S(1)} %pad_maximum_fusion.1), channel_id=1, source_target_pairs={{0,1},{1,0},{2,3},{3,2},{4,5},{5,4},{6,7},{7,6},{8,9},{9,8},{10,11... | collective-permute-start | bytes 393224 | tf_op jit(solution)/shard_map/ppermute | solution.py:381
  (1 other events, 0.7 us)

commit v10 on v8

--- a/solution.py
+++ b/solution.py
@@ -257,7 +257,7 @@
 
 
 def cut_of(width):
-    return width * 3 // 8 // HEAD_DIM * HEAD_DIM
+    return width // 2 // HEAD_DIM * HEAD_DIM
 
 
 def split_of(k, width):

time: 80.6 us -> 80.9 us (level)
  waiting for transfers between devices: 39.4 us -> 40.7 us
  starting transfers between devices: 20.2 us -> 19.2 us
    ppermute x11, waiting for transfers between devices: 35.9 us -> 37.2 us  [across(): return lax.ppermute(x, 'seq', [(i, i ^ stride) for i in range(n)])]
    ppermute x11, starting transfers between devices: 18.4 us -> 17.4 us  [across(): return lax.ppermute(x, 'seq', [(i, i ^ stride) for i in range(n)])]
where the time goes in v10:
time: 80.9 us; the launch traced here: 80.6 us
  waiting for transfers between devices  40.7 us (50%)
  starting transfers between devices  19.2 us (24%)
  Pallas kernels  16.2 us (20%)
  local copies, waits for them, and re-layouts  3.54 us (4%)
  between operations  0.83 us (1%)
    ppermute x11, waiting for transfers between devices, across(): return lax.ppermute(x, 'seq', [(i, i ^ stride) for i in range(n)])  37.2 us
    ppermute x11, starting transfers between devices, across(): return lax.ppermute(x, 'seq', [(i, i ^ stride) for i in range(n)])  17.4 us
    pallas_call x3, Pallas kernels, attention(): pl.pallas_call(functools.partial(kernel, tuple(origins), per_key, rows_tr...  8.19 us
    pallas_call x1, Pallas kernels, expert_call(): pl.pallas_call(functools.partial(expert_kernel, tuple(origins), tuple(ord...  6.39 us
    unnamed x14, local copies, waits for them, and re-layouts  3.52 us
    ppermute x7, waiting for transfers between devices, swap(): return lax.ppermute(x, 'tp', [(0, 1), (1, 0)])  3.49 us
    ppermute x7, starting transfers between devices, swap(): return lax.ppermute(x, 'tp', [(0, 1), (1, 0)])  1.78 us
  transfers between devices with their start and end apart: 19, of which 10 were waited for; matrix products, arithmetic and copies ran while one was open for 0% of the time, Pallas kernels for 11%

profile of v10, /device:TPU:0, one launch (start us, length us, event | category | flops | bytes accessed | tf_op | source)
XLA Modules:
  0.0 80.6 jit_solution(11019873140100697395)
XLA Ops:
  0.0 1.1 %copy.10 = bf16[12,8,2,1024]{3,1,2,0:T(8,128)(2,1)S(1)} copy(bf16[12,8,2,1024]{3,2,1,0:T(2,128)(2,1)} %bitcast.31) | data formatting | bytes 786432
  1.1 4.1 %collective-permute-start = (bf16[96,2048]{1,0:T(8,128)(2,1)S(1)}, bf16[96,2048]{1,0:T(8,128)(2,1)S(1)}, u32[]{:S(2)}, u32[]{:S(2)}) collective-permute-start(bf16[96,2048]{1,0:T(8,128)(2,1)S(1)} %bitcast.16), channel_id=1, source_target_pairs={{0,8},{4,12},{8,0},{12,4},{1,9},{5,13},{9,1},{13,5},{2,10},{6,14},... | collective-permute-start | bytes 1179656 | tf_op jit(solution)/shard_map/ppermute | solution.py:373
  5.2 1.6 %collective-permute-start.3 = (bf16[96,2048]{1,0:T(8,128)(2,1)S(1)}, bf16[96,2048]{1,0:T(8,128)(2,1)S(1)}, u32[]{:S(2)}, u32[]{:S(2)}) collective-permute-start(bf16[96,2048]{1,0:T(8,128)(2,1)S(1)} %bitcast.17), channel_id=1, source_target_pairs={{0,4},{4,0},{8,12},{12,8},{1,5},{5,1},{9,13},{13,9},{2,6},{6,2},{1... | collective-permute-start | bytes 1179656 | tf_op jit(solution)/shard_map/ppermute | solution.py:373
  6.8 1.0 %copy-done.1 = bf16[1,64,4096]{2,1,0:T(8,128)(2,1)S(1)} copy-done((bf16[1,64,4096]{2,1,0:T(8,128)(2,1)S(1)}, bf16[1,64,4096]{2,1,0:T(8,128)(2,1)}, u32[]{:S(2)}) %copy-start.1) | copy-done | bytes 524312
  7.8 0.7 copy-done.4
  10.1 1.0 %collective-permute-done.1 = bf16[16,4096]{1,0:T(8,128)(2,1)S(1)} collective-permute-done((bf16[16,4096]{1,0:T(8,128)(2,1)S(1)}, bf16[16,4096]{1,0:T(8,128)(2,1)S(1)}, u32[]{:S(2)}, u32[]{:S(2)}) %collective-permute-start.1) | collective-permute-done | bytes 131104 | tf_op jit(solution)/shard_map/ppermute | solution.py:377
  11.7 22.4 %collective-permute-done.2.refs_1_ = bf16[32,4096]{1,0:T(8,128)(2,1)S(1)} collective-permute-done((bf16[32,4096]{1,0:T(8,128)(2,1)S(1)}, bf16[32,4096]{1,0:T(8,128)(2,1)S(1)}, u32[]{:S(2)}, u32[]{:S(2)}) %collective-permute-start.2) | collective-permute-done | bytes 262176 | tf_op jit(solution)/shard_map/ppermute | solution.py:373
  34.9 1.5 %collective-permute-start.9 = (bf16[96,2048]{1,0:T(8,128)(2,1)S(1)}, bf16[96,2048]{1,0:T(8,128)(2,1)S(1)}, u32[]{:S(2)}, u32[]{:S(2)}) collective-permute-start(bf16[96,2048]{1,0:T(8,128)(2,1)S(1)} %collective-permute-done.refs_4_.refs_1_), channel_id=1, source_target_pairs={{0,4},{4,0},{8,12},{12,8},{1,5},{5,1},{9,13},{13,9},{2,6},{6,2},{1... | collective-permute-start | bytes 1179656 | tf_op jit(solution)/shard_map/ppermute | solution.py:373
  37.1 3.9 %begin.1 = (f32[3072,256]{1,0:T(8,128)S(1)}, f32[3072,128]{1,0:T(8,128)S(1)}, f32[8,128]{1,0:T(8,128)S(1)}) custom-call(s32[1]{0:T(128)S(6)} %copy.12.length_ref, bf16[32,4096]{1,0:T(8,128)(2,1)S(1)} %constant_dynamic-update-slice_fusion.refs_0_, bf16[32,4096]{1,0:T(8,128)(2,1)S(1)} %collective-permute-done.2.refs_1_, ...), custom_call_target="tpu_custom_call" | custom-call | flops 1 | bytes 1 | tf_op jit(solution)/shard_map/begin/pallas_call | solution.py:194
  41.0 1.2 %collective-permute-start.8 = (bf16[32,4096]{1,0:T(8,128)(2,1)S(1)}, bf16[32,4096]{1,0:T(8,128)(2,1)S(1)}, u32[]{:S(2)}, u32[]{:S(2)}) collective-permute-start(bf16[32,4096]{1,0:T(8,128)(2,1)S(1)} %collective-permute-done.2.refs_1_), channel_id=1, source_target_pairs={{0,4},{4,0},{8,12},{12,8},{1,5},{5,1},{9,13},{13,9},{2,6},{6,2},{1... | collective-permute-start | bytes 786440 | tf_op jit(solution)/shard_map/ppermute | solution.py:373
  42.1 4.7 %collective-permute-done.9.whole_ref.refs_3_.refs_6_ = bf16[96,2048]{1,0:T(8,128)(2,1)S(1)} collective-permute-done((bf16[96,2048]{1,0:T(8,128)(2,1)S(1)}, bf16[96,2048]{1,0:T(8,128)(2,1)S(1)}, u32[]{:S(2)}, u32[]{:S(2)}) %collective-permute-start.9) | collective-permute-done | bytes 393248 | tf_op jit(solution)/shard_map/ppermute | solution.py:373
  47.4 0.9 %collective-permute-done.10.refs_4_.refs_7_ = bf16[48,2048]{1,0:T(8,128)(2,1)S(1)} collective-permute-done((bf16[48,2048]{1,0:T(8,128)(2,1)S(1)}, bf16[48,2048]{1,0:T(8,128)(2,1)S(1)}, u32[]{:S(2)}, u32[]{:S(2)}) %collective-permute-start.10) | collective-permute-done | bytes 196640 | tf_op jit(solution)/shard_map/ppermute | solution.py:377
  48.7 1.9 %finish.1.done_ref = bf16[96,4096]{1,0:T(8,128)(2,1)S(1)} custom-call(s32[1]{0:T(128)S(6)} %copy.12.length_ref, bf16[32,4096]{1,0:T(8,128)(2,1)S(1)} %constant_dynamic-update-slice_fusion.refs_0_, bf16[32,4096]{1,0:T(8,128)(2,1)S(1)} %collective-permute-done.2.refs_1_, bf16[32,4096]{1,0:T(8,128)(2,1)S(1)} %collective-permute-done.5.refs_2_, ...), custom_call_target="tpu_custom_call" | custom-call | flops 1 | bytes 1 | tf_op jit(solution)/shard_map/finish/pallas_call | solution.py:194
  50.6 1.0 %collective-permute-done.8.last_ref = bf16[32,4096]{1,0:T(8,128)(2,1)S(1)} collective-permute-done((bf16[32,4096]{1,0:T(8,128)(2,1)S(1)}, bf16[32,4096]{1,0:T(8,128)(2,1)S(1)}, u32[]{:S(2)}, u32[]{:S(2)}) %collective-permute-start.8) | collective-permute-done | bytes 262176 | tf_op jit(solution)/shard_map/ppermute | solution.py:373
  51.6 6.4 %experts.1 = (bf16[32,4096]{1,0:T(8,128)(2,1)S(1)}, bf16[32,2048]{1,0:T(8,128)(2,1)S(1)}, bf16[32,2048]{1,0:T(8,128)(2,1)S(1)}, bf16[32,4096]{1,0:T(8,128)(2,1)S...) custom-call(bf16[32,4096]{1,0:T(8,128)(2,1)S(1)} %collective-permute-done.8.last_ref, ...), custom_call_target="tpu_custom_call" | custom-call | flops 1610612736 | bytes 12582912 | tf_op jit(solution)/shard_map/experts/pallas_call | solution.py:315
  58.0 1.6 %collective-permute-start.12 = (bf16[32,2048]{1,0:T(8,128)(2,1)S(1)}, bf16[32,2048]{1,0:T(8,128)(2,1)S(1)}, u32[]{:S(2)}, u32[]{:S(2)}) collective-permute-start(bf16[32,2048]{1,0:T(8,128)(2,1)S(1)} %get-tuple-element.69), channel_id=1, source_target_pairs={{0,4},{4,0},{8,12},{12,8},{1,5},{5,1},{9,13},{13,9},{2,6},{6,2},{1... | collective-permute-start | bytes 393224 | tf_op jit(solution)/shard_map/ppermute | solution.py:373
  59.6 2.3 %collective-permute-start.15 = (bf16[32,2048]{1,0:T(8,128)(2,1)S(1)}, bf16[32,2048]{1,0:T(8,128)(2,1)S(1)}, u32[]{:S(2)}, u32[]{:S(2)}) collective-permute-start(bf16[32,2048]{1,0:T(8,128)(2,1)S(1)} %get-tuple-element.77), channel_id=1, source_target_pairs={{0,8},{4,12},{8,0},{12,4},{1,9},{5,13},{9,1},{13,5},{2,10},{6,14},... | collective-permute-start | bytes 393224 | tf_op jit(solution)/shard_map/ppermute | solution.py:373
  62.4 2.4 %attend.1.attended_ref = bf16[64,4096]{1,0:T(8,128)(2,1)S(1)} custom-call(s32[1]{0:T(128)S(6)} %copy.12.length_ref, bf16[64,4096]{1,0:T(8,128)(2,1)S(1)} %bitcast.24, bf16[96,2048]{1,0:T(8,128)(2,1)S(1)} %bitcast.21, bf16[96,2048]{1,0:T(8,128)(2,1)S(1)} %collective-permute-done.refs_4_.refs_1_, bf16[96,2048]{1,0:T(8,128)(2,1)S(1)} %collective-permute-done.3.refs_5_.refs_2_, ...), custom_call_target="tpu_custom_call" | custom-call | flops 805306368 | bytes 4194304 | tf_op jit(solution)/shard_map/attend/pallas_call | solution.py:194
  64.9 0.9 %collective-permute-start.16 = (bf16[32,4096]{1,0:T(8,128)(2,1)S(1)}, bf16[32,4096]{1,0:T(8,128)(2,1)S(1)}, u32[]{:S(2)}, u32[]{:S(2)}) collective-permute-start(bf16[32,4096]{1,0:T(8,128)(2,1)S(1)} %get-tuple-element.78), channel_id=1, source_target_pairs={{0,4},{4,0},{8,12},{12,8},{1,5},{5,1},{9,13},{13,9},{2,6},{6,2},{1... | collective-permute-start | bytes 786440 | tf_op jit(solution)/shard_map/ppermute | solution.py:373
  65.8 3.1 %collective-permute-start.13 = (bf16[16,2048]{1,0:T(8,128)(2,1)S(1)}, bf16[16,2048]{1,0:T(8,128)(2,1)S(1)}, u32[]{:S(2)}, u32[]{:S(2)}) collective-permute-start(bf16[16,2048]{1,0:T(8,128)(2,1)S(1)} %get-tuple-element.88), channel_id=1, source_target_pairs={{0,8},{4,12},{8,0},{12,4},{1,9},{5,13},{9,1},{13,5},{2,10},{6,14},... | collective-permute-start | bytes 196616 | tf_op jit(solution)/shard_map/ppermute | solution.py:373
  68.9 3.2 %collective-permute-done.15 = bf16[32,2048]{1,0:T(8,128)(2,1)S(1)} collective-permute-done((bf16[32,2048]{1,0:T(8,128)(2,1)S(1)}, bf16[32,2048]{1,0:T(8,128)(2,1)S(1)}, u32[]{:S(2)}, u32[]{:S(2)}) %collective-permute-start.15) | collective-permute-done | bytes 131104 | tf_op jit(solution)/shard_map/ppermute | solution.py:373
  72.1 5.8 %collective-permute-done.16 = bf16[32,4096]{1,0:T(8,128)(2,1)S(1)} collective-permute-done((bf16[32,4096]{1,0:T(8,128)(2,1)S(1)}, bf16[32,4096]{1,0:T(8,128)(2,1)S(1)}, u32[]{:S(2)}, u32[]{:S(2)}) %collective-permute-start.16) | collective-permute-done | bytes 262176 | tf_op jit(solution)/shard_map/ppermute | solution.py:373
  78.1 1.3 %collective-permute-done.18.theirs_ref = bf16[16,4096]{1,0:T(8,128)(2,1)S(1)} collective-permute-done((bf16[16,4096]{1,0:T(8,128)(2,1)S(1)}, bf16[16,4096]{1,0:T(8,128)(2,1)S(1)}, u32[]{:S(2)}, u32[]{:S(2)}) %collective-permute-start.18) | collective-permute-done | bytes 131104 | tf_op jit(solution)/shard_map/ppermute | solution.py:377
  79.4 1.3 %combine.1 = bf16[64,4096]{1,0:T(8,128)(2,1)} custom-call(bf16[16,2048]{1,0:T(8,128)(2,1)S(1)} %collective-permute-done.13.late_ref, bf16[16,2048]{1,0:T(8,128)(2,1)S(1)} %collective-permute-done.14.late_theirs_ref, f32[32,64]{1,0:T(8,128)S(1)} %get-tuple-element.72.comb_ref, bf16[64,4096]{1,0:T(8,128)(2,1)S(1)} %attend.1.attended_ref, ...), custom_call_target="tpu_custom_call" | custom-call | flops 33554432 | bytes 1048576 | tf_op jit(solution)/shard_map/combine/pallas_call | solution.py:500
  (41 shorter events, 4.6 us)
Async XLA Ops:
  0.0 48.7 %copy-start.3 = (f32[4096]{0:T(1024)S(1)}, f32[4096]{0:T(1024)}, u32[]{:S(2)}) copy-start(f32[4096]{0:T(1024)} %param.14) | copy-start | bytes 49156
  1.1 33.2 %collective-permute-start = (bf16[96,2048]{1,0:T(8,128)(2,1)S(1)}, bf16[96,2048]{1,0:T(8,128)(2,1)S(1)}, u32[]{:S(2)}, u32[]{:S(2)}) collective-permute-start(bf16[96,2048]{1,0:T(8,128)(2,1)S(1)} %bitcast.16), channel_id=1, source_target_pairs={{0,8},{4,12},{8,0},{12,4},{1,9},{5,13},{9,1},{13,5},{2,10},{6,14},... | collective-permute-start | bytes 1179656 | tf_op jit(solution)/shard_map/ppermute | solution.py:373
  5.2 29.1 %collective-permute-start.3 = (bf16[96,2048]{1,0:T(8,128)(2,1)S(1)}, bf16[96,2048]{1,0:T(8,128)(2,1)S(1)}, u32[]{:S(2)}, u32[]{:S(2)}) collective-permute-start(bf16[96,2048]{1,0:T(8,128)(2,1)S(1)} %bitcast.17), channel_id=1, source_target_pairs={{0,4},{4,0},{8,12},{12,8},{1,5},{5,1},{9,13},{13,9},{2,6},{6,2},{1... | collective-permute-start | bytes 1179656 | tf_op jit(solution)/shard_map/ppermute | solution.py:373
  6.8 27.5 %collective-permute-start.4 = (bf16[96,2048]{1,0:T(8,128)(2,1)S(1)}, bf16[96,2048]{1,0:T(8,128)(2,1)S(1)}, u32[]{:S(2)}, u32[]{:S(2)}) collective-permute-start(bf16[96,2048]{1,0:T(8,128)(2,1)S(1)} %bitcast.18), channel_id=1, source_target_pairs={{0,1},{1,0},{2,3},{3,2},{4,5},{5,4},{6,7},{7,6},{8,9},{9,8},{10,11... | collective-permute-start | bytes 1179656 | tf_op jit(solution)/shard_map/ppermute | solution.py:377
  6.8 1.0 %copy-start.1 = (bf16[1,64,4096]{2,1,0:T(8,128)(2,1)S(1)}, bf16[1,64,4096]{2,1,0:T(8,128)(2,1)}, u32[]{:S(2)}) copy-start(bf16[1,64,4096]{2,1,0:T(8,128)(2,1)} %param.9) | copy-start | bytes 1572868
  8.5 0.7 copy-start.5
  9.5 1.6 %collective-permute-start.1 = (bf16[16,4096]{1,0:T(8,128)(2,1)S(1)}, bf16[16,4096]{1,0:T(8,128)(2,1)S(1)}, u32[]{:S(2)}, u32[]{:S(2)}) collective-permute-start(bf16[16,4096]{1,0:T(8,128)(2,1)S(1)} %get-tuple-element.45), channel_id=1, source_target_pairs={{0,1},{1,0},{2,3},{3,2},{4,5},{5,4},{6,7},{7,6},{8,9},{9,8},{10,11... | collective-permute-start | bytes 393224 | tf_op jit(solution)/shard_map/ppermute | solution.py:377
  11.1 23.0 %collective-permute-start.2 = (bf16[32,4096]{1,0:T(8,128)(2,1)S(1)}, bf16[32,4096]{1,0:T(8,128)(2,1)S(1)}, u32[]{:S(2)}, u32[]{:S(2)}) collective-permute-start(bf16[32,4096]{1,0:T(8,128)(2,1)S(1)} %constant_dynamic-update-slice_fusion.refs_0_), channel_id=1, source_target_pairs={{0,8},{4,12},{8,0},{12,4},{1,9},{5,13},{9,1},{13,5},{2,10},{6,14},... | collective-permute-start | bytes 786440 | tf_op jit(solution)/shard_map/ppermute | solution.py:373
  11.5 22.8 %collective-permute-start.5 = (bf16[32,4096]{1,0:T(8,128)(2,1)S(1)}, bf16[32,4096]{1,0:T(8,128)(2,1)S(1)}, u32[]{:S(2)}, u32[]{:S(2)}) collective-permute-start(bf16[32,4096]{1,0:T(8,128)(2,1)S(1)} %constant_dynamic-update-slice_fusion.refs_0_), channel_id=1, source_target_pairs={{0,4},{4,0},{8,12},{12,8},{1,5},{5,1},{9,13},{13,9},{2,6},{6,2},{1... | collective-permute-start | bytes 786440 | tf_op jit(solution)/shard_map/ppermute | solution.py:373
  34.3 2.8 %collective-permute-start.6 = (bf16[96,2048]{1,0:T(8,128)(2,1)S(1)}, bf16[96,2048]{1,0:T(8,128)(2,1)S(1)}, u32[]{:S(2)}, u32[]{:S(2)}) collective-permute-start(bf16[96,2048]{1,0:T(8,128)(2,1)S(1)} %collective-permute-done.refs_4_.refs_1_), channel_id=1, source_target_pairs={{0,1},{1,0},{2,3},{3,2},{4,5},{5,4},{6,7},{7,6},{8,9},{9,8},{10,11... | collective-permute-start | bytes 1179656 | tf_op jit(solution)/shard_map/ppermute | solution.py:377
  34.4 2.7 %collective-permute-start.7 = (bf16[96,2048]{1,0:T(8,128)(2,1)S(1)}, bf16[96,2048]{1,0:T(8,128)(2,1)S(1)}, u32[]{:S(2)}, u32[]{:S(2)}) collective-permute-start(bf16[96,2048]{1,0:T(8,128)(2,1)S(1)} %collective-permute-done.3.refs_5_.refs_2_), channel_id=1, source_target_pairs={{0,1},{1,0},{2,3},{3,2},{4,5},{5,4},{6,7},{7,6},{8,9},{9,8},{10,11... | collective-permute-start | bytes 1179656 | tf_op jit(solution)/shard_map/ppermute | solution.py:377
  34.9 12.0 %collective-permute-start.9 = (bf16[96,2048]{1,0:T(8,128)(2,1)S(1)}, bf16[96,2048]{1,0:T(8,128)(2,1)S(1)}, u32[]{:S(2)}, u32[]{:S(2)}) collective-permute-start(bf16[96,2048]{1,0:T(8,128)(2,1)S(1)} %collective-permute-done.refs_4_.refs_1_), channel_id=1, source_target_pairs={{0,4},{4,0},{8,12},{12,8},{1,5},{5,1},{9,13},{13,9},{2,6},{6,2},{1... | collective-permute-start | bytes 1179656 | tf_op jit(solution)/shard_map/ppermute | solution.py:373
  41.0 10.6 %copy-start = (bf16[1,4096,512]{2,1,0:T(8,128)(2,1)S(1)}, bf16[1,4096,512]{2,1,0:T(8,128)(2,1)}, u32[]{:S(2)}) copy-start(bf16[1,4096,512]{2,1,0:T(8,128)(2,1)} %param.15) | copy-start | bytes 12582916
  41.0 10.6 %collective-permute-start.8 = (bf16[32,4096]{1,0:T(8,128)(2,1)S(1)}, bf16[32,4096]{1,0:T(8,128)(2,1)S(1)}, u32[]{:S(2)}, u32[]{:S(2)}) collective-permute-start(bf16[32,4096]{1,0:T(8,128)(2,1)S(1)} %collective-permute-done.2.refs_1_), channel_id=1, source_target_pairs={{0,4},{4,0},{8,12},{12,8},{1,5},{5,1},{9,13},{13,9},{2,6},{6,2},{1... | collective-permute-start | bytes 786440 | tf_op jit(solution)/shard_map/ppermute | solution.py:373
  46.9 1.5 %collective-permute-start.10 = (bf16[48,2048]{1,0:T(8,128)(2,1)S(1)}, bf16[48,2048]{1,0:T(8,128)(2,1)S(1)}, u32[]{:S(2)}, u32[]{:S(2)}) collective-permute-start(bf16[48,2048]{1,0:T(8,128)(2,1)S(1)} %get-tuple-element.57), channel_id=1, source_target_pairs={{0,1},{1,0},{2,3},{3,2},{4,5},{5,4},{6,7},{7,6},{8,9},{9,8},{10,11... | collective-permute-start | bytes 589832 | tf_op jit(solution)/shard_map/ppermute | solution.py:377
  46.9 1.7 %collective-permute-start.11 = (bf16[48,2048]{1,0:T(8,128)(2,1)S(1)}, bf16[48,2048]{1,0:T(8,128)(2,1)S(1)}, u32[]{:S(2)}, u32[]{:S(2)}) collective-permute-start(bf16[48,2048]{1,0:T(8,128)(2,1)S(1)} %get-tuple-element.58), channel_id=1, source_target_pairs={{0,1},{1,0},{2,3},{3,2},{4,5},{5,4},{6,7},{7,6},{8,9},{9,8},{10,11... | collective-permute-start | bytes 589832 | tf_op jit(solution)/shard_map/ppermute | solution.py:377
  51.6 10.9 %copy-start.2 = (bf16[1,64,4096]{2,1,0:T(8,128)(2,1)S(1)}, bf16[1,64,4096]{2,1,0:T(8,128)(2,1)}, u32[]{:S(2)}) copy-start(bf16[1,64,4096]{2,1,0:T(8,128)(2,1)} %param.9) | copy-start | bytes 1572868
  58.0 6.8 %collective-permute-start.12 = (bf16[32,2048]{1,0:T(8,128)(2,1)S(1)}, bf16[32,2048]{1,0:T(8,128)(2,1)S(1)}, u32[]{:S(2)}, u32[]{:S(2)}) collective-permute-start(bf16[32,2048]{1,0:T(8,128)(2,1)S(1)} %get-tuple-element.69), channel_id=1, source_target_pairs={{0,4},{4,0},{8,12},{12,8},{1,5},{5,1},{9,13},{13,9},{2,6},{6,2},{1... | collective-permute-start | bytes 393224 | tf_op jit(solution)/shard_map/ppermute | solution.py:373
  59.6 12.5 %collective-permute-start.15 = (bf16[32,2048]{1,0:T(8,128)(2,1)S(1)}, bf16[32,2048]{1,0:T(8,128)(2,1)S(1)}, u32[]{:S(2)}, u32[]{:S(2)}) collective-permute-start(bf16[32,2048]{1,0:T(8,128)(2,1)S(1)} %get-tuple-element.77), channel_id=1, source_target_pairs={{0,8},{4,12},{8,0},{12,4},{1,9},{5,13},{9,1},{13,5},{2,10},{6,14},... | collective-permute-start | bytes 393224 | tf_op jit(solution)/shard_map/ppermute | solution.py:373
  61.9 10.2 %collective-permute-start.17 = (bf16[32,2048]{1,0:T(8,128)(2,1)S(1)}, bf16[32,2048]{1,0:T(8,128)(2,1)S(1)}, u32[]{:S(2)}, u32[]{:S(2)}) collective-permute-start(bf16[32,2048]{1,0:T(8,128)(2,1)S(1)} %get-tuple-element.79), channel_id=1, source_target_pairs={{0,12},{4,8},{8,4},{12,0},{1,13},{5,9},{9,5},{13,1},{2,14},{6,10},... | collective-permute-start | bytes 393224 | tf_op jit(solution)/shard_map/ppermute | solution.py:373
  64.9 13.0 %collective-permute-start.16 = (bf16[32,4096]{1,0:T(8,128)(2,1)S(1)}, bf16[32,4096]{1,0:T(8,128)(2,1)S(1)}, u32[]{:S(2)}, u32[]{:S(2)}) collective-permute-start(bf16[32,4096]{1,0:T(8,128)(2,1)S(1)} %get-tuple-element.78), channel_id=1, source_target_pairs={{0,4},{4,0},{8,12},{12,8},{1,5},{5,1},{9,13},{13,9},{2,6},{6,2},{1... | collective-permute-start | bytes 786440 | tf_op jit(solution)/shard_map/ppermute | solution.py:373
  65.8 12.3 %collective-permute-start.13 = (bf16[16,2048]{1,0:T(8,128)(2,1)S(1)}, bf16[16,2048]{1,0:T(8,128)(2,1)S(1)}, u32[]{:S(2)}, u32[]{:S(2)}) collective-permute-start(bf16[16,2048]{1,0:T(8,128)(2,1)S(1)} %get-tuple-element.88), channel_id=1, source_target_pairs={{0,8},{4,12},{8,0},{12,4},{1,9},{5,13},{9,1},{13,5},{2,10},{6,14},... | collective-permute-start | bytes 196616 | tf_op jit(solution)/shard_map/ppermute | solution.py:373
  68.9 9.2 %collective-permute-start.14 = (bf16[16,2048]{1,0:T(8,128)(2,1)S(1)}, bf16[16,2048]{1,0:T(8,128)(2,1)S(1)}, u32[]{:S(2)}, u32[]{:S(2)}) collective-permute-start(bf16[16,2048]{1,0:T(8,128)(2,1)S(1)} %get-tuple-element.87), channel_id=1, source_target_pairs={{0,9},{1,8},{4,13},{5,12},{8,1},{9,0},{12,5},{13,4},{2,11},{3,10},... | collective-permute-start | bytes 196616 | tf_op jit(solution)/shard_map/ppermute | solution.py:385
  78.0 1.4 %collective-permute-start.18 = (bf16[16,4096]{1,0:T(8,128)(2,1)S(1)}, bf16[16,4096]{1,0:T(8,128)(2,1)S(1)}, u32[]{:S(2)}, u32[]{:S(2)}) collective-permute-start(bf16[16,4096]{1,0:T(8,128)(2,1)S(1)} %pad_maximum_fusion.1), channel_id=1, source_target_pairs={{0,1},{1,0},{2,3},{3,2},{4,5},{5,4},{6,7},{7,6},{8,9},{9,8},{10,11... | collective-permute-start | bytes 393224 | tf_op jit(solution)/shard_map/ppermute | solution.py:377
  (1 other events, 0.7 us)

commit v11 on v8

--- a/solution.py
+++ b/solution.py
@@ -20,6 +20,7 @@
 VMEM = pl.BlockSpec(memory_space=pltpu.VMEM)
 SMEM = pl.BlockSpec(memory_space=pltpu.SMEM)
 HBM = pl.BlockSpec(memory_space=pltpu.HBM)
+ANY = pl.BlockSpec(memory_space=pl.ANY)
 
 
 def params(mib):
@@ -339,7 +340,7 @@
 
 
 def combine_kernel(
-    late_ref, late_theirs_ref, comb_ref, attended_ref, mine_ref, theirs_ref, out_ref
+    late_ref, late_theirs_ref, comb_ref, attended_ref, mine_ref, theirs_ref, out_hbm, out_ref, sems
 ):
     width = out_ref.shape[1]
     half = width - late_ref.shape[1]
@@ -347,6 +348,8 @@
     high = comb.astype(jnp.bfloat16)
     low = (comb - high.astype(jnp.float32)).astype(jnp.bfloat16)
     both = (((0,), (0,)), ((), ()))
+
+    copies = []
 
     def finish(rows, begin, end):
         rows = jnp.concatenate(rows, axis=0)
@@ -356,6 +359,13 @@
         out_ref[:, begin:end] = (
             attended_ref[:, begin:end].astype(jnp.float32) + added
         ).astype(jnp.bfloat16)
+        columns = pl.ds(begin, end - begin)
+        copies.append(
+            pltpu.make_async_copy(
+                out_ref.at[:, columns], out_hbm.at[:, columns], sems.at[len(copies)]
+            )
+        )
+        copies[-1].start()
 
     finish([mine_ref[:, :half], theirs_ref[:, :half]], 0, half)
     finish(
@@ -366,6 +376,8 @@
         half,
         width,
     )
+    for c in copies:
+        c.wait()
 
 
 def across(x, stride):
@@ -501,7 +513,11 @@
         combine_kernel,
         out_shape=jax.ShapeDtypeStruct((tokens, width), jnp.bfloat16),
         in_specs=[VMEM] * 6,
-        out_specs=VMEM,
+        out_specs=ANY,
+        scratch_shapes=[
+            pltpu.VMEM((tokens, width), jnp.bfloat16),
+            pltpu.SemaphoreType.DMA((2,)),
+        ],
         compiler_params=params(16),
         cost_estimate=cost(8 * CAP * tokens * width, 4 * tokens * width),
         name="combine",

time: 80.6 us -> 80.6 us (level)
  no operation moved by 1% of the time
where the time goes in v11:
time: 80.6 us; the launch traced here: 80.3 us
  waiting for transfers between devices  39.4 us (49%)
  starting transfers between devices  20.2 us (25%)
  Pallas kernels  16.1 us (20%)
  local copies, waits for them, and re-layouts  3.54 us (4%)
  between operations  0.83 us (1%)
    ppermute x11, waiting for transfers between devices, across(): return lax.ppermute(x, 'seq', [(i, i ^ stride) for i in range(n)])  35.9 us
    ppermute x11, starting transfers between devices, across(): return lax.ppermute(x, 'seq', [(i, i ^ stride) for i in range(n)])  18.4 us
    pallas_call x3, Pallas kernels, attention(): pl.pallas_call(functools.partial(kernel, tuple(origins), per_key, rows_tr...  8.19 us
    pallas_call x1, Pallas kernels, expert_call(): pl.pallas_call(functools.partial(expert_kernel, tuple(origins), tuple(ord...  6.39 us
    unnamed x14, local copies, waits for them, and re-layouts  3.52 us
    ppermute x7, waiting for transfers between devices, swap(): return lax.ppermute(x, 'tp', [(0, 1), (1, 0)])  3.49 us
    ppermute x7, starting transfers between devices, swap(): return lax.ppermute(x, 'tp', [(0, 1), (1, 0)])  1.78 us
  transfers between devices with their start and end apart: 19, of which 10 were waited for; matrix products, arithmetic and copies ran while one was open for 0% of the time, Pallas kernels for 11%

profile of v11, /device:TPU:0, one launch (start us, length us, event | category | flops | bytes accessed | tf_op | source)
XLA Modules:
  0.0 80.3 jit_solution(4187290301283913032)
XLA Ops:
  0.0 1.1 %copy.10 = bf16[12,8,2,1024]{3,1,2,0:T(8,128)(2,1)S(1)} copy(bf16[12,8,2,1024]{3,2,1,0:T(2,128)(2,1)} %bitcast.31) | data formatting | bytes 786432
  1.1 4.1 %collective-permute-start = (bf16[96,2048]{1,0:T(8,128)(2,1)S(1)}, bf16[96,2048]{1,0:T(8,128)(2,1)S(1)}, u32[]{:S(2)}, u32[]{:S(2)}) collective-permute-start(bf16[96,2048]{1,0:T(8,128)(2,1)S(1)} %bitcast.16), channel_id=1, source_target_pairs={{0,8},{4,12},{8,0},{12,4},{1,9},{5,13},{9,1},{13,5},{2,10},{6,14},... | collective-permute-start | bytes 1179656 | tf_op jit(solution)/shard_map/ppermute | solution.py:385
  5.2 1.6 %collective-permute-start.3 = (bf16[96,2048]{1,0:T(8,128)(2,1)S(1)}, bf16[96,2048]{1,0:T(8,128)(2,1)S(1)}, u32[]{:S(2)}, u32[]{:S(2)}) collective-permute-start(bf16[96,2048]{1,0:T(8,128)(2,1)S(1)} %bitcast.17), channel_id=1, source_target_pairs={{0,4},{4,0},{8,12},{12,8},{1,5},{5,1},{9,13},{13,9},{2,6},{6,2},{1... | collective-permute-start | bytes 1179656 | tf_op jit(solution)/shard_map/ppermute | solution.py:385
  6.8 1.0 %copy-done.1 = bf16[1,64,4096]{2,1,0:T(8,128)(2,1)S(1)} copy-done((bf16[1,64,4096]{2,1,0:T(8,128)(2,1)S(1)}, bf16[1,64,4096]{2,1,0:T(8,128)(2,1)}, u32[]{:S(2)}) %copy-start.1) | copy-done | bytes 524312
  7.8 0.7 copy-done.4
  10.1 1.0 %collective-permute-done.1 = bf16[16,4096]{1,0:T(8,128)(2,1)S(1)} collective-permute-done((bf16[16,4096]{1,0:T(8,128)(2,1)S(1)}, bf16[16,4096]{1,0:T(8,128)(2,1)S(1)}, u32[]{:S(2)}, u32[]{:S(2)}) %collective-permute-start.1) | collective-permute-done | bytes 131104 | tf_op jit(solution)/shard_map/ppermute | solution.py:389
  11.7 22.4 %collective-permute-done.2.refs_1_ = bf16[32,4096]{1,0:T(8,128)(2,1)S(1)} collective-permute-done((bf16[32,4096]{1,0:T(8,128)(2,1)S(1)}, bf16[32,4096]{1,0:T(8,128)(2,1)S(1)}, u32[]{:S(2)}, u32[]{:S(2)}) %collective-permute-start.2) | collective-permute-done | bytes 262176 | tf_op jit(solution)/shard_map/ppermute | solution.py:385
  34.9 1.5 %collective-permute-start.9 = (bf16[96,2048]{1,0:T(8,128)(2,1)S(1)}, bf16[96,2048]{1,0:T(8,128)(2,1)S(1)}, u32[]{:S(2)}, u32[]{:S(2)}) collective-permute-start(bf16[96,2048]{1,0:T(8,128)(2,1)S(1)} %collective-permute-done.refs_4_.refs_1_), channel_id=1, source_target_pairs={{0,4},{4,0},{8,12},{12,8},{1,5},{5,1},{9,13},{13,9},{2,6},{6,2},{1... | collective-permute-start | bytes 1179656 | tf_op jit(solution)/shard_map/ppermute | solution.py:385
  37.1 3.9 %begin.1 = (f32[3072,256]{1,0:T(8,128)S(1)}, f32[3072,128]{1,0:T(8,128)S(1)}, f32[8,128]{1,0:T(8,128)S(1)}) custom-call(s32[1]{0:T(128)S(6)} %copy.12.length_ref, bf16[32,4096]{1,0:T(8,128)(2,1)S(1)} %constant_dynamic-update-slice_fusion.refs_0_, bf16[32,4096]{1,0:T(8,128)(2,1)S(1)} %collective-permute-done.2.refs_1_, ...), custom_call_target="tpu_custom_call" | custom-call | flops 1 | bytes 1 | tf_op jit(solution)/shard_map/begin/pallas_call | solution.py:195
  41.0 1.2 %collective-permute-start.8 = (bf16[32,4096]{1,0:T(8,128)(2,1)S(1)}, bf16[32,4096]{1,0:T(8,128)(2,1)S(1)}, u32[]{:S(2)}, u32[]{:S(2)}) collective-permute-start(bf16[32,4096]{1,0:T(8,128)(2,1)S(1)} %collective-permute-done.2.refs_1_), channel_id=1, source_target_pairs={{0,4},{4,0},{8,12},{12,8},{1,5},{5,1},{9,13},{13,9},{2,6},{6,2},{1... | collective-permute-start | bytes 786440 | tf_op jit(solution)/shard_map/ppermute | solution.py:385
  42.1 4.7 %collective-permute-done.9.whole_ref.refs_3_.refs_6_ = bf16[96,2048]{1,0:T(8,128)(2,1)S(1)} collective-permute-done((bf16[96,2048]{1,0:T(8,128)(2,1)S(1)}, bf16[96,2048]{1,0:T(8,128)(2,1)S(1)}, u32[]{:S(2)}, u32[]{:S(2)}) %collective-permute-start.9) | collective-permute-done | bytes 393248 | tf_op jit(solution)/shard_map/ppermute | solution.py:385
  47.4 0.9 %collective-permute-done.10.refs_4_.refs_7_ = bf16[48,2048]{1,0:T(8,128)(2,1)S(1)} collective-permute-done((bf16[48,2048]{1,0:T(8,128)(2,1)S(1)}, bf16[48,2048]{1,0:T(8,128)(2,1)S(1)}, u32[]{:S(2)}, u32[]{:S(2)}) %collective-permute-start.10) | collective-permute-done | bytes 196640 | tf_op jit(solution)/shard_map/ppermute | solution.py:389
  48.7 1.9 %finish.1.done_ref = bf16[96,4096]{1,0:T(8,128)(2,1)S(1)} custom-call(s32[1]{0:T(128)S(6)} %copy.12.length_ref, bf16[32,4096]{1,0:T(8,128)(2,1)S(1)} %constant_dynamic-update-slice_fusion.refs_0_, bf16[32,4096]{1,0:T(8,128)(2,1)S(1)} %collective-permute-done.2.refs_1_, bf16[32,4096]{1,0:T(8,128)(2,1)S(1)} %collective-permute-done.5.refs_2_, ...), custom_call_target="tpu_custom_call" | custom-call | flops 1 | bytes 1 | tf_op jit(solution)/shard_map/finish/pallas_call | solution.py:195
  50.6 1.0 %collective-permute-done.8.last_ref = bf16[32,4096]{1,0:T(8,128)(2,1)S(1)} collective-permute-done((bf16[32,4096]{1,0:T(8,128)(2,1)S(1)}, bf16[32,4096]{1,0:T(8,128)(2,1)S(1)}, u32[]{:S(2)}, u32[]{:S(2)}) %collective-permute-start.8) | collective-permute-done | bytes 262176 | tf_op jit(solution)/shard_map/ppermute | solution.py:385
  51.6 6.4 %experts.1 = (bf16[32,4096]{1,0:T(8,128)(2,1)S(1)}, bf16[32,1536]{1,0:T(8,128)(2,1)S(1)}, bf16[32,2560]{1,0:T(8,128)(2,1)S(1)}, bf16[32,4096]{1,0:T(8,128)(2,1)S...) custom-call(bf16[32,4096]{1,0:T(8,128)(2,1)S(1)} %collective-permute-done.8.last_ref, ...), custom_call_target="tpu_custom_call" | custom-call | flops 1610612736 | bytes 12582912 | tf_op jit(solution)/shard_map/experts/pallas_call | solution.py:316
  58.0 1.6 %collective-permute-start.12 = (bf16[32,2560]{1,0:T(8,128)(2,1)S(1)}, bf16[32,2560]{1,0:T(8,128)(2,1)S(1)}, u32[]{:S(2)}, u32[]{:S(2)}) collective-permute-start(bf16[32,2560]{1,0:T(8,128)(2,1)S(1)} %get-tuple-element.69), channel_id=1, source_target_pairs={{0,4},{4,0},{8,12},{12,8},{1,5},{5,1},{9,13},{13,9},{2,6},{6,2},{1... | collective-permute-start | bytes 491528 | tf_op jit(solution)/shard_map/ppermute | solution.py:385
  59.6 2.3 %collective-permute-start.15 = (bf16[32,1536]{1,0:T(8,128)(2,1)S(1)}, bf16[32,1536]{1,0:T(8,128)(2,1)S(1)}, u32[]{:S(2)}, u32[]{:S(2)}) collective-permute-start(bf16[32,1536]{1,0:T(8,128)(2,1)S(1)} %get-tuple-element.77), channel_id=1, source_target_pairs={{0,8},{4,12},{8,0},{12,4},{1,9},{5,13},{9,1},{13,5},{2,10},{6,14},... | collective-permute-start | bytes 294920 | tf_op jit(solution)/shard_map/ppermute | solution.py:385
  62.4 2.4 %attend.1.attended_ref = bf16[64,4096]{1,0:T(8,128)(2,1)S(1)} custom-call(s32[1]{0:T(128)S(6)} %copy.12.length_ref, bf16[64,4096]{1,0:T(8,128)(2,1)S(1)} %bitcast.24, bf16[96,2048]{1,0:T(8,128)(2,1)S(1)} %bitcast.21, bf16[96,2048]{1,0:T(8,128)(2,1)S(1)} %collective-permute-done.refs_4_.refs_1_, bf16[96,2048]{1,0:T(8,128)(2,1)S(1)} %collective-permute-done.3.refs_5_.refs_2_, ...), custom_call_target="tpu_custom_call" | custom-call | flops 805306368 | bytes 4194304 | tf_op jit(solution)/shard_map/attend/pallas_call | solution.py:195
  64.9 1.7 %collective-permute-start.16 = (bf16[32,4096]{1,0:T(8,128)(2,1)S(1)}, bf16[32,4096]{1,0:T(8,128)(2,1)S(1)}, u32[]{:S(2)}, u32[]{:S(2)}) collective-permute-start(bf16[32,4096]{1,0:T(8,128)(2,1)S(1)} %get-tuple-element.78), channel_id=1, source_target_pairs={{0,4},{4,0},{8,12},{12,8},{1,5},{5,1},{9,13},{13,9},{2,6},{6,2},{1... | collective-permute-start | bytes 786440 | tf_op jit(solution)/shard_map/ppermute | solution.py:385
  66.5 3.4 %collective-permute-start.13 = (bf16[16,2560]{1,0:T(8,128)(2,1)S(1)}, bf16[16,2560]{1,0:T(8,128)(2,1)S(1)}, u32[]{:S(2)}, u32[]{:S(2)}) collective-permute-start(bf16[16,2560]{1,0:T(8,128)(2,1)S(1)} %get-tuple-element.88), channel_id=1, source_target_pairs={{0,8},{4,12},{8,0},{12,4},{1,9},{5,13},{9,1},{13,5},{2,10},{6,14},... | collective-permute-start | bytes 245768 | tf_op jit(solution)/shard_map/ppermute | solution.py:385
  69.9 1.1 %collective-permute-done.17 = bf16[32,1536]{1,0:T(8,128)(2,1)S(1)} collective-permute-done((bf16[32,1536]{1,0:T(8,128)(2,1)S(1)}, bf16[32,1536]{1,0:T(8,128)(2,1)S(1)}, u32[]{:S(2)}, u32[]{:S(2)}) %collective-permute-start.17) | collective-permute-done | bytes 98336 | tf_op jit(solution)/shard_map/ppermute | solution.py:385
  71.0 6.6 %collective-permute-done.16 = bf16[32,4096]{1,0:T(8,128)(2,1)S(1)} collective-permute-done((bf16[32,4096]{1,0:T(8,128)(2,1)S(1)}, bf16[32,4096]{1,0:T(8,128)(2,1)S(1)}, u32[]{:S(2)}, u32[]{:S(2)}) %collective-permute-start.16) | collective-permute-done | bytes 262176 | tf_op jit(solution)/shard_map/ppermute | solution.py:385
  77.9 1.3 %collective-permute-done.18.theirs_ref = bf16[16,4096]{1,0:T(8,128)(2,1)S(1)} collective-permute-done((bf16[16,4096]{1,0:T(8,128)(2,1)S(1)}, bf16[16,4096]{1,0:T(8,128)(2,1)S(1)}, u32[]{:S(2)}, u32[]{:S(2)}) %collective-permute-start.18) | collective-permute-done | bytes 131104 | tf_op jit(solution)/shard_map/ppermute | solution.py:389
  79.1 1.2 %combine.1 = bf16[64,4096]{1,0:T(8,128)(2,1)} custom-call(bf16[16,2560]{1,0:T(8,128)(2,1)S(1)} %collective-permute-done.13.late_ref, bf16[16,2560]{1,0:T(8,128)(2,1)S(1)} %collective-permute-done.14.late_theirs_ref, f32[32,64]{1,0:T(8,128)S(1)} %get-tuple-element.72.comb_ref, bf16[64,4096]{1,0:T(8,128)(2,1)S(1)} %attend.1.attended_ref, ...), custom_call_target="tpu_custom_call" | custom-call | flops 33554432 | bytes 1048576 | tf_op jit(solution)/shard_map/combine/pallas_call | solution.py:512
  (42 shorter events, 4.6 us)
Async XLA Ops:
  0.0 48.7 %copy-start.3 = (f32[4096]{0:T(1024)S(1)}, f32[4096]{0:T(1024)}, u32[]{:S(2)}) copy-start(f32[4096]{0:T(1024)} %param.14) | copy-start | bytes 49156
  1.1 33.2 %collective-permute-start = (bf16[96,2048]{1,0:T(8,128)(2,1)S(1)}, bf16[96,2048]{1,0:T(8,128)(2,1)S(1)}, u32[]{:S(2)}, u32[]{:S(2)}) collective-permute-start(bf16[96,2048]{1,0:T(8,128)(2,1)S(1)} %bitcast.16), channel_id=1, source_target_pairs={{0,8},{4,12},{8,0},{12,4},{1,9},{5,13},{9,1},{13,5},{2,10},{6,14},... | collective-permute-start | bytes 1179656 | tf_op jit(solution)/shard_map/ppermute | solution.py:385
  5.2 29.1 %collective-permute-start.3 = (bf16[96,2048]{1,0:T(8,128)(2,1)S(1)}, bf16[96,2048]{1,0:T(8,128)(2,1)S(1)}, u32[]{:S(2)}, u32[]{:S(2)}) collective-permute-start(bf16[96,2048]{1,0:T(8,128)(2,1)S(1)} %bitcast.17), channel_id=1, source_target_pairs={{0,4},{4,0},{8,12},{12,8},{1,5},{5,1},{9,13},{13,9},{2,6},{6,2},{1... | collective-permute-start | bytes 1179656 | tf_op jit(solution)/shard_map/ppermute | solution.py:385
  6.8 27.5 %collective-permute-start.4 = (bf16[96,2048]{1,0:T(8,128)(2,1)S(1)}, bf16[96,2048]{1,0:T(8,128)(2,1)S(1)}, u32[]{:S(2)}, u32[]{:S(2)}) collective-permute-start(bf16[96,2048]{1,0:T(8,128)(2,1)S(1)} %bitcast.18), channel_id=1, source_target_pairs={{0,1},{1,0},{2,3},{3,2},{4,5},{5,4},{6,7},{7,6},{8,9},{9,8},{10,11... | collective-permute-start | bytes 1179656 | tf_op jit(solution)/shard_map/ppermute | solution.py:389
  6.8 1.0 %copy-start.1 = (bf16[1,64,4096]{2,1,0:T(8,128)(2,1)S(1)}, bf16[1,64,4096]{2,1,0:T(8,128)(2,1)}, u32[]{:S(2)}) copy-start(bf16[1,64,4096]{2,1,0:T(8,128)(2,1)} %param.9) | copy-start | bytes 1572868
  7.8 0.7 copy-start.4
  9.5 1.6 %collective-permute-start.1 = (bf16[16,4096]{1,0:T(8,128)(2,1)S(1)}, bf16[16,4096]{1,0:T(8,128)(2,1)S(1)}, u32[]{:S(2)}, u32[]{:S(2)}) collective-permute-start(bf16[16,4096]{1,0:T(8,128)(2,1)S(1)} %get-tuple-element.45), channel_id=1, source_target_pairs={{0,1},{1,0},{2,3},{3,2},{4,5},{5,4},{6,7},{7,6},{8,9},{9,8},{10,11... | collective-permute-start | bytes 393224 | tf_op jit(solution)/shard_map/ppermute | solution.py:389
  11.1 23.0 %collective-permute-start.2 = (bf16[32,4096]{1,0:T(8,128)(2,1)S(1)}, bf16[32,4096]{1,0:T(8,128)(2,1)S(1)}, u32[]{:S(2)}, u32[]{:S(2)}) collective-permute-start(bf16[32,4096]{1,0:T(8,128)(2,1)S(1)} %constant_dynamic-update-slice_fusion.refs_0_), channel_id=1, source_target_pairs={{0,8},{4,12},{8,0},{12,4},{1,9},{5,13},{9,1},{13,5},{2,10},{6,14},... | collective-permute-start | bytes 786440 | tf_op jit(solution)/shard_map/ppermute | solution.py:385
  11.5 22.8 %collective-permute-start.5 = (bf16[32,4096]{1,0:T(8,128)(2,1)S(1)}, bf16[32,4096]{1,0:T(8,128)(2,1)S(1)}, u32[]{:S(2)}, u32[]{:S(2)}) collective-permute-start(bf16[32,4096]{1,0:T(8,128)(2,1)S(1)} %constant_dynamic-update-slice_fusion.refs_0_), channel_id=1, source_target_pairs={{0,4},{4,0},{8,12},{12,8},{1,5},{5,1},{9,13},{13,9},{2,6},{6,2},{1... | collective-permute-start | bytes 786440 | tf_op jit(solution)/shard_map/ppermute | solution.py:385
  34.3 2.8 %collective-permute-start.6 = (bf16[96,2048]{1,0:T(8,128)(2,1)S(1)}, bf16[96,2048]{1,0:T(8,128)(2,1)S(1)}, u32[]{:S(2)}, u32[]{:S(2)}) collective-permute-start(bf16[96,2048]{1,0:T(8,128)(2,1)S(1)} %collective-permute-done.refs_4_.refs_1_), channel_id=1, source_target_pairs={{0,1},{1,0},{2,3},{3,2},{4,5},{5,4},{6,7},{7,6},{8,9},{9,8},{10,11... | collective-permute-start | bytes 1179656 | tf_op jit(solution)/shard_map/ppermute | solution.py:389
  34.4 2.7 %collective-permute-start.7 = (bf16[96,2048]{1,0:T(8,128)(2,1)S(1)}, bf16[96,2048]{1,0:T(8,128)(2,1)S(1)}, u32[]{:S(2)}, u32[]{:S(2)}) collective-permute-start(bf16[96,2048]{1,0:T(8,128)(2,1)S(1)} %collective-permute-done.3.refs_5_.refs_2_), channel_id=1, source_target_pairs={{0,1},{1,0},{2,3},{3,2},{4,5},{5,4},{6,7},{7,6},{8,9},{9,8},{10,11... | collective-permute-start | bytes 1179656 | tf_op jit(solution)/shard_map/ppermute | solution.py:389
  34.9 12.0 %collective-permute-start.9 = (bf16[96,2048]{1,0:T(8,128)(2,1)S(1)}, bf16[96,2048]{1,0:T(8,128)(2,1)S(1)}, u32[]{:S(2)}, u32[]{:S(2)}) collective-permute-start(bf16[96,2048]{1,0:T(8,128)(2,1)S(1)} %collective-permute-done.refs_4_.refs_1_), channel_id=1, source_target_pairs={{0,4},{4,0},{8,12},{12,8},{1,5},{5,1},{9,13},{13,9},{2,6},{6,2},{1... | collective-permute-start | bytes 1179656 | tf_op jit(solution)/shard_map/ppermute | solution.py:385
  41.0 10.6 %copy-start = (bf16[1,4096,512]{2,1,0:T(8,128)(2,1)S(1)}, bf16[1,4096,512]{2,1,0:T(8,128)(2,1)}, u32[]{:S(2)}) copy-start(bf16[1,4096,512]{2,1,0:T(8,128)(2,1)} %param.15) | copy-start | bytes 12582916
  41.0 10.6 %collective-permute-start.8 = (bf16[32,4096]{1,0:T(8,128)(2,1)S(1)}, bf16[32,4096]{1,0:T(8,128)(2,1)S(1)}, u32[]{:S(2)}, u32[]{:S(2)}) collective-permute-start(bf16[32,4096]{1,0:T(8,128)(2,1)S(1)} %collective-permute-done.2.refs_1_), channel_id=1, source_target_pairs={{0,4},{4,0},{8,12},{12,8},{1,5},{5,1},{9,13},{13,9},{2,6},{6,2},{1... | collective-permute-start | bytes 786440 | tf_op jit(solution)/shard_map/ppermute | solution.py:385
  46.9 1.5 %collective-permute-start.10 = (bf16[48,2048]{1,0:T(8,128)(2,1)S(1)}, bf16[48,2048]{1,0:T(8,128)(2,1)S(1)}, u32[]{:S(2)}, u32[]{:S(2)}) collective-permute-start(bf16[48,2048]{1,0:T(8,128)(2,1)S(1)} %get-tuple-element.57), channel_id=1, source_target_pairs={{0,1},{1,0},{2,3},{3,2},{4,5},{5,4},{6,7},{7,6},{8,9},{9,8},{10,11... | collective-permute-start | bytes 589832 | tf_op jit(solution)/shard_map/ppermute | solution.py:389
  46.9 1.7 %collective-permute-start.11 = (bf16[48,2048]{1,0:T(8,128)(2,1)S(1)}, bf16[48,2048]{1,0:T(8,128)(2,1)S(1)}, u32[]{:S(2)}, u32[]{:S(2)}) collective-permute-start(bf16[48,2048]{1,0:T(8,128)(2,1)S(1)} %get-tuple-element.58), channel_id=1, source_target_pairs={{0,1},{1,0},{2,3},{3,2},{4,5},{5,4},{6,7},{7,6},{8,9},{9,8},{10,11... | collective-permute-start | bytes 589832 | tf_op jit(solution)/shard_map/ppermute | solution.py:389
  51.6 10.9 %copy-start.2 = (bf16[1,64,4096]{2,1,0:T(8,128)(2,1)S(1)}, bf16[1,64,4096]{2,1,0:T(8,128)(2,1)}, u32[]{:S(2)}) copy-start(bf16[1,64,4096]{2,1,0:T(8,128)(2,1)} %param.9) | copy-start | bytes 1572868
  58.0 6.8 %collective-permute-start.12 = (bf16[32,2560]{1,0:T(8,128)(2,1)S(1)}, bf16[32,2560]{1,0:T(8,128)(2,1)S(1)}, u32[]{:S(2)}, u32[]{:S(2)}) collective-permute-start(bf16[32,2560]{1,0:T(8,128)(2,1)S(1)} %get-tuple-element.69), channel_id=1, source_target_pairs={{0,4},{4,0},{8,12},{12,8},{1,5},{5,1},{9,13},{13,9},{2,6},{6,2},{1... | collective-permute-start | bytes 491528 | tf_op jit(solution)/shard_map/ppermute | solution.py:385
  59.6 10.3 %collective-permute-start.15 = (bf16[32,1536]{1,0:T(8,128)(2,1)S(1)}, bf16[32,1536]{1,0:T(8,128)(2,1)S(1)}, u32[]{:S(2)}, u32[]{:S(2)}) collective-permute-start(bf16[32,1536]{1,0:T(8,128)(2,1)S(1)} %get-tuple-element.77), channel_id=1, source_target_pairs={{0,8},{4,12},{8,0},{12,4},{1,9},{5,13},{9,1},{13,5},{2,10},{6,14},... | collective-permute-start | bytes 294920 | tf_op jit(solution)/shard_map/ppermute | solution.py:385
  61.9 9.1 %collective-permute-start.17 = (bf16[32,1536]{1,0:T(8,128)(2,1)S(1)}, bf16[32,1536]{1,0:T(8,128)(2,1)S(1)}, u32[]{:S(2)}, u32[]{:S(2)}) collective-permute-start(bf16[32,1536]{1,0:T(8,128)(2,1)S(1)} %get-tuple-element.79), channel_id=1, source_target_pairs={{0,12},{4,8},{8,4},{12,0},{1,13},{5,9},{9,5},{13,1},{2,14},{6,10},... | collective-permute-start | bytes 294920 | tf_op jit(solution)/shard_map/ppermute | solution.py:385
  64.9 12.7 %collective-permute-start.16 = (bf16[32,4096]{1,0:T(8,128)(2,1)S(1)}, bf16[32,4096]{1,0:T(8,128)(2,1)S(1)}, u32[]{:S(2)}, u32[]{:S(2)}) collective-permute-start(bf16[32,4096]{1,0:T(8,128)(2,1)S(1)} %get-tuple-element.78), channel_id=1, source_target_pairs={{0,4},{4,0},{8,12},{12,8},{1,5},{5,1},{9,13},{13,9},{2,6},{6,2},{1... | collective-permute-start | bytes 786440 | tf_op jit(solution)/shard_map/ppermute | solution.py:385
  66.5 11.3 %collective-permute-start.13 = (bf16[16,2560]{1,0:T(8,128)(2,1)S(1)}, bf16[16,2560]{1,0:T(8,128)(2,1)S(1)}, u32[]{:S(2)}, u32[]{:S(2)}) collective-permute-start(bf16[16,2560]{1,0:T(8,128)(2,1)S(1)} %get-tuple-element.88), channel_id=1, source_target_pairs={{0,8},{4,12},{8,0},{12,4},{1,9},{5,13},{9,1},{13,5},{2,10},{6,14},... | collective-permute-start | bytes 245768 | tf_op jit(solution)/shard_map/ppermute | solution.py:385
  69.9 7.9 %collective-permute-start.14 = (bf16[16,2560]{1,0:T(8,128)(2,1)S(1)}, bf16[16,2560]{1,0:T(8,128)(2,1)S(1)}, u32[]{:S(2)}, u32[]{:S(2)}) collective-permute-start(bf16[16,2560]{1,0:T(8,128)(2,1)S(1)} %get-tuple-element.87), channel_id=1, source_target_pairs={{0,9},{1,8},{4,13},{5,12},{8,1},{9,0},{12,5},{13,4},{2,11},{3,10},... | collective-permute-start | bytes 245768 | tf_op jit(solution)/shard_map/ppermute | solution.py:397
  77.7 1.4 %collective-permute-start.18 = (bf16[16,4096]{1,0:T(8,128)(2,1)S(1)}, bf16[16,4096]{1,0:T(8,128)(2,1)S(1)}, u32[]{:S(2)}, u32[]{:S(2)}) collective-permute-start(bf16[16,4096]{1,0:T(8,128)(2,1)S(1)} %pad_maximum_fusion.1), channel_id=1, source_target_pairs={{0,1},{1,0},{2,3},{3,2},{4,5},{5,4},{6,7},{7,6},{8,9},{9,8},{10,11... | collective-permute-start | bytes 393224 | tf_op jit(solution)/shard_map/ppermute | solution.py:389
  (1 other events, 0.7 us)

commit v12 on v11

--- a/solution.py
+++ b/solution.py
@@ -270,13 +270,13 @@
 ):
     pieces = len(origins)
     kv_refs = refs[:pieces]
-    gain_ref, gate_ref, up_hbm, down_hbm = refs[pieces : pieces + 4]
-    out_refs = refs[pieces + 4 : -4]
-    x_ref, up_ref, down_ref, sems = refs[-4:]
+    gain_ref, gate_ref, up_ref, down_hbm = refs[pieces : pieces + 4]
+    out_refs = refs[pieces + 4 : -3]
+    x_ref, down_ref, sems = refs[-3:]
     copies = [
         pltpu.make_async_copy(src, dst, sems.at[i])
         for i, (src, dst) in enumerate(
-            ((up_hbm, up_ref), (down_hbm, down_ref))
+            ((down_hbm, down_ref),)
         )
     ]
     for c in copies:
@@ -286,10 +286,9 @@
     last = attended_rows(columns_of([last_ref]), kv_refs, bias, x_ref, per_key)
     normed = jnp.concatenate([done_ref[...], norm(last, gain_ref[...])], axis=0)
     gate = jnp.dot(normed, gate_ref[...], preferred_element_type=jnp.float32)
-    copies[0].wait()
     up = jnp.dot(normed, up_ref[...], preferred_element_type=jnp.float32)
     hidden = (gate / (1.0 + jnp.exp(-gate)) * up).astype(jnp.bfloat16)
-    copies[1].wait()
+    copies[0].wait()
     part = jnp.dot(hidden, down_ref[...], preferred_element_type=jnp.float32).astype(
         jnp.bfloat16
     )
@@ -316,11 +315,10 @@
         pl.pallas_call(
             functools.partial(expert_kernel, tuple(origins), tuple(order), per_key, rows_true),
             out_shape=shapes,
-            in_specs=[VMEM, SMEM] + [VMEM] * (3 + len(kv_pieces)) + [HBM] * 2,
+            in_specs=[VMEM, SMEM] + [VMEM] * (4 + len(kv_pieces)) + [HBM],
             out_specs=[VMEM] * len(shapes),
             scratch_shapes=[
                 pltpu.VMEM((each, width), jnp.bfloat16),
-                pltpu.VMEM(w_up.shape, jnp.bfloat16),
                 pltpu.VMEM(w_down.shape, jnp.bfloat16),
                 pltpu.SemaphoreType.DMA((2,)),
             ],
@@ -472,7 +470,7 @@
     gain = norm_gain.reshape(1, width)
     done = finish_call(length, early, last_pieces, rows_true, gain, [*begun, mark])
     parts = expert_call(
-        length, done, last_routed, pieces, gain, w_gate[0], in_hbm(w_up[0]), in_hbm(w_down[0]),
+        length, done, last_routed, pieces, gain, w_gate[0], w_up[0], in_hbm(w_down[0]),
         order, rows_true,
     )
 

time: 80.6 us -> 79.9 us (level)
    unnamed x14 -> x16, local copies, waits for them, and re-layouts: 3.52 us -> 3.53 us
where the time goes in v12:
time: 79.9 us; the launch traced here: 79.6 us
  waiting for transfers between devices  39.4 us (49%)
  starting transfers between devices  20.2 us (25%)
  Pallas kernels  15.4 us (19%)
  local copies, waits for them, and re-layouts  3.55 us (4%)
  between operations  0.84 us (1%)
    ppermute x11, waiting for transfers between devices, across(): return lax.ppermute(x, 'seq', [(i, i ^ stride) for i in range(n)])  35.9 us
    ppermute x11, starting transfers between devices, across(): return lax.ppermute(x, 'seq', [(i, i ^ stride) for i in range(n)])  18.4 us
    pallas_call x3, Pallas kernels, attention(): pl.pallas_call(functools.partial(kernel, tuple(origins), per_key, rows_tr...  8.2 us
    pallas_call x1, Pallas kernels, expert_call(): pl.pallas_call(functools.partial(expert_kernel, tuple(origins), tuple(ord...  5.68 us
    unnamed x16, local copies, waits for them, and re-layouts  3.53 us
    ppermute x7, waiting for transfers between devices, swap(): return lax.ppermute(x, 'tp', [(0, 1), (1, 0)])  3.49 us
    ppermute x7, starting transfers between devices, swap(): return lax.ppermute(x, 'tp', [(0, 1), (1, 0)])  1.78 us
  transfers between devices with their start and end apart: 19, of which 10 were waited for; matrix products, arithmetic and copies ran while one was open for 0% of the time, Pallas kernels for 11%

profile of v12, /device:TPU:0, one launch (start us, length us, event | category | flops | bytes accessed | tf_op | source)
XLA Modules:
  0.0 79.6 jit_solution(5708878108730375588)
XLA Ops:
  0.0 1.1 %copy.10 = bf16[12,8,2,1024]{3,1,2,0:T(8,128)(2,1)S(1)} copy(bf16[12,8,2,1024]{3,2,1,0:T(2,128)(2,1)} %bitcast.31) | data formatting | bytes 786432
  1.1 4.1 %collective-permute-start = (bf16[96,2048]{1,0:T(8,128)(2,1)S(1)}, bf16[96,2048]{1,0:T(8,128)(2,1)S(1)}, u32[]{:S(2)}, u32[]{:S(2)}) collective-permute-start(bf16[96,2048]{1,0:T(8,128)(2,1)S(1)} %bitcast.16), channel_id=1, source_target_pairs={{0,8},{4,12},{8,0},{12,4},{1,9},{5,13},{9,1},{13,5},{2,10},{6,14},... | collective-permute-start | bytes 1179656 | tf_op jit(solution)/shard_map/ppermute | solution.py:383
  5.2 1.6 %collective-permute-start.3 = (bf16[96,2048]{1,0:T(8,128)(2,1)S(1)}, bf16[96,2048]{1,0:T(8,128)(2,1)S(1)}, u32[]{:S(2)}, u32[]{:S(2)}) collective-permute-start(bf16[96,2048]{1,0:T(8,128)(2,1)S(1)} %bitcast.17), channel_id=1, source_target_pairs={{0,4},{4,0},{8,12},{12,8},{1,5},{5,1},{9,13},{13,9},{2,6},{6,2},{1... | collective-permute-start | bytes 1179656 | tf_op jit(solution)/shard_map/ppermute | solution.py:383
  6.8 1.0 %copy-done.2 = bf16[1,64,4096]{2,1,0:T(8,128)(2,1)S(1)} copy-done((bf16[1,64,4096]{2,1,0:T(8,128)(2,1)S(1)}, bf16[1,64,4096]{2,1,0:T(8,128)(2,1)}, u32[]{:S(2)}) %copy-start.2) | copy-done | bytes 524312
  7.8 0.7 copy-done.5
  10.1 1.0 %collective-permute-done.1 = bf16[16,4096]{1,0:T(8,128)(2,1)S(1)} collective-permute-done((bf16[16,4096]{1,0:T(8,128)(2,1)S(1)}, bf16[16,4096]{1,0:T(8,128)(2,1)S(1)}, u32[]{:S(2)}, u32[]{:S(2)}) %collective-permute-start.1) | collective-permute-done | bytes 131104 | tf_op jit(solution)/shard_map/ppermute | solution.py:387
  11.7 22.4 %collective-permute-done.2.refs_1_ = bf16[32,4096]{1,0:T(8,128)(2,1)S(1)} collective-permute-done((bf16[32,4096]{1,0:T(8,128)(2,1)S(1)}, bf16[32,4096]{1,0:T(8,128)(2,1)S(1)}, u32[]{:S(2)}, u32[]{:S(2)}) %collective-permute-start.2) | collective-permute-done | bytes 262176 | tf_op jit(solution)/shard_map/ppermute | solution.py:383
  34.9 1.5 %collective-permute-start.9 = (bf16[96,2048]{1,0:T(8,128)(2,1)S(1)}, bf16[96,2048]{1,0:T(8,128)(2,1)S(1)}, u32[]{:S(2)}, u32[]{:S(2)}) collective-permute-start(bf16[96,2048]{1,0:T(8,128)(2,1)S(1)} %collective-permute-done.refs_4_.refs_1_), channel_id=1, source_target_pairs={{0,4},{4,0},{8,12},{12,8},{1,5},{5,1},{9,13},{13,9},{2,6},{6,2},{1... | collective-permute-start | bytes 1179656 | tf_op jit(solution)/shard_map/ppermute | solution.py:383
  37.1 3.9 %begin.1 = (f32[3072,256]{1,0:T(8,128)S(1)}, f32[3072,128]{1,0:T(8,128)S(1)}, f32[8,128]{1,0:T(8,128)S(1)}) custom-call(s32[1]{0:T(128)S(6)} %copy.12.length_ref, bf16[32,4096]{1,0:T(8,128)(2,1)S(1)} %constant_dynamic-update-slice_fusion.refs_0_, bf16[32,4096]{1,0:T(8,128)(2,1)S(1)} %collective-permute-done.2.refs_1_, ...), custom_call_target="tpu_custom_call" | custom-call | flops 1 | bytes 1 | tf_op jit(solution)/shard_map/begin/pallas_call | solution.py:195
  41.0 1.1 %collective-permute-start.8 = (bf16[32,4096]{1,0:T(8,128)(2,1)S(1)}, bf16[32,4096]{1,0:T(8,128)(2,1)S(1)}, u32[]{:S(2)}, u32[]{:S(2)}) collective-permute-start(bf16[32,4096]{1,0:T(8,128)(2,1)S(1)} %collective-permute-done.2.refs_1_), channel_id=1, source_target_pairs={{0,4},{4,0},{8,12},{12,8},{1,5},{5,1},{9,13},{13,9},{2,6},{6,2},{1... | collective-permute-start | bytes 786440 | tf_op jit(solution)/shard_map/ppermute | solution.py:383
  42.1 4.7 %collective-permute-done.9.whole_ref.refs_3_.refs_6_ = bf16[96,2048]{1,0:T(8,128)(2,1)S(1)} collective-permute-done((bf16[96,2048]{1,0:T(8,128)(2,1)S(1)}, bf16[96,2048]{1,0:T(8,128)(2,1)S(1)}, u32[]{:S(2)}, u32[]{:S(2)}) %collective-permute-start.9) | collective-permute-done | bytes 393248 | tf_op jit(solution)/shard_map/ppermute | solution.py:383
  47.4 0.9 %collective-permute-done.10.refs_4_.refs_7_ = bf16[48,2048]{1,0:T(8,128)(2,1)S(1)} collective-permute-done((bf16[48,2048]{1,0:T(8,128)(2,1)S(1)}, bf16[48,2048]{1,0:T(8,128)(2,1)S(1)}, u32[]{:S(2)}, u32[]{:S(2)}) %collective-permute-start.10) | collective-permute-done | bytes 196640 | tf_op jit(solution)/shard_map/ppermute | solution.py:387
  48.7 1.9 %finish.1.done_ref = bf16[96,4096]{1,0:T(8,128)(2,1)S(1)} custom-call(s32[1]{0:T(128)S(6)} %copy.12.length_ref, bf16[32,4096]{1,0:T(8,128)(2,1)S(1)} %constant_dynamic-update-slice_fusion.refs_0_, bf16[32,4096]{1,0:T(8,128)(2,1)S(1)} %collective-permute-done.2.refs_1_, bf16[32,4096]{1,0:T(8,128)(2,1)S(1)} %collective-permute-done.5.refs_2_, ...), custom_call_target="tpu_custom_call" | custom-call | flops 1 | bytes 1 | tf_op jit(solution)/shard_map/finish/pallas_call | solution.py:195
  50.6 1.0 %collective-permute-done.8.last_ref = bf16[32,4096]{1,0:T(8,128)(2,1)S(1)} collective-permute-done((bf16[32,4096]{1,0:T(8,128)(2,1)S(1)}, bf16[32,4096]{1,0:T(8,128)(2,1)S(1)}, u32[]{:S(2)}, u32[]{:S(2)}) %collective-permute-start.8) | collective-permute-done | bytes 262176 | tf_op jit(solution)/shard_map/ppermute | solution.py:383
  51.6 5.7 %experts.1 = (bf16[32,4096]{1,0:T(8,128)(2,1)S(1)}, bf16[32,1536]{1,0:T(8,128)(2,1)S(1)}, bf16[32,2560]{1,0:T(8,128)(2,1)S(1)}, bf16[32,4096]{1,0:T(8,128)(2,1)S...) custom-call(bf16[32,4096]{1,0:T(8,128)(2,1)S(1)} %collective-permute-done.8.last_ref, ...), custom_call_target="tpu_custom_call" | custom-call | flops 1610612736 | bytes 12582912 | tf_op jit(solution)/shard_map/experts/pallas_call | solution.py:315
  57.3 1.6 %collective-permute-start.12 = (bf16[32,2560]{1,0:T(8,128)(2,1)S(1)}, bf16[32,2560]{1,0:T(8,128)(2,1)S(1)}, u32[]{:S(2)}, u32[]{:S(2)}) collective-permute-start(bf16[32,2560]{1,0:T(8,128)(2,1)S(1)} %get-tuple-element.69), channel_id=1, source_target_pairs={{0,4},{4,0},{8,12},{12,8},{1,5},{5,1},{9,13},{13,9},{2,6},{6,2},{1... | collective-permute-start | bytes 491528 | tf_op jit(solution)/shard_map/ppermute | solution.py:383
  58.9 2.3 %collective-permute-start.15 = (bf16[32,1536]{1,0:T(8,128)(2,1)S(1)}, bf16[32,1536]{1,0:T(8,128)(2,1)S(1)}, u32[]{:S(2)}, u32[]{:S(2)}) collective-permute-start(bf16[32,1536]{1,0:T(8,128)(2,1)S(1)} %get-tuple-element.77), channel_id=1, source_target_pairs={{0,8},{4,12},{8,0},{12,4},{1,9},{5,13},{9,1},{13,5},{2,10},{6,14},... | collective-permute-start | bytes 294920 | tf_op jit(solution)/shard_map/ppermute | solution.py:383
  61.7 2.4 %attend.1.attended_ref = bf16[64,4096]{1,0:T(8,128)(2,1)S(1)} custom-call(s32[1]{0:T(128)S(6)} %copy.12.length_ref, bf16[64,4096]{1,0:T(8,128)(2,1)S(1)} %bitcast.25, bf16[96,2048]{1,0:T(8,128)(2,1)S(1)} %bitcast.21, bf16[96,2048]{1,0:T(8,128)(2,1)S(1)} %collective-permute-done.refs_4_.refs_1_, bf16[96,2048]{1,0:T(8,128)(2,1)S(1)} %collective-permute-done.3.refs_5_.refs_2_, ...), custom_call_target="tpu_custom_call" | custom-call | flops 805306368 | bytes 4194304 | tf_op jit(solution)/shard_map/attend/pallas_call | solution.py:195
  64.2 1.7 %collective-permute-start.16 = (bf16[32,4096]{1,0:T(8,128)(2,1)S(1)}, bf16[32,4096]{1,0:T(8,128)(2,1)S(1)}, u32[]{:S(2)}, u32[]{:S(2)}) collective-permute-start(bf16[32,4096]{1,0:T(8,128)(2,1)S(1)} %get-tuple-element.78), channel_id=1, source_target_pairs={{0,4},{4,0},{8,12},{12,8},{1,5},{5,1},{9,13},{13,9},{2,6},{6,2},{1... | collective-permute-start | bytes 786440 | tf_op jit(solution)/shard_map/ppermute | solution.py:383
  65.8 3.4 %collective-permute-start.13 = (bf16[16,2560]{1,0:T(8,128)(2,1)S(1)}, bf16[16,2560]{1,0:T(8,128)(2,1)S(1)}, u32[]{:S(2)}, u32[]{:S(2)}) collective-permute-start(bf16[16,2560]{1,0:T(8,128)(2,1)S(1)} %get-tuple-element.88), channel_id=1, source_target_pairs={{0,8},{4,12},{8,0},{12,4},{1,9},{5,13},{9,1},{13,5},{2,10},{6,14},... | collective-permute-start | bytes 245768 | tf_op jit(solution)/shard_map/ppermute | solution.py:383
  69.2 1.1 %collective-permute-done.17 = bf16[32,1536]{1,0:T(8,128)(2,1)S(1)} collective-permute-done((bf16[32,1536]{1,0:T(8,128)(2,1)S(1)}, bf16[32,1536]{1,0:T(8,128)(2,1)S(1)}, u32[]{:S(2)}, u32[]{:S(2)}) %collective-permute-start.17) | collective-permute-done | bytes 98336 | tf_op jit(solution)/shard_map/ppermute | solution.py:383
  70.3 6.6 %collective-permute-done.16 = bf16[32,4096]{1,0:T(8,128)(2,1)S(1)} collective-permute-done((bf16[32,4096]{1,0:T(8,128)(2,1)S(1)}, bf16[32,4096]{1,0:T(8,128)(2,1)S(1)}, u32[]{:S(2)}, u32[]{:S(2)}) %collective-permute-start.16) | collective-permute-done | bytes 262176 | tf_op jit(solution)/shard_map/ppermute | solution.py:383
  77.1 1.3 %collective-permute-done.18.theirs_ref = bf16[16,4096]{1,0:T(8,128)(2,1)S(1)} collective-permute-done((bf16[16,4096]{1,0:T(8,128)(2,1)S(1)}, bf16[16,4096]{1,0:T(8,128)(2,1)S(1)}, u32[]{:S(2)}, u32[]{:S(2)}) %collective-permute-start.18) | collective-permute-done | bytes 131104 | tf_op jit(solution)/shard_map/ppermute | solution.py:387
  78.4 1.2 %combine.1 = bf16[64,4096]{1,0:T(8,128)(2,1)} custom-call(bf16[16,2560]{1,0:T(8,128)(2,1)S(1)} %collective-permute-done.13.late_ref, bf16[16,2560]{1,0:T(8,128)(2,1)S(1)} %collective-permute-done.14.late_theirs_ref, f32[32,64]{1,0:T(8,128)S(1)} %get-tuple-element.72.comb_ref, bf16[64,4096]{1,0:T(8,128)(2,1)S(1)} %attend.1.attended_ref, ...), custom_call_target="tpu_custom_call" | custom-call | flops 33554432 | bytes 1048576 | tf_op jit(solution)/shard_map/combine/pallas_call | solution.py:510
  (44 shorter events, 4.6 us)
Async XLA Ops:
  0.0 48.7 %copy-start.4 = (f32[4096]{0:T(1024)S(1)}, f32[4096]{0:T(1024)}, u32[]{:S(2)}) copy-start(f32[4096]{0:T(1024)} %param.14) | copy-start | bytes 49156
  1.1 33.2 %collective-permute-start = (bf16[96,2048]{1,0:T(8,128)(2,1)S(1)}, bf16[96,2048]{1,0:T(8,128)(2,1)S(1)}, u32[]{:S(2)}, u32[]{:S(2)}) collective-permute-start(bf16[96,2048]{1,0:T(8,128)(2,1)S(1)} %bitcast.16), channel_id=1, source_target_pairs={{0,8},{4,12},{8,0},{12,4},{1,9},{5,13},{9,1},{13,5},{2,10},{6,14},... | collective-permute-start | bytes 1179656 | tf_op jit(solution)/shard_map/ppermute | solution.py:383
  5.2 29.1 %collective-permute-start.3 = (bf16[96,2048]{1,0:T(8,128)(2,1)S(1)}, bf16[96,2048]{1,0:T(8,128)(2,1)S(1)}, u32[]{:S(2)}, u32[]{:S(2)}) collective-permute-start(bf16[96,2048]{1,0:T(8,128)(2,1)S(1)} %bitcast.17), channel_id=1, source_target_pairs={{0,4},{4,0},{8,12},{12,8},{1,5},{5,1},{9,13},{13,9},{2,6},{6,2},{1... | collective-permute-start | bytes 1179656 | tf_op jit(solution)/shard_map/ppermute | solution.py:383
  6.8 27.5 %collective-permute-start.4 = (bf16[96,2048]{1,0:T(8,128)(2,1)S(1)}, bf16[96,2048]{1,0:T(8,128)(2,1)S(1)}, u32[]{:S(2)}, u32[]{:S(2)}) collective-permute-start(bf16[96,2048]{1,0:T(8,128)(2,1)S(1)} %bitcast.18), channel_id=1, source_target_pairs={{0,1},{1,0},{2,3},{3,2},{4,5},{5,4},{6,7},{7,6},{8,9},{9,8},{10,11... | collective-permute-start | bytes 1179656 | tf_op jit(solution)/shard_map/ppermute | solution.py:387
  6.8 1.0 %copy-start.2 = (bf16[1,64,4096]{2,1,0:T(8,128)(2,1)S(1)}, bf16[1,64,4096]{2,1,0:T(8,128)(2,1)}, u32[]{:S(2)}) copy-start(bf16[1,64,4096]{2,1,0:T(8,128)(2,1)} %param.9) | copy-start | bytes 1572868
  9.5 1.6 %collective-permute-start.1 = (bf16[16,4096]{1,0:T(8,128)(2,1)S(1)}, bf16[16,4096]{1,0:T(8,128)(2,1)S(1)}, u32[]{:S(2)}, u32[]{:S(2)}) collective-permute-start(bf16[16,4096]{1,0:T(8,128)(2,1)S(1)} %get-tuple-element.45), channel_id=1, source_target_pairs={{0,1},{1,0},{2,3},{3,2},{4,5},{5,4},{6,7},{7,6},{8,9},{9,8},{10,11... | collective-permute-start | bytes 393224 | tf_op jit(solution)/shard_map/ppermute | solution.py:387
  11.1 23.0 %collective-permute-start.2 = (bf16[32,4096]{1,0:T(8,128)(2,1)S(1)}, bf16[32,4096]{1,0:T(8,128)(2,1)S(1)}, u32[]{:S(2)}, u32[]{:S(2)}) collective-permute-start(bf16[32,4096]{1,0:T(8,128)(2,1)S(1)} %constant_dynamic-update-slice_fusion.refs_0_), channel_id=1, source_target_pairs={{0,8},{4,12},{8,0},{12,4},{1,9},{5,13},{9,1},{13,5},{2,10},{6,14},... | collective-permute-start | bytes 786440 | tf_op jit(solution)/shard_map/ppermute | solution.py:383
  11.5 22.8 %collective-permute-start.5 = (bf16[32,4096]{1,0:T(8,128)(2,1)S(1)}, bf16[32,4096]{1,0:T(8,128)(2,1)S(1)}, u32[]{:S(2)}, u32[]{:S(2)}) collective-permute-start(bf16[32,4096]{1,0:T(8,128)(2,1)S(1)} %constant_dynamic-update-slice_fusion.refs_0_), channel_id=1, source_target_pairs={{0,4},{4,0},{8,12},{12,8},{1,5},{5,1},{9,13},{13,9},{2,6},{6,2},{1... | collective-permute-start | bytes 786440 | tf_op jit(solution)/shard_map/ppermute | solution.py:383
  34.3 2.8 %collective-permute-start.6 = (bf16[96,2048]{1,0:T(8,128)(2,1)S(1)}, bf16[96,2048]{1,0:T(8,128)(2,1)S(1)}, u32[]{:S(2)}, u32[]{:S(2)}) collective-permute-start(bf16[96,2048]{1,0:T(8,128)(2,1)S(1)} %collective-permute-done.refs_4_.refs_1_), channel_id=1, source_target_pairs={{0,1},{1,0},{2,3},{3,2},{4,5},{5,4},{6,7},{7,6},{8,9},{9,8},{10,11... | collective-permute-start | bytes 1179656 | tf_op jit(solution)/shard_map/ppermute | solution.py:387
  34.4 2.7 %collective-permute-start.7 = (bf16[96,2048]{1,0:T(8,128)(2,1)S(1)}, bf16[96,2048]{1,0:T(8,128)(2,1)S(1)}, u32[]{:S(2)}, u32[]{:S(2)}) collective-permute-start(bf16[96,2048]{1,0:T(8,128)(2,1)S(1)} %collective-permute-done.3.refs_5_.refs_2_), channel_id=1, source_target_pairs={{0,1},{1,0},{2,3},{3,2},{4,5},{5,4},{6,7},{7,6},{8,9},{9,8},{10,11... | collective-permute-start | bytes 1179656 | tf_op jit(solution)/shard_map/ppermute | solution.py:387
  34.9 12.0 %collective-permute-start.9 = (bf16[96,2048]{1,0:T(8,128)(2,1)S(1)}, bf16[96,2048]{1,0:T(8,128)(2,1)S(1)}, u32[]{:S(2)}, u32[]{:S(2)}) collective-permute-start(bf16[96,2048]{1,0:T(8,128)(2,1)S(1)} %collective-permute-done.refs_4_.refs_1_), channel_id=1, source_target_pairs={{0,4},{4,0},{8,12},{12,8},{1,5},{5,1},{9,13},{13,9},{2,6},{6,2},{1... | collective-permute-start | bytes 1179656 | tf_op jit(solution)/shard_map/ppermute | solution.py:383
  37.1 14.5 %copy-start.1 = (bf16[1,4096,512]{2,1,0:T(8,128)(2,1)S(1)}, bf16[1,4096,512]{2,1,0:T(8,128)(2,1)}, u32[]{:S(2)}) copy-start(bf16[1,4096,512]{2,1,0:T(8,128)(2,1)} %param.16) | copy-start | bytes 12582916
  41.0 10.6 %copy-start = (bf16[1,4096,512]{2,1,0:T(8,128)(2,1)S(1)}, bf16[1,4096,512]{2,1,0:T(8,128)(2,1)}, u32[]{:S(2)}) copy-start(bf16[1,4096,512]{2,1,0:T(8,128)(2,1)} %param.15) | copy-start | bytes 12582916
  41.0 10.6 %collective-permute-start.8 = (bf16[32,4096]{1,0:T(8,128)(2,1)S(1)}, bf16[32,4096]{1,0:T(8,128)(2,1)S(1)}, u32[]{:S(2)}, u32[]{:S(2)}) collective-permute-start(bf16[32,4096]{1,0:T(8,128)(2,1)S(1)} %collective-permute-done.2.refs_1_), channel_id=1, source_target_pairs={{0,4},{4,0},{8,12},{12,8},{1,5},{5,1},{9,13},{13,9},{2,6},{6,2},{1... | collective-permute-start | bytes 786440 | tf_op jit(solution)/shard_map/ppermute | solution.py:383
  46.9 1.5 %collective-permute-start.10 = (bf16[48,2048]{1,0:T(8,128)(2,1)S(1)}, bf16[48,2048]{1,0:T(8,128)(2,1)S(1)}, u32[]{:S(2)}, u32[]{:S(2)}) collective-permute-start(bf16[48,2048]{1,0:T(8,128)(2,1)S(1)} %get-tuple-element.57), channel_id=1, source_target_pairs={{0,1},{1,0},{2,3},{3,2},{4,5},{5,4},{6,7},{7,6},{8,9},{9,8},{10,11... | collective-permute-start | bytes 589832 | tf_op jit(solution)/shard_map/ppermute | solution.py:387
  46.9 1.7 %collective-permute-start.11 = (bf16[48,2048]{1,0:T(8,128)(2,1)S(1)}, bf16[48,2048]{1,0:T(8,128)(2,1)S(1)}, u32[]{:S(2)}, u32[]{:S(2)}) collective-permute-start(bf16[48,2048]{1,0:T(8,128)(2,1)S(1)} %get-tuple-element.58), channel_id=1, source_target_pairs={{0,1},{1,0},{2,3},{3,2},{4,5},{5,4},{6,7},{7,6},{8,9},{9,8},{10,11... | collective-permute-start | bytes 589832 | tf_op jit(solution)/shard_map/ppermute | solution.py:387
  51.6 10.1 %copy-start.3 = (bf16[1,64,4096]{2,1,0:T(8,128)(2,1)S(1)}, bf16[1,64,4096]{2,1,0:T(8,128)(2,1)}, u32[]{:S(2)}) copy-start(bf16[1,64,4096]{2,1,0:T(8,128)(2,1)} %param.9) | copy-start | bytes 1572868
  57.3 6.8 %collective-permute-start.12 = (bf16[32,2560]{1,0:T(8,128)(2,1)S(1)}, bf16[32,2560]{1,0:T(8,128)(2,1)S(1)}, u32[]{:S(2)}, u32[]{:S(2)}) collective-permute-start(bf16[32,2560]{1,0:T(8,128)(2,1)S(1)} %get-tuple-element.69), channel_id=1, source_target_pairs={{0,4},{4,0},{8,12},{12,8},{1,5},{5,1},{9,13},{13,9},{2,6},{6,2},{1... | collective-permute-start | bytes 491528 | tf_op jit(solution)/shard_map/ppermute | solution.py:383
  58.9 10.3 %collective-permute-start.15 = (bf16[32,1536]{1,0:T(8,128)(2,1)S(1)}, bf16[32,1536]{1,0:T(8,128)(2,1)S(1)}, u32[]{:S(2)}, u32[]{:S(2)}) collective-permute-start(bf16[32,1536]{1,0:T(8,128)(2,1)S(1)} %get-tuple-element.77), channel_id=1, source_target_pairs={{0,8},{4,12},{8,0},{12,4},{1,9},{5,13},{9,1},{13,5},{2,10},{6,14},... | collective-permute-start | bytes 294920 | tf_op jit(solution)/shard_map/ppermute | solution.py:383
  61.2 9.1 %collective-permute-start.17 = (bf16[32,1536]{1,0:T(8,128)(2,1)S(1)}, bf16[32,1536]{1,0:T(8,128)(2,1)S(1)}, u32[]{:S(2)}, u32[]{:S(2)}) collective-permute-start(bf16[32,1536]{1,0:T(8,128)(2,1)S(1)} %get-tuple-element.79), channel_id=1, source_target_pairs={{0,12},{4,8},{8,4},{12,0},{1,13},{5,9},{9,5},{13,1},{2,14},{6,10},... | collective-permute-start | bytes 294920 | tf_op jit(solution)/shard_map/ppermute | solution.py:383
  64.2 12.7 %collective-permute-start.16 = (bf16[32,4096]{1,0:T(8,128)(2,1)S(1)}, bf16[32,4096]{1,0:T(8,128)(2,1)S(1)}, u32[]{:S(2)}, u32[]{:S(2)}) collective-permute-start(bf16[32,4096]{1,0:T(8,128)(2,1)S(1)} %get-tuple-element.78), channel_id=1, source_target_pairs={{0,4},{4,0},{8,12},{12,8},{1,5},{5,1},{9,13},{13,9},{2,6},{6,2},{1... | collective-permute-start | bytes 786440 | tf_op jit(solution)/shard_map/ppermute | solution.py:383
  65.8 11.3 %collective-permute-start.13 = (bf16[16,2560]{1,0:T(8,128)(2,1)S(1)}, bf16[16,2560]{1,0:T(8,128)(2,1)S(1)}, u32[]{:S(2)}, u32[]{:S(2)}) collective-permute-start(bf16[16,2560]{1,0:T(8,128)(2,1)S(1)} %get-tuple-element.88), channel_id=1, source_target_pairs={{0,8},{4,12},{8,0},{12,4},{1,9},{5,13},{9,1},{13,5},{2,10},{6,14},... | collective-permute-start | bytes 245768 | tf_op jit(solution)/shard_map/ppermute | solution.py:383
  69.2 7.9 %collective-permute-start.14 = (bf16[16,2560]{1,0:T(8,128)(2,1)S(1)}, bf16[16,2560]{1,0:T(8,128)(2,1)S(1)}, u32[]{:S(2)}, u32[]{:S(2)}) collective-permute-start(bf16[16,2560]{1,0:T(8,128)(2,1)S(1)} %get-tuple-element.87), channel_id=1, source_target_pairs={{0,9},{1,8},{4,13},{5,12},{8,1},{9,0},{12,5},{13,4},{2,11},{3,10},... | collective-permute-start | bytes 245768 | tf_op jit(solution)/shard_map/ppermute | solution.py:395
  77.0 1.4 %collective-permute-start.18 = (bf16[16,4096]{1,0:T(8,128)(2,1)S(1)}, bf16[16,4096]{1,0:T(8,128)(2,1)S(1)}, u32[]{:S(2)}, u32[]{:S(2)}) collective-permute-start(bf16[16,4096]{1,0:T(8,128)(2,1)S(1)} %pad_maximum_fusion.1), channel_id=1, source_target_pairs={{0,1},{1,0},{2,3},{3,2},{4,5},{5,4},{6,7},{7,6},{8,9},{9,8},{10,11... | collective-permute-start | bytes 393224 | tf_op jit(solution)/shard_map/ppermute | solution.py:387
  (2 other events, 1.4 us)
